TPU v7x, 32 devices: a whole 2x2x4 slice. The times are simulated.
32 devices in a mesh: row: 4 (over y, x), col: 8 (over z, core).
Axes of the slice: x: 2, y: 2, z: 4, core: 2. Of those that a mesh axis runs over, the one named last changes fastest.
Arguments:
- right_side: float32 [64, 20480], P(None, ('row', 'col')), may hold values from -6 to 6
- self_term: float32 [20480], P(('row', 'col')), may hold values from 1 to 4
- near_tiles: bfloat16 [4, 8, 32, 128, 128], P('row', 'col'), may hold values from -0.03125 to 0.03125
- near_rows: int32 [4, 8, 32], P('row', 'col'), may hold values from 0 to 39, as said below
- near_cols: int32 [4, 8, 32], P('row', 'col'), may hold values from 0 to 19, as said below
- near_count: int32 [4, 8], P('row', 'col'), may hold values from 8 to 32, as said below
- far_left: bfloat16 [4, 8, 64, 32, 128], P('row', 'col'), may hold values from -0.09375 to 0.09375
- far_right: bfloat16 [4, 8, 64, 32, 128], P('row', 'col'), may hold values from -0.09375 to 0.09375
- far_rows: int32 [4, 8, 64], P('row', 'col'), may hold values from 0 to 39, as said below
- far_cols: int32 [4, 8, 64], P('row', 'col'), may hold values from 0 to 19, as said below
- far_rank: int32 [4, 8, 64], P('row', 'col'), may hold values from 1 to 32
Outputs:
- solution: float32 [64, 20480], P(None, ('row', 'col'))
- residual: float32 [64, 20480], P(None, ('row', 'col'))
Inputs may be any that keep to these rules, and one draw needn't show every extreme that they name: Slots 0 to near_count - 1 of a device's near-field lists hold tiles and the others are ignored; on some device all 32 slots are occupied. Factor rows from far_rank on of a far tile are ignored. On one device, the (near_rows, near_cols) and (far_rows, far_cols) pairs of all slots are distinct from one another. `near_cols`: see near_rows. `far_rows`: see near_rows. `far_cols`: see near_rows.
All inputs are finite; a program needn't handle non-finite values.
Results may differ from a plain program's by a relative error of at most 0.02.
Values may be sent and summed in bfloat16 or wider, within the bound.
No kernel may reach another device: no remote copies, remote signals or barrier semaphores. Data moves between devices by JAX's collectives and lax.ppermute only.
A program may use at most 64 MiB of HBM per device.

v0:
```python
import jax
import jax.numpy as jnp
from jax import lax
from jax.sharding import PartitionSpec as P

ITERS = 3


def small_solve(matrix, rhs):
    lower = jnp.linalg.cholesky(matrix)
    return jax.scipy.linalg.cho_solve((lower, True), rhs)


def inner_gram(left_rows, right_rows):
    return jnp.dot(
        left_rows, right_rows.T, preferred_element_type=jnp.float32, precision=lax.Precision.HIGHEST
    )


def combine_rows(weights, rows_in):
    return jnp.dot(
        weights.T, rows_in, preferred_element_type=jnp.float32, precision=lax.Precision.HIGHEST
    )


def local(
    right_side,
    self_term,
    near_tiles,
    near_rows,
    near_cols,
    near_count,
    far_left,
    far_right,
    far_rows,
    far_cols,
    far_rank,
):
    cases, width = right_side.shape
    leaf = near_tiles.shape[-1]
    rank_most = far_left.shape[3]
    block_slots = 16
    tiles_all = near_tiles[0, 0]
    near_p_all = near_rows[0, 0]
    near_q_all = near_cols[0, 0]
    occupied = near_count[0, 0]
    left_all = far_left[0, 0]
    right_all = far_right[0, 0]
    far_p = far_rows[0, 0]
    far_q = far_cols[0, 0]
    keep = (lax.iota(jnp.int32, rank_most)[None, :] < far_rank[0, 0][:, None]).astype(jnp.float32)[
        None
    ]
    solution = jnp.zeros_like(right_side)
    residual = right_side
    direction = right_side
    res_gram = lax.psum(inner_gram(residual, residual), ("row", "col"))
    for turn in range(ITERS):
        rounded = direction.astype(jnp.bfloat16)
        row_group = lax.all_gather(rounded, "col", axis=1, tiled=True)
        col_group = lax.all_gather(rounded, "row", axis=1, tiled=True)
        row_cells_cl = row_group.reshape(cases, -1, leaf)
        col_cells_cl = col_group.reshape(cases, -1, leaf)
        row_acc = jnp.zeros(row_cells_cl.shape, jnp.float32)
        col_acc = jnp.zeros(col_cells_cl.shape, jnp.float32)

        def near_block(index, carry):
            row_total, col_total = carry
            start = index * block_slots
            tiles = lax.dynamic_slice_in_dim(tiles_all, start, block_slots, 0)
            near_p = lax.dynamic_slice_in_dim(near_p_all, start, block_slots, 0)
            near_q = lax.dynamic_slice_in_dim(near_q_all, start, block_slots, 0)
            live = (start + lax.iota(jnp.int32, block_slots) < occupied).astype(jnp.float32)[
                None, :, None
            ]
            to_rows = (
                jnp.einsum(
                    "sij,lsj->lsi",
                    tiles,
                    col_cells_cl[:, near_q],
                    preferred_element_type=jnp.float32,
                )
                * live
            )
            to_cols = (
                jnp.einsum(
                    "sij,lsi->lsj",
                    tiles,
                    row_cells_cl[:, near_p],
                    preferred_element_type=jnp.float32,
                )
                * live
            )
            return (row_total.at[:, near_p].add(to_rows), col_total.at[:, near_q].add(to_cols))

        block_count = (occupied + block_slots - 1) // block_slots
        row_acc, col_acc = lax.fori_loop(0, block_count, near_block, (row_acc, col_acc))
        coeff_q = (
            jnp.einsum(
                "skj,lsj->lsk",
                right_all,
                col_cells_cl[:, far_q],
                preferred_element_type=jnp.float32,
            )
            * keep
        ).astype(jnp.bfloat16)
        coeff_p = (
            jnp.einsum(
                "ski,lsi->lsk", left_all, row_cells_cl[:, far_p], preferred_element_type=jnp.float32
            )
            * keep
        ).astype(jnp.bfloat16)
        far_to_rows = jnp.einsum(
            "ski,lsk->lsi", left_all, coeff_q, preferred_element_type=jnp.float32
        )
        far_to_cols = jnp.einsum(
            "skj,lsk->lsj", right_all, coeff_p, preferred_element_type=jnp.float32
        )
        row_acc = row_acc.at[:, far_p].add(far_to_rows)
        col_acc = col_acc.at[:, far_q].add(far_to_cols)
        row_part = row_acc.reshape(cases, -1)
        col_part = col_acc.reshape(cases, -1)
        row_sum = lax.psum(row_part.astype(jnp.bfloat16), "col").astype(jnp.float32)
        col_sum = lax.psum(col_part.astype(jnp.bfloat16), "row").astype(jnp.float32)
        own_rows = lax.dynamic_slice_in_dim(row_sum, lax.axis_index("col") * width, width, 1)
        own_cols = lax.dynamic_slice_in_dim(col_sum, lax.axis_index("row") * width, width, 1)
        image = self_term[None, :] * direction + own_rows + own_cols
        curvature = lax.psum(inner_gram(direction, image), ("row", "col"))
        alpha = small_solve(curvature, res_gram)
        solution = solution + combine_rows(alpha, direction)
        residual = residual - combine_rows(alpha, image)
        if turn + 1 < ITERS:
            new_gram = lax.psum(inner_gram(residual, residual), ("row", "col"))
            beta = small_solve(res_gram, new_gram)
            direction = residual + combine_rows(beta, direction)
            res_gram = new_gram
    return (solution, residual)


def solution(mesh):
    in_specs = (
        P(None, ("row", "col")),
        P(("row", "col")),
        P("row", "col", None, None, None),
        P("row", "col", None),
        P("row", "col", None),
        P("row", "col"),
        P("row", "col", None, None, None),
        P("row", "col", None, None, None),
        P("row", "col", None),
        P("row", "col", None),
        P("row", "col", None),
    )
    out_specs = (P(None, ("row", "col")), P(None, ("row", "col")))
    return jax.shard_map(local, mesh=mesh, in_specs=in_specs, out_specs=out_specs, check_vma=False)
```

profile of v0, /device:TPU:0, one launch (start us, length us, event | category | flops | bytes accessed | tf_op | source)
XLA Modules:
  0.0 766.5 jit_solution(14164207369503967711)
XLA Ops:
  8.9 11.0 %all_gather.18 = bf16[64,2560]{1,0:T(8,128)(2,1)S(1)} all-gather(bf16[64,640]{1,0:T(8,128)(2,1)S(1)} %convert_element_type.127), channel_id=1, replica_groups=mesh['row'=4,'col'=8] {'row'}, dimensions={1}, use_global_device_ids=true | all-gather | bytes 409600 | tf_op jit(solution)/shard_map/all_gather | solution.py:61
  19.8 15.8 %all_gather.19 = bf16[64,5120]{1,0:T(8,128)(2,1)S(1)} all-gather(bf16[64,640]{1,0:T(8,128)(2,1)S(1)} %convert_element_type.127), channel_id=1, replica_groups=mesh['row'=4,'col'=8] {'col'}, dimensions={1}, use_global_device_ids=true | all-gather | bytes 737280 | tf_op jit(solution)/shard_map/all_gather | solution.py:60
  38.4 8.5 %while.36 = (s32[]{:T(128)}, f32[64,40,128]{2,0,1:T(8,128)}, f32[64,20,128]{2,0,1:T(8,128)S(1)}, s32[]{:T(128)}, s32[32]{0:T(128)S(1)}, /*index=5*/s32[32]{0:T(1...) while((s32[]{:T(128)}, f32[64,40,128]{2,0,1:T(8,128)}, ...), condition=%wide.region_3.4_spmd, body=%wide.region_0.3_spmd.sunk | while | flops 67635344 | bytes 6825871 | solution.py:97
  40.9 2.7 scatter_fusion
  43.6 1.7 gather_fusion.1
  45.5 1.3 scatter_fusion.1
  47.0 2.8 gather_fusion.7
  49.9 3.5 fusion.33
  53.5 7.0 scatter_fusion.7
  61.4 1.7 gather_fusion.6
  63.0 3.6 fusion.35
  66.7 7.0 scatter_fusion.6
  75.1 38.2 %all-reduce.10.cloned.1.call-done = bf16[64,2560]{1,0:T(8,128)(2,1)} async-done(((bf16[64,2560]{1,0:T(8,128)(2,1)}), bf16[64,2560]{1,0:T(8,128)(2,1)}) %all-reduce.10.cloned.1.call-update) | async-done | bytes 327696 | tf_op jit(solution)/shard_map/psum | solution.py:124
  113.3 59.3 %all-reduce.8.cloned.1.call-done = bf16[64,5120]{1,0:T(8,128)(2,1)} async-done(((bf16[64,5120]{1,0:T(8,128)(2,1)}), bf16[64,5120]{1,0:T(8,128)(2,1)}) %all-reduce.8.cloned.1.call-update) | async-done | bytes 655376 | tf_op jit(solution)/shard_map/psum | solution.py:123
  172.6 1.2 convolution_bitcast_fusion
  173.9 39.8 %all-reduce = (f32[64,64]{0,1:T(8,128)S(1)}, f32[64,64]{0,1:T(8,128)S(1)}) all-reduce(f32[64,64]{0,1:T(8,128)S(1)} %fusion.133, f32[64,64]{0,1:T(8,128)S(1)} %convolution_bitcast_fusion), channel_id=1, replica_groups=mesh['row'=4,'col'=8] {'row','col'}, use_global_device_ids=true, to_apply=%region_11.13 | all-reduce | flops 8192 | bytes 65536 | tf_op jit(solution)/shard_map/psum | solution.py:57
  213.9 5.8 cholesky.89
  221.0 4.9 custom-call.11
  226.4 1.3 convolution_subtract_fusion.2
  228.0 40.2 %psum.88 = f32[64,64]{0,1:T(8,128)S(1)} all-reduce(f32[64,64]{0,1:T(8,128)S(1)} %fusion.135), channel_id=1, replica_groups=mesh['row'=4,'col'=8] {'row','col'}, use_global_device_ids=true, to_apply=%region_12.15 | all-reduce | flops 4096 | bytes 32768 | tf_op jit(solution)/shard_map/psum | solution.py:133
  268.2 5.8 cholesky.100
  275.4 4.9 custom-call.12
  281.8 10.8 %all_gather.20 = bf16[64,2560]{1,0:T(8,128)(2,1)S(1)} all-gather(bf16[64,640]{1,0:T(8,128)(2,1)S(1)} %get-tuple-element.300), channel_id=1, replica_groups=mesh['row'=4,'col'=8] {'row'}, dimensions={1}, use_global_device_ids=true | all-gather | bytes 409600 | tf_op jit(solution)/shard_map/all_gather | solution.py:61
  292.6 15.3 %all_gather.21 = bf16[64,5120]{1,0:T(8,128)(2,1)S(1)} all-gather(bf16[64,640]{1,0:T(8,128)(2,1)S(1)} %get-tuple-element.300), channel_id=1, replica_groups=mesh['row'=4,'col'=8] {'col'}, dimensions={1}, use_global_device_ids=true | all-gather | bytes 737280 | tf_op jit(solution)/shard_map/all_gather | solution.py:60
  308.8 1.7 gather_fusion.9
  310.5 1.7 gather_fusion.8
  312.2 1.2 broadcast.165.clone.1
  313.5 8.5 %while.37 = (s32[]{:T(128)}, f32[64,40,128]{2,0,1:T(8,128)}, f32[64,20,128]{2,0,1:T(8,128)S(1)}, s32[]{:T(128)}, s32[32]{0:T(128)S(1)}, /*index=5*/s32[32]{0:T(1...) while((s32[]{:T(128)}, f32[64,40,128]{2,0,1:T(8,128)}, ...), condition=%wide.region_16.19_spmd, body=%wide.region_13.18_spmd.sunk | while | flops 67635344 | bytes 6825871 | solution.py:97
  316.0 2.7 scatter_fusion.2
  318.6 1.7 gather_fusion.3
  320.6 1.3 scatter_fusion.3
  322.0 3.7 fusion.29
  325.7 7.0 scatter_fusion.9
  333.8 3.6 fusion.31
  337.4 7.0 scatter_fusion.8
  345.4 5.8 cholesky.122
  352.9 4.9 custom-call.14
  357.8 26.4 %all-reduce.14.cloned.1.call-done = bf16[64,2560]{1,0:T(8,128)(2,1)} async-done(((bf16[64,2560]{1,0:T(8,128)(2,1)}), bf16[64,2560]{1,0:T(8,128)(2,1)}) %all-reduce.14.cloned.1.call-update) | async-done | bytes 327696 | tf_op jit(solution)/shard_map/psum | solution.py:124
  384.2 59.1 %all-reduce.12.cloned.1.call-done = bf16[64,5120]{1,0:T(8,128)(2,1)} async-done(((bf16[64,5120]{1,0:T(8,128)(2,1)}), bf16[64,5120]{1,0:T(8,128)(2,1)}) %all-reduce.12.cloned.1.call-update) | async-done | bytes 655376 | tf_op jit(solution)/shard_map/psum | solution.py:123
  443.2 1.2 fusion.72
  444.5 39.4 %psum.91 = f32[64,64]{0,1:T(8,128)S(1)} all-reduce(f32[64,64]{0,1:T(8,128)S(1)} %fusion.72), channel_id=1, replica_groups=mesh['row'=4,'col'=8] {'row','col'}, use_global_device_ids=true, to_apply=%region_21.24 | all-reduce | flops 4096 | bytes 32768 | tf_op jit(solution)/shard_map/psum | solution.py:128
  484.0 5.8 cholesky.111
  491.2 4.9 custom-call.13
  496.5 1.3 convolution_subtract_fusion.1
  498.1 40.1 %psum.92 = f32[64,64]{1,0:T(8,128)S(1)} all-reduce(f32[64,64]{1,0:T(8,128)S(1)} %fusion.136), channel_id=1, replica_groups=mesh['row'=4,'col'=8] {'row','col'}, use_global_device_ids=true, to_apply=%region_22.25 | all-reduce | flops 4096 | bytes 32768 | tf_op jit(solution)/shard_map/psum | solution.py:133
  539.7 10.8 %all_gather.22 = bf16[64,2560]{1,0:T(8,128)(2,1)S(1)} all-gather(bf16[64,640]{1,0:T(8,128)(2,1)S(1)} %get-tuple-element.302), channel_id=1, replica_groups=mesh['row'=4,'col'=8] {'row'}, dimensions={1}, use_global_device_ids=true | all-gather | bytes 409600 | tf_op jit(solution)/shard_map/all_gather | solution.py:61
  550.5 15.3 %all_gather.23 = bf16[64,5120]{1,0:T(8,128)(2,1)S(1)} all-gather(bf16[64,640]{1,0:T(8,128)(2,1)S(1)} %get-tuple-element.302), channel_id=1, replica_groups=mesh['row'=4,'col'=8] {'col'}, dimensions={1}, use_global_device_ids=true | all-gather | bytes 737280 | tf_op jit(solution)/shard_map/all_gather | solution.py:60
  566.0 1.8 gather_fusion.11
  567.8 1.8 gather_fusion.10
  570.9 9.6 %while.38 = (s32[]{:T(128)}, f32[64,40,128]{2,0,1:T(8,128)}, f32[64,20,128]{2,0,1:T(8,128)S(1)}, s32[]{:T(128)}, s32[32]{0:T(128)S(1)}, /*index=5*/s32[32]{0:T(1...) while((s32[]{:T(128)}, f32[64,40,128]{2,0,1:T(8,128)}, ...), condition=%wide.region_26.29_spmd, body=%wide.region_23.28_spmd.sunk | while | flops 67635344 | bytes 6825707 | solution.py:97
  573.9 2.7 scatter_fusion.4
  576.6 1.7 gather_fusion.5
  579.1 1.3 scatter_fusion.5
  580.5 3.7 fusion.25
  584.2 7.0 scatter_fusion.11
  592.4 3.6 fusion.27
  596.0 7.0 scatter_fusion.10
  604.7 39.0 %all-reduce.18.cloned.1.call-done = bf16[64,2560]{1,0:T(8,128)(2,1)} async-done(((bf16[64,2560]{1,0:T(8,128)(2,1)}), bf16[64,2560]{1,0:T(8,128)(2,1)}) %all-reduce.18.cloned.1.call-update) | async-done | bytes 327696 | tf_op jit(solution)/shard_map/psum | solution.py:124
  643.7 59.2 %all-reduce.16.cloned.1.call-done = bf16[64,5120]{1,0:T(8,128)(2,1)} async-done(((bf16[64,5120]{1,0:T(8,128)(2,1)}), bf16[64,5120]{1,0:T(8,128)(2,1)}) %all-reduce.16.cloned.1.call-update) | async-done | bytes 655376 | tf_op jit(solution)/shard_map/psum | solution.py:123
  702.9 1.2 fusion.73
  704.2 39.4 %psum.95 = f32[64,64]{0,1:T(8,128)S(1)} all-reduce(f32[64,64]{0,1:T(8,128)S(1)} %fusion.73), channel_id=1, replica_groups=mesh['row'=4,'col'=8] {'row','col'}, use_global_device_ids=true, to_apply=%region_31.34 | all-reduce | flops 4096 | bytes 32768 | tf_op jit(solution)/shard_map/psum | solution.py:128
  743.7 5.8 cholesky.133
  750.9 4.9 custom-call.15
  757.2 1.9 convolution_subtract_fusion
  (176 shorter events, 35.6 us)
Async XLA Ops:
  7.2 42.7 %copy-start = (bf16[1,1,64,32,128]{4,3,2,1,0:T(8,128)(2,1)S(1)}, bf16[1,1,64,32,128]{4,3,2,1,0:T(8,128)(2,1)}, u32[]{:S(2)}) copy-start(bf16[1,1,64,32,128]{4,3,2,1,0:T(8,128)(2,1)} %param.26) | copy-start | bytes 1572868
  7.2 106.1 %all-reduce.10.cloned.1.call-start = ((), (), s32[]{:S(2)}) async-start(), calls=%async_computation.1 | async-start | bytes 655360 | tf_op jit(solution)/shard_map/psum | solution.py:124
  36.8 1.6 copy-start.1
  36.8 1.6 copy-start.28
  38.4 8.5 %copy-start.37 = (s32[1,1,64]{2,1,0:T(1,128)S(1)}, s32[1,1,64]{2,1,0:T(1,128)}, u32[]{:S(2)}) copy-start(s32[1,1,64]{2,1,0:T(1,128)} %param.29) | copy-start | bytes 772
  38.4 8.6 %copy-start.38 = (s32[1,1,64]{2,1,0:T(1,128)S(1)}, s32[1,1,64]{2,1,0:T(1,128)}, u32[]{:S(2)}) copy-start(s32[1,1,64]{2,1,0:T(1,128)} %param.28) | copy-start | bytes 772
  46.9 2.9 copy-start.36
  46.9 3.0 copy-start.5
  46.9 278.7 %copy-start.32 = (s32[64]{0:T(128)}, s32[64]{0:T(128)S(1)}, u32[]{:S(2)}) copy-start(s32[64]{0:T(128)S(1)} %fusion.130) | copy-start | bytes 772
  47.0 290.5 %copy-start.30 = (s32[64]{0:T(128)}, s32[64]{0:T(128)S(1)}, u32[]{:S(2)}) copy-start(s32[64]{0:T(128)S(1)} %fusion.129) | copy-start | bytes 772
  47.0 261.8 %copy-start.34 = (s32[1024]{0:T(1024)}, s32[1024]{0:T(1024)S(1)}, u32[]{:S(2)}) copy-start(s32[1024]{0:T(1024)S(1)} %pad_clamp_fusion.6) | copy-start | bytes 12292
  61.3 111.3 %all-reduce.8.cloned.1.call-start = ((), (), s32[]{:S(2)}) async-start(), calls=%async_computation | async-start | bytes 1310720 | tf_op jit(solution)/shard_map/psum | solution.py:123
  61.3 249.2 %copy-start.35 = (s32[1024]{0:T(1024)}, s32[1024]{0:T(1024)S(1)}, u32[]{:S(2)}) copy-start(s32[1024]{0:T(1024)S(1)} %pad_clamp_fusion.7) | copy-start | bytes 12292
  63.0 3.6 copy-start.3
  73.7 1.0 copy-start.10
  73.7 98.9 %copy-start.26 = (f32[640]{0:T(1024)S(1)}, f32[640]{0:T(1024)}, u32[]{:S(2)}) copy-start(f32[640]{0:T(1024)} %param.21) | copy-start | bytes 7684
  74.7 309.5 %all-reduce.14.cloned.1.call-start = ((), (), s32[]{:S(2)}) async-start(), calls=%async_computation.3 | async-start | bytes 655360 | tf_op jit(solution)/shard_map/psum | solution.py:124
  226.4 55.4 %copy-start.22 = (f32[64,64]{1,0:T(8,128)}, f32[64,64]{1,0:T(8,128)S(1)}, u32[]{:S(2)}) copy-start(f32[64,64]{1,0:T(8,128)S(1)} %fusion.117) | copy-start | bytes 49156
  227.7 80.9 %copy-start.13 = (f32[64,640]{1,0:T(8,128)}, f32[64,640]{1,0:T(8,128)S(1)}, u32[]{:S(2)}) copy-start(f32[64,640]{1,0:T(8,128)S(1)} %convolution_subtract_fusion.2) | copy-start | bytes 491524
  268.2 40.4 %copy-start.18 = (f32[64,64]{0,1:T(8,128)}, f32[64,64]{0,1:T(8,128)S(1)}, u32[]{:S(2)}) copy-start(f32[64,64]{0,1:T(8,128)S(1)} %psum.88) | copy-start | bytes 49156
  308.8 3.3 copy-start.9
  332.7 1.2 copy-start.6
  333.5 3.9 copy-start.4
  333.5 109.7 %all-reduce.12.cloned.1.call-start = ((), (), s32[]{:S(2)}) async-start(), calls=%async_computation.2 | async-start | bytes 1310720 | tf_op jit(solution)/shard_map/psum | solution.py:123
  344.4 0.9 copy-start.19
  344.5 0.9 copy-start.27
  344.5 98.8 %copy-start.12 = (f32[64,640]{1,0:T(8,128)S(1)}, f32[64,640]{1,0:T(8,128)}, u32[]{:S(2)}) copy-start(f32[64,640]{1,0:T(8,128)} %get-tuple-element.301) | copy-start | bytes 491524
  345.4 151.1 %copy-start.14 = (f32[64,640]{1,0:T(8,128)S(1)}, f32[64,640]{1,0:T(8,128)}, u32[]{:S(2)}) copy-start(f32[64,640]{1,0:T(8,128)} %copy-done.13) | copy-start | bytes 491524
  351.3 292.4 %all-reduce.18.cloned.1.call-start = ((), (), s32[]{:S(2)}) async-start(), calls=%async_computation.5 | async-start | bytes 655360 | tf_op jit(solution)/shard_map/psum | solution.py:124
  496.5 43.1 %copy-start.24 = (f32[64,64]{1,0:T(8,128)}, f32[64,64]{1,0:T(8,128)S(1)}, u32[]{:S(2)}) copy-start(f32[64,64]{1,0:T(8,128)S(1)} %fusion.107) | copy-start | bytes 49156
  497.8 67.9 %copy-start.15 = (f32[64,640]{1,0:T(8,128)}, f32[64,640]{1,0:T(8,128)S(1)}, u32[]{:S(2)}) copy-start(f32[64,640]{1,0:T(8,128)S(1)} %convolution_subtract_fusion.1) | copy-start | bytes 491524
  538.2 27.5 %copy-start.20 = (f32[64,64]{1,0:T(8,128)}, f32[64,64]{1,0:T(8,128)S(1)}, u32[]{:S(2)}) copy-start(f32[64,64]{1,0:T(8,128)S(1)} %psum.92) | copy-start | bytes 49156
  566.0 3.6 copy-start.8
  572.9 0.5 copy-start.29
  580.5 3.7 copy-start.33
  591.2 1.2 copy-start.7
  592.0 3.9 copy-start.2
  592.0 3.9 copy-start.31
  592.1 110.9 %all-reduce.16.cloned.1.call-start = ((), (), s32[]{:S(2)}) async-start(), calls=%async_computation.4 | async-start | bytes 1310720 | tf_op jit(solution)/shard_map/psum | solution.py:123
  603.0 1.0 copy-start.11
  603.0 1.0 copy-start.23
  603.0 1.4 copy-start.25
  603.0 99.9 %copy-start.17 = (f32[64,640]{1,0:T(8,128)S(1)}, f32[64,640]{1,0:T(8,128)}, u32[]{:S(2)}) copy-start(f32[64,640]{1,0:T(8,128)} %get-tuple-element.303) | copy-start | bytes 491524
  604.0 151.8 %copy-start.21 = (f32[64,64]{1,0:T(8,128)S(1)}, f32[64,64]{1,0:T(8,128)}, u32[]{:S(2)}) copy-start(f32[64,64]{1,0:T(8,128)} %copy-done.20) | copy-start | bytes 49156
  604.0 153.2 %copy-start.16 = (f32[64,640]{1,0:T(8,128)S(1)}, f32[64,640]{1,0:T(8,128)}, u32[]{:S(2)}) copy-start(f32[64,640]{1,0:T(8,128)} %copy-done.15) | copy-start | bytes 491524
Sparse Core Ops, SparseCore 0:
  61.4 51.8 all-reduce.9
  115.8 56.8 all-reduce.7
  333.6 50.5 all-reduce.13
  386.4 56.8 all-reduce.11
  592.2 51.5 all-reduce.17
  646.1 56.8 all-reduce.15
where the time goes:
time: 778 us; the launch traced here: 766 us
  waiting for transfers between devices  281 us (36%)
  blocking collectives  278 us (36%)
  other arithmetic  125 us (16%)
  matrix products  39.5 us (5%)
  local copies, waits for them, and re-layouts  26 us (3%)
  between operations  16.1 us (2%)
    psum x3, waiting for transfers between devices, local(): row_sum = lax.psum(row_part.astype(jnp.bfloat16), 'col').astype(jnp.float32)  178 us
    psum x3, waiting for transfers between devices, local(): col_sum = lax.psum(col_part.astype(jnp.bfloat16), 'row').astype(jnp.float32)  104 us
    psum x2, blocking collectives, local(): new_gram = lax.psum(inner_gram(residual, residual), ('row', 'col'))  80.3 us
    psum x2, blocking collectives, local(): curvature = lax.psum(inner_gram(direction, image), ('row', 'col'))  78.9 us
    all_gather x3, blocking collectives, local(): row_group = lax.all_gather(rounded, 'col', axis=1, tiled=True)  46.4 us
    psum x1, blocking collectives, local(): res_gram = lax.psum(inner_gram(residual, residual), ('row', 'col'))  39.8 us
    another operation x15, other arithmetic, small_solve(): lower = jnp.linalg.cholesky(matrix)  32.6 us
    all_gather x3, blocking collectives, local(): col_group = lax.all_gather(rounded, 'row', axis=1, tiled=True)  32.6 us
  transfers between devices with their start and end apart: 6, of which 6 were waited for; matrix products, arithmetic and copies ran while one was open for 6% of the time, Pallas kernels for 0%

commit v1 on v0

v1 whole, which is shorter than its diff:
```python
import functools

import jax
import jax.numpy as jnp
from jax import lax
from jax.experimental import pallas as pl
from jax.experimental.pallas import tpu as pltpu
from jax.sharding import PartitionSpec as P

SHIFT = 2.5
VMEM_BYTES = 48 * 1024 * 1024
HIGHEST = lax.Precision.HIGHEST

vmem = pl.BlockSpec(memory_space=pltpu.VMEM)
smem = pl.BlockSpec(memory_space=pltpu.SMEM)
params = pltpu.CompilerParams(vmem_limit_bytes=VMEM_BYTES)


def f32(*shape):
    return jax.ShapeDtypeStruct(shape, jnp.float32)


def bf16(*shape):
    return jax.ShapeDtypeStruct(shape, jnp.bfloat16)


def contract(left, right, dims, precision=None):
    return lax.dot_general(
        left, right, (dims, ((), ())), precision=precision, preferred_element_type=jnp.float32
    )


def partner_permute(value, axis, flip):
    size = lax.axis_size(axis)
    return lax.ppermute(value, axis, [(i, i ^ flip) for i in range(size)])


def dense_kernel(count_ref, rank_ref, near_ref, left_ref, right_ref, tile_ref, turned_ref):
    near_slots, far_slots = near_ref.shape[0], left_ref.shape[0]

    def near(s, _):
        tile = near_ref[s].astype(jnp.float32)
        tile = jnp.where(s < count_ref[0], tile, 0.0)
        tile_ref[s] = tile.astype(jnp.bfloat16)
        turned_ref[s] = tile.T.astype(jnp.bfloat16)
        return 0

    def far(s, _):
        row = lax.broadcasted_iota(jnp.int32, left_ref.shape[1:], 0)
        left = jnp.where(row < rank_ref[s], left_ref[s].astype(jnp.float32), 0.0)
        right = right_ref[s]
        left = left.astype(jnp.bfloat16)
        tile = contract(left, right, ((0,), (0,)))
        tile_ref[near_slots + s] = tile.astype(jnp.bfloat16)
        turned_ref[near_slots + s] = tile.T.astype(jnp.bfloat16)
        return 0

    lax.fori_loop(0, near_slots, near, 0, unroll=4)
    lax.fori_loop(0, far_slots, far, 0, unroll=4)


def tile_sums(from_ref, to_ref, tile_ref, cells, total):
    total[...] = jnp.zeros_like(total)

    def step(s, _):
        product = contract(cells[from_ref[s]], tile_ref[s], ((1,), (0,)))
        total[to_ref[s]] = total[to_ref[s]] + product
        return 0

    lax.fori_loop(0, tile_ref.shape[0], step, 0, unroll=8)


def place(block, ref, cells):
    leaf = cells.shape[-1]
    per = ref.shape[-1] // leaf
    for j in range(per):
        cells[block * per + j] = ref[:, j * leaf : (j + 1) * leaf]


def rows_kernel(place_ref, from_ref, to_ref, tile_ref, *refs):
    blocks, (send_ref, keep_ref, cells, total) = refs[:-4], refs[-4:]
    leaf = cells.shape[-1]
    me, core = place_ref[0], place_ref[1] % 2
    for flip, ref in enumerate(blocks):
        place(me ^ flip, ref, cells)
    tile_sums(from_ref, to_ref, tile_ref, cells, total)
    chips, _, width = send_ref.shape
    per = width // leaf
    for z in range(chips):
        for j in range(per):
            part = slice(j * leaf, (j + 1) * leaf)
            send_ref[z, :, part] = total[(2 * z + 1 - core) * per + j].astype(jnp.bfloat16)
            keep_ref[z, :, part] = total[(2 * z + core) * per + j]


def cols_kernel(place_ref, from_ref, to_ref, tile_ref, *refs):
    chips = lax.axis_size("col") // 2
    count = 2 * chips
    blocks, rest = refs[:count], refs[count:]
    outs, (cells, total) = rest[:-2], rest[-2:]
    leaf = cells.shape[-1]
    me = place_ref[1]
    for flip, ref in enumerate(blocks):
        place(me ^ flip, ref, cells)
    tile_sums(from_ref, to_ref, tile_ref, cells, total)
    per = outs[0].shape[-1] // leaf
    for flip, out in enumerate(outs):
        for j in range(per):
            part = total[(place_ref[0] ^ flip) * per + j]
            out[:, j * leaf : (j + 1) * leaf] = part.astype(out.dtype)


def pair_kernel(place_ref, keep_ref, got_ref, *outs):
    chip = place_ref[1] // 2
    for flip, out in enumerate(outs):
        z = chip ^ flip
        out[...] = (keep_ref[z] + got_ref[z].astype(jnp.float32)).astype(out.dtype)


def solve_kernel(matrix_ref, rhs_ref, out_ref):
    size = matrix_ref.shape[0]
    work = jnp.concatenate([matrix_ref[...], rhs_ref[...]], axis=1)
    row = lax.broadcasted_iota(jnp.int32, work.shape, 0)
    for k in range(size):
        pivot_row = work[k : k + 1, :] / work[k : k + 1, k : k + 1]
        work = jnp.where(row == k, pivot_row, work - work[:, k : k + 1] * pivot_row)
    out_ref[...] = work[:, size:]


def small_solve(matrix, rhs):
    return pl.pallas_call(
        solve_kernel,
        out_shape=f32(*rhs.shape),
        in_specs=[vmem, vmem],
        out_specs=vmem,
        compiler_params=params,
        name="small_solve",
    )(matrix, rhs)


def inner(left_rows, right_rows):
    return jnp.dot(
        left_rows, right_rows.T, preferred_element_type=jnp.float32, precision=HIGHEST
    )


def combine(weights, rows_in):
    return jnp.dot(weights.T, rows_in, preferred_element_type=jnp.float32, precision=HIGHEST)


def sum_all(value):
    value = value + partner_permute(value, "col", 1)
    parts = [partner_permute(value, "col", 2 * k) for k in range(1, lax.axis_size("col") // 2)]
    value = functools.reduce(jnp.add, parts, value)
    parts = [partner_permute(value, "row", k) for k in range(1, lax.axis_size("row"))]
    return functools.reduce(jnp.add, parts, value)


def local(
    right_side,
    self_term,
    near_tiles,
    near_rows,
    near_cols,
    near_count,
    far_left,
    far_right,
    far_rows,
    far_cols,
    far_rank,
):
    cases, width = right_side.shape
    leaf = near_tiles.shape[-1]
    per = width // leaf
    rows, cols = lax.axis_size("row"), lax.axis_size("col")
    chips = cols // 2
    slots = near_tiles.shape[2] + far_left.shape[2]
    here = jnp.stack([lax.axis_index("row"), lax.axis_index("col")]).astype(jnp.int32)
    list_p = jnp.concatenate([near_rows[0, 0], far_rows[0, 0]])
    list_q = jnp.concatenate([near_cols[0, 0], far_cols[0, 0]])
    tiles, turned = pl.pallas_call(
        dense_kernel,
        out_shape=[bf16(slots, leaf, leaf)] * 2,
        in_specs=[smem, smem, vmem, vmem, vmem],
        out_specs=[vmem, vmem],
        compiler_params=params,
        name="dense_tiles",
    )(near_count[0], far_rank[0, 0], near_tiles[0, 0], far_left[0, 0], far_right[0, 0])

    def off_diagonal(vector):
        over_row = [partner_permute(vector, "row", k) for k in range(1, rows)]
        over_chip = [partner_permute(vector, "col", 2 * k) for k in range(1, chips)]
        other_core = [partner_permute(v, "col", 1) for v in [vector] + over_chip]
        send, keep = pl.pallas_call(
            rows_kernel,
            out_shape=[bf16(chips, cases, width), f32(chips, cases, width)],
            in_specs=[smem, smem, smem] + [vmem] * (1 + rows),
            out_specs=[vmem, vmem],
            scratch_shapes=[
                pltpu.VMEM((rows * per, cases, leaf), jnp.bfloat16),
                pltpu.VMEM((cols * per, cases, leaf), jnp.float32),
            ],
            compiler_params=params,
            cost_estimate=pl.CostEstimate(
                flops=2 * slots * cases * leaf * leaf * 8, bytes_accessed=0, transcendentals=0
            ),
            name="rows_half",
        )(here, list_q, list_p, turned, vector, *over_row)
        got = partner_permute(send, "col", 1)
        row_group = [None] * cols
        for k, (a, b) in enumerate(zip([vector] + over_chip, other_core)):
            row_group[2 * k], row_group[2 * k + 1] = a, b
        col_outs = pl.pallas_call(
            cols_kernel,
            out_shape=[f32(cases, width)] + [bf16(cases, width)] * (rows - 1),
            in_specs=[smem, smem, smem] + [vmem] * (1 + cols),
            out_specs=[vmem] * rows,
            scratch_shapes=[
                pltpu.VMEM((cols * per, cases, leaf), jnp.bfloat16),
                pltpu.VMEM((rows * per, cases, leaf), jnp.float32),
            ],
            compiler_params=params,
            cost_estimate=pl.CostEstimate(
                flops=2 * slots * cases * leaf * leaf * 8, bytes_accessed=0, transcendentals=0
            ),
            name="cols_half",
        )(here, list_p, list_q, tiles, *row_group)
        pair_outs = pl.pallas_call(
            pair_kernel,
            out_shape=[f32(cases, width)] + [bf16(cases, width)] * (chips - 1),
            in_specs=[smem, vmem, vmem],
            out_specs=[vmem] * chips,
            compiler_params=params,
            name="pair_sums",
        )(here, keep, got)
        arrived = [partner_permute(m, "col", 2 * k) for k, m in enumerate(pair_outs) if k]
        arrived += [partner_permute(m, "row", k) for k, m in enumerate(col_outs) if k]
        total = pair_outs[0] + col_outs[0]
        for message in arrived:
            total = total + message.astype(jnp.float32)
        return total

    diagonal = self_term[None, :]
    b = right_side
    w0 = diagonal * b + off_diagonal(b.astype(jnp.bfloat16))
    u0 = w0 - SHIFT * b
    gram = sum_all(jnp.concatenate([inner(b, b), inner(b, w0)], axis=1))
    rr0, curvature0 = gram[:, :cases], gram[:, cases:]
    aw0 = diagonal * u0 + off_diagonal(u0.astype(jnp.bfloat16)) + SHIFT * w0
    alpha0 = small_solve(curvature0, rr0)
    x1 = combine(alpha0, b)
    r1 = b - combine(alpha0, w0)
    w1 = w0 - combine(alpha0, aw0)
    u1 = w1 - SHIFT * r1
    gram = sum_all(jnp.concatenate([inner(r1, r1), inner(r1, w1)], axis=1))
    rr1, r1w1 = gram[:, :cases], gram[:, cases:]
    aw1 = diagonal * u1 + off_diagonal(u1.astype(jnp.bfloat16)) + SHIFT * w1
    beta0 = small_solve(rr0, rr1)
    curvature1 = r1w1 - combine(beta0, jnp.dot(curvature0, beta0, precision=HIGHEST))
    alpha1 = small_solve(curvature1, rr1)
    d1 = r1 + combine(beta0, b)
    s1 = w1 + combine(beta0, w0)
    x2 = x1 + combine(alpha1, d1)
    r2 = r1 - combine(alpha1, s1)
    w2 = w1 - combine(alpha1, aw1 + combine(beta0, aw0))
    gram = sum_all(jnp.concatenate([inner(r2, r2), inner(r2, w2)], axis=1))
    rr2, r2w2 = gram[:, :cases], gram[:, cases:]
    beta1 = small_solve(rr1, rr2)
    curvature2 = r2w2 - combine(beta1, jnp.dot(curvature1, beta1, precision=HIGHEST))
    alpha2 = small_solve(curvature2, rr2)
    d2 = r2 + combine(beta1, d1)
    s2 = w2 + combine(beta1, s1)
    return (x2 + combine(alpha2, d2), r2 - combine(alpha2, s2))


def solution(mesh):
    in_specs = (
        P(None, ("row", "col")),
        P(("row", "col")),
        P("row", "col", None, None, None),
        P("row", "col", None),
        P("row", "col", None),
        P("row", "col"),
        P("row", "col", None, None, None),
        P("row", "col", None, None, None),
        P("row", "col", None),
        P("row", "col", None),
        P("row", "col", None),
    )
    out_specs = (P(None, ("row", "col")), P(None, ("row", "col")))
    return jax.shard_map(local, mesh=mesh, in_specs=in_specs, out_specs=out_specs, check_vma=False)
```

time: 778 us -> 181 us (0.23); the launches traced: 766 us -> 181 us
  blocking collectives: 278 us -> 0 us
  waiting for transfers between devices: 281 us -> 28.1 us
  other arithmetic: 125 us -> 2.56 us
  starting transfers between devices: 0.71 us -> 76.1 us
  Pallas kernels: 0 us -> 57.4 us
  matrix products: 39.5 us -> 8.58 us
  local copies, waits for them, and re-layouts: 26 us -> 5.94 us
  between operations: 16.1 us -> 1.84 us
    psum x6 -> x0, waiting for transfers between devices: 281 us -> none  [the longest x3 178 us: local(): row_sum = lax.psum(row_part.astype(jnp.bfloat16), 'col').astype(jnp.float32)]
    psum x5 -> x0, blocking collectives: 199 us -> none  [the longest x2 80.3 us: local(): new_gram = lax.psum(inner_gram(residual, residual), ('row', 'col'))]
    all_gather x6 -> x0, blocking collectives: 79 us -> none  [the longest x3 46.4 us: local(): row_group = lax.all_gather(rounded, 'col', axis=1, tiled=True)]
    ppermute x0 -> x72, starting transfers between devices: none -> 76.1 us  [partner_permute(): return lax.ppermute(value, axis, [(i, i ^ flip) for i in range(size)])]
    another operation x25 -> x1, other arithmetic: 60.3 us -> 0.07 us  [local(): jnp.stack([lax.axis_index('row'), lax.axis_index('col')]).astype(jnp.int32)]
    pallas_call x0 -> x15, Pallas kernels: none -> 57.4 us  [the longest x5 27.8 us: small_solve(): pl.pallas_call(solve_kernel, out_shape=f32(*rhs.shape), in_specs=[vmem, v...]
    scatter-add x12 -> x0, other arithmetic: 54.1 us -> none  [the longest x3 21 us: local(): col_acc = col_acc.at[:, far_q].add(far_to_cols)]
    dot_general x26 -> x23, matrix products: 37.4 us -> 8.58 us  [the longest x15 6.38 us: combine(): jnp.dot(weights.T, rows_in, preferred_element_type=jnp.float32, precision...]
  transfers between devices with their start and end apart: 6 -> 72, of which waited for: 6 -> 20; matrix products, arithmetic and copies ran while one was open for 6% -> 2% of each run, Pallas kernels for 0% -> 26%
where the time goes in v1:
time: 181 us
  starting transfers between devices  76.1 us (42%)
  Pallas kernels  57.4 us (32%)
  waiting for transfers between devices  28.1 us (16%)
  matrix products  8.58 us (5%)
  local copies, waits for them, and re-layouts  5.94 us (3%)
  other arithmetic  2.56 us (1%)
  between operations  1.84 us (1%)
    ppermute x72, starting transfers between devices, partner_permute(): return lax.ppermute(value, axis, [(i, i ^ flip) for i in range(size)])  76.1 us
    ppermute x72, waiting for transfers between devices, partner_permute(): return lax.ppermute(value, axis, [(i, i ^ flip) for i in range(size)])  28.1 us
    pallas_call x5, Pallas kernels, small_solve(): pl.pallas_call(solve_kernel, out_shape=f32(*rhs.shape), in_specs=[vmem, v...  27.8 us
    pallas_call x3, Pallas kernels, off_diagonal(): pl.pallas_call(rows_kernel, out_shape=[bf16(chips, cases, width), f32(chi...  10 us
    pallas_call x3, Pallas kernels, off_diagonal(): pl.pallas_call(cols_kernel, out_shape=[f32(cases, width)] + [bf16(cases,...  9.81 us
    pallas_call x1, Pallas kernels, local(): pl.pallas_call(dense_kernel, out_shape=[bf16(slots, leaf, leaf)] * 2, in_...  7.98 us
    dot_general x15, matrix products, combine(): jnp.dot(weights.T, rows_in, preferred_element_type=jnp.float32, precision...  6.38 us
    unnamed x16, local copies, waits for them, and re-layouts  5.86 us
  transfers between devices with their start and end apart: 72, of which 20 were waited for; matrix products, arithmetic and copies ran while one was open for 2% of the time, Pallas kernels for 26%

profile of v1, /device:TPU:0, one launch (start us, length us, event | category | flops | bytes accessed | tf_op | source)
XLA Modules:
  0.0 180.5 jit_solution(1531607232357097966)
XLA Ops:
  1.6 3.0 %collective-permute-start = (bf16[64,640]{1,0:T(8,128)(2,1)S(1)}, bf16[64,640]{1,0:T(8,128)(2,1)S(1)}, u32[]{:S(2)}, u32[]{:S(2)}) collective-permute-start(bf16[64,640]{1,0:T(8,128)(2,1)S(1)} %convert_element_type.63.refs_0_), channel_id=1, source_target_pairs={{0,8},{8,0},{16,24},{24,16},{1,9},{9,1},{17,25},{25,17},{2,10},{10... | collective-permute-start | bytes 245768 | tf_op jit(solution)/shard_map/ppermute | solution.py:35
  4.6 1.5 collective-permute-start.1
  6.1 4.1 %collective-permute-start.9 = (bf16[64,640]{1,0:T(8,128)(2,1)S(1)}, bf16[64,640]{1,0:T(8,128)(2,1)S(1)}, u32[]{:S(2)}, u32[]{:S(2)}) collective-permute-start(bf16[64,640]{1,0:T(8,128)(2,1)S(1)} %convert_element_type.63.refs_0_), channel_id=1, source_target_pairs={{0,6},{1,7},{2,4},{3,5},{4,2},{5,3},{6,0},{7,1},{8,14},{9,15},{10,... | collective-permute-start | bytes 245768 | tf_op jit(solution)/shard_map/ppermute | solution.py:35
  11.6 1.2 copy-done
  13.9 1.0 copy-done.2
  15.6 8.0 %dense_tiles.1 = (bf16[96,128,128]{2,1,0:T(8,128)(2,1)S(1)}, bf16[96,128,128]{2,1,0:T(8,128)(2,1)}) custom-call(s32[1]{0:T(128)} %bitcast.59.count_ref, s32[64]{0:T(128)S(1)} %bitcast.68, bf16[32,128,128]{2,1,0:T(8,128)(2,1)S(1)} %bitcast.60, bf16[64,32,128]{2,1,0:T(8,128)(2,1)S(1)} %bitcast.66, bf16[64,32,128]{2,1,0:T(8,128)(2,1)S(1)} %bitcast.67), custom_call_target="tpu_custom_call" | custom-call | tf_op jit(solution)/shard_map/dense_tiles/pallas_call | solution.py:181
  24.2 1.9 %copy-done.4 = bf16[96,128,128]{2,1,0:T(8,128)(2,1)S(1)} copy-done((bf16[96,128,128]{2,1,0:T(8,128)(2,1)S(1)}, bf16[96,128,128]{2,1,0:T(8,128)(2,1)}, u32[]{:S(2)}) %copy-start.4) | copy-done | bytes 3145752
  26.1 3.3 %rows_half.3 = (bf16[4,64,640]{2,1,0:T(8,128)(2,1)S(1)}, f32[4,64,640]{2,1,0:T(8,128)S(1)}) custom-call(s32[2]{0:T(128)S(1)} %pad_add_fusion.place_ref, s32[96]{0:T(128)S(1)} %get-tuple-element.72.from_ref.to_ref, s32[96]{0:T(128)S(1)} %get-tuple-element.73.to_ref.from_ref, bf16[96,128,128]{2,1,0:T(8,128)(2,1)S(1)} %copy-done.4, ...), custom_call_target="tpu_custom_call" | custom-call | flops 1610612736 | tf_op jit(solution)/shard_map/rows_half/pallas_call | solution.py:194
  31.8 3.3 %cols_half.3 = (f32[64,640]{1,0:T(8,128)S(1)}, bf16[64,640]{1,0:T(8,128)(2,1)S(1)}, bf16[64,640]{1,0:T(8,128)(2,1)S(1)}, bf16[64,640]{1,0:T(8,128)(2,1)S(1)}) custom-call(s32[2]{0:T(128)S(1)} %pad_add_fusion.place_ref, s32[96]{0:T(128)S(1)} %get-tuple-element.73.to_ref.from_ref, s32[96]{0:T(128)S(1)} %get-tuple-element.72.from_ref.to_ref, ...), custom_call_target="tpu_custom_call" | custom-call | flops 1610612736 | tf_op jit(solution)/shard_map/cols_half/pallas_call | solution.py:213
  35.0 1.8 collective-permute-start.14
  36.8 1.5 collective-permute-start.15
  39.2 1.6 collective-permute-start.11
  40.8 2.9 %collective-permute-start.12 = (bf16[64,640]{1,0:T(8,128)(2,1)S(1)}, bf16[64,640]{1,0:T(8,128)(2,1)S(1)}, u32[]{:S(2)}, u32[]{:S(2)}) collective-permute-start(bf16[64,640]{1,0:T(8,128)(2,1)S(1)} %get-tuple-element.41), channel_id=1, source_target_pairs={{0,4},{1,5},{2,6},{3,7},{4,0},{5,1},{6,2},{7,3},{8,12},{9,13},{10,... | collective-permute-start | bytes 245768 | tf_op jit(solution)/shard_map/ppermute | solution.py:35
  44.4 4.4 %collective-permute-done.12 = bf16[64,640]{1,0:T(8,128)(2,1)S(1)} collective-permute-done((bf16[64,640]{1,0:T(8,128)(2,1)S(1)}, bf16[64,640]{1,0:T(8,128)(2,1)S(1)}, u32[]{:S(2)}, u32[]{:S(2)}) %collective-permute-start.12) | collective-permute-done | bytes 81952 | tf_op jit(solution)/shard_map/ppermute | solution.py:35
  48.8 1.2 collective-permute-done.13
  50.5 1.2 collective-permute-done.17
  51.8 1.1 collective-permute-start.18
  53.0 1.6 collective-permute-start.19
  54.5 1.7 collective-permute-start.20
  56.2 1.5 collective-permute-start.24
  57.7 1.5 collective-permute-start.25
  60.2 2.2 %collective-permute-start.31 = (bf16[64,640]{1,0:T(8,128)(2,1)S(1)}, bf16[64,640]{1,0:T(8,128)(2,1)S(1)}, u32[]{:S(2)}, u32[]{:S(2)}) collective-permute-start(bf16[64,640]{1,0:T(8,128)(2,1)S(1)} %get-tuple-element.66.refs_0_), channel_id=1, source_target_pairs={{0,4},{1,5},{2,6},{3,7},{4,0},{5,1},{6,2},{7,3},{8,12},{9,13},{10,... | collective-permute-start | bytes 245768 | tf_op jit(solution)/shard_map/ppermute | solution.py:35
  62.4 1.8 collective-permute-start.33
  64.2 1.5 collective-permute-start.21
  65.7 1.5 collective-permute-start.22
  67.7 3.3 %rows_half.4 = (bf16[4,64,640]{2,1,0:T(8,128)(2,1)S(1)}, f32[4,64,640]{2,1,0:T(8,128)S(1)}) custom-call(s32[2]{0:T(128)S(1)} %pad_add_fusion.place_ref, s32[96]{0:T(128)S(1)} %get-tuple-element.72.from_ref.to_ref, s32[96]{0:T(128)S(1)} %get-tuple-element.73.to_ref.from_ref, bf16[96,128,128]{2,1,0:T(8,128)(2,1)S(1)} %copy-done.5, ...), custom_call_target="tpu_custom_call" | custom-call | flops 1610612736 | tf_op jit(solution)/shard_map/rows_half/pallas_call | solution.py:194
  72.3 5.6 %small_solve.5 = f32[64,64]{1,0:T(8,128)S(1)} custom-call(f32[64,64]{1,0:T(8,128)S(1)} %get-tuple-element.69.matrix_ref, f32[64,64]{1,0:T(8,128)S(1)} %get-tuple-element.68.rhs_ref.matrix_ref), custom_call_target="tpu_custom_call" | custom-call | tf_op jit(solution)/shard_map/small_solve/pallas_call | solution.py:131
  77.9 3.3 %cols_half.4 = (f32[64,640]{1,0:T(8,128)S(1)}, bf16[64,640]{1,0:T(8,128)(2,1)S(1)}, bf16[64,640]{1,0:T(8,128)(2,1)S(1)}, bf16[64,640]{1,0:T(8,128)(2,1)S(1)}) custom-call(s32[2]{0:T(128)S(1)} %pad_add_fusion.place_ref, s32[96]{0:T(128)S(1)} %get-tuple-element.73.to_ref.from_ref, s32[96]{0:T(128)S(1)} %get-tuple-element.72.from_ref.to_ref, ...), custom_call_target="tpu_custom_call" | custom-call | flops 1610612736 | tf_op jit(solution)/shard_map/cols_half/pallas_call | solution.py:213
  81.2 1.6 collective-permute-start.38
  83.1 1.6 collective-permute-start.39
  85.8 2.7 %collective-permute-start.36 = (bf16[64,640]{1,0:T(8,128)(2,1)S(1)}, bf16[64,640]{1,0:T(8,128)(2,1)S(1)}, u32[]{:S(2)}, u32[]{:S(2)}) collective-permute-start(bf16[64,640]{1,0:T(8,128)(2,1)S(1)} %get-tuple-element.51), channel_id=1, source_target_pairs={{0,4},{1,5},{2,6},{3,7},{4,0},{5,1},{6,2},{7,3},{8,12},{9,13},{10,... | collective-permute-start | bytes 245768 | tf_op jit(solution)/shard_map/ppermute | solution.py:35
  88.5 1.7 collective-permute-start.37
  90.8 4.4 %collective-permute-done.36 = bf16[64,640]{1,0:T(8,128)(2,1)S(1)} collective-permute-done((bf16[64,640]{1,0:T(8,128)(2,1)S(1)}, bf16[64,640]{1,0:T(8,128)(2,1)S(1)}, u32[]{:S(2)}, u32[]{:S(2)}) %collective-permute-start.36) | collective-permute-done | bytes 81952 | tf_op jit(solution)/shard_map/ppermute | solution.py:35
  96.1 1.2 collective-permute-done.41
  97.4 1.4 collective-permute-start.42
  98.8 1.2 collective-permute-start.43
  100.0 1.8 collective-permute-start.44
  101.8 1.5 collective-permute-start.48
  103.3 1.5 collective-permute-start.49
  105.8 2.1 %collective-permute-start.55 = (bf16[64,640]{1,0:T(8,128)(2,1)S(1)}, bf16[64,640]{1,0:T(8,128)(2,1)S(1)}, u32[]{:S(2)}, u32[]{:S(2)}) collective-permute-start(bf16[64,640]{1,0:T(8,128)(2,1)S(1)} %get-tuple-element.70.refs_0_), channel_id=1, source_target_pairs={{0,4},{1,5},{2,6},{3,7},{4,0},{5,1},{6,2},{7,3},{8,12},{9,13},{10,... | collective-permute-start | bytes 245768 | tf_op jit(solution)/shard_map/ppermute | solution.py:35
  107.9 1.8 %collective-permute-start.57 = (bf16[64,640]{1,0:T(8,128)(2,1)S(1)}, bf16[64,640]{1,0:T(8,128)(2,1)S(1)}, u32[]{:S(2)}, u32[]{:S(2)}) collective-permute-start(bf16[64,640]{1,0:T(8,128)(2,1)S(1)} %get-tuple-element.70.refs_0_), channel_id=1, source_target_pairs={{0,6},{1,7},{2,4},{3,5},{4,2},{5,3},{6,0},{7,1},{8,14},{9,15},{10,... | collective-permute-start | bytes 245768 | tf_op jit(solution)/shard_map/ppermute | solution.py:35
  109.8 1.5 collective-permute-start.45
  111.3 1.5 collective-permute-start.46
  113.3 3.5 %rows_half.5 = (bf16[4,64,640]{2,1,0:T(8,128)(2,1)S(1)}, f32[4,64,640]{2,1,0:T(8,128)S(1)}) custom-call(s32[2]{0:T(128)S(1)} %pad_add_fusion.place_ref, s32[96]{0:T(128)S(1)} %get-tuple-element.72.from_ref.to_ref, s32[96]{0:T(128)S(1)} %get-tuple-element.73.to_ref.from_ref, bf16[96,128,128]{2,1,0:T(8,128)(2,1)S(1)} %copy-done.5, ...), custom_call_target="tpu_custom_call" | custom-call | flops 1610612736 | tf_op jit(solution)/shard_map/rows_half/pallas_call | solution.py:194
  118.0 5.6 %small_solve.6 = f32[64,64]{1,0:T(8,128)S(1)} custom-call(f32[64,64]{1,0:T(8,128)S(1)} %get-tuple-element.68.rhs_ref.matrix_ref, f32[64,64]{1,0:T(8,128)S(1)} %bitcast.61), custom_call_target="tpu_custom_call" | custom-call | tf_op jit(solution)/shard_map/small_solve/pallas_call | solution.py:131
  124.4 5.6 %small_solve.7 = f32[64,64]{1,0:T(8,128)S(1)} custom-call(f32[64,64]{1,0:T(8,128)S(1)} %slice_subtract_fusion.1.matrix_ref, f32[64,64]{1,0:T(8,128)S(1)} %bitcast.62), custom_call_target="tpu_custom_call" | custom-call | tf_op jit(solution)/shard_map/small_solve/pallas_call | solution.py:131
  130.3 3.3 %cols_half.5 = (f32[64,640]{1,0:T(8,128)S(1)}, bf16[64,640]{1,0:T(8,128)(2,1)S(1)}, bf16[64,640]{1,0:T(8,128)(2,1)S(1)}, bf16[64,640]{1,0:T(8,128)(2,1)S(1)}) custom-call(s32[2]{0:T(128)S(1)} %pad_add_fusion.place_ref, s32[96]{0:T(128)S(1)} %get-tuple-element.73.to_ref.from_ref, s32[96]{0:T(128)S(1)} %get-tuple-element.72.from_ref.to_ref, ...), custom_call_target="tpu_custom_call" | custom-call | flops 1610612736 | tf_op jit(solution)/shard_map/cols_half/pallas_call | solution.py:213
  133.6 1.6 collective-permute-start.62
  135.5 1.6 collective-permute-start.63
  138.3 2.6 %collective-permute-start.60 = (bf16[64,640]{1,0:T(8,128)(2,1)S(1)}, bf16[64,640]{1,0:T(8,128)(2,1)S(1)}, u32[]{:S(2)}, u32[]{:S(2)}) collective-permute-start(bf16[64,640]{1,0:T(8,128)(2,1)S(1)} %get-tuple-element.61), channel_id=1, source_target_pairs={{0,4},{1,5},{2,6},{3,7},{4,0},{5,1},{6,2},{7,3},{8,12},{9,13},{10,... | collective-permute-start | bytes 245768 | tf_op jit(solution)/shard_map/ppermute | solution.py:35
  140.9 1.8 collective-permute-start.61
  143.2 4.3 %collective-permute-done.60 = bf16[64,640]{1,0:T(8,128)(2,1)S(1)} collective-permute-done((bf16[64,640]{1,0:T(8,128)(2,1)S(1)}, bf16[64,640]{1,0:T(8,128)(2,1)S(1)}, u32[]{:S(2)}, u32[]{:S(2)}) %collective-permute-start.60) | collective-permute-done | bytes 81952 | tf_op jit(solution)/shard_map/ppermute | solution.py:35
  148.4 1.2 collective-permute-done.65
  149.7 1.4 collective-permute-start.66
  151.1 1.2 collective-permute-start.67
  152.3 1.8 collective-permute-start.68
  154.4 2.3 %collective-permute-done.67 = f32[64,128]{1,0:T(8,128)S(1)} collective-permute-done((f32[64,128]{1,0:T(8,128)S(1)}, f32[64,128]{1,0:T(8,128)S(1)}, u32[]{:S(2)}, u32[]{:S(2)}) %collective-permute-start.67) | collective-permute-done | bytes 32800 | tf_op jit(solution)/shard_map/ppermute | solution.py:35
  156.8 1.2 collective-permute-done.68
  158.0 1.5 collective-permute-start.69
  159.6 1.5 collective-permute-start.70
  162.2 1.3 collective-permute-done.70
  163.5 2.4 %collective-permute-done.71 = f32[64,128]{1,0:T(8,128)S(1)} collective-permute-done((f32[64,128]{1,0:T(8,128)S(1)}, f32[64,128]{1,0:T(8,128)S(1)}, u32[]{:S(2)}, u32[]{:S(2)}) %collective-permute-start.71) | collective-permute-done | bytes 32800 | tf_op jit(solution)/shard_map/ppermute | solution.py:35
  165.9 5.6 %small_solve.8 = f32[64,64]{1,0:T(8,128)S(1)} custom-call(f32[64,64]{1,0:T(8,128)S(1)} %bitcast.63, f32[64,64]{1,0:T(8,128)S(1)} %bitcast.64), custom_call_target="tpu_custom_call" | custom-call | tf_op jit(solution)/shard_map/small_solve/pallas_call | solution.py:131
  172.6 5.6 %small_solve.9 = f32[64,64]{1,0:T(8,128)S(1)} custom-call(f32[64,64]{1,0:T(8,128)S(1)} %slice_subtract_fusion.matrix_ref, f32[64,64]{1,0:T(8,128)S(1)} %bitcast.65), custom_call_target="tpu_custom_call" | custom-call | tf_op jit(solution)/shard_map/small_solve/pallas_call | solution.py:131
  (152 shorter events, 26.2 us)
Async XLA Ops:
  1.6 22.1 %collective-permute-start = (bf16[64,640]{1,0:T(8,128)(2,1)S(1)}, bf16[64,640]{1,0:T(8,128)(2,1)S(1)}, u32[]{:S(2)}, u32[]{:S(2)}) collective-permute-start(bf16[64,640]{1,0:T(8,128)(2,1)S(1)} %convert_element_type.63.refs_0_), channel_id=1, source_target_pairs={{0,8},{8,0},{16,24},{24,16},{1,9},{9,1},{17,25},{25,17},{2,10},{10... | collective-permute-start | bytes 245768 | tf_op jit(solution)/shard_map/ppermute | solution.py:35
  4.6 19.6 %collective-permute-start.1 = (bf16[64,640]{1,0:T(8,128)(2,1)S(1)}, bf16[64,640]{1,0:T(8,128)(2,1)S(1)}, u32[]{:S(2)}, u32[]{:S(2)}) collective-permute-start(bf16[64,640]{1,0:T(8,128)(2,1)S(1)} %convert_element_type.63.refs_0_), channel_id=1, source_target_pairs={{0,16},{8,24},{16,0},{24,8},{1,17},{9,25},{17,1},{25,9},{2,18},{10... | collective-permute-start | bytes 245768 | tf_op jit(solution)/shard_map/ppermute | solution.py:35
  6.1 18.1 %collective-permute-start.2 = (bf16[64,640]{1,0:T(8,128)(2,1)S(1)}, bf16[64,640]{1,0:T(8,128)(2,1)S(1)}, u32[]{:S(2)}, u32[]{:S(2)}) collective-permute-start(bf16[64,640]{1,0:T(8,128)(2,1)S(1)} %convert_element_type.63.refs_0_), channel_id=1, source_target_pairs={{0,24},{8,16},{16,8},{24,0},{1,25},{9,17},{17,9},{25,1},{2,26},{10... | collective-permute-start | bytes 245768 | tf_op jit(solution)/shard_map/ppermute | solution.py:35
  6.1 23.8 %collective-permute-start.9 = (bf16[64,640]{1,0:T(8,128)(2,1)S(1)}, bf16[64,640]{1,0:T(8,128)(2,1)S(1)}, u32[]{:S(2)}, u32[]{:S(2)}) collective-permute-start(bf16[64,640]{1,0:T(8,128)(2,1)S(1)} %convert_element_type.63.refs_0_), channel_id=1, source_target_pairs={{0,6},{1,7},{2,4},{3,5},{4,2},{5,3},{6,0},{7,1},{8,14},{9,15},{10,... | collective-permute-start | bytes 245768 | tf_op jit(solution)/shard_map/ppermute | solution.py:35
  10.2 19.9 %collective-permute-start.5 = (bf16[64,640]{1,0:T(8,128)(2,1)S(1)}, bf16[64,640]{1,0:T(8,128)(2,1)S(1)}, u32[]{:S(2)}, u32[]{:S(2)}) collective-permute-start(bf16[64,640]{1,0:T(8,128)(2,1)S(1)} %convert_element_type.63.refs_0_), channel_id=1, source_target_pairs={{0,2},{1,3},{2,0},{3,1},{4,6},{5,7},{6,4},{7,5},{8,10},{9,11},{10,... | collective-permute-start | bytes 245768 | tf_op jit(solution)/shard_map/ppermute | solution.py:35
  23.6 6.8 %collective-permute-start.7 = (bf16[64,640]{1,0:T(8,128)(2,1)S(1)}, bf16[64,640]{1,0:T(8,128)(2,1)S(1)}, u32[]{:S(2)}, u32[]{:S(2)}) collective-permute-start(bf16[64,640]{1,0:T(8,128)(2,1)S(1)} %convert_element_type.63.refs_0_), channel_id=1, source_target_pairs={{0,4},{1,5},{2,6},{3,7},{4,0},{5,1},{6,2},{7,3},{8,12},{9,13},{10,... | collective-permute-start | bytes 245768 | tf_op jit(solution)/shard_map/ppermute | solution.py:35
  29.4 9.2 %collective-permute-start.3 = (bf16[4,64,640]{2,1,0:T(8,128)(2,1)S(1)}, bf16[4,64,640]{2,1,0:T(8,128)(2,1)S(1)}, u32[]{:S(2)}, u32[]{:S(2)}) collective-permute-start(bf16[4,64,640]{2,1,0:T(8,128)(2,1)S(1)} %get-tuple-element.36), channel_id=1, source_target_pairs={{0,1},{1,0},{2,3},{3,2},{4,5},{5,4},{6,7},{7,6},{8,9},{9,8},{10,11... | collective-permute-start | bytes 983048 | tf_op jit(solution)/shard_map/ppermute | solution.py:35
  35.0 8.6 %collective-permute-start.14 = (bf16[64,640]{1,0:T(8,128)(2,1)S(1)}, bf16[64,640]{1,0:T(8,128)(2,1)S(1)}, u32[]{:S(2)}, u32[]{:S(2)}) collective-permute-start(bf16[64,640]{1,0:T(8,128)(2,1)S(1)} %get-tuple-element.43), channel_id=1, source_target_pairs={{0,8},{8,0},{16,24},{24,16},{1,9},{9,1},{17,25},{25,17},{2,10},{10... | collective-permute-start | bytes 245768 | tf_op jit(solution)/shard_map/ppermute | solution.py:35
  36.8 7.2 %collective-permute-start.15 = (bf16[64,640]{1,0:T(8,128)(2,1)S(1)}, bf16[64,640]{1,0:T(8,128)(2,1)S(1)}, u32[]{:S(2)}, u32[]{:S(2)}) collective-permute-start(bf16[64,640]{1,0:T(8,128)(2,1)S(1)} %get-tuple-element.44), channel_id=1, source_target_pairs={{0,16},{8,24},{16,0},{24,8},{1,17},{9,25},{17,1},{25,9},{2,18},{10... | collective-permute-start | bytes 245768 | tf_op jit(solution)/shard_map/ppermute | solution.py:35
  38.3 5.7 %collective-permute-start.16 = (bf16[64,640]{1,0:T(8,128)(2,1)S(1)}, bf16[64,640]{1,0:T(8,128)(2,1)S(1)}, u32[]{:S(2)}, u32[]{:S(2)}) collective-permute-start(bf16[64,640]{1,0:T(8,128)(2,1)S(1)} %get-tuple-element.45), channel_id=1, source_target_pairs={{0,24},{8,16},{16,8},{24,0},{1,25},{9,17},{17,9},{25,1},{2,26},{10... | collective-permute-start | bytes 245768 | tf_op jit(solution)/shard_map/ppermute | solution.py:35
  39.2 5.2 %collective-permute-start.11 = (bf16[64,640]{1,0:T(8,128)(2,1)S(1)}, bf16[64,640]{1,0:T(8,128)(2,1)S(1)}, u32[]{:S(2)}, u32[]{:S(2)}) collective-permute-start(bf16[64,640]{1,0:T(8,128)(2,1)S(1)} %get-tuple-element.40), channel_id=1, source_target_pairs={{0,2},{1,3},{2,0},{3,1},{4,6},{5,7},{6,4},{7,5},{8,10},{9,11},{10,... | collective-permute-start | bytes 245768 | tf_op jit(solution)/shard_map/ppermute | solution.py:35
  40.8 8.1 %collective-permute-start.12 = (bf16[64,640]{1,0:T(8,128)(2,1)S(1)}, bf16[64,640]{1,0:T(8,128)(2,1)S(1)}, u32[]{:S(2)}, u32[]{:S(2)}) collective-permute-start(bf16[64,640]{1,0:T(8,128)(2,1)S(1)} %get-tuple-element.41), channel_id=1, source_target_pairs={{0,4},{1,5},{2,6},{3,7},{4,0},{5,1},{6,2},{7,3},{8,12},{9,13},{10,... | collective-permute-start | bytes 245768 | tf_op jit(solution)/shard_map/ppermute | solution.py:35
  43.7 6.3 %collective-permute-start.13 = (bf16[64,640]{1,0:T(8,128)(2,1)S(1)}, bf16[64,640]{1,0:T(8,128)(2,1)S(1)}, u32[]{:S(2)}, u32[]{:S(2)}) collective-permute-start(bf16[64,640]{1,0:T(8,128)(2,1)S(1)} %get-tuple-element.42), channel_id=1, source_target_pairs={{0,6},{1,7},{2,4},{3,5},{4,2},{5,3},{6,0},{7,1},{8,14},{9,15},{10,... | collective-permute-start | bytes 245768 | tf_op jit(solution)/shard_map/ppermute | solution.py:35
  51.8 7.4 %collective-permute-start.18 = (f32[64,128]{1,0:T(8,128)S(1)}, f32[64,128]{1,0:T(8,128)S(1)}, u32[]{:S(2)}, u32[]{:S(2)}) collective-permute-start(f32[64,128]{1,0:T(8,128)S(1)} %fusion.82), channel_id=1, source_target_pairs={{0,2},{1,3},{2,0},{3,1},{4,6},{5,7},{6,4},{7,5},{8,10},{9,11},{10,... | collective-permute-start | bytes 98312 | tf_op jit(solution)/shard_map/ppermute | solution.py:35
  53.0 6.8 %collective-permute-start.19 = (f32[64,128]{1,0:T(8,128)S(1)}, f32[64,128]{1,0:T(8,128)S(1)}, u32[]{:S(2)}, u32[]{:S(2)}) collective-permute-start(f32[64,128]{1,0:T(8,128)S(1)} %fusion.82), channel_id=1, source_target_pairs={{0,4},{1,5},{2,6},{3,7},{4,0},{5,1},{6,2},{7,3},{8,12},{9,13},{10,... | collective-permute-start | bytes 98312 | tf_op jit(solution)/shard_map/ppermute | solution.py:35
  54.5 5.7 %collective-permute-start.20 = (f32[64,128]{1,0:T(8,128)S(1)}, f32[64,128]{1,0:T(8,128)S(1)}, u32[]{:S(2)}, u32[]{:S(2)}) collective-permute-start(f32[64,128]{1,0:T(8,128)S(1)} %fusion.82), channel_id=1, source_target_pairs={{0,6},{1,7},{2,4},{3,5},{4,2},{5,3},{6,0},{7,1},{8,14},{9,15},{10,... | collective-permute-start | bytes 98312 | tf_op jit(solution)/shard_map/ppermute | solution.py:35
  56.2 6.2 %collective-permute-start.24 = (bf16[64,640]{1,0:T(8,128)(2,1)S(1)}, bf16[64,640]{1,0:T(8,128)(2,1)S(1)}, u32[]{:S(2)}, u32[]{:S(2)}) collective-permute-start(bf16[64,640]{1,0:T(8,128)(2,1)S(1)} %get-tuple-element.66.refs_0_), channel_id=1, source_target_pairs={{0,8},{8,0},{16,24},{24,16},{1,9},{9,1},{17,25},{25,17},{2,10},{10... | collective-permute-start | bytes 245768 | tf_op jit(solution)/shard_map/ppermute | solution.py:35
  57.7 6.5 %collective-permute-start.25 = (bf16[64,640]{1,0:T(8,128)(2,1)S(1)}, bf16[64,640]{1,0:T(8,128)(2,1)S(1)}, u32[]{:S(2)}, u32[]{:S(2)}) collective-permute-start(bf16[64,640]{1,0:T(8,128)(2,1)S(1)} %get-tuple-element.66.refs_0_), channel_id=1, source_target_pairs={{0,16},{8,24},{16,0},{24,8},{1,17},{9,25},{17,1},{25,9},{2,18},{10... | collective-permute-start | bytes 245768 | tf_op jit(solution)/shard_map/ppermute | solution.py:35
  59.2 6.5 %collective-permute-start.26 = (bf16[64,640]{1,0:T(8,128)(2,1)S(1)}, bf16[64,640]{1,0:T(8,128)(2,1)S(1)}, u32[]{:S(2)}, u32[]{:S(2)}) collective-permute-start(bf16[64,640]{1,0:T(8,128)(2,1)S(1)} %get-tuple-element.66.refs_0_), channel_id=1, source_target_pairs={{0,24},{8,16},{16,8},{24,0},{1,25},{9,17},{17,9},{25,1},{2,26},{10... | collective-permute-start | bytes 245768 | tf_op jit(solution)/shard_map/ppermute | solution.py:35
  59.7 7.5 %collective-permute-start.29 = (bf16[64,640]{1,0:T(8,128)(2,1)S(1)}, bf16[64,640]{1,0:T(8,128)(2,1)S(1)}, u32[]{:S(2)}, u32[]{:S(2)}) collective-permute-start(bf16[64,640]{1,0:T(8,128)(2,1)S(1)} %get-tuple-element.66.refs_0_), channel_id=1, source_target_pairs={{0,2},{1,3},{2,0},{3,1},{4,6},{5,7},{6,4},{7,5},{8,10},{9,11},{10,... | collective-permute-start | bytes 245768 | tf_op jit(solution)/shard_map/ppermute | solution.py:35
  60.2 10.8 %collective-permute-start.31 = (bf16[64,640]{1,0:T(8,128)(2,1)S(1)}, bf16[64,640]{1,0:T(8,128)(2,1)S(1)}, u32[]{:S(2)}, u32[]{:S(2)}) collective-permute-start(bf16[64,640]{1,0:T(8,128)(2,1)S(1)} %get-tuple-element.66.refs_0_), channel_id=1, source_target_pairs={{0,4},{1,5},{2,6},{3,7},{4,0},{5,1},{6,2},{7,3},{8,12},{9,13},{10,... | collective-permute-start | bytes 245768 | tf_op jit(solution)/shard_map/ppermute | solution.py:35
  62.4 8.7 %collective-permute-start.33 = (bf16[64,640]{1,0:T(8,128)(2,1)S(1)}, bf16[64,640]{1,0:T(8,128)(2,1)S(1)}, u32[]{:S(2)}, u32[]{:S(2)}) collective-permute-start(bf16[64,640]{1,0:T(8,128)(2,1)S(1)} %get-tuple-element.66.refs_0_), channel_id=1, source_target_pairs={{0,6},{1,7},{2,4},{3,5},{4,2},{5,3},{6,0},{7,1},{8,14},{9,15},{10,... | collective-permute-start | bytes 245768 | tf_op jit(solution)/shard_map/ppermute | solution.py:35
  64.2 7.4 %collective-permute-start.21 = (f32[64,128]{1,0:T(8,128)S(1)}, f32[64,128]{1,0:T(8,128)S(1)}, u32[]{:S(2)}, u32[]{:S(2)}) collective-permute-start(f32[64,128]{1,0:T(8,128)S(1)} %add_add_fusion.6), channel_id=1, source_target_pairs={{0,8},{8,0},{16,24},{24,16},{1,9},{9,1},{17,25},{25,17},{2,10},{10... | collective-permute-start | bytes 98312 | tf_op jit(solution)/shard_map/ppermute | solution.py:35
  65.7 6.0 %collective-permute-start.22 = (f32[64,128]{1,0:T(8,128)S(1)}, f32[64,128]{1,0:T(8,128)S(1)}, u32[]{:S(2)}, u32[]{:S(2)}) collective-permute-start(f32[64,128]{1,0:T(8,128)S(1)} %add_add_fusion.6), channel_id=1, source_target_pairs={{0,16},{8,24},{16,0},{24,8},{1,17},{9,25},{17,1},{25,9},{2,18},{10... | collective-permute-start | bytes 98312 | tf_op jit(solution)/shard_map/ppermute | solution.py:35
  67.2 4.9 %collective-permute-start.23 = (f32[64,128]{1,0:T(8,128)S(1)}, f32[64,128]{1,0:T(8,128)S(1)}, u32[]{:S(2)}, u32[]{:S(2)}) collective-permute-start(f32[64,128]{1,0:T(8,128)S(1)} %add_add_fusion.6), channel_id=1, source_target_pairs={{0,24},{8,16},{16,8},{24,0},{1,25},{9,17},{17,9},{25,1},{2,26},{10... | collective-permute-start | bytes 98312 | tf_op jit(solution)/shard_map/ppermute | solution.py:35
  71.0 6.8 %collective-permute-start.28 = (bf16[64,640]{1,0:T(8,128)(2,1)S(1)}, bf16[64,640]{1,0:T(8,128)(2,1)S(1)}, u32[]{:S(2)}, u32[]{:S(2)}) collective-permute-start(bf16[64,640]{1,0:T(8,128)(2,1)S(1)} %get-tuple-element.66.refs_0_), channel_id=1, source_target_pairs={{0,1},{1,0},{2,3},{3,2},{4,5},{5,4},{6,7},{7,6},{8,9},{9,8},{10,11... | collective-permute-start | bytes 245768 | tf_op jit(solution)/shard_map/ppermute | solution.py:35
  71.1 14.0 %collective-permute-start.27 = (bf16[4,64,640]{2,1,0:T(8,128)(2,1)S(1)}, bf16[4,64,640]{2,1,0:T(8,128)(2,1)S(1)}, u32[]{:S(2)}, u32[]{:S(2)}) collective-permute-start(bf16[4,64,640]{2,1,0:T(8,128)(2,1)S(1)} %get-tuple-element.47), channel_id=1, source_target_pairs={{0,1},{1,0},{2,3},{3,2},{4,5},{5,4},{6,7},{7,6},{8,9},{9,8},{10,11... | collective-permute-start | bytes 983048 | tf_op jit(solution)/shard_map/ppermute | solution.py:35
  71.6 6.3 %collective-permute-start.30 = (bf16[64,640]{1,0:T(8,128)(2,1)S(1)}, bf16[64,640]{1,0:T(8,128)(2,1)S(1)}, u32[]{:S(2)}, u32[]{:S(2)}) collective-permute-start(bf16[64,640]{1,0:T(8,128)(2,1)S(1)} %collective-permute-done.29.refs_2_), channel_id=1, source_target_pairs={{0,1},{1,0},{2,3},{3,2},{4,5},{5,4},{6,7},{7,6},{8,9},{9,8},{10,11... | collective-permute-start | bytes 245768 | tf_op jit(solution)/shard_map/ppermute | solution.py:35
  71.7 6.2 %collective-permute-start.32 = (bf16[64,640]{1,0:T(8,128)(2,1)S(1)}, bf16[64,640]{1,0:T(8,128)(2,1)S(1)}, u32[]{:S(2)}, u32[]{:S(2)}) collective-permute-start(bf16[64,640]{1,0:T(8,128)(2,1)S(1)} %collective-permute-done.31.refs_4_), channel_id=1, source_target_pairs={{0,1},{1,0},{2,3},{3,2},{4,5},{5,4},{6,7},{7,6},{8,9},{9,8},{10,11... | collective-permute-start | bytes 245768 | tf_op jit(solution)/shard_map/ppermute | solution.py:35
  72.1 5.8 %collective-permute-start.34 = (bf16[64,640]{1,0:T(8,128)(2,1)S(1)}, bf16[64,640]{1,0:T(8,128)(2,1)S(1)}, u32[]{:S(2)}, u32[]{:S(2)}) collective-permute-start(bf16[64,640]{1,0:T(8,128)(2,1)S(1)} %collective-permute-done.33.refs_6_), channel_id=1, source_target_pairs={{0,1},{1,0},{2,3},{3,2},{4,5},{5,4},{6,7},{7,6},{8,9},{9,8},{10,11... | collective-permute-start | bytes 245768 | tf_op jit(solution)/shard_map/ppermute | solution.py:35
  81.2 7.4 %collective-permute-start.38 = (bf16[64,640]{1,0:T(8,128)(2,1)S(1)}, bf16[64,640]{1,0:T(8,128)(2,1)S(1)}, u32[]{:S(2)}, u32[]{:S(2)}) collective-permute-start(bf16[64,640]{1,0:T(8,128)(2,1)S(1)} %get-tuple-element.53), channel_id=1, source_target_pairs={{0,8},{8,0},{16,24},{24,16},{1,9},{9,1},{17,25},{25,17},{2,10},{10... | collective-permute-start | bytes 245768 | tf_op jit(solution)/shard_map/ppermute | solution.py:35
  83.1 7.4 %collective-permute-start.39 = (bf16[64,640]{1,0:T(8,128)(2,1)S(1)}, bf16[64,640]{1,0:T(8,128)(2,1)S(1)}, u32[]{:S(2)}, u32[]{:S(2)}) collective-permute-start(bf16[64,640]{1,0:T(8,128)(2,1)S(1)} %get-tuple-element.54), channel_id=1, source_target_pairs={{0,16},{8,24},{16,0},{24,8},{1,17},{9,25},{17,1},{25,9},{2,18},{10... | collective-permute-start | bytes 245768 | tf_op jit(solution)/shard_map/ppermute | solution.py:35
  84.7 5.9 %collective-permute-start.40 = (bf16[64,640]{1,0:T(8,128)(2,1)S(1)}, bf16[64,640]{1,0:T(8,128)(2,1)S(1)}, u32[]{:S(2)}, u32[]{:S(2)}) collective-permute-start(bf16[64,640]{1,0:T(8,128)(2,1)S(1)} %get-tuple-element.55), channel_id=1, source_target_pairs={{0,24},{8,16},{16,8},{24,0},{1,25},{9,17},{17,9},{25,1},{2,26},{10... | collective-permute-start | bytes 245768 | tf_op jit(solution)/shard_map/ppermute | solution.py:35
  85.7 5.1 %collective-permute-start.35 = (bf16[64,640]{1,0:T(8,128)(2,1)S(1)}, bf16[64,640]{1,0:T(8,128)(2,1)S(1)}, u32[]{:S(2)}, u32[]{:S(2)}) collective-permute-start(bf16[64,640]{1,0:T(8,128)(2,1)S(1)} %get-tuple-element.50), channel_id=1, source_target_pairs={{0,2},{1,3},{2,0},{3,1},{4,6},{5,7},{6,4},{7,5},{8,10},{9,11},{10,... | collective-permute-start | bytes 245768 | tf_op jit(solution)/shard_map/ppermute | solution.py:35
  85.8 9.4 %collective-permute-start.36 = (bf16[64,640]{1,0:T(8,128)(2,1)S(1)}, bf16[64,640]{1,0:T(8,128)(2,1)S(1)}, u32[]{:S(2)}, u32[]{:S(2)}) collective-permute-start(bf16[64,640]{1,0:T(8,128)(2,1)S(1)} %get-tuple-element.51), channel_id=1, source_target_pairs={{0,4},{1,5},{2,6},{3,7},{4,0},{5,1},{6,2},{7,3},{8,12},{9,13},{10,... | collective-permute-start | bytes 245768 | tf_op jit(solution)/shard_map/ppermute | solution.py:35
  88.5 6.7 %collective-permute-start.37 = (bf16[64,640]{1,0:T(8,128)(2,1)S(1)}, bf16[64,640]{1,0:T(8,128)(2,1)S(1)}, u32[]{:S(2)}, u32[]{:S(2)}) collective-permute-start(bf16[64,640]{1,0:T(8,128)(2,1)S(1)} %get-tuple-element.52), channel_id=1, source_target_pairs={{0,6},{1,7},{2,4},{3,5},{4,2},{5,3},{6,0},{7,1},{8,14},{9,15},{10,... | collective-permute-start | bytes 245768 | tf_op jit(solution)/shard_map/ppermute | solution.py:35
  97.4 7.4 %collective-permute-start.42 = (f32[64,128]{1,0:T(8,128)S(1)}, f32[64,128]{1,0:T(8,128)S(1)}, u32[]{:S(2)}, u32[]{:S(2)}) collective-permute-start(f32[64,128]{1,0:T(8,128)S(1)} %fusion.81), channel_id=1, source_target_pairs={{0,2},{1,3},{2,0},{3,1},{4,6},{5,7},{6,4},{7,5},{8,10},{9,11},{10,... | collective-permute-start | bytes 98312 | tf_op jit(solution)/shard_map/ppermute | solution.py:35
  98.8 6.4 %collective-permute-start.43 = (f32[64,128]{1,0:T(8,128)S(1)}, f32[64,128]{1,0:T(8,128)S(1)}, u32[]{:S(2)}, u32[]{:S(2)}) collective-permute-start(f32[64,128]{1,0:T(8,128)S(1)} %fusion.81), channel_id=1, source_target_pairs={{0,4},{1,5},{2,6},{3,7},{4,0},{5,1},{6,2},{7,3},{8,12},{9,13},{10,... | collective-permute-start | bytes 98312 | tf_op jit(solution)/shard_map/ppermute | solution.py:35
  100.0 5.8 %collective-permute-start.44 = (f32[64,128]{1,0:T(8,128)S(1)}, f32[64,128]{1,0:T(8,128)S(1)}, u32[]{:S(2)}, u32[]{:S(2)}) collective-permute-start(f32[64,128]{1,0:T(8,128)S(1)} %fusion.81), channel_id=1, source_target_pairs={{0,6},{1,7},{2,4},{3,5},{4,2},{5,3},{6,0},{7,1},{8,14},{9,15},{10,... | collective-permute-start | bytes 98312 | tf_op jit(solution)/shard_map/ppermute | solution.py:35
  101.8 6.1 %collective-permute-start.48 = (bf16[64,640]{1,0:T(8,128)(2,1)S(1)}, bf16[64,640]{1,0:T(8,128)(2,1)S(1)}, u32[]{:S(2)}, u32[]{:S(2)}) collective-permute-start(bf16[64,640]{1,0:T(8,128)(2,1)S(1)} %get-tuple-element.70.refs_0_), channel_id=1, source_target_pairs={{0,8},{8,0},{16,24},{24,16},{1,9},{9,1},{17,25},{25,17},{2,10},{10... | collective-permute-start | bytes 245768 | tf_op jit(solution)/shard_map/ppermute | solution.py:35
  103.3 6.5 %collective-permute-start.49 = (bf16[64,640]{1,0:T(8,128)(2,1)S(1)}, bf16[64,640]{1,0:T(8,128)(2,1)S(1)}, u32[]{:S(2)}, u32[]{:S(2)}) collective-permute-start(bf16[64,640]{1,0:T(8,128)(2,1)S(1)} %get-tuple-element.70.refs_0_), channel_id=1, source_target_pairs={{0,16},{8,24},{16,0},{24,8},{1,17},{9,25},{17,1},{25,9},{2,18},{10... | collective-permute-start | bytes 245768 | tf_op jit(solution)/shard_map/ppermute | solution.py:35
  104.8 6.5 %collective-permute-start.50 = (bf16[64,640]{1,0:T(8,128)(2,1)S(1)}, bf16[64,640]{1,0:T(8,128)(2,1)S(1)}, u32[]{:S(2)}, u32[]{:S(2)}) collective-permute-start(bf16[64,640]{1,0:T(8,128)(2,1)S(1)} %get-tuple-element.70.refs_0_), channel_id=1, source_target_pairs={{0,24},{8,16},{16,8},{24,0},{1,25},{9,17},{17,9},{25,1},{2,26},{10... | collective-permute-start | bytes 245768 | tf_op jit(solution)/shard_map/ppermute | solution.py:35
  105.3 7.5 %collective-permute-start.53 = (bf16[64,640]{1,0:T(8,128)(2,1)S(1)}, bf16[64,640]{1,0:T(8,128)(2,1)S(1)}, u32[]{:S(2)}, u32[]{:S(2)}) collective-permute-start(bf16[64,640]{1,0:T(8,128)(2,1)S(1)} %get-tuple-element.70.refs_0_), channel_id=1, source_target_pairs={{0,2},{1,3},{2,0},{3,1},{4,6},{5,7},{6,4},{7,5},{8,10},{9,11},{10,... | collective-permute-start | bytes 245768 | tf_op jit(solution)/shard_map/ppermute | solution.py:35
  105.8 10.9 %collective-permute-start.55 = (bf16[64,640]{1,0:T(8,128)(2,1)S(1)}, bf16[64,640]{1,0:T(8,128)(2,1)S(1)}, u32[]{:S(2)}, u32[]{:S(2)}) collective-permute-start(bf16[64,640]{1,0:T(8,128)(2,1)S(1)} %get-tuple-element.70.refs_0_), channel_id=1, source_target_pairs={{0,4},{1,5},{2,6},{3,7},{4,0},{5,1},{6,2},{7,3},{8,12},{9,13},{10,... | collective-permute-start | bytes 245768 | tf_op jit(solution)/shard_map/ppermute | solution.py:35
  107.9 8.9 %collective-permute-start.57 = (bf16[64,640]{1,0:T(8,128)(2,1)S(1)}, bf16[64,640]{1,0:T(8,128)(2,1)S(1)}, u32[]{:S(2)}, u32[]{:S(2)}) collective-permute-start(bf16[64,640]{1,0:T(8,128)(2,1)S(1)} %get-tuple-element.70.refs_0_), channel_id=1, source_target_pairs={{0,6},{1,7},{2,4},{3,5},{4,2},{5,3},{6,0},{7,1},{8,14},{9,15},{10,... | collective-permute-start | bytes 245768 | tf_op jit(solution)/shard_map/ppermute | solution.py:35
  109.8 7.6 %collective-permute-start.45 = (f32[64,128]{1,0:T(8,128)S(1)}, f32[64,128]{1,0:T(8,128)S(1)}, u32[]{:S(2)}, u32[]{:S(2)}) collective-permute-start(f32[64,128]{1,0:T(8,128)S(1)} %add_add_fusion.4), channel_id=1, source_target_pairs={{0,8},{8,0},{16,24},{24,16},{1,9},{9,1},{17,25},{25,17},{2,10},{10... | collective-permute-start | bytes 98312 | tf_op jit(solution)/shard_map/ppermute | solution.py:35
  111.3 6.2 %collective-permute-start.46 = (f32[64,128]{1,0:T(8,128)S(1)}, f32[64,128]{1,0:T(8,128)S(1)}, u32[]{:S(2)}, u32[]{:S(2)}) collective-permute-start(f32[64,128]{1,0:T(8,128)S(1)} %add_add_fusion.4), channel_id=1, source_target_pairs={{0,16},{8,24},{16,0},{24,8},{1,17},{9,25},{17,1},{25,9},{2,18},{10... | collective-permute-start | bytes 98312 | tf_op jit(solution)/shard_map/ppermute | solution.py:35
  112.8 5.1 %collective-permute-start.47 = (f32[64,128]{1,0:T(8,128)S(1)}, f32[64,128]{1,0:T(8,128)S(1)}, u32[]{:S(2)}, u32[]{:S(2)}) collective-permute-start(f32[64,128]{1,0:T(8,128)S(1)} %add_add_fusion.4), channel_id=1, source_target_pairs={{0,24},{8,16},{16,8},{24,0},{1,25},{9,17},{17,9},{25,1},{2,26},{10... | collective-permute-start | bytes 98312 | tf_op jit(solution)/shard_map/ppermute | solution.py:35
  116.8 13.5 %collective-permute-start.52 = (bf16[64,640]{1,0:T(8,128)(2,1)S(1)}, bf16[64,640]{1,0:T(8,128)(2,1)S(1)}, u32[]{:S(2)}, u32[]{:S(2)}) collective-permute-start(bf16[64,640]{1,0:T(8,128)(2,1)S(1)} %get-tuple-element.70.refs_0_), channel_id=1, source_target_pairs={{0,1},{1,0},{2,3},{3,2},{4,5},{5,4},{6,7},{7,6},{8,9},{9,8},{10,11... | collective-permute-start | bytes 245768 | tf_op jit(solution)/shard_map/ppermute | solution.py:35
  116.8 20.7 %collective-permute-start.51 = (bf16[4,64,640]{2,1,0:T(8,128)(2,1)S(1)}, bf16[4,64,640]{2,1,0:T(8,128)(2,1)S(1)}, u32[]{:S(2)}, u32[]{:S(2)}) collective-permute-start(bf16[4,64,640]{2,1,0:T(8,128)(2,1)S(1)} %get-tuple-element.57), channel_id=1, source_target_pairs={{0,1},{1,0},{2,3},{3,2},{4,5},{5,4},{6,7},{7,6},{8,9},{9,8},{10,11... | collective-permute-start | bytes 983048 | tf_op jit(solution)/shard_map/ppermute | solution.py:35
  117.3 12.9 %collective-permute-start.54 = (bf16[64,640]{1,0:T(8,128)(2,1)S(1)}, bf16[64,640]{1,0:T(8,128)(2,1)S(1)}, u32[]{:S(2)}, u32[]{:S(2)}) collective-permute-start(bf16[64,640]{1,0:T(8,128)(2,1)S(1)} %collective-permute-done.53.refs_2_), channel_id=1, source_target_pairs={{0,1},{1,0},{2,3},{3,2},{4,5},{5,4},{6,7},{7,6},{8,9},{9,8},{10,11... | collective-permute-start | bytes 245768 | tf_op jit(solution)/shard_map/ppermute | solution.py:35
  117.4 12.9 %collective-permute-start.56 = (bf16[64,640]{1,0:T(8,128)(2,1)S(1)}, bf16[64,640]{1,0:T(8,128)(2,1)S(1)}, u32[]{:S(2)}, u32[]{:S(2)}) collective-permute-start(bf16[64,640]{1,0:T(8,128)(2,1)S(1)} %collective-permute-done.55.refs_4_), channel_id=1, source_target_pairs={{0,1},{1,0},{2,3},{3,2},{4,5},{5,4},{6,7},{7,6},{8,9},{9,8},{10,11... | collective-permute-start | bytes 245768 | tf_op jit(solution)/shard_map/ppermute | solution.py:35
  117.9 12.4 %collective-permute-start.58 = (bf16[64,640]{1,0:T(8,128)(2,1)S(1)}, bf16[64,640]{1,0:T(8,128)(2,1)S(1)}, u32[]{:S(2)}, u32[]{:S(2)}) collective-permute-start(bf16[64,640]{1,0:T(8,128)(2,1)S(1)} %collective-permute-done.57.refs_6_), channel_id=1, source_target_pairs={{0,1},{1,0},{2,3},{3,2},{4,5},{5,4},{6,7},{7,6},{8,9},{9,8},{10,11... | collective-permute-start | bytes 245768 | tf_op jit(solution)/shard_map/ppermute | solution.py:35
  133.6 7.3 %collective-permute-start.62 = (bf16[64,640]{1,0:T(8,128)(2,1)S(1)}, bf16[64,640]{1,0:T(8,128)(2,1)S(1)}, u32[]{:S(2)}, u32[]{:S(2)}) collective-permute-start(bf16[64,640]{1,0:T(8,128)(2,1)S(1)} %get-tuple-element.63), channel_id=1, source_target_pairs={{0,8},{8,0},{16,24},{24,16},{1,9},{9,1},{17,25},{25,17},{2,10},{10... | collective-permute-start | bytes 245768 | tf_op jit(solution)/shard_map/ppermute | solution.py:35
  135.5 7.4 %collective-permute-start.63 = (bf16[64,640]{1,0:T(8,128)(2,1)S(1)}, bf16[64,640]{1,0:T(8,128)(2,1)S(1)}, u32[]{:S(2)}, u32[]{:S(2)}) collective-permute-start(bf16[64,640]{1,0:T(8,128)(2,1)S(1)} %get-tuple-element.64), channel_id=1, source_target_pairs={{0,16},{8,24},{16,0},{24,8},{1,17},{9,25},{17,1},{25,9},{2,18},{10... | collective-permute-start | bytes 245768 | tf_op jit(solution)/shard_map/ppermute | solution.py:35
  137.1 5.9 %collective-permute-start.64 = (bf16[64,640]{1,0:T(8,128)(2,1)S(1)}, bf16[64,640]{1,0:T(8,128)(2,1)S(1)}, u32[]{:S(2)}, u32[]{:S(2)}) collective-permute-start(bf16[64,640]{1,0:T(8,128)(2,1)S(1)} %get-tuple-element.65), channel_id=1, source_target_pairs={{0,24},{8,16},{16,8},{24,0},{1,25},{9,17},{17,9},{25,1},{2,26},{10... | collective-permute-start | bytes 245768 | tf_op jit(solution)/shard_map/ppermute | solution.py:35
  138.2 5.0 %collective-permute-start.59 = (bf16[64,640]{1,0:T(8,128)(2,1)S(1)}, bf16[64,640]{1,0:T(8,128)(2,1)S(1)}, u32[]{:S(2)}, u32[]{:S(2)}) collective-permute-start(bf16[64,640]{1,0:T(8,128)(2,1)S(1)} %get-tuple-element.60), channel_id=1, source_target_pairs={{0,2},{1,3},{2,0},{3,1},{4,6},{5,7},{6,4},{7,5},{8,10},{9,11},{10,... | collective-permute-start | bytes 245768 | tf_op jit(solution)/shard_map/ppermute | solution.py:35
  138.3 9.3 %collective-permute-start.60 = (bf16[64,640]{1,0:T(8,128)(2,1)S(1)}, bf16[64,640]{1,0:T(8,128)(2,1)S(1)}, u32[]{:S(2)}, u32[]{:S(2)}) collective-permute-start(bf16[64,640]{1,0:T(8,128)(2,1)S(1)} %get-tuple-element.61), channel_id=1, source_target_pairs={{0,4},{1,5},{2,6},{3,7},{4,0},{5,1},{6,2},{7,3},{8,12},{9,13},{10,... | collective-permute-start | bytes 245768 | tf_op jit(solution)/shard_map/ppermute | solution.py:35
  140.9 6.7 %collective-permute-start.61 = (bf16[64,640]{1,0:T(8,128)(2,1)S(1)}, bf16[64,640]{1,0:T(8,128)(2,1)S(1)}, u32[]{:S(2)}, u32[]{:S(2)}) collective-permute-start(bf16[64,640]{1,0:T(8,128)(2,1)S(1)} %get-tuple-element.62), channel_id=1, source_target_pairs={{0,6},{1,7},{2,4},{3,5},{4,2},{5,3},{6,0},{7,1},{8,14},{9,15},{10,... | collective-permute-start | bytes 245768 | tf_op jit(solution)/shard_map/ppermute | solution.py:35
  149.7 4.7 %collective-permute-start.66 = (f32[64,128]{1,0:T(8,128)S(1)}, f32[64,128]{1,0:T(8,128)S(1)}, u32[]{:S(2)}, u32[]{:S(2)}) collective-permute-start(f32[64,128]{1,0:T(8,128)S(1)} %fusion.80), channel_id=1, source_target_pairs={{0,2},{1,3},{2,0},{3,1},{4,6},{5,7},{6,4},{7,5},{8,10},{9,11},{10,... | collective-permute-start | bytes 98312 | tf_op jit(solution)/shard_map/ppermute | solution.py:35
  151.1 5.7 %collective-permute-start.67 = (f32[64,128]{1,0:T(8,128)S(1)}, f32[64,128]{1,0:T(8,128)S(1)}, u32[]{:S(2)}, u32[]{:S(2)}) collective-permute-start(f32[64,128]{1,0:T(8,128)S(1)} %fusion.80), channel_id=1, source_target_pairs={{0,4},{1,5},{2,6},{3,7},{4,0},{5,1},{6,2},{7,3},{8,12},{9,13},{10,... | collective-permute-start | bytes 98312 | tf_op jit(solution)/shard_map/ppermute | solution.py:35
  152.3 5.7 %collective-permute-start.68 = (f32[64,128]{1,0:T(8,128)S(1)}, f32[64,128]{1,0:T(8,128)S(1)}, u32[]{:S(2)}, u32[]{:S(2)}) collective-permute-start(f32[64,128]{1,0:T(8,128)S(1)} %fusion.80), channel_id=1, source_target_pairs={{0,6},{1,7},{2,4},{3,5},{4,2},{5,3},{6,0},{7,1},{8,14},{9,15},{10,... | collective-permute-start | bytes 98312 | tf_op jit(solution)/shard_map/ppermute | solution.py:35
  158.0 4.2 %collective-permute-start.69 = (f32[64,128]{1,0:T(8,128)S(1)}, f32[64,128]{1,0:T(8,128)S(1)}, u32[]{:S(2)}, u32[]{:S(2)}) collective-permute-start(f32[64,128]{1,0:T(8,128)S(1)} %add_add_fusion.2), channel_id=1, source_target_pairs={{0,8},{8,0},{16,24},{24,16},{1,9},{9,1},{17,25},{25,17},{2,10},{10... | collective-permute-start | bytes 98312 | tf_op jit(solution)/shard_map/ppermute | solution.py:35
  161.1 4.8 %collective-permute-start.71 = (f32[64,128]{1,0:T(8,128)S(1)}, f32[64,128]{1,0:T(8,128)S(1)}, u32[]{:S(2)}, u32[]{:S(2)}) collective-permute-start(f32[64,128]{1,0:T(8,128)S(1)} %add_add_fusion.2), channel_id=1, source_target_pairs={{0,24},{8,16},{16,8},{24,0},{1,25},{9,17},{17,9},{25,1},{2,26},{10... | collective-permute-start | bytes 98312 | tf_op jit(solution)/shard_map/ppermute | solution.py:35
  (16 other events, 82.0 us)

commit v2 on v1

v2 whole, which is shorter than its diff:
```python
import functools

import jax
import jax.numpy as jnp
from jax import lax
from jax.experimental import pallas as pl
from jax.experimental.pallas import tpu as pltpu
from jax.sharding import PartitionSpec as P

VMEM_BYTES = 48 * 1024 * 1024
HIGHEST = lax.Precision.HIGHEST
GRAM = 128
PIECES = 3

vmem = pl.BlockSpec(memory_space=pltpu.VMEM)
smem = pl.BlockSpec(memory_space=pltpu.SMEM)
params = pltpu.CompilerParams(vmem_limit_bytes=VMEM_BYTES)


def f32(*shape):
    return jax.ShapeDtypeStruct(shape, jnp.float32)


def bf16(*shape):
    return jax.ShapeDtypeStruct(shape, jnp.bfloat16)


def contract(left, right, dims, precision=None):
    return lax.dot_general(
        left, right, (dims, ((), ())), precision=precision, preferred_element_type=jnp.float32
    )


def mul(left, right):
    return contract(left, right, ((1,), (0,)), HIGHEST)


def mul_t(left, right):
    return contract(left, right, ((0,), (0,)), HIGHEST)


def symmetric(matrix):
    return 0.5 * (matrix + matrix.T)


def partner_permute(value, axis, flip):
    size = lax.axis_size(axis)
    return lax.ppermute(value, axis, [(i, i ^ flip) for i in range(size)])


def put_gram(ref, width, gram):
    columns = gram.shape[1]
    for k in range(PIECES):
        piece = gram.astype(jnp.bfloat16)
        ref[:, width + k * columns : width + (k + 1) * columns] = piece
        gram = gram - piece.astype(jnp.float32)


def get_gram(ref, width):
    columns = (ref.shape[1] - width) // PIECES
    parts = [
        ref[:, width + k * columns : width + (k + 1) * columns].astype(jnp.float32)
        for k in range(PIECES)
    ]
    return (parts[2] + parts[1]) + parts[0]


def dense_kernel(count_ref, rank_ref, near_ref, left_ref, right_ref, tile_ref, turned_ref):
    near_slots, far_slots = near_ref.shape[0], left_ref.shape[0]

    def far(s, _):
        row = lax.broadcasted_iota(jnp.int32, left_ref.shape[1:], 0)
        left = jnp.where(row < rank_ref[s], left_ref[s].astype(jnp.float32), 0.0)
        left, right = left.astype(jnp.bfloat16), right_ref[s]
        tile_ref[near_slots + s] = contract(left, right, ((0,), (0,))).astype(jnp.bfloat16)
        turned_ref[near_slots + s] = contract(right, left, ((0,), (0,))).astype(jnp.bfloat16)
        return 0

    def near(s, _):
        tile = near_ref[s]
        tile = jnp.where(s < count_ref[0], tile, jnp.zeros_like(tile))
        tile_ref[s] = tile
        turned_ref[s] = tile.T
        return 0

    lax.fori_loop(0, far_slots, far, 0, unroll=8)
    lax.fori_loop(0, near_slots, near, 0, unroll=8)


def tile_sums(from_ref, to_ref, tile_ref, cells, total):
    total[...] = jnp.zeros_like(total)

    def step(s, _):
        product = contract(cells[from_ref[s]], tile_ref[s], ((1,), (0,)))
        total[to_ref[s]] = total[to_ref[s]] + product
        return 0

    lax.fori_loop(0, tile_ref.shape[0], step, 0, unroll=16)


def place(block, ref, cells, per):
    leaf = cells.shape[-1]
    for j in range(per):
        cells[block * per + j] = ref[:, j * leaf : (j + 1) * leaf]


def rows_kernel(place_ref, from_ref, to_ref, tile_ref, *refs):
    blocks, (send_ref, keep_ref, cells, total) = refs[:-4], refs[-4:]
    chips, _, width = send_ref.shape
    leaf = cells.shape[-1]
    per = width // leaf
    me, core = place_ref[0], place_ref[1] % 2
    for flip, ref in enumerate(blocks):
        place(me ^ flip, ref, cells, per)
    tile_sums(from_ref, to_ref, tile_ref, cells, total)
    for z in range(chips):
        for j in range(per):
            part = slice(j * leaf, (j + 1) * leaf)
            send_ref[z, :, part] = total[(2 * z + 1 - core) * per + j].astype(jnp.bfloat16)
            keep_ref[z, :, part] = total[(2 * z + core) * per + j]


def cols_kernel(rows, cols, place_ref, from_ref, to_ref, tile_ref, *refs):
    blocks, refs = refs[:cols], refs[cols:]
    outs, (cells, total) = refs[-rows - 3 : -2], refs[-2:]
    last = refs[: -rows - 3]
    own_ref, gram_ref, messages = outs[0], outs[1], outs[2:]
    width = own_ref.shape[1]
    leaf = cells.shape[-1]
    per = width // leaf
    me = place_ref[0]
    for flip, ref in enumerate(blocks):
        place(place_ref[1] ^ flip, ref, cells, per)
    tile_sums(from_ref, to_ref, tile_ref, cells, total)
    gram = get_gram(blocks[0], width)
    for ref in blocks[1:]:
        gram = gram + get_gram(ref, width)
    if last:
        vector_ref, diagonal_ref = last[rows:]
        vector = vector_ref[...]
        both = contract(vector, vector * diagonal_ref[...], ((1,), (1,)), HIGHEST)
        half = jnp.zeros_like(both)
        for flip, ref in enumerate(last[:rows]):
            for j in range(per):
                cluster = ref[:, j * leaf : (j + 1) * leaf]
                image = total[(me ^ flip) * per + j].astype(jnp.bfloat16)
                half = half + contract(cluster, image, ((1,), (1,)))
        both = both + 2.0 * half
        gram = jnp.concatenate([gram, both, jnp.zeros_like(both)], axis=1)
    gram_ref[...] = gram
    for flip, out in enumerate((own_ref, *messages)):
        for j in range(per):
            part = total[(me ^ flip) * per + j]
            out[:, j * leaf : (j + 1) * leaf] = part.astype(out.dtype)
    for out in messages:
        put_gram(out, width, gram)


def pair_kernel(place_ref, keep_ref, got_ref, *outs):
    chip = place_ref[1] // 2
    for flip, out in enumerate(outs):
        z = chip ^ flip
        out[...] = (keep_ref[z] + got_ref[z].astype(jnp.float32)).astype(out.dtype)


def first_kernel(vector_ref, diagonal_ref, message_ref):
    vector = vector_ref[...]
    width = vector.shape[1]
    message_ref[:, :width] = vector.astype(jnp.bfloat16)
    gram = contract(vector, vector, ((1,), (1,)), HIGHEST)
    weighted = jnp.sum(vector * vector * diagonal_ref[...], axis=1, keepdims=True)
    put_gram(
        message_ref, width, jnp.concatenate([gram, jnp.broadcast_to(weighted, gram.shape)], axis=1)
    )


def off_diagonal(rows, refs):
    width = refs[0].shape[1]
    total = refs[0][...] + refs[1][...]
    for ref in refs[2:]:
        total = total + ref[:, :width].astype(jnp.float32)
    return total


def sum_grams(own_ref, refs, width):
    gram = own_ref[...]
    for ref in refs:
        gram = gram + get_gram(ref, width)
    return gram


def combine_kernel(rows, first, vector_ref, diagonal_ref, shift_ref, gram_ref, *refs):
    sums, (next_ref, message_ref, total_ref) = refs[:-3], refs[-3:]
    width = vector_ref.shape[1]
    vector = vector_ref[...]
    gram = sum_grams(gram_ref, sums[1 - rows :], width)
    if first:
        cases = gram.shape[0]
        row = lax.broadcasted_iota(jnp.int32, (cases, cases), 0)
        column = lax.broadcasted_iota(jnp.int32, (cases, cases), 1)
        norm = jnp.sum(jnp.where(row == column, gram[:, :cases], 0.0), keepdims=True)
        shift = jnp.sum(gram[:, cases : cases + 1], keepdims=True) / norm
    else:
        shift = shift_ref[0:1, 0:1]
    total_ref[...] = gram
    following = (diagonal_ref[...] - shift) * vector + off_diagonal(rows, sums)
    next_ref[...] = following
    message_ref[:, :width] = following.astype(jnp.bfloat16)
    cross = contract(vector, following, ((1,), (1,)), HIGHEST)
    square = contract(following, following, ((1,), (1,)), HIGHEST)
    put_gram(message_ref, width, jnp.concatenate([cross, square], axis=1))


def shift_kernel(gram_ref, shift_ref):
    gram = gram_ref[...]
    cases = gram.shape[0]
    row = lax.broadcasted_iota(jnp.int32, (cases, cases), 0)
    column = lax.broadcasted_iota(jnp.int32, (cases, cases), 1)
    norm = jnp.sum(jnp.where(row == column, gram[:, :cases], 0.0), keepdims=True)
    shift = jnp.sum(gram[:, cases : cases + 1], keepdims=True) / norm
    shift_ref[...] = jnp.broadcast_to(shift, shift_ref.shape)


def last_gram_kernel(gram_ref, *refs):
    messages, (total_ref, both_ref) = refs[:-2], refs[-2:]
    width = messages[0].shape[1] - PIECES * gram_ref.shape[1]
    gram = sum_grams(gram_ref, messages, width)
    total_ref[...] = gram[:, :GRAM]
    both_ref[...] = gram[:, GRAM:]


def solve(*pairs):
    size = pairs[0][0].shape[0]
    works = [jnp.concatenate(pair, axis=1) for pair in pairs]
    row = lax.broadcasted_iota(jnp.int32, works[0].shape, 0)
    for k in range(size):
        pivots = [work[k : k + 1, :] / work[k : k + 1, k : k + 1] for work in works]
        works = [
            jnp.where(row == k, pivot, work - work[:, k : k + 1] * pivot)
            for work, pivot in zip(works, pivots)
        ]
    return [work[:, size:] for work in works]


def identity(size):
    row = lax.broadcasted_iota(jnp.int32, (size, size), 0)
    column = lax.broadcasted_iota(jnp.int32, (size, size), 1)
    return jnp.where(row == column, 1.0, 0.0)


def first_coefficients_kernel(shift_ref, gram0_ref, gram1_ref, out_ref):
    cases = gram0_ref.shape[0]
    shift = shift_ref[0:1, 0:1]
    bb = gram0_ref[:, :cases]
    bu, uu = gram1_ref[:, :cases], gram1_ref[:, cases:]
    one = identity(cases)
    alpha0, inverse = solve((shift * bb + symmetric(bu), bb), (bb, one))
    r_b = one - shift * alpha0
    r = jnp.concatenate([r_b, -alpha0], axis=0)
    gram = jnp.concatenate(
        [jnp.concatenate([bb, bu], axis=1), jnp.concatenate([bu.T, uu], axis=1)], axis=0
    )
    rr1 = symmetric(mul_t(r, mul(gram, r)))
    d_b = r_b + mul(inverse, rr1)
    out_ref[...] = jnp.concatenate([alpha0, rr1, r_b, d_b], axis=1)


def second_coefficients_kernel(
    shift_ref, gram0_ref, gram1_ref, gram2_ref, first_ref, vectors_ref, small_ref
):
    cases = gram0_ref.shape[0]
    shift = shift_ref[0:1, 0:1]
    bb = gram0_ref[:, :cases]
    bu, uu = gram1_ref[:, :cases], gram1_ref[:, cases:]
    uv, vv = gram2_ref[:, :cases], gram2_ref[:, cases:]
    bv = uu
    alpha0, rr1, r_b, d_b = [first_ref[:, k * cases : (k + 1) * cases] for k in range(4)]
    zero = jnp.zeros_like(bb)
    stack = functools.partial(jnp.concatenate, axis=0)
    side = functools.partial(jnp.concatenate, axis=1)
    gram = stack([side([bb, bu, bv]), side([bu.T, uu, uv]), side([bv, uv.T, vv])])
    r1 = stack([r_b, -alpha0, zero])
    d1 = stack([d_b, -alpha0, zero])
    s1 = stack([shift * d_b, d_b - shift * alpha0, -alpha0])
    curvature1 = symmetric(mul_t(d1, mul(gram, s1)))
    alpha1, inverse = solve((curvature1, rr1), (rr1, identity(cases)))
    r2 = r1 - mul(s1, alpha1)
    rr2 = symmetric(mul_t(r2, mul(gram, r2)))
    d2 = r2 + mul(d1, mul(inverse, rr2))
    d2_b, d2_u, d2_v = d2[:cases], d2[cases : 2 * cases], d2[2 * cases :]
    s2 = stack([shift * d2_b, d2_b + shift * d2_u, d2_u])
    with_y = mul_t(d2_b, uv + shift * bv) + mul_t(d2_u, vv + shift * uv)
    curvature2 = mul_t(d2, mul(gram, s2)) + mul(with_y, d2_v)
    x2 = stack([alpha0, zero, zero]) + mul(d1, alpha1)
    vectors_ref[...] = side([d2, r2, s2, x2])
    small_ref[...] = side([curvature2, rr2])


def finish_kernel(
    vectors_ref, small_ref, both_ref, other_ref, b_ref, u_ref, v_ref, diagonal_ref, *refs
):
    sums, (solution_ref, residual_ref) = refs[:-2], refs[-2:]
    cases = b_ref.shape[0]
    d2, r2, s2, x2 = [vectors_ref[:, k * cases : (k + 1) * cases] for k in range(4)]
    d2_v = d2[2 * cases :]
    both = symmetric(both_ref[:, :cases] + other_ref[:, :cases])
    curvature2 = symmetric(small_ref[:, :cases] + mul_t(d2_v, mul(both, d2_v)))
    (alpha2,) = solve((curvature2, small_ref[:, cases:]))
    y = diagonal_ref[...] * v_ref[...] + off_diagonal(0, sums)
    basis = jnp.concatenate([b_ref[...], u_ref[...], v_ref[...]], axis=0)
    solution_ref[...] = mul_t(x2 + mul(d2, alpha2), basis)
    residual_ref[...] = mul_t(r2 - mul(s2, alpha2), basis) - mul_t(mul(d2_v, alpha2), y)


def call(kernel, name, outs, *args, scratch=(), scalars=(), flops=0):
    scalars = set(scalars)
    return pl.pallas_call(
        kernel,
        out_shape=outs,
        in_specs=[smem if k in scalars else vmem for k in range(len(args))],
        out_specs=jax.tree.map(lambda _: vmem, outs),
        scratch_shapes=list(scratch),
        compiler_params=params,
        cost_estimate=pl.CostEstimate(flops=flops, bytes_accessed=0, transcendentals=0),
        name=name,
    )(*args)


def local(
    right_side,
    self_term,
    near_tiles,
    near_rows,
    near_cols,
    near_count,
    far_left,
    far_right,
    far_rows,
    far_cols,
    far_rank,
):
    cases, width = right_side.shape
    leaf = near_tiles.shape[-1]
    per = width // leaf
    rows, cols = lax.axis_size("row"), lax.axis_size("col")
    chips = cols // 2
    slots = near_tiles.shape[2] + far_left.shape[2]
    long = width + PIECES * GRAM
    here = jnp.stack([lax.axis_index("row"), lax.axis_index("col")]).astype(jnp.int32)
    list_p = jnp.concatenate([near_rows[0, 0], far_rows[0, 0]])
    list_q = jnp.concatenate([near_cols[0, 0], far_cols[0, 0]])
    diagonal = self_term[None, :]
    tiles, turned = call(
        dense_kernel,
        "dense_tiles",
        [bf16(slots, leaf, leaf)] * 2,
        near_count[0],
        far_rank[0, 0],
        near_tiles[0, 0],
        far_left[0, 0],
        far_right[0, 0],
        scalars=(0, 1),
    )
    half_flops = 2 * slots * cases * leaf * leaf * 8

    def apply(message, last=()):
        over_row = [partner_permute(message, "row", k) for k in range(1, rows)]
        over_chip = [partner_permute(message, "col", 2 * k) for k in range(1, chips)]
        other_core = [partner_permute(v, "col", 1) for v in [message] + over_chip]
        send, keep = call(
            rows_kernel,
            "rows_half",
            [bf16(chips, cases, width), f32(chips, cases, width)],
            here,
            list_q,
            list_p,
            turned,
            message,
            *over_row,
            scalars=(0, 1, 2),
            scratch=[
                pltpu.VMEM((rows * per, cases, leaf), jnp.bfloat16),
                pltpu.VMEM((cols * per, cases, leaf), jnp.float32),
            ],
            flops=half_flops,
        )
        got = partner_permute(send, "col", 1)
        row_group = [None] * cols
        for k, (a, b) in enumerate(zip([message] + over_chip, other_core)):
            row_group[2 * k], row_group[2 * k + 1] = a, b
        wide = 2 * GRAM if last else GRAM
        extra = [message, *over_row, *last] if last else []
        own_col, gram, *col_messages = call(
            functools.partial(cols_kernel, rows, cols),
            "cols_half",
            [f32(cases, width), f32(cases, wide)]
            + [bf16(cases, width + PIECES * wide)] * (rows - 1),
            here,
            list_p,
            list_q,
            tiles,
            *row_group,
            *extra,
            scalars=(0, 1, 2),
            scratch=[
                pltpu.VMEM((cols * per, cases, leaf), jnp.bfloat16),
                pltpu.VMEM((rows * per, cases, leaf), jnp.float32),
            ],
            flops=half_flops,
        )
        own_row, *row_messages = call(
            pair_kernel,
            "pair_sums",
            [f32(cases, width)] + [bf16(cases, width)] * (chips - 1),
            here,
            keep,
            got,
            scalars=(0,),
        )
        from_chips = [partner_permute(m, "col", 2 * k) for k, m in enumerate(row_messages, 1)]
        from_rows = [partner_permute(m, "row", k) for k, m in enumerate(col_messages, 1)]
        return [own_row, own_col, *from_chips], from_rows, gram

    def advance(first, vector, shift, parts):
        sums, from_rows, gram = parts
        return call(
            functools.partial(combine_kernel, rows, first),
            "combine",
            [f32(cases, width), bf16(cases, long), f32(cases, GRAM)],
            vector,
            diagonal,
            shift,
            gram,
            *sums,
            *from_rows,
        )

    b = right_side
    message = call(first_kernel, "first_message", bf16(cases, long), b, diagonal)
    u, message, gram0 = advance(True, b, diagonal, apply(message))
    shift = call(shift_kernel, "shift", f32(8, 128), gram0)
    v, message, gram1 = advance(False, u, shift, apply(message))
    first = call(
        first_coefficients_kernel, "coefficients", f32(cases, 4 * cases), shift, gram0, gram1
    )
    sums, from_rows, gram = apply(message, last=(v, diagonal))
    gram2, both = call(
        last_gram_kernel, "last_gram", [f32(cases, GRAM), f32(cases, GRAM)], gram, *from_rows
    )
    over_chip = [partner_permute(both, "col", 2 * k) for k in range(1, chips)]
    both = functools.reduce(jnp.add, over_chip, both)
    other = partner_permute(both, "col", 1)
    vectors, small = call(
        second_coefficients_kernel,
        "coefficients",
        [f32(3 * cases, 4 * cases), f32(cases, 2 * cases)],
        shift,
        gram0,
        gram1,
        gram2,
        first,
    )
    return call(
        finish_kernel,
        "finish",
        [f32(cases, width), f32(cases, width)],
        vectors,
        small,
        both,
        other,
        b,
        u,
        v,
        diagonal,
        *sums,
        *from_rows,
    )


def solution(mesh):
    in_specs = (
        P(None, ("row", "col")),
        P(("row", "col")),
        P("row", "col", None, None, None),
        P("row", "col", None),
        P("row", "col", None),
        P("row", "col"),
        P("row", "col", None, None, None),
        P("row", "col", None, None, None),
        P("row", "col", None),
        P("row", "col", None),
        P("row", "col", None),
    )
    out_specs = (P(None, ("row", "col")), P(None, ("row", "col")))
    return jax.shard_map(local, mesh=mesh, in_specs=in_specs, out_specs=out_specs, check_vma=False)
```

time: 181 us -> 151 us (0.83)
  starting transfers between devices: 76.1 us -> 58.3 us
  matrix products: 8.58 us -> 0 us
  Pallas kernels: 57.4 us -> 49.6 us
  waiting for transfers between devices: 28.1 us -> 32.8 us
    ppermute x72 -> x55, starting transfers between devices: 76.1 us -> 58.3 us  [partner_permute(): return lax.ppermute(value, axis, [(i, i ^ flip) for i in range(size)])]
    dot_general x23 -> x0, matrix products: 8.58 us -> none  [the longest x15 6.38 us: combine(): jnp.dot(weights.T, rows_in, preferred_element_type=jnp.float32, precision...]
    pallas_call x15 -> x18, Pallas kernels: 57.4 us -> 49.6 us  [call(): pl.pallas_call(kernel, out_shape=outs, in_specs=[smem if k in scalars els...]
    ppermute x72 -> x55, waiting for transfers between devices: 28.1 us -> 32.8 us  [partner_permute(): return lax.ppermute(value, axis, [(i, i ^ flip) for i in range(size)])]
  transfers between devices with their start and end apart: 72 -> 55, of which waited for: 20 -> 8; matrix products, arithmetic and copies ran while one was open for 2% -> 1% of each run, Pallas kernels for 26% -> 26%
where the time goes in v2:
time: 151 us
  starting transfers between devices  58.3 us (39%)
  Pallas kernels  49.6 us (33%)
  waiting for transfers between devices  32.8 us (22%)
  local copies, waits for them, and re-layouts  7.46 us (5%)
  between operations  1.63 us (1%)
    ppermute x55, starting transfers between devices, partner_permute(): return lax.ppermute(value, axis, [(i, i ^ flip) for i in range(size)])  58.3 us
    pallas_call x18, Pallas kernels, call(): pl.pallas_call(kernel, out_shape=outs, in_specs=[smem if k in scalars els...  49.6 us
    ppermute x55, waiting for transfers between devices, partner_permute(): return lax.ppermute(value, axis, [(i, i ^ flip) for i in range(size)])  32.8 us
    unnamed x16, local copies, waits for them, and re-layouts  6.77 us
  transfers between devices with their start and end apart: 55, of which 8 were waited for; matrix products, arithmetic and copies ran while one was open for 1% of the time, Pallas kernels for 26%

profile of v2, /device:TPU:0, one launch (start us, length us, event | category | flops | bytes accessed | tf_op | source)
XLA Modules:
  0.0 150.7 jit_solution(16917972627558825328)
XLA Ops:
  0.6 0.7 broadcast_in_dim.3.diagonal_ref.shift_ref.refs_13_
  1.3 0.9 copy-done
  2.6 3.0 %collective-permute-start.7 = (bf16[64,1024]{1,0:T(8,128)(2,1)S(1)}, bf16[64,1024]{1,0:T(8,128)(2,1)S(1)}, u32[]{:S(2)}, u32[]{:S(2)}) collective-permute-start(bf16[64,1024]{1,0:T(8,128)(2,1)S(1)} %first_message.1.refs_0_), channel_id=1, source_target_pairs={{0,8},{8,0},{16,24},{24,16},{1,9},{9,1},{17,25},{25,17},{2,10},{10... | collective-permute-start | bytes 393224 | tf_op jit(solution)/shard_map/ppermute | solution.py:48
  5.6 1.5 %collective-permute-start.8 = (bf16[64,1024]{1,0:T(8,128)(2,1)S(1)}, bf16[64,1024]{1,0:T(8,128)(2,1)S(1)}, u32[]{:S(2)}, u32[]{:S(2)}) collective-permute-start(bf16[64,1024]{1,0:T(8,128)(2,1)S(1)} %first_message.1.refs_0_), channel_id=1, source_target_pairs={{0,16},{8,24},{16,0},{24,8},{1,17},{9,25},{17,1},{25,9},{2,18},{10... | collective-permute-start | bytes 393224 | tf_op jit(solution)/shard_map/ppermute | solution.py:48
  7.1 2.0 %collective-permute-start.1 = (bf16[64,1024]{1,0:T(8,128)(2,1)S(1)}, bf16[64,1024]{1,0:T(8,128)(2,1)S(1)}, u32[]{:S(2)}, u32[]{:S(2)}) collective-permute-start(bf16[64,1024]{1,0:T(8,128)(2,1)S(1)} %first_message.1.refs_0_), channel_id=1, source_target_pairs={{0,2},{1,3},{2,0},{3,1},{4,6},{5,7},{6,4},{7,5},{8,10},{9,11},{10,... | collective-permute-start | bytes 393224 | tf_op jit(solution)/shard_map/ppermute | solution.py:48
  9.1 2.6 %collective-permute-start.3 = (bf16[64,1024]{1,0:T(8,128)(2,1)S(1)}, bf16[64,1024]{1,0:T(8,128)(2,1)S(1)}, u32[]{:S(2)}, u32[]{:S(2)}) collective-permute-start(bf16[64,1024]{1,0:T(8,128)(2,1)S(1)} %first_message.1.refs_0_), channel_id=1, source_target_pairs={{0,4},{1,5},{2,6},{3,7},{4,0},{5,1},{6,2},{7,3},{8,12},{9,13},{10,... | collective-permute-start | bytes 393224 | tf_op jit(solution)/shard_map/ppermute | solution.py:48
  11.7 1.6 %collective-permute-start.5 = (bf16[64,1024]{1,0:T(8,128)(2,1)S(1)}, bf16[64,1024]{1,0:T(8,128)(2,1)S(1)}, u32[]{:S(2)}, u32[]{:S(2)}) collective-permute-start(bf16[64,1024]{1,0:T(8,128)(2,1)S(1)} %first_message.1.refs_0_), channel_id=1, source_target_pairs={{0,6},{1,7},{2,4},{3,5},{4,2},{5,3},{6,0},{7,1},{8,14},{9,15},{10,... | collective-permute-start | bytes 393224 | tf_op jit(solution)/shard_map/ppermute | solution.py:48
  14.0 1.2 copy-done.2
  15.2 1.0 copy-done.3
  16.3 1.0 copy-done.4
  17.3 0.7 copy-done.5
  18.0 5.5 %dense_tiles.1 = (bf16[96,128,128]{2,1,0:T(8,128)(2,1)S(1)}, bf16[96,128,128]{2,1,0:T(8,128)(2,1)}) custom-call(s32[1]{0:T(128)} %bitcast.11.count_ref, s32[64]{0:T(128)S(1)} %bitcast.15, bf16[32,128,128]{2,1,0:T(8,128)(2,1)S(1)} %bitcast.12, bf16[64,32,128]{2,1,0:T(8,128)(2,1)S(1)} %bitcast.13, bf16[64,32,128]{2,1,0:T(8,128)(2,1)S(1)} %bitcast.14), custom_call_target="tpu_custom_call" | custom-call | tf_op jit(solution)/shard_map/dense_tiles/pallas_call | solution.py:317
  23.5 0.8 pad_add_fusion.1
  25.3 1.9 %copy-done.6 = bf16[96,128,128]{2,1,0:T(8,128)(2,1)S(1)} copy-done((bf16[96,128,128]{2,1,0:T(8,128)(2,1)S(1)}, bf16[96,128,128]{2,1,0:T(8,128)(2,1)}, u32[]{:S(2)}) %copy-start.6) | copy-done | bytes 3145752
  27.2 2.4 %rows_half.3 = (bf16[4,64,640]{2,1,0:T(8,128)(2,1)S(1)}, f32[4,64,640]{2,1,0:T(8,128)S(1)}) custom-call(s32[2]{0:T(128)S(1)} %pad_add_fusion.place_ref, s32[96]{0:T(128)S(1)} %get-tuple-element.93.to_ref.from_ref, s32[96]{0:T(128)S(1)} %get-tuple-element.92.from_ref.to_ref, bf16[96,128,128]{2,1,0:T(8,128)(2,1)S(1)} %copy-done.6, ...), custom_call_target="tpu_custom_call" | custom-call | flops 1610612736 | tf_op jit(solution)/shard_map/rows_half/pallas_call | solution.py:317
  29.8 2.5 %cols_half.3 = (f32[64,640]{1,0:T(8,128)S(1)}, f32[64,128]{1,0:T(8,128)S(1)}, bf16[64,1024]{1,0:T(8,128)(2,1)S(1)}, bf16[64,1024]{1,0:T(8,128)(2,1)S(1)}, bf16[64,1024]{1,0:T(8,128)(2,1)S(1)}) custom-call(s32[2]{0:T(128)S(1)} %pad_add_fusion.place_ref, s32[96]{0:T(128)S(1)} %get-tuple-element.92.from_ref.to_ref, s32[96]{0:T(128)S(1)} %get-tuple-element.93.to_ref.from_ref, ...), custom_call_target="tpu_custom_call" | custom-call | flops 1610612736 | tf_op jit(solution)/shard_map/cols_half/pallas_call | solution.py:317
  32.3 2.3 %collective-permute-start.14 = (bf16[64,1024]{1,0:T(8,128)(2,1)S(1)}, bf16[64,1024]{1,0:T(8,128)(2,1)S(1)}, u32[]{:S(2)}, u32[]{:S(2)}) collective-permute-start(bf16[64,1024]{1,0:T(8,128)(2,1)S(1)} %get-tuple-element.57), channel_id=1, source_target_pairs={{0,8},{8,0},{16,24},{24,16},{1,9},{9,1},{17,25},{25,17},{2,10},{10... | collective-permute-start | bytes 393224 | tf_op jit(solution)/shard_map/ppermute | solution.py:48
  34.6 1.5 %collective-permute-start.15 = (bf16[64,1024]{1,0:T(8,128)(2,1)S(1)}, bf16[64,1024]{1,0:T(8,128)(2,1)S(1)}, u32[]{:S(2)}, u32[]{:S(2)}) collective-permute-start(bf16[64,1024]{1,0:T(8,128)(2,1)S(1)} %get-tuple-element.58), channel_id=1, source_target_pairs={{0,16},{8,24},{16,0},{24,8},{1,17},{9,25},{17,1},{25,9},{2,18},{10... | collective-permute-start | bytes 393224 | tf_op jit(solution)/shard_map/ppermute | solution.py:48
  36.2 0.6 pair_sums.3
  36.9 2.5 %collective-permute-start.12 = (bf16[64,640]{1,0:T(8,128)(2,1)S(1)}, bf16[64,640]{1,0:T(8,128)(2,1)S(1)}, u32[]{:S(2)}, u32[]{:S(2)}) collective-permute-start(bf16[64,640]{1,0:T(8,128)(2,1)S(1)} %get-tuple-element.55), channel_id=1, source_target_pairs={{0,4},{1,5},{2,6},{3,7},{4,0},{5,1},{6,2},{7,3},{8,12},{9,13},{10,... | collective-permute-start | bytes 245768 | tf_op jit(solution)/shard_map/ppermute | solution.py:48
  39.4 1.9 %collective-permute-start.13 = (bf16[64,640]{1,0:T(8,128)(2,1)S(1)}, bf16[64,640]{1,0:T(8,128)(2,1)S(1)}, u32[]{:S(2)}, u32[]{:S(2)}) collective-permute-start(bf16[64,640]{1,0:T(8,128)(2,1)S(1)} %get-tuple-element.56), channel_id=1, source_target_pairs={{0,6},{1,7},{2,4},{3,5},{4,2},{5,3},{6,0},{7,1},{8,14},{9,15},{10,... | collective-permute-start | bytes 245768 | tf_op jit(solution)/shard_map/ppermute | solution.py:48
  41.3 1.7 %collective-permute-done.15.refs_6_ = bf16[64,1024]{1,0:T(8,128)(2,1)S(1)} collective-permute-done((bf16[64,1024]{1,0:T(8,128)(2,1)S(1)}, bf16[64,1024]{1,0:T(8,128)(2,1)S(1)}, u32[]{:S(2)}, u32[]{:S(2)}) %collective-permute-start.15) | collective-permute-done | bytes 131104 | tf_op jit(solution)/shard_map/ppermute | solution.py:48
  43.0 3.5 %collective-permute-done.12.refs_3_ = bf16[64,640]{1,0:T(8,128)(2,1)S(1)} collective-permute-done((bf16[64,640]{1,0:T(8,128)(2,1)S(1)}, bf16[64,640]{1,0:T(8,128)(2,1)S(1)}, u32[]{:S(2)}, u32[]{:S(2)}) %collective-permute-start.12) | collective-permute-done | bytes 81952 | tf_op jit(solution)/shard_map/ppermute | solution.py:48
  46.5 0.8 combine.2
  47.2 1.7 %collective-permute-start.24 = (bf16[64,1024]{1,0:T(8,128)(2,1)S(1)}, bf16[64,1024]{1,0:T(8,128)(2,1)S(1)}, u32[]{:S(2)}, u32[]{:S(2)}) collective-permute-start(bf16[64,1024]{1,0:T(8,128)(2,1)S(1)} %get-tuple-element.62.refs_0_), channel_id=1, source_target_pairs={{0,8},{8,0},{16,24},{24,16},{1,9},{9,1},{17,25},{25,17},{2,10},{10... | collective-permute-start | bytes 393224 | tf_op jit(solution)/shard_map/ppermute | solution.py:48
  49.0 1.5 %collective-permute-start.25 = (bf16[64,1024]{1,0:T(8,128)(2,1)S(1)}, bf16[64,1024]{1,0:T(8,128)(2,1)S(1)}, u32[]{:S(2)}, u32[]{:S(2)}) collective-permute-start(bf16[64,1024]{1,0:T(8,128)(2,1)S(1)} %get-tuple-element.62.refs_0_), channel_id=1, source_target_pairs={{0,16},{8,24},{16,0},{24,8},{1,17},{9,25},{17,1},{25,9},{2,18},{10... | collective-permute-start | bytes 393224 | tf_op jit(solution)/shard_map/ppermute | solution.py:48
  50.5 1.4 collective-permute-start.18
  51.9 0.9 collective-permute-start.20
  52.8 2.1 %collective-permute-start.22 = (bf16[64,1024]{1,0:T(8,128)(2,1)S(1)}, bf16[64,1024]{1,0:T(8,128)(2,1)S(1)}, u32[]{:S(2)}, u32[]{:S(2)}) collective-permute-start(bf16[64,1024]{1,0:T(8,128)(2,1)S(1)} %get-tuple-element.62.refs_0_), channel_id=1, source_target_pairs={{0,6},{1,7},{2,4},{3,5},{4,2},{5,3},{6,0},{7,1},{8,14},{9,15},{10,... | collective-permute-start | bytes 393224 | tf_op jit(solution)/shard_map/ppermute | solution.py:48
  55.2 0.5 collective-permute-done.18.refs_2_
  55.7 7.3 %collective-permute-done.20.refs_4_ = bf16[64,1024]{1,0:T(8,128)(2,1)S(1)} collective-permute-done((bf16[64,1024]{1,0:T(8,128)(2,1)S(1)}, bf16[64,1024]{1,0:T(8,128)(2,1)S(1)}, u32[]{:S(2)}, u32[]{:S(2)}) %collective-permute-start.20) | collective-permute-done | bytes 131104 | tf_op jit(solution)/shard_map/ppermute | solution.py:48
  63.0 0.5 collective-permute-start.23
  63.5 2.4 %rows_half.4 = (bf16[4,64,640]{2,1,0:T(8,128)(2,1)S(1)}, f32[4,64,640]{2,1,0:T(8,128)S(1)}) custom-call(s32[2]{0:T(128)S(1)} %pad_add_fusion.place_ref, s32[96]{0:T(128)S(1)} %get-tuple-element.93.to_ref.from_ref, s32[96]{0:T(128)S(1)} %get-tuple-element.92.from_ref.to_ref, bf16[96,128,128]{2,1,0:T(8,128)(2,1)S(1)} %copy-done.7, ...), custom_call_target="tpu_custom_call" | custom-call | flops 1610612736 | tf_op jit(solution)/shard_map/rows_half/pallas_call | solution.py:317
  66.1 2.5 %cols_half.4 = (f32[64,640]{1,0:T(8,128)S(1)}, f32[64,128]{1,0:T(8,128)S(1)}, bf16[64,1024]{1,0:T(8,128)(2,1)S(1)}, bf16[64,1024]{1,0:T(8,128)(2,1)S(1)}, bf16[64,1024]{1,0:T(8,128)(2,1)S(1)}) custom-call(s32[2]{0:T(128)S(1)} %pad_add_fusion.place_ref, s32[96]{0:T(128)S(1)} %get-tuple-element.92.from_ref.to_ref, s32[96]{0:T(128)S(1)} %get-tuple-element.93.to_ref.from_ref, ...), custom_call_target="tpu_custom_call" | custom-call | flops 1610612736 | tf_op jit(solution)/shard_map/cols_half/pallas_call | solution.py:317
  69.5 2.6 %collective-permute-start.33 = (bf16[64,1024]{1,0:T(8,128)(2,1)S(1)}, bf16[64,1024]{1,0:T(8,128)(2,1)S(1)}, u32[]{:S(2)}, u32[]{:S(2)}) collective-permute-start(bf16[64,1024]{1,0:T(8,128)(2,1)S(1)} %get-tuple-element.73), channel_id=1, source_target_pairs={{0,24},{8,16},{16,8},{24,0},{1,25},{9,17},{17,9},{25,1},{2,26},{10... | collective-permute-start | bytes 393224 | tf_op jit(solution)/shard_map/ppermute | solution.py:48
  72.1 0.6 pair_sums.4
  72.8 2.0 %collective-permute-start.28 = (bf16[64,640]{1,0:T(8,128)(2,1)S(1)}, bf16[64,640]{1,0:T(8,128)(2,1)S(1)}, u32[]{:S(2)}, u32[]{:S(2)}) collective-permute-start(bf16[64,640]{1,0:T(8,128)(2,1)S(1)} %get-tuple-element.68), channel_id=1, source_target_pairs={{0,2},{1,3},{2,0},{3,1},{4,6},{5,7},{6,4},{7,5},{8,10},{9,11},{10,... | collective-permute-start | bytes 245768 | tf_op jit(solution)/shard_map/ppermute | solution.py:48
  74.8 0.6 collective-permute-start.29
  75.4 1.8 %collective-permute-start.30 = (bf16[64,640]{1,0:T(8,128)(2,1)S(1)}, bf16[64,640]{1,0:T(8,128)(2,1)S(1)}, u32[]{:S(2)}, u32[]{:S(2)}) collective-permute-start(bf16[64,640]{1,0:T(8,128)(2,1)S(1)} %get-tuple-element.70), channel_id=1, source_target_pairs={{0,6},{1,7},{2,4},{3,5},{4,2},{5,3},{6,0},{7,1},{8,14},{9,15},{10,... | collective-permute-start | bytes 245768 | tf_op jit(solution)/shard_map/ppermute | solution.py:48
  77.4 5.9 %collective-permute-done.29.refs_3_ = bf16[64,640]{1,0:T(8,128)(2,1)S(1)} collective-permute-done((bf16[64,640]{1,0:T(8,128)(2,1)S(1)}, bf16[64,640]{1,0:T(8,128)(2,1)S(1)}, u32[]{:S(2)}, u32[]{:S(2)}) %collective-permute-start.29) | collective-permute-done | bytes 81952 | tf_op jit(solution)/shard_map/ppermute | solution.py:48
  83.3 0.6 combine.3
  83.9 0.6 collective-permute-start.41
  85.0 1.4 collective-permute-start.35
  86.5 1.0 collective-permute-start.37
  87.5 1.9 %collective-permute-start.39 = (bf16[64,1024]{1,0:T(8,128)(2,1)S(1)}, bf16[64,1024]{1,0:T(8,128)(2,1)S(1)}, u32[]{:S(2)}, u32[]{:S(2)}) collective-permute-start(bf16[64,1024]{1,0:T(8,128)(2,1)S(1)} %get-tuple-element.75.refs_0_.refs_8_), channel_id=1, source_target_pairs={{0,6},{1,7},{2,4},{3,5},{4,2},{5,3},{6,0},{7,1},{8,14},{9,15},{10,... | collective-permute-start | bytes 393224 | tf_op jit(solution)/shard_map/ppermute | solution.py:48
  89.4 2.5 %collective-permute-start.43 = (bf16[64,1024]{1,0:T(8,128)(2,1)S(1)}, bf16[64,1024]{1,0:T(8,128)(2,1)S(1)}, u32[]{:S(2)}, u32[]{:S(2)}) collective-permute-start(bf16[64,1024]{1,0:T(8,128)(2,1)S(1)} %get-tuple-element.75.refs_0_.refs_8_), channel_id=1, source_target_pairs={{0,24},{8,16},{16,8},{24,0},{1,25},{9,17},{17,9},{25,1},{2,26},{10... | collective-permute-start | bytes 393224 | tf_op jit(solution)/shard_map/ppermute | solution.py:48
  92.4 5.2 %collective-permute-done.37.refs_4_ = bf16[64,1024]{1,0:T(8,128)(2,1)S(1)} collective-permute-done((bf16[64,1024]{1,0:T(8,128)(2,1)S(1)}, bf16[64,1024]{1,0:T(8,128)(2,1)S(1)}, u32[]{:S(2)}, u32[]{:S(2)}) %collective-permute-start.37) | collective-permute-done | bytes 131104 | tf_op jit(solution)/shard_map/ppermute | solution.py:48
  97.7 0.5 collective-permute-start.40
  98.2 2.4 %rows_half.5 = (bf16[4,64,640]{2,1,0:T(8,128)(2,1)S(1)}, f32[4,64,640]{2,1,0:T(8,128)S(1)}) custom-call(s32[2]{0:T(128)S(1)} %pad_add_fusion.place_ref, s32[96]{0:T(128)S(1)} %get-tuple-element.93.to_ref.from_ref, s32[96]{0:T(128)S(1)} %get-tuple-element.92.from_ref.to_ref, bf16[96,128,128]{2,1,0:T(8,128)(2,1)S(1)} %copy-done.7, ...), custom_call_target="tpu_custom_call" | custom-call | flops 1610612736 | tf_op jit(solution)/shard_map/rows_half/pallas_call | solution.py:317
  100.7 3.1 %cols_half.5 = (f32[64,640]{1,0:T(8,128)S(1)}, f32[64,256]{1,0:T(8,128)S(1)}, bf16[64,1408]{1,0:T(8,128)(2,1)S(1)}, bf16[64,1408]{1,0:T(8,128)(2,1)S(1)}, bf16[64,1408]{1,0:T(8,128)(2,1)S(1)}) custom-call(s32[2]{0:T(128)S(1)} %pad_add_fusion.place_ref, s32[96]{0:T(128)S(1)} %get-tuple-element.92.from_ref.to_ref, s32[96]{0:T(128)S(1)} %get-tuple-element.93.to_ref.from_ref, ...), custom_call_target="tpu_custom_call" | custom-call | flops 1610612736 | tf_op jit(solution)/shard_map/cols_half/pallas_call | solution.py:317
  103.8 1.7 %collective-permute-start.44 = (bf16[64,1408]{1,0:T(8,128)(2,1)S(1)}, bf16[64,1408]{1,0:T(8,128)(2,1)S(1)}, u32[]{:S(2)}, u32[]{:S(2)}) collective-permute-start(bf16[64,1408]{1,0:T(8,128)(2,1)S(1)} %get-tuple-element.78), channel_id=1, source_target_pairs={{0,8},{8,0},{16,24},{24,16},{1,9},{9,1},{17,25},{25,17},{2,10},{10... | collective-permute-start | bytes 540680 | tf_op jit(solution)/shard_map/ppermute | solution.py:48
  105.5 1.5 %collective-permute-start.45 = (bf16[64,1408]{1,0:T(8,128)(2,1)S(1)}, bf16[64,1408]{1,0:T(8,128)(2,1)S(1)}, u32[]{:S(2)}, u32[]{:S(2)}) collective-permute-start(bf16[64,1408]{1,0:T(8,128)(2,1)S(1)} %get-tuple-element.79), channel_id=1, source_target_pairs={{0,16},{8,24},{16,0},{24,8},{1,17},{9,25},{17,1},{25,9},{2,18},{10... | collective-permute-start | bytes 540680 | tf_op jit(solution)/shard_map/ppermute | solution.py:48
  107.4 3.9 %collective-permute-done.44.refs_0_.refs_5_ = bf16[64,1408]{1,0:T(8,128)(2,1)S(1)} collective-permute-done((bf16[64,1408]{1,0:T(8,128)(2,1)S(1)}, bf16[64,1408]{1,0:T(8,128)(2,1)S(1)}, u32[]{:S(2)}, u32[]{:S(2)}) %collective-permute-start.44) | collective-permute-done | bytes 180256 | tf_op jit(solution)/shard_map/ppermute | solution.py:48
  111.3 4.8 %collective-permute-done.45.refs_1_.refs_6_ = bf16[64,1408]{1,0:T(8,128)(2,1)S(1)} collective-permute-done((bf16[64,1408]{1,0:T(8,128)(2,1)S(1)}, bf16[64,1408]{1,0:T(8,128)(2,1)S(1)}, u32[]{:S(2)}, u32[]{:S(2)}) %collective-permute-start.45) | collective-permute-done | bytes 180256 | tf_op jit(solution)/shard_map/ppermute | solution.py:48
  116.1 1.7 %collective-permute-start.47 = (f32[64,128]{1,0:T(8,128)S(1)}, f32[64,128]{1,0:T(8,128)S(1)}, u32[]{:S(2)}, u32[]{:S(2)}) collective-permute-start(f32[64,128]{1,0:T(8,128)S(1)} %get-tuple-element.84), channel_id=1, source_target_pairs={{0,2},{1,3},{2,0},{3,1},{4,6},{5,7},{6,4},{7,5},{8,10},{9,11},{10,... | collective-permute-start | bytes 98312 | tf_op jit(solution)/shard_map/ppermute | solution.py:48
  117.8 0.8 collective-permute-start.48
  118.6 1.9 %collective-permute-start.49 = (f32[64,128]{1,0:T(8,128)S(1)}, f32[64,128]{1,0:T(8,128)S(1)}, u32[]{:S(2)}, u32[]{:S(2)}) collective-permute-start(f32[64,128]{1,0:T(8,128)S(1)} %get-tuple-element.84), channel_id=1, source_target_pairs={{0,6},{1,7},{2,4},{3,5},{4,2},{5,3},{6,0},{7,1},{8,14},{9,15},{10,... | collective-permute-start | bytes 98312 | tf_op jit(solution)/shard_map/ppermute | solution.py:48
  120.5 0.6 pair_sums.5
  121.1 0.8 collective-permute-start.52
  122.0 1.7 %collective-permute-start.53 = (bf16[64,640]{1,0:T(8,128)(2,1)S(1)}, bf16[64,640]{1,0:T(8,128)(2,1)S(1)}, u32[]{:S(2)}, u32[]{:S(2)}) collective-permute-start(bf16[64,640]{1,0:T(8,128)(2,1)S(1)} %get-tuple-element.90), channel_id=1, source_target_pairs={{0,4},{1,5},{2,6},{3,7},{4,0},{5,1},{6,2},{7,3},{8,12},{9,13},{10,... | collective-permute-start | bytes 245768 | tf_op jit(solution)/shard_map/ppermute | solution.py:48
  123.7 1.9 %collective-permute-start.54 = (bf16[64,640]{1,0:T(8,128)(2,1)S(1)}, bf16[64,640]{1,0:T(8,128)(2,1)S(1)}, u32[]{:S(2)}, u32[]{:S(2)}) collective-permute-start(bf16[64,640]{1,0:T(8,128)(2,1)S(1)} %get-tuple-element.91), channel_id=1, source_target_pairs={{0,6},{1,7},{2,4},{3,5},{4,2},{5,3},{6,0},{7,1},{8,14},{9,15},{10,... | collective-permute-start | bytes 245768 | tf_op jit(solution)/shard_map/ppermute | solution.py:48
  125.7 6.7 %coefficients.2.first_ref = f32[64,256]{1,0:T(8,128)S(1)} custom-call(f32[8,128]{1,0:T(8,128)S(1)} %shift.1.shift_ref, f32[64,128]{1,0:T(8,128)S(1)} %get-tuple-element.60.gram_ref.gram0_ref, f32[64,128]{1,0:T(8,128)S(1)} %get-tuple-element.74.gram1_ref), custom_call_target="tpu_custom_call" | custom-call | tf_op jit(solution)/shard_map/coefficients/pallas_call | solution.py:317
  132.4 9.7 %coefficients.3 = (f32[192,256]{1,0:T(8,128)S(1)}, f32[64,128]{1,0:T(8,128)S(1)}) custom-call(f32[8,128]{1,0:T(8,128)S(1)} %shift.1.shift_ref, f32[64,128]{1,0:T(8,128)S(1)} %get-tuple-element.60.gram_ref.gram0_ref, f32[64,128]{1,0:T(8,128)S(1)} %get-tuple-element.74.gram1_ref, f32[64,128]{1,0:T(8,128)S(1)} %get-tuple-element.81.gram2_ref, ...), custom_call_target="tpu_custom_call" | custom-call | tf_op jit(solution)/shard_map/coefficients/pallas_call | solution.py:317
  142.1 8.6 %finish.1 = (f32[64,640]{1,0:T(8,128)}, f32[64,640]{1,0:T(8,128)}) custom-call(f32[192,256]{1,0:T(8,128)S(1)} %get-tuple-element.82.vectors_ref, f32[64,128]{1,0:T(8,128)S(1)} %get-tuple-element.83.small_ref, f32[64,128]{1,0:T(8,128)S(1)} %add_add_fusion.both_ref, f32[64,128]{1,0:T(8,128)S(1)} %collective-permute-done.50.other_ref, f32[64,640]{1,0:T(8,128)S(1)} %copy-done.1, ...), custom_call_target="tpu_custom_call" | custom-call | tf_op jit(solution)/shard_map/finish/pallas_call | solution.py:317
  (84 shorter events, 4.9 us)
Async XLA Ops:
  1.3 0.9 copy-start
  2.6 9.2 %collective-permute-start.7 = (bf16[64,1024]{1,0:T(8,128)(2,1)S(1)}, bf16[64,1024]{1,0:T(8,128)(2,1)S(1)}, u32[]{:S(2)}, u32[]{:S(2)}) collective-permute-start(bf16[64,1024]{1,0:T(8,128)(2,1)S(1)} %first_message.1.refs_0_), channel_id=1, source_target_pairs={{0,8},{8,0},{16,24},{24,16},{1,9},{9,1},{17,25},{25,17},{2,10},{10... | collective-permute-start | bytes 393224 | tf_op jit(solution)/shard_map/ppermute | solution.py:48
  5.6 18.7 %collective-permute-start.8 = (bf16[64,1024]{1,0:T(8,128)(2,1)S(1)}, bf16[64,1024]{1,0:T(8,128)(2,1)S(1)}, u32[]{:S(2)}, u32[]{:S(2)}) collective-permute-start(bf16[64,1024]{1,0:T(8,128)(2,1)S(1)} %first_message.1.refs_0_), channel_id=1, source_target_pairs={{0,16},{8,24},{16,0},{24,8},{1,17},{9,25},{17,1},{25,9},{2,18},{10... | collective-permute-start | bytes 393224 | tf_op jit(solution)/shard_map/ppermute | solution.py:48
  7.1 18.2 %collective-permute-start.9 = (bf16[64,1024]{1,0:T(8,128)(2,1)S(1)}, bf16[64,1024]{1,0:T(8,128)(2,1)S(1)}, u32[]{:S(2)}, u32[]{:S(2)}) collective-permute-start(bf16[64,1024]{1,0:T(8,128)(2,1)S(1)} %first_message.1.refs_0_), channel_id=1, source_target_pairs={{0,24},{8,16},{16,8},{24,0},{1,25},{9,17},{17,9},{25,1},{2,26},{10... | collective-permute-start | bytes 393224 | tf_op jit(solution)/shard_map/ppermute | solution.py:48
  7.1 17.2 %collective-permute-start.1 = (bf16[64,1024]{1,0:T(8,128)(2,1)S(1)}, bf16[64,1024]{1,0:T(8,128)(2,1)S(1)}, u32[]{:S(2)}, u32[]{:S(2)}) collective-permute-start(bf16[64,1024]{1,0:T(8,128)(2,1)S(1)} %first_message.1.refs_0_), channel_id=1, source_target_pairs={{0,2},{1,3},{2,0},{3,1},{4,6},{5,7},{6,4},{7,5},{8,10},{9,11},{10,... | collective-permute-start | bytes 393224 | tf_op jit(solution)/shard_map/ppermute | solution.py:48
  9.1 15.6 %collective-permute-start.3 = (bf16[64,1024]{1,0:T(8,128)(2,1)S(1)}, bf16[64,1024]{1,0:T(8,128)(2,1)S(1)}, u32[]{:S(2)}, u32[]{:S(2)}) collective-permute-start(bf16[64,1024]{1,0:T(8,128)(2,1)S(1)} %first_message.1.refs_0_), channel_id=1, source_target_pairs={{0,4},{1,5},{2,6},{3,7},{4,0},{5,1},{6,2},{7,3},{8,12},{9,13},{10,... | collective-permute-start | bytes 393224 | tf_op jit(solution)/shard_map/ppermute | solution.py:48
  11.7 13.1 %collective-permute-start.5 = (bf16[64,1024]{1,0:T(8,128)(2,1)S(1)}, bf16[64,1024]{1,0:T(8,128)(2,1)S(1)}, u32[]{:S(2)}, u32[]{:S(2)}) collective-permute-start(bf16[64,1024]{1,0:T(8,128)(2,1)S(1)} %first_message.1.refs_0_), channel_id=1, source_target_pairs={{0,6},{1,7},{2,4},{3,5},{4,2},{5,3},{6,0},{7,1},{8,14},{9,15},{10,... | collective-permute-start | bytes 393224 | tf_op jit(solution)/shard_map/ppermute | solution.py:48
  14.0 1.2 copy-start.2
  15.2 1.0 copy-start.3
  16.3 1.0 copy-start.4
  17.3 0.7 copy-start.5
  24.2 5.5 %collective-permute-start = (bf16[64,1024]{1,0:T(8,128)(2,1)S(1)}, bf16[64,1024]{1,0:T(8,128)(2,1)S(1)}, u32[]{:S(2)}, u32[]{:S(2)}) collective-permute-start(bf16[64,1024]{1,0:T(8,128)(2,1)S(1)} %first_message.1.refs_0_), channel_id=1, source_target_pairs={{0,1},{1,0},{2,3},{3,2},{4,5},{5,4},{6,7},{7,6},{8,9},{9,8},{10,11... | collective-permute-start | bytes 393224 | tf_op jit(solution)/shard_map/ppermute | solution.py:48
  24.3 5.5 %collective-permute-start.2 = (bf16[64,1024]{1,0:T(8,128)(2,1)S(1)}, bf16[64,1024]{1,0:T(8,128)(2,1)S(1)}, u32[]{:S(2)}, u32[]{:S(2)}) collective-permute-start(bf16[64,1024]{1,0:T(8,128)(2,1)S(1)} %collective-permute-done.1.refs_2_), channel_id=1, source_target_pairs={{0,1},{1,0},{2,3},{3,2},{4,5},{5,4},{6,7},{7,6},{8,9},{9,8},{10,11... | collective-permute-start | bytes 393224 | tf_op jit(solution)/shard_map/ppermute | solution.py:48
  24.8 5.0 %collective-permute-start.4 = (bf16[64,1024]{1,0:T(8,128)(2,1)S(1)}, bf16[64,1024]{1,0:T(8,128)(2,1)S(1)}, u32[]{:S(2)}, u32[]{:S(2)}) collective-permute-start(bf16[64,1024]{1,0:T(8,128)(2,1)S(1)} %collective-permute-done.3.refs_4_), channel_id=1, source_target_pairs={{0,1},{1,0},{2,3},{3,2},{4,5},{5,4},{6,7},{7,6},{8,9},{9,8},{10,11... | collective-permute-start | bytes 393224 | tf_op jit(solution)/shard_map/ppermute | solution.py:48
  24.9 4.9 %collective-permute-start.6 = (bf16[64,1024]{1,0:T(8,128)(2,1)S(1)}, bf16[64,1024]{1,0:T(8,128)(2,1)S(1)}, u32[]{:S(2)}, u32[]{:S(2)}) collective-permute-start(bf16[64,1024]{1,0:T(8,128)(2,1)S(1)} %collective-permute-done.5.refs_6_), channel_id=1, source_target_pairs={{0,1},{1,0},{2,3},{3,2},{4,5},{5,4},{6,7},{7,6},{8,9},{9,8},{10,11... | collective-permute-start | bytes 393224 | tf_op jit(solution)/shard_map/ppermute | solution.py:48
  25.3 1.9 %copy-start.6 = (bf16[96,128,128]{2,1,0:T(8,128)(2,1)S(1)}, bf16[96,128,128]{2,1,0:T(8,128)(2,1)}, u32[]{:S(2)}) copy-start(bf16[96,128,128]{2,1,0:T(8,128)(2,1)} %get-tuple-element.49.tile_ref) | copy-start | bytes 9437188
  29.6 6.6 %collective-permute-start.10 = (bf16[4,64,640]{2,1,0:T(8,128)(2,1)S(1)}, bf16[4,64,640]{2,1,0:T(8,128)(2,1)S(1)}, u32[]{:S(2)}, u32[]{:S(2)}) collective-permute-start(bf16[4,64,640]{2,1,0:T(8,128)(2,1)S(1)} %get-tuple-element.51), channel_id=1, source_target_pairs={{0,1},{1,0},{2,3},{3,2},{4,5},{5,4},{6,7},{7,6},{8,9},{9,8},{10,11... | collective-permute-start | bytes 983048 | tf_op jit(solution)/shard_map/ppermute | solution.py:48
  29.8 16.7 %copy-start.1 = (f32[64,640]{1,0:T(8,128)S(1)}, f32[64,640]{1,0:T(8,128)}, u32[]{:S(2)}) copy-start(f32[64,640]{1,0:T(8,128)} %b_ref.1) | copy-start | bytes 491524
  29.8 33.7 %copy-start.7 = (bf16[96,128,128]{2,1,0:T(8,128)(2,1)S(1)}, bf16[96,128,128]{2,1,0:T(8,128)(2,1)}, u32[]{:S(2)}) copy-start(bf16[96,128,128]{2,1,0:T(8,128)(2,1)} %get-tuple-element.49.tile_ref) | copy-start | bytes 9437188
  32.3 7.1 %collective-permute-start.14 = (bf16[64,1024]{1,0:T(8,128)(2,1)S(1)}, bf16[64,1024]{1,0:T(8,128)(2,1)S(1)}, u32[]{:S(2)}, u32[]{:S(2)}) collective-permute-start(bf16[64,1024]{1,0:T(8,128)(2,1)S(1)} %get-tuple-element.57), channel_id=1, source_target_pairs={{0,8},{8,0},{16,24},{24,16},{1,9},{9,1},{17,25},{25,17},{2,10},{10... | collective-permute-start | bytes 393224 | tf_op jit(solution)/shard_map/ppermute | solution.py:48
  34.6 8.4 %collective-permute-start.15 = (bf16[64,1024]{1,0:T(8,128)(2,1)S(1)}, bf16[64,1024]{1,0:T(8,128)(2,1)S(1)}, u32[]{:S(2)}, u32[]{:S(2)}) collective-permute-start(bf16[64,1024]{1,0:T(8,128)(2,1)S(1)} %get-tuple-element.58), channel_id=1, source_target_pairs={{0,16},{8,24},{16,0},{24,8},{1,17},{9,25},{17,1},{25,9},{2,18},{10... | collective-permute-start | bytes 393224 | tf_op jit(solution)/shard_map/ppermute | solution.py:48
  36.2 6.8 %collective-permute-start.16 = (bf16[64,1024]{1,0:T(8,128)(2,1)S(1)}, bf16[64,1024]{1,0:T(8,128)(2,1)S(1)}, u32[]{:S(2)}, u32[]{:S(2)}) collective-permute-start(bf16[64,1024]{1,0:T(8,128)(2,1)S(1)} %get-tuple-element.59), channel_id=1, source_target_pairs={{0,24},{8,16},{16,8},{24,0},{1,25},{9,17},{17,9},{25,1},{2,26},{10... | collective-permute-start | bytes 393224 | tf_op jit(solution)/shard_map/ppermute | solution.py:48
  36.8 6.2 %collective-permute-start.11 = (bf16[64,640]{1,0:T(8,128)(2,1)S(1)}, bf16[64,640]{1,0:T(8,128)(2,1)S(1)}, u32[]{:S(2)}, u32[]{:S(2)}) collective-permute-start(bf16[64,640]{1,0:T(8,128)(2,1)S(1)} %get-tuple-element.54), channel_id=1, source_target_pairs={{0,2},{1,3},{2,0},{3,1},{4,6},{5,7},{6,4},{7,5},{8,10},{9,11},{10,... | collective-permute-start | bytes 245768 | tf_op jit(solution)/shard_map/ppermute | solution.py:48
  36.9 9.6 %collective-permute-start.12 = (bf16[64,640]{1,0:T(8,128)(2,1)S(1)}, bf16[64,640]{1,0:T(8,128)(2,1)S(1)}, u32[]{:S(2)}, u32[]{:S(2)}) collective-permute-start(bf16[64,640]{1,0:T(8,128)(2,1)S(1)} %get-tuple-element.55), channel_id=1, source_target_pairs={{0,4},{1,5},{2,6},{3,7},{4,0},{5,1},{6,2},{7,3},{8,12},{9,13},{10,... | collective-permute-start | bytes 245768 | tf_op jit(solution)/shard_map/ppermute | solution.py:48
  39.4 7.1 %collective-permute-start.13 = (bf16[64,640]{1,0:T(8,128)(2,1)S(1)}, bf16[64,640]{1,0:T(8,128)(2,1)S(1)}, u32[]{:S(2)}, u32[]{:S(2)}) collective-permute-start(bf16[64,640]{1,0:T(8,128)(2,1)S(1)} %get-tuple-element.56), channel_id=1, source_target_pairs={{0,6},{1,7},{2,4},{3,5},{4,2},{5,3},{6,0},{7,1},{8,14},{9,15},{10,... | collective-permute-start | bytes 245768 | tf_op jit(solution)/shard_map/ppermute | solution.py:48
  47.2 7.6 %collective-permute-start.24 = (bf16[64,1024]{1,0:T(8,128)(2,1)S(1)}, bf16[64,1024]{1,0:T(8,128)(2,1)S(1)}, u32[]{:S(2)}, u32[]{:S(2)}) collective-permute-start(bf16[64,1024]{1,0:T(8,128)(2,1)S(1)} %get-tuple-element.62.refs_0_), channel_id=1, source_target_pairs={{0,8},{8,0},{16,24},{24,16},{1,9},{9,1},{17,25},{25,17},{2,10},{10... | collective-permute-start | bytes 393224 | tf_op jit(solution)/shard_map/ppermute | solution.py:48
  49.0 6.2 %collective-permute-start.25 = (bf16[64,1024]{1,0:T(8,128)(2,1)S(1)}, bf16[64,1024]{1,0:T(8,128)(2,1)S(1)}, u32[]{:S(2)}, u32[]{:S(2)}) collective-permute-start(bf16[64,1024]{1,0:T(8,128)(2,1)S(1)} %get-tuple-element.62.refs_0_), channel_id=1, source_target_pairs={{0,16},{8,24},{16,0},{24,8},{1,17},{9,25},{17,1},{25,9},{2,18},{10... | collective-permute-start | bytes 393224 | tf_op jit(solution)/shard_map/ppermute | solution.py:48
  50.5 5.2 %collective-permute-start.18 = (bf16[64,1024]{1,0:T(8,128)(2,1)S(1)}, bf16[64,1024]{1,0:T(8,128)(2,1)S(1)}, u32[]{:S(2)}, u32[]{:S(2)}) collective-permute-start(bf16[64,1024]{1,0:T(8,128)(2,1)S(1)} %get-tuple-element.62.refs_0_), channel_id=1, source_target_pairs={{0,2},{1,3},{2,0},{3,1},{4,6},{5,7},{6,4},{7,5},{8,10},{9,11},{10,... | collective-permute-start | bytes 393224 | tf_op jit(solution)/shard_map/ppermute | solution.py:48
  51.9 11.0 %collective-permute-start.20 = (bf16[64,1024]{1,0:T(8,128)(2,1)S(1)}, bf16[64,1024]{1,0:T(8,128)(2,1)S(1)}, u32[]{:S(2)}, u32[]{:S(2)}) collective-permute-start(bf16[64,1024]{1,0:T(8,128)(2,1)S(1)} %get-tuple-element.62.refs_0_), channel_id=1, source_target_pairs={{0,4},{1,5},{2,6},{3,7},{4,0},{5,1},{6,2},{7,3},{8,12},{9,13},{10,... | collective-permute-start | bytes 393224 | tf_op jit(solution)/shard_map/ppermute | solution.py:48
  52.8 10.2 %collective-permute-start.22 = (bf16[64,1024]{1,0:T(8,128)(2,1)S(1)}, bf16[64,1024]{1,0:T(8,128)(2,1)S(1)}, u32[]{:S(2)}, u32[]{:S(2)}) collective-permute-start(bf16[64,1024]{1,0:T(8,128)(2,1)S(1)} %get-tuple-element.62.refs_0_), channel_id=1, source_target_pairs={{0,6},{1,7},{2,4},{3,5},{4,2},{5,3},{6,0},{7,1},{8,14},{9,15},{10,... | collective-permute-start | bytes 393224 | tf_op jit(solution)/shard_map/ppermute | solution.py:48
  54.9 8.6 %collective-permute-start.26 = (bf16[64,1024]{1,0:T(8,128)(2,1)S(1)}, bf16[64,1024]{1,0:T(8,128)(2,1)S(1)}, u32[]{:S(2)}, u32[]{:S(2)}) collective-permute-start(bf16[64,1024]{1,0:T(8,128)(2,1)S(1)} %get-tuple-element.62.refs_0_), channel_id=1, source_target_pairs={{0,24},{8,16},{16,8},{24,0},{1,25},{9,17},{17,9},{25,1},{2,26},{10... | collective-permute-start | bytes 393224 | tf_op jit(solution)/shard_map/ppermute | solution.py:48
  55.2 10.8 %collective-permute-start.17 = (bf16[64,1024]{1,0:T(8,128)(2,1)S(1)}, bf16[64,1024]{1,0:T(8,128)(2,1)S(1)}, u32[]{:S(2)}, u32[]{:S(2)}) collective-permute-start(bf16[64,1024]{1,0:T(8,128)(2,1)S(1)} %get-tuple-element.62.refs_0_), channel_id=1, source_target_pairs={{0,1},{1,0},{2,3},{3,2},{4,5},{5,4},{6,7},{7,6},{8,9},{9,8},{10,11... | collective-permute-start | bytes 393224 | tf_op jit(solution)/shard_map/ppermute | solution.py:48
  55.7 10.3 %collective-permute-start.19 = (bf16[64,1024]{1,0:T(8,128)(2,1)S(1)}, bf16[64,1024]{1,0:T(8,128)(2,1)S(1)}, u32[]{:S(2)}, u32[]{:S(2)}) collective-permute-start(bf16[64,1024]{1,0:T(8,128)(2,1)S(1)} %collective-permute-done.18.refs_2_), channel_id=1, source_target_pairs={{0,1},{1,0},{2,3},{3,2},{4,5},{5,4},{6,7},{7,6},{8,9},{9,8},{10,11... | collective-permute-start | bytes 393224 | tf_op jit(solution)/shard_map/ppermute | solution.py:48
  63.0 3.1 %collective-permute-start.21 = (bf16[64,1024]{1,0:T(8,128)(2,1)S(1)}, bf16[64,1024]{1,0:T(8,128)(2,1)S(1)}, u32[]{:S(2)}, u32[]{:S(2)}) collective-permute-start(bf16[64,1024]{1,0:T(8,128)(2,1)S(1)} %collective-permute-done.20.refs_4_), channel_id=1, source_target_pairs={{0,1},{1,0},{2,3},{3,2},{4,5},{5,4},{6,7},{7,6},{8,9},{9,8},{10,11... | collective-permute-start | bytes 393224 | tf_op jit(solution)/shard_map/ppermute | solution.py:48
  63.0 3.1 %collective-permute-start.23 = (bf16[64,1024]{1,0:T(8,128)(2,1)S(1)}, bf16[64,1024]{1,0:T(8,128)(2,1)S(1)}, u32[]{:S(2)}, u32[]{:S(2)}) collective-permute-start(bf16[64,1024]{1,0:T(8,128)(2,1)S(1)} %collective-permute-done.22.refs_6_), channel_id=1, source_target_pairs={{0,1},{1,0},{2,3},{3,2},{4,5},{5,4},{6,7},{7,6},{8,9},{9,8},{10,11... | collective-permute-start | bytes 393224 | tf_op jit(solution)/shard_map/ppermute | solution.py:48
  65.9 6.2 %collective-permute-start.27 = (bf16[4,64,640]{2,1,0:T(8,128)(2,1)S(1)}, bf16[4,64,640]{2,1,0:T(8,128)(2,1)S(1)}, u32[]{:S(2)}, u32[]{:S(2)}) collective-permute-start(bf16[4,64,640]{2,1,0:T(8,128)(2,1)S(1)} %get-tuple-element.65), channel_id=1, source_target_pairs={{0,1},{1,0},{2,3},{3,2},{4,5},{5,4},{6,7},{7,6},{8,9},{9,8},{10,11... | collective-permute-start | bytes 983048 | tf_op jit(solution)/shard_map/ppermute | solution.py:48
  68.6 6.8 %collective-permute-start.31 = (bf16[64,1024]{1,0:T(8,128)(2,1)S(1)}, bf16[64,1024]{1,0:T(8,128)(2,1)S(1)}, u32[]{:S(2)}, u32[]{:S(2)}) collective-permute-start(bf16[64,1024]{1,0:T(8,128)(2,1)S(1)} %get-tuple-element.71), channel_id=1, source_target_pairs={{0,8},{8,0},{16,24},{24,16},{1,9},{9,1},{17,25},{25,17},{2,10},{10... | collective-permute-start | bytes 393224 | tf_op jit(solution)/shard_map/ppermute | solution.py:48
  69.0 8.4 %collective-permute-start.32 = (bf16[64,1024]{1,0:T(8,128)(2,1)S(1)}, bf16[64,1024]{1,0:T(8,128)(2,1)S(1)}, u32[]{:S(2)}, u32[]{:S(2)}) collective-permute-start(bf16[64,1024]{1,0:T(8,128)(2,1)S(1)} %get-tuple-element.72), channel_id=1, source_target_pairs={{0,16},{8,24},{16,0},{24,8},{1,17},{9,25},{17,1},{25,9},{2,18},{10... | collective-permute-start | bytes 393224 | tf_op jit(solution)/shard_map/ppermute | solution.py:48
  69.5 7.9 %collective-permute-start.33 = (bf16[64,1024]{1,0:T(8,128)(2,1)S(1)}, bf16[64,1024]{1,0:T(8,128)(2,1)S(1)}, u32[]{:S(2)}, u32[]{:S(2)}) collective-permute-start(bf16[64,1024]{1,0:T(8,128)(2,1)S(1)} %get-tuple-element.73), channel_id=1, source_target_pairs={{0,24},{8,16},{16,8},{24,0},{1,25},{9,17},{17,9},{25,1},{2,26},{10... | collective-permute-start | bytes 393224 | tf_op jit(solution)/shard_map/ppermute | solution.py:48
  72.8 4.7 %collective-permute-start.28 = (bf16[64,640]{1,0:T(8,128)(2,1)S(1)}, bf16[64,640]{1,0:T(8,128)(2,1)S(1)}, u32[]{:S(2)}, u32[]{:S(2)}) collective-permute-start(bf16[64,640]{1,0:T(8,128)(2,1)S(1)} %get-tuple-element.68), channel_id=1, source_target_pairs={{0,2},{1,3},{2,0},{3,1},{4,6},{5,7},{6,4},{7,5},{8,10},{9,11},{10,... | collective-permute-start | bytes 245768 | tf_op jit(solution)/shard_map/ppermute | solution.py:48
  74.8 8.6 %collective-permute-start.29 = (bf16[64,640]{1,0:T(8,128)(2,1)S(1)}, bf16[64,640]{1,0:T(8,128)(2,1)S(1)}, u32[]{:S(2)}, u32[]{:S(2)}) collective-permute-start(bf16[64,640]{1,0:T(8,128)(2,1)S(1)} %get-tuple-element.69), channel_id=1, source_target_pairs={{0,4},{1,5},{2,6},{3,7},{4,0},{5,1},{6,2},{7,3},{8,12},{9,13},{10,... | collective-permute-start | bytes 245768 | tf_op jit(solution)/shard_map/ppermute | solution.py:48
  75.4 7.9 %collective-permute-start.30 = (bf16[64,640]{1,0:T(8,128)(2,1)S(1)}, bf16[64,640]{1,0:T(8,128)(2,1)S(1)}, u32[]{:S(2)}, u32[]{:S(2)}) collective-permute-start(bf16[64,640]{1,0:T(8,128)(2,1)S(1)} %get-tuple-element.70), channel_id=1, source_target_pairs={{0,6},{1,7},{2,4},{3,5},{4,2},{5,3},{6,0},{7,1},{8,14},{9,15},{10,... | collective-permute-start | bytes 245768 | tf_op jit(solution)/shard_map/ppermute | solution.py:48
  83.9 5.5 %collective-permute-start.41 = (bf16[64,1024]{1,0:T(8,128)(2,1)S(1)}, bf16[64,1024]{1,0:T(8,128)(2,1)S(1)}, u32[]{:S(2)}, u32[]{:S(2)}) collective-permute-start(bf16[64,1024]{1,0:T(8,128)(2,1)S(1)} %get-tuple-element.75.refs_0_.refs_8_), channel_id=1, source_target_pairs={{0,8},{8,0},{16,24},{24,16},{1,9},{9,1},{17,25},{25,17},{2,10},{10... | collective-permute-start | bytes 393224 | tf_op jit(solution)/shard_map/ppermute | solution.py:48
  84.5 7.4 %collective-permute-start.42 = (bf16[64,1024]{1,0:T(8,128)(2,1)S(1)}, bf16[64,1024]{1,0:T(8,128)(2,1)S(1)}, u32[]{:S(2)}, u32[]{:S(2)}) collective-permute-start(bf16[64,1024]{1,0:T(8,128)(2,1)S(1)} %get-tuple-element.75.refs_0_.refs_8_), channel_id=1, source_target_pairs={{0,16},{8,24},{16,0},{24,8},{1,17},{9,25},{17,1},{25,9},{2,18},{10... | collective-permute-start | bytes 393224 | tf_op jit(solution)/shard_map/ppermute | solution.py:48
  85.0 6.9 %collective-permute-start.35 = (bf16[64,1024]{1,0:T(8,128)(2,1)S(1)}, bf16[64,1024]{1,0:T(8,128)(2,1)S(1)}, u32[]{:S(2)}, u32[]{:S(2)}) collective-permute-start(bf16[64,1024]{1,0:T(8,128)(2,1)S(1)} %get-tuple-element.75.refs_0_.refs_8_), channel_id=1, source_target_pairs={{0,2},{1,3},{2,0},{3,1},{4,6},{5,7},{6,4},{7,5},{8,10},{9,11},{10,... | collective-permute-start | bytes 393224 | tf_op jit(solution)/shard_map/ppermute | solution.py:48
  86.5 11.2 %collective-permute-start.37 = (bf16[64,1024]{1,0:T(8,128)(2,1)S(1)}, bf16[64,1024]{1,0:T(8,128)(2,1)S(1)}, u32[]{:S(2)}, u32[]{:S(2)}) collective-permute-start(bf16[64,1024]{1,0:T(8,128)(2,1)S(1)} %get-tuple-element.75.refs_0_.refs_8_), channel_id=1, source_target_pairs={{0,4},{1,5},{2,6},{3,7},{4,0},{5,1},{6,2},{7,3},{8,12},{9,13},{10,... | collective-permute-start | bytes 393224 | tf_op jit(solution)/shard_map/ppermute | solution.py:48
  87.5 10.2 %collective-permute-start.39 = (bf16[64,1024]{1,0:T(8,128)(2,1)S(1)}, bf16[64,1024]{1,0:T(8,128)(2,1)S(1)}, u32[]{:S(2)}, u32[]{:S(2)}) collective-permute-start(bf16[64,1024]{1,0:T(8,128)(2,1)S(1)} %get-tuple-element.75.refs_0_.refs_8_), channel_id=1, source_target_pairs={{0,6},{1,7},{2,4},{3,5},{4,2},{5,3},{6,0},{7,1},{8,14},{9,15},{10,... | collective-permute-start | bytes 393224 | tf_op jit(solution)/shard_map/ppermute | solution.py:48
  89.4 8.8 %collective-permute-start.43 = (bf16[64,1024]{1,0:T(8,128)(2,1)S(1)}, bf16[64,1024]{1,0:T(8,128)(2,1)S(1)}, u32[]{:S(2)}, u32[]{:S(2)}) collective-permute-start(bf16[64,1024]{1,0:T(8,128)(2,1)S(1)} %get-tuple-element.75.refs_0_.refs_8_), channel_id=1, source_target_pairs={{0,24},{8,16},{16,8},{24,0},{1,25},{9,17},{17,9},{25,1},{2,26},{10... | collective-permute-start | bytes 393224 | tf_op jit(solution)/shard_map/ppermute | solution.py:48
  91.9 8.8 %collective-permute-start.34 = (bf16[64,1024]{1,0:T(8,128)(2,1)S(1)}, bf16[64,1024]{1,0:T(8,128)(2,1)S(1)}, u32[]{:S(2)}, u32[]{:S(2)}) collective-permute-start(bf16[64,1024]{1,0:T(8,128)(2,1)S(1)} %get-tuple-element.75.refs_0_.refs_8_), channel_id=1, source_target_pairs={{0,1},{1,0},{2,3},{3,2},{4,5},{5,4},{6,7},{7,6},{8,9},{9,8},{10,11... | collective-permute-start | bytes 393224 | tf_op jit(solution)/shard_map/ppermute | solution.py:48
  91.9 8.8 %collective-permute-start.36 = (bf16[64,1024]{1,0:T(8,128)(2,1)S(1)}, bf16[64,1024]{1,0:T(8,128)(2,1)S(1)}, u32[]{:S(2)}, u32[]{:S(2)}) collective-permute-start(bf16[64,1024]{1,0:T(8,128)(2,1)S(1)} %collective-permute-done.35.refs_2_), channel_id=1, source_target_pairs={{0,1},{1,0},{2,3},{3,2},{4,5},{5,4},{6,7},{7,6},{8,9},{9,8},{10,11... | collective-permute-start | bytes 393224 | tf_op jit(solution)/shard_map/ppermute | solution.py:48
  97.7 3.1 %collective-permute-start.38 = (bf16[64,1024]{1,0:T(8,128)(2,1)S(1)}, bf16[64,1024]{1,0:T(8,128)(2,1)S(1)}, u32[]{:S(2)}, u32[]{:S(2)}) collective-permute-start(bf16[64,1024]{1,0:T(8,128)(2,1)S(1)} %collective-permute-done.37.refs_4_), channel_id=1, source_target_pairs={{0,1},{1,0},{2,3},{3,2},{4,5},{5,4},{6,7},{7,6},{8,9},{9,8},{10,11... | collective-permute-start | bytes 393224 | tf_op jit(solution)/shard_map/ppermute | solution.py:48
  97.7 3.1 %collective-permute-start.40 = (bf16[64,1024]{1,0:T(8,128)(2,1)S(1)}, bf16[64,1024]{1,0:T(8,128)(2,1)S(1)}, u32[]{:S(2)}, u32[]{:S(2)}) collective-permute-start(bf16[64,1024]{1,0:T(8,128)(2,1)S(1)} %collective-permute-done.39.refs_6_), channel_id=1, source_target_pairs={{0,1},{1,0},{2,3},{3,2},{4,5},{5,4},{6,7},{7,6},{8,9},{9,8},{10,11... | collective-permute-start | bytes 393224 | tf_op jit(solution)/shard_map/ppermute | solution.py:48
  100.6 19.9 %collective-permute-start.51 = (bf16[4,64,640]{2,1,0:T(8,128)(2,1)S(1)}, bf16[4,64,640]{2,1,0:T(8,128)(2,1)S(1)}, u32[]{:S(2)}, u32[]{:S(2)}) collective-permute-start(bf16[4,64,640]{2,1,0:T(8,128)(2,1)S(1)} %get-tuple-element.86), channel_id=1, source_target_pairs={{0,1},{1,0},{2,3},{3,2},{4,5},{5,4},{6,7},{7,6},{8,9},{9,8},{10,11... | collective-permute-start | bytes 983048 | tf_op jit(solution)/shard_map/ppermute | solution.py:48
  103.8 7.4 %collective-permute-start.44 = (bf16[64,1408]{1,0:T(8,128)(2,1)S(1)}, bf16[64,1408]{1,0:T(8,128)(2,1)S(1)}, u32[]{:S(2)}, u32[]{:S(2)}) collective-permute-start(bf16[64,1408]{1,0:T(8,128)(2,1)S(1)} %get-tuple-element.78), channel_id=1, source_target_pairs={{0,8},{8,0},{16,24},{24,16},{1,9},{9,1},{17,25},{25,17},{2,10},{10... | collective-permute-start | bytes 540680 | tf_op jit(solution)/shard_map/ppermute | solution.py:48
  105.5 10.5 %collective-permute-start.45 = (bf16[64,1408]{1,0:T(8,128)(2,1)S(1)}, bf16[64,1408]{1,0:T(8,128)(2,1)S(1)}, u32[]{:S(2)}, u32[]{:S(2)}) collective-permute-start(bf16[64,1408]{1,0:T(8,128)(2,1)S(1)} %get-tuple-element.79), channel_id=1, source_target_pairs={{0,16},{8,24},{16,0},{24,8},{1,17},{9,25},{17,1},{25,9},{2,18},{10... | collective-permute-start | bytes 540680 | tf_op jit(solution)/shard_map/ppermute | solution.py:48
  107.0 9.0 %collective-permute-start.46 = (bf16[64,1408]{1,0:T(8,128)(2,1)S(1)}, bf16[64,1408]{1,0:T(8,128)(2,1)S(1)}, u32[]{:S(2)}, u32[]{:S(2)}) collective-permute-start(bf16[64,1408]{1,0:T(8,128)(2,1)S(1)} %get-tuple-element.80), channel_id=1, source_target_pairs={{0,24},{8,16},{16,8},{24,0},{1,25},{9,17},{17,9},{25,1},{2,26},{10... | collective-permute-start | bytes 540680 | tf_op jit(solution)/shard_map/ppermute | solution.py:48
  116.1 7.6 %collective-permute-start.47 = (f32[64,128]{1,0:T(8,128)S(1)}, f32[64,128]{1,0:T(8,128)S(1)}, u32[]{:S(2)}, u32[]{:S(2)}) collective-permute-start(f32[64,128]{1,0:T(8,128)S(1)} %get-tuple-element.84), channel_id=1, source_target_pairs={{0,2},{1,3},{2,0},{3,1},{4,6},{5,7},{6,4},{7,5},{8,10},{9,11},{10,... | collective-permute-start | bytes 98312 | tf_op jit(solution)/shard_map/ppermute | solution.py:48
  117.8 7.8 %collective-permute-start.48 = (f32[64,128]{1,0:T(8,128)S(1)}, f32[64,128]{1,0:T(8,128)S(1)}, u32[]{:S(2)}, u32[]{:S(2)}) collective-permute-start(f32[64,128]{1,0:T(8,128)S(1)} %get-tuple-element.84), channel_id=1, source_target_pairs={{0,4},{1,5},{2,6},{3,7},{4,0},{5,1},{6,2},{7,3},{8,12},{9,13},{10,... | collective-permute-start | bytes 98312 | tf_op jit(solution)/shard_map/ppermute | solution.py:48
  118.6 7.0 %collective-permute-start.49 = (f32[64,128]{1,0:T(8,128)S(1)}, f32[64,128]{1,0:T(8,128)S(1)}, u32[]{:S(2)}, u32[]{:S(2)}) collective-permute-start(f32[64,128]{1,0:T(8,128)S(1)} %get-tuple-element.84), channel_id=1, source_target_pairs={{0,6},{1,7},{2,4},{3,5},{4,2},{5,3},{6,0},{7,1},{8,14},{9,15},{10,... | collective-permute-start | bytes 98312 | tf_op jit(solution)/shard_map/ppermute | solution.py:48
  121.1 21.0 %collective-permute-start.52 = (bf16[64,640]{1,0:T(8,128)(2,1)S(1)}, bf16[64,640]{1,0:T(8,128)(2,1)S(1)}, u32[]{:S(2)}, u32[]{:S(2)}) collective-permute-start(bf16[64,640]{1,0:T(8,128)(2,1)S(1)} %get-tuple-element.89), channel_id=1, source_target_pairs={{0,2},{1,3},{2,0},{3,1},{4,6},{5,7},{6,4},{7,5},{8,10},{9,11},{10,... | collective-permute-start | bytes 245768 | tf_op jit(solution)/shard_map/ppermute | solution.py:48
  122.0 20.1 %collective-permute-start.53 = (bf16[64,640]{1,0:T(8,128)(2,1)S(1)}, bf16[64,640]{1,0:T(8,128)(2,1)S(1)}, u32[]{:S(2)}, u32[]{:S(2)}) collective-permute-start(bf16[64,640]{1,0:T(8,128)(2,1)S(1)} %get-tuple-element.90), channel_id=1, source_target_pairs={{0,4},{1,5},{2,6},{3,7},{4,0},{5,1},{6,2},{7,3},{8,12},{9,13},{10,... | collective-permute-start | bytes 245768 | tf_op jit(solution)/shard_map/ppermute | solution.py:48
  123.7 18.4 %collective-permute-start.54 = (bf16[64,640]{1,0:T(8,128)(2,1)S(1)}, bf16[64,640]{1,0:T(8,128)(2,1)S(1)}, u32[]{:S(2)}, u32[]{:S(2)}) collective-permute-start(bf16[64,640]{1,0:T(8,128)(2,1)S(1)} %get-tuple-element.91), channel_id=1, source_target_pairs={{0,6},{1,7},{2,4},{3,5},{4,2},{5,3},{6,0},{7,1},{8,14},{9,15},{10,... | collective-permute-start | bytes 245768 | tf_op jit(solution)/shard_map/ppermute | solution.py:48
  125.6 16.5 %collective-permute-start.50 = (f32[64,128]{1,0:T(8,128)S(1)}, f32[64,128]{1,0:T(8,128)S(1)}, u32[]{:S(2)}, u32[]{:S(2)}) collective-permute-start(f32[64,128]{1,0:T(8,128)S(1)} %add_add_fusion.both_ref), channel_id=1, source_target_pairs={{0,1},{1,0},{2,3},{3,2},{4,5},{5,4},{6,7},{7,6},{8,9},{9,8},{10,11... | collective-permute-start | bytes 98312 | tf_op jit(solution)/shard_map/ppermute | solution.py:48

commit v3 on v2

--- a/solution.py
+++ b/solution.py
@@ -7,14 +7,17 @@
 from jax.experimental.pallas import tpu as pltpu
 from jax.sharding import PartitionSpec as P
 
-VMEM_BYTES = 48 * 1024 * 1024
+VMEM_BYTES = 24 * 1024 * 1024
+DENSE_BYTES = 24 * 1024 * 1024
 HIGHEST = lax.Precision.HIGHEST
 GRAM = 128
-PIECES = 3
+PIECES = 2
+PANEL = 8
+UNROLL = 32
 
 vmem = pl.BlockSpec(memory_space=pltpu.VMEM)
 smem = pl.BlockSpec(memory_space=pltpu.SMEM)
-params = pltpu.CompilerParams(vmem_limit_bytes=VMEM_BYTES)
+hbm = pl.BlockSpec(memory_space=pltpu.HBM)
 
 
 def f32(*shape):
@@ -62,40 +65,60 @@
         ref[:, width + k * columns : width + (k + 1) * columns].astype(jnp.float32)
         for k in range(PIECES)
     ]
-    return (parts[2] + parts[1]) + parts[0]
-
-
-def dense_kernel(count_ref, rank_ref, near_ref, left_ref, right_ref, tile_ref, turned_ref):
+    return functools.reduce(jnp.add, reversed(parts))
+
+
+def dense_kernel(
+    table, near_ref, left_ref, right_ref, tile_ref, turned_ref, lefts, rights, sems
+):
     near_slots, far_slots = near_ref.shape[0], left_ref.shape[0]
+    ranks = 2 + 2 * (near_slots + far_slots)
+    count = table[ranks + far_slots]
+    copies = [
+        pltpu.make_async_copy(source, target, sems.at[k])
+        for k, (source, target) in enumerate(
+            [
+                (left_ref, lefts),
+                (right_ref, rights),
+                (near_ref, tile_ref.at[pl.ds(0, near_slots)]),
+            ]
+        )
+    ]
+    for copy in copies:
+        copy.start()
+    copies[0].wait()
+    copies[1].wait()
 
     def far(s, _):
-        row = lax.broadcasted_iota(jnp.int32, left_ref.shape[1:], 0)
-        left = jnp.where(row < rank_ref[s], left_ref[s].astype(jnp.float32), 0.0)
-        left, right = left.astype(jnp.bfloat16), right_ref[s]
+        row = lax.broadcasted_iota(jnp.int32, lefts.shape[1:], 0)
+        left = jnp.where(row < table[ranks + s], lefts[s].astype(jnp.float32), 0.0)
+        left, right = left.astype(jnp.bfloat16), rights[s]
         tile_ref[near_slots + s] = contract(left, right, ((0,), (0,))).astype(jnp.bfloat16)
         turned_ref[near_slots + s] = contract(right, left, ((0,), (0,))).astype(jnp.bfloat16)
         return 0
 
     def near(s, _):
-        tile = near_ref[s]
-        tile = jnp.where(s < count_ref[0], tile, jnp.zeros_like(tile))
+        tile = tile_ref[s]
+        tile = jnp.where(s < count, tile, jnp.zeros_like(tile))
         tile_ref[s] = tile
         turned_ref[s] = tile.T
         return 0
 
-    lax.fori_loop(0, far_slots, far, 0, unroll=8)
+    lax.fori_loop(0, far_slots, far, 0, unroll=16)
+    copies[2].wait()
     lax.fori_loop(0, near_slots, near, 0, unroll=8)
 
 
-def tile_sums(from_ref, to_ref, tile_ref, cells, total):
+def tile_sums(table, inputs, outputs, tile_ref, cells, total):
     total[...] = jnp.zeros_like(total)
 
     def step(s, _):
-        product = contract(cells[from_ref[s]], tile_ref[s], ((1,), (0,)))
-        total[to_ref[s]] = total[to_ref[s]] + product
+        product = contract(cells[table[inputs + s]], tile_ref[s], ((1,), (0,)))
+        to = table[outputs + s]
+        total[to] = total[to] + product
         return 0
 
-    lax.fori_loop(0, tile_ref.shape[0], step, 0, unroll=16)
+    lax.fori_loop(0, tile_ref.shape[0], step, 0, unroll=UNROLL)
 
 
 def place(block, ref, cells, per):
@@ -104,15 +127,16 @@
         cells[block * per + j] = ref[:, j * leaf : (j + 1) * leaf]
 
 
-def rows_kernel(place_ref, from_ref, to_ref, tile_ref, *refs):
+def rows_kernel(table, tile_ref, *refs):
     blocks, (send_ref, keep_ref, cells, total) = refs[:-4], refs[-4:]
     chips, _, width = send_ref.shape
     leaf = cells.shape[-1]
     per = width // leaf
-    me, core = place_ref[0], place_ref[1] % 2
+    me, core = table[0], table[1] % 2
     for flip, ref in enumerate(blocks):
         place(me ^ flip, ref, cells, per)
-    tile_sums(from_ref, to_ref, tile_ref, cells, total)
+    slots = tile_ref.shape[0]
+    tile_sums(table, 2 + slots, 2, tile_ref, cells, total)
     for z in range(chips):
         for j in range(per):
             part = slice(j * leaf, (j + 1) * leaf)
@@ -120,7 +144,7 @@
             keep_ref[z, :, part] = total[(2 * z + core) * per + j]
 
 
-def cols_kernel(rows, cols, place_ref, from_ref, to_ref, tile_ref, *refs):
+def cols_kernel(rows, cols, table, tile_ref, *refs):
     blocks, refs = refs[:cols], refs[cols:]
     outs, (cells, total) = refs[-rows - 3 : -2], refs[-2:]
     last = refs[: -rows - 3]
@@ -128,10 +152,11 @@
     width = own_ref.shape[1]
     leaf = cells.shape[-1]
     per = width // leaf
-    me = place_ref[0]
+    me = table[0]
     for flip, ref in enumerate(blocks):
-        place(place_ref[1] ^ flip, ref, cells, per)
-    tile_sums(from_ref, to_ref, tile_ref, cells, total)
+        place(table[1] ^ flip, ref, cells, per)
+    slots = tile_ref.shape[0]
+    tile_sums(table, 2, 2 + slots, tile_ref, cells, total)
     gram = get_gram(blocks[0], width)
     for ref in blocks[1:]:
         gram = gram + get_gram(ref, width)
@@ -146,7 +171,7 @@
                 image = total[(me ^ flip) * per + j].astype(jnp.bfloat16)
                 half = half + contract(cluster, image, ((1,), (1,)))
         both = both + 2.0 * half
-        gram = jnp.concatenate([gram, both, jnp.zeros_like(both)], axis=1)
+        gram = jnp.concatenate([gram, both], axis=1)
     gram_ref[...] = gram
     for flip, out in enumerate((own_ref, *messages)):
         for j in range(per):
@@ -156,11 +181,18 @@
         put_gram(out, width, gram)
 
 
-def pair_kernel(place_ref, keep_ref, got_ref, *outs):
-    chip = place_ref[1] // 2
+def pair_kernel(table, keep_ref, got_ref, *outs):
+    chip = table[1] // 2
     for flip, out in enumerate(outs):
         z = chip ^ flip
         out[...] = (keep_ref[z] + got_ref[z].astype(jnp.float32)).astype(out.dtype)
+
+
+def chip_sums_kernel(own_ref, *refs):
+    total = own_ref[...]
+    for ref in refs[:-1]:
+        total = total + ref[...].astype(jnp.float32)
+    refs[-1][...] = total
 
 
 def first_kernel(vector_ref, diagonal_ref, message_ref):
@@ -174,7 +206,7 @@
     )
 
 
-def off_diagonal(rows, refs):
+def off_diagonal(refs):
     width = refs[0].shape[1]
     total = refs[0][...] + refs[1][...]
     for ref in refs[2:]:
@@ -203,7 +235,7 @@
     else:
         shift = shift_ref[0:1, 0:1]
     total_ref[...] = gram
-    following = (diagonal_ref[...] - shift) * vector + off_diagonal(rows, sums)
+    following = (diagonal_ref[...] - shift) * vector + off_diagonal(sums)
     next_ref[...] = following
     message_ref[:, :width] = following.astype(jnp.bfloat16)
     cross = contract(vector, following, ((1,), (1,)), HIGHEST)
@@ -232,13 +264,22 @@
 def solve(*pairs):
     size = pairs[0][0].shape[0]
     works = [jnp.concatenate(pair, axis=1) for pair in pairs]
-    row = lax.broadcasted_iota(jnp.int32, works[0].shape, 0)
-    for k in range(size):
-        pivots = [work[k : k + 1, :] / work[k : k + 1, k : k + 1] for work in works]
-        works = [
-            jnp.where(row == k, pivot, work - work[:, k : k + 1] * pivot)
-            for work, pivot in zip(works, pivots)
-        ]
+    shape = works[0].shape
+    row = lax.broadcasted_iota(jnp.int32, shape, 0)
+    for start in range(0, size, PANEL):
+        panel = range(start, start + PANEL)
+        spread = [[jnp.broadcast_to(w[:, k : k + 1], shape) for k in panel] for w in works]
+        for k in panel:
+            for n, columns in enumerate(spread):
+                pivot = columns[0]
+                inverse = 1.0 / pivot[k : k + 1, :]
+
+                def eliminate(matrix):
+                    pivot_row = matrix[k : k + 1, :] * inverse
+                    return jnp.where(row == k, pivot_row, matrix - pivot * pivot_row)
+
+                works[n] = eliminate(works[n])
+                spread[n] = [eliminate(column) for column in columns[1:]]
     return [work[:, size:] for work in works]
 
 
@@ -266,7 +307,7 @@
 
 
 def second_coefficients_kernel(
-    shift_ref, gram0_ref, gram1_ref, gram2_ref, first_ref, vectors_ref, small_ref
+    shift_ref, gram0_ref, gram1_ref, gram2_ref, first_ref, big_ref, small_ref
 ):
     cases = gram0_ref.shape[0]
     shift = shift_ref[0:1, 0:1]
@@ -292,36 +333,38 @@
     with_y = mul_t(d2_b, uv + shift * bv) + mul_t(d2_u, vv + shift * uv)
     curvature2 = mul_t(d2, mul(gram, s2)) + mul(with_y, d2_v)
     x2 = stack([alpha0, zero, zero]) + mul(d1, alpha1)
-    vectors_ref[...] = side([d2, r2, s2, x2])
-    small_ref[...] = side([curvature2, rr2])
-
-
-def finish_kernel(
-    vectors_ref, small_ref, both_ref, other_ref, b_ref, u_ref, v_ref, diagonal_ref, *refs
-):
+    small_ref[...] = side([curvature2, rr2, d2_v, zero])
+    big_ref[...] = side([d2, r2, s2, x2])
+
+
+def vectors_kernel(big_ref, b_ref, u_ref, v_ref, vectors_ref):
+    basis = jnp.concatenate([b_ref[...], u_ref[...], v_ref[...]], axis=0)
+    vectors_ref[...] = mul_t(big_ref[...], basis)
+
+
+def finish_kernel(vectors_ref, small_ref, both_ref, other_ref, v_ref, diagonal_ref, *refs):
     sums, (solution_ref, residual_ref) = refs[:-2], refs[-2:]
-    cases = b_ref.shape[0]
-    d2, r2, s2, x2 = [vectors_ref[:, k * cases : (k + 1) * cases] for k in range(4)]
-    d2_v = d2[2 * cases :]
-    both = symmetric(both_ref[:, :cases] + other_ref[:, :cases])
-    curvature2 = symmetric(small_ref[:, :cases] + mul_t(d2_v, mul(both, d2_v)))
-    (alpha2,) = solve((curvature2, small_ref[:, cases:]))
-    y = diagonal_ref[...] * v_ref[...] + off_diagonal(0, sums)
-    basis = jnp.concatenate([b_ref[...], u_ref[...], v_ref[...]], axis=0)
-    solution_ref[...] = mul_t(x2 + mul(d2, alpha2), basis)
-    residual_ref[...] = mul_t(r2 - mul(s2, alpha2), basis) - mul_t(mul(d2_v, alpha2), y)
-
-
-def call(kernel, name, outs, *args, scratch=(), scalars=(), flops=0):
-    scalars = set(scalars)
+    cases = v_ref.shape[0]
+    d2, r2, s2, x2 = [vectors_ref[k * cases : (k + 1) * cases, :] for k in range(4)]
+    curvature2, rr2, d2_v = [small_ref[:, k * cases : (k + 1) * cases] for k in range(3)]
+    both = symmetric(both_ref[...] + other_ref[...])
+    (alpha2,) = solve((symmetric(curvature2 + mul_t(d2_v, mul(both, d2_v))), rr2))
+    y = diagonal_ref[...] * v_ref[...] + off_diagonal(sums)
+    s2 = s2 + mul_t(d2_v, y)
+    solution_ref[...] = x2 + mul_t(alpha2, d2)
+    residual_ref[...] = r2 - mul_t(alpha2, s2)
+
+
+def call(kernel, name, outs, *args, scratch=(), scalars=(), far=(), cost=0, room=VMEM_BYTES):
+    spaces = {**dict.fromkeys(scalars, smem), **dict.fromkeys(far, hbm)}
     return pl.pallas_call(
         kernel,
         out_shape=outs,
-        in_specs=[smem if k in scalars else vmem for k in range(len(args))],
+        in_specs=[spaces.get(k, vmem) for k in range(len(args))],
         out_specs=jax.tree.map(lambda _: vmem, outs),
         scratch_shapes=list(scratch),
-        compiler_params=params,
-        cost_estimate=pl.CostEstimate(flops=flops, bytes_accessed=0, transcendentals=0),
+        compiler_params=pltpu.CompilerParams(vmem_limit_bytes=room),
+        cost_estimate=pl.CostEstimate(flops=int(cost * 1e9), bytes_accessed=0, transcendentals=0),
         name=name,
     )(*args)
 
@@ -346,83 +389,98 @@
     chips = cols // 2
     slots = near_tiles.shape[2] + far_left.shape[2]
     long = width + PIECES * GRAM
-    here = jnp.stack([lax.axis_index("row"), lax.axis_index("col")]).astype(jnp.int32)
-    list_p = jnp.concatenate([near_rows[0, 0], far_rows[0, 0]])
-    list_q = jnp.concatenate([near_cols[0, 0], far_cols[0, 0]])
+    table = jnp.concatenate(
+        [
+            jnp.stack([lax.axis_index("row"), lax.axis_index("col")]).astype(jnp.int32),
+            near_rows[0, 0],
+            far_rows[0, 0],
+            near_cols[0, 0],
+            far_cols[0, 0],
+            far_rank[0, 0],
+            near_count[0],
+        ]
+    )
     diagonal = self_term[None, :]
     tiles, turned = call(
         dense_kernel,
         "dense_tiles",
         [bf16(slots, leaf, leaf)] * 2,
-        near_count[0],
-        far_rank[0, 0],
+        table,
         near_tiles[0, 0],
         far_left[0, 0],
         far_right[0, 0],
-        scalars=(0, 1),
-    )
-    half_flops = 2 * slots * cases * leaf * leaf * 8
-
-    def apply(message, last=()):
+        scalars=(0,),
+        far=(1, 2, 3),
+        room=DENSE_BYTES,
+        scratch=[
+            pltpu.VMEM(far_left.shape[2:], jnp.bfloat16),
+            pltpu.VMEM(far_right.shape[2:], jnp.bfloat16),
+            pltpu.SemaphoreType.DMA((3,)),
+        ],
+    )
+
+    def apply(message, last=(), beside=()):
         over_row = [partner_permute(message, "row", k) for k in range(1, rows)]
         over_chip = [partner_permute(message, "col", 2 * k) for k in range(1, chips)]
-        other_core = [partner_permute(v, "col", 1) for v in [message] + over_chip]
         send, keep = call(
             rows_kernel,
             "rows_half",
             [bf16(chips, cases, width), f32(chips, cases, width)],
-            here,
-            list_q,
-            list_p,
+            table,
             turned,
             message,
             *over_row,
-            scalars=(0, 1, 2),
+            scalars=(0,),
             scratch=[
                 pltpu.VMEM((rows * per, cases, leaf), jnp.bfloat16),
                 pltpu.VMEM((cols * per, cases, leaf), jnp.float32),
             ],
-            flops=half_flops,
+            cost=0,
         )
+        over_chip, beside, send, keep = lax.optimization_barrier((over_chip, beside, send, keep))
         got = partner_permute(send, "col", 1)
+        own_chip, *row_messages = call(
+            pair_kernel,
+            "pair_sums",
+            [f32(cases, width)] + [bf16(cases, width)] * (chips - 1),
+            table,
+            keep,
+            got,
+            scalars=(0,),
+        )
+        from_chips = [partner_permute(m, "col", 2 * k) for k, m in enumerate(row_messages, 1)]
+        other_core = [partner_permute(v, "col", 1) for v in [message] + over_chip]
+        own_row = call(
+            chip_sums_kernel, "chip_sums", f32(cases, width), own_chip, *from_chips, cost=1
+        )
         row_group = [None] * cols
         for k, (a, b) in enumerate(zip([message] + over_chip, other_core)):
             row_group[2 * k], row_group[2 * k + 1] = a, b
-        wide = 2 * GRAM if last else GRAM
+        wide = GRAM + cases if last else GRAM
         extra = [message, *over_row, *last] if last else []
         own_col, gram, *col_messages = call(
             functools.partial(cols_kernel, rows, cols),
             "cols_half",
             [f32(cases, width), f32(cases, wide)]
             + [bf16(cases, width + PIECES * wide)] * (rows - 1),
-            here,
-            list_p,
-            list_q,
+            table,
             tiles,
             *row_group,
             *extra,
-            scalars=(0, 1, 2),
+            scalars=(0,),
             scratch=[
                 pltpu.VMEM((cols * per, cases, leaf), jnp.bfloat16),
                 pltpu.VMEM((rows * per, cases, leaf), jnp.float32),
             ],
-            flops=half_flops,
+            cost=0,
         )
-        own_row, *row_messages = call(
-            pair_kernel,
-            "pair_sums",
-            [f32(cases, width)] + [bf16(cases, width)] * (chips - 1),
-            here,
-            keep,
-            got,
-            scalars=(0,),
-        )
-        from_chips = [partner_permute(m, "col", 2 * k) for k, m in enumerate(row_messages, 1)]
         from_rows = [partner_permute(m, "row", k) for k, m in enumerate(col_messages, 1)]
-        return [own_row, own_col, *from_chips], from_rows, gram
+        if last:
+            from_rows, _ = lax.optimization_barrier((from_rows, own_row))
+        return [own_row, own_col, *from_rows], from_rows, gram, beside
 
     def advance(first, vector, shift, parts):
-        sums, from_rows, gram = parts
+        sums, from_rows, gram, _ = parts
         return call(
             functools.partial(combine_kernel, rows, first),
             "combine",
@@ -432,34 +490,37 @@
             shift,
             gram,
             *sums,
-            *from_rows,
         )
 
     b = right_side
-    message = call(first_kernel, "first_message", bf16(cases, long), b, diagonal)
+    message = call(first_kernel, "first_message", bf16(cases, long), b, diagonal, cost=10)
     u, message, gram0 = advance(True, b, diagonal, apply(message))
     shift = call(shift_kernel, "shift", f32(8, 128), gram0)
     v, message, gram1 = advance(False, u, shift, apply(message))
     first = call(
         first_coefficients_kernel, "coefficients", f32(cases, 4 * cases), shift, gram0, gram1
     )
-    sums, from_rows, gram = apply(message, last=(v, diagonal))
+    sums, from_rows, gram, first = apply(message, last=(v, diagonal), beside=first)
     gram2, both = call(
-        last_gram_kernel, "last_gram", [f32(cases, GRAM), f32(cases, GRAM)], gram, *from_rows
+        last_gram_kernel, "last_gram", [f32(cases, GRAM), f32(cases, cases)], gram, *from_rows
     )
     over_chip = [partner_permute(both, "col", 2 * k) for k in range(1, chips)]
-    both = functools.reduce(jnp.add, over_chip, both)
-    other = partner_permute(both, "col", 1)
-    vectors, small = call(
+    big, small = call(
         second_coefficients_kernel,
         "coefficients",
-        [f32(3 * cases, 4 * cases), f32(cases, 2 * cases)],
+        [f32(3 * cases, 4 * cases), f32(cases, 4 * cases)],
         shift,
         gram0,
         gram1,
         gram2,
         first,
     )
+    over_chip, big = lax.optimization_barrier((over_chip, big))
+    both = functools.reduce(jnp.add, over_chip, both)
+    other = partner_permute(both, "col", 1)
+    big, _ = lax.optimization_barrier((big, both))
+    vectors = call(vectors_kernel, "vectors", f32(4 * cases, width), big, b, u, v)
+    other, vectors = lax.optimization_barrier((other, vectors))
     return call(
         finish_kernel,
         "finish",
@@ -468,12 +529,9 @@
         small,
         both,
         other,
-        b,
-        u,
         v,
         diagonal,
         *sums,
-        *from_rows,
     )
 
 

time: 151 us -> 117 us (0.77)
  Pallas kernels: 49.6 us -> 34.2 us
  waiting for transfers between devices: 32.8 us -> 21.9 us
  local copies, waits for them, and re-layouts: 7.46 us -> 1.73 us
    pallas_call x18 -> x22, Pallas kernels: 49.6 us -> 34.2 us  [call(): pl.pallas_call(kernel, out_shape=outs, in_specs=[spaces.get(k, vmem) for...]
    ppermute x55, waiting for transfers between devices: 32.8 us -> 21.9 us  [partner_permute(): return lax.ppermute(value, axis, [(i, i ^ flip) for i in range(size)])]
    unnamed x16 -> x20, local copies, waits for them, and re-layouts: 6.77 us -> 0.96 us
  transfers between devices with their start and end apart: 55 -> 55, of which waited for: 8 -> 17; matrix products, arithmetic and copies ran while one was open for 1% -> 0% of each run, Pallas kernels for 26% -> 25%
where the time goes in v3:
time: 117 us
  starting transfers between devices  57.5 us (49%)
  Pallas kernels  34.2 us (29%)
  waiting for transfers between devices  21.9 us (19%)
  local copies, waits for them, and re-layouts  1.73 us (1%)
  between operations  1.66 us (1%)
    ppermute x55, starting transfers between devices, partner_permute(): return lax.ppermute(value, axis, [(i, i ^ flip) for i in range(size)])  57.5 us
    pallas_call x22, Pallas kernels, call(): pl.pallas_call(kernel, out_shape=outs, in_specs=[spaces.get(k, vmem) for...  34.2 us
    ppermute x55, waiting for transfers between devices, partner_permute(): return lax.ppermute(value, axis, [(i, i ^ flip) for i in range(size)])  21.9 us
  transfers between devices with their start and end apart: 55, of which 17 were waited for; matrix products, arithmetic and copies ran while one was open for 0% of the time, Pallas kernels for 25%

profile of v3, /device:TPU:0, one launch (start us, length us, event | category | flops | bytes accessed | tf_op | source)
XLA Modules:
  0.0 117.0 jit_solution(14128377786482065784)
XLA Ops:
  0.6 0.7 broadcast_in_dim.3.diagonal_ref.shift_ref.refs_13_
  1.3 0.9 copy-done.1
  2.6 3.0 %collective-permute-start.4 = (bf16[64,896]{1,0:T(8,128)(2,1)S(1)}, bf16[64,896]{1,0:T(8,128)(2,1)S(1)}, u32[]{:S(2)}, u32[]{:S(2)}) collective-permute-start(bf16[64,896]{1,0:T(8,128)(2,1)S(1)} %first_message.1.refs_0_), channel_id=1, source_target_pairs={{0,8},{8,0},{16,24},{24,16},{1,9},{9,1},{17,25},{25,17},{2,10},{10... | collective-permute-start | bytes 344072 | tf_op jit(solution)/shard_map/ppermute | solution.py:51
  5.6 1.5 %collective-permute-start.5 = (bf16[64,896]{1,0:T(8,128)(2,1)S(1)}, bf16[64,896]{1,0:T(8,128)(2,1)S(1)}, u32[]{:S(2)}, u32[]{:S(2)}) collective-permute-start(bf16[64,896]{1,0:T(8,128)(2,1)S(1)} %first_message.1.refs_0_), channel_id=1, source_target_pairs={{0,16},{8,24},{16,0},{24,8},{1,17},{9,25},{17,1},{25,9},{2,18},{10... | collective-permute-start | bytes 344072 | tf_op jit(solution)/shard_map/ppermute | solution.py:51
  7.2 2.0 %collective-permute-start.1 = (bf16[64,896]{1,0:T(8,128)(2,1)S(1)}, bf16[64,896]{1,0:T(8,128)(2,1)S(1)}, u32[]{:S(2)}, u32[]{:S(2)}) collective-permute-start(bf16[64,896]{1,0:T(8,128)(2,1)S(1)} %first_message.1.refs_0_), channel_id=1, source_target_pairs={{0,2},{1,3},{2,0},{3,1},{4,6},{5,7},{6,4},{7,5},{8,10},{9,11},{10,... | collective-permute-start | bytes 344072 | tf_op jit(solution)/shard_map/ppermute | solution.py:51
  9.2 2.6 %collective-permute-start.2 = (bf16[64,896]{1,0:T(8,128)(2,1)S(1)}, bf16[64,896]{1,0:T(8,128)(2,1)S(1)}, u32[]{:S(2)}, u32[]{:S(2)}) collective-permute-start(bf16[64,896]{1,0:T(8,128)(2,1)S(1)} %first_message.1.refs_0_), channel_id=1, source_target_pairs={{0,4},{1,5},{2,6},{3,7},{4,0},{5,1},{6,2},{7,3},{8,12},{9,13},{10,... | collective-permute-start | bytes 344072 | tf_op jit(solution)/shard_map/ppermute | solution.py:51
  11.8 0.9 collective-permute-start.3
  13.5 3.3 %dense_tiles.1 = (bf16[96,128,128]{2,1,0:T(8,128)(2,1)S(1)}, bf16[96,128,128]{2,1,0:T(8,128)(2,1)S(1)}) custom-call(s32[259]{0:T(512)S(1)} %concatenate.3.table, bf16[32,128,128]{2,1,0:T(8,128)(2,1)S(1)} %bitcast.12, bf16[64,32,128]{2,1,0:T(8,128)(2,1)S(1)} %bitcast.13, bf16[64,32,128]{2,1,0:T(8,128)(2,1)S(1)} %bitcast.14), custom_call_target="tpu_custom_call" | custom-call | tf_op jit(solution)/shard_map/dense_tiles/pallas_call | solution.py:360
  16.7 2.1 %rows_half.3 = (bf16[4,64,640]{2,1,0:T(8,128)(2,1)S(1)}, f32[4,64,640]{2,1,0:T(8,128)S(1)}) custom-call(s32[259]{0:T(512)S(1)} %concatenate.3.table, bf16[96,128,128]{2,1,0:T(8,128)(2,1)S(1)} %get-tuple-element.74.tile_ref, bf16[64,896]{1,0:T(8,128)(2,1)S(1)} %first_message.1.refs_0_, bf16[64,896]{1,0:T(8,128)(2,1)S(1)} %collective-permute-done.4.refs_1_, ...), custom_call_target="tpu_custom_call" | custom-call | tf_op jit(solution)/shard_map/rows_half/pallas_call | solution.py:360
  18.8 1.2 %collective-permute-done.2.refs_4_ = bf16[64,896]{1,0:T(8,128)(2,1)S(1)} collective-permute-done((bf16[64,896]{1,0:T(8,128)(2,1)S(1)}, bf16[64,896]{1,0:T(8,128)(2,1)S(1)}, u32[]{:S(2)}, u32[]{:S(2)}) %collective-permute-start.2) | collective-permute-done | bytes 114720 | tf_op jit(solution)/shard_map/ppermute | solution.py:51
  21.7 0.6 pair_sums.3
  22.3 1.9 %collective-permute-start.11 = (bf16[64,640]{1,0:T(8,128)(2,1)S(1)}, bf16[64,640]{1,0:T(8,128)(2,1)S(1)}, u32[]{:S(2)}, u32[]{:S(2)}) collective-permute-start(bf16[64,640]{1,0:T(8,128)(2,1)S(1)} %get-tuple-element.84), channel_id=1, source_target_pairs={{0,2},{1,3},{2,0},{3,1},{4,6},{5,7},{6,4},{7,5},{8,10},{9,11},{10,... | collective-permute-start | bytes 245768 | tf_op jit(solution)/shard_map/ppermute | solution.py:51
  24.2 1.2 %collective-permute-start.12 = (bf16[64,640]{1,0:T(8,128)(2,1)S(1)}, bf16[64,640]{1,0:T(8,128)(2,1)S(1)}, u32[]{:S(2)}, u32[]{:S(2)}) collective-permute-start(bf16[64,640]{1,0:T(8,128)(2,1)S(1)} %get-tuple-element.85), channel_id=1, source_target_pairs={{0,4},{1,5},{2,6},{3,7},{4,0},{5,1},{6,2},{7,3},{8,12},{9,13},{10,... | collective-permute-start | bytes 245768 | tf_op jit(solution)/shard_map/ppermute | solution.py:51
  25.4 1.4 %collective-permute-start.13 = (bf16[64,640]{1,0:T(8,128)(2,1)S(1)}, bf16[64,640]{1,0:T(8,128)(2,1)S(1)}, u32[]{:S(2)}, u32[]{:S(2)}) collective-permute-start(bf16[64,640]{1,0:T(8,128)(2,1)S(1)} %get-tuple-element.86), channel_id=1, source_target_pairs={{0,6},{1,7},{2,4},{3,5},{4,2},{5,3},{6,0},{7,1},{8,14},{9,15},{10,... | collective-permute-start | bytes 245768 | tf_op jit(solution)/shard_map/ppermute | solution.py:51
  26.8 2.1 %cols_half.3 = (f32[64,640]{1,0:T(8,128)S(1)}, f32[64,128]{1,0:T(8,128)S(1)}, bf16[64,896]{1,0:T(8,128)(2,1)S(1)}, bf16[64,896]{1,0:T(8,128)(2,1)S(1)}, bf16[64,896]{1,0:T(8,128)(2,1)S(1)}) custom-call(s32[259]{0:T(512)S(1)} %concatenate.3.table, bf16[96,128,128]{2,1,0:T(8,128)(2,1)S(1)} %get-tuple-element.73.tile_ref, ...), custom_call_target="tpu_custom_call" | custom-call | tf_op jit(solution)/shard_map/cols_half/pallas_call | solution.py:360
  28.9 1.6 %collective-permute-start.14 = (bf16[64,896]{1,0:T(8,128)(2,1)S(1)}, bf16[64,896]{1,0:T(8,128)(2,1)S(1)}, u32[]{:S(2)}, u32[]{:S(2)}) collective-permute-start(bf16[64,896]{1,0:T(8,128)(2,1)S(1)} %get-tuple-element.88), channel_id=1, source_target_pairs={{0,8},{8,0},{16,24},{24,16},{1,9},{9,1},{17,25},{25,17},{2,10},{10... | collective-permute-start | bytes 344072 | tf_op jit(solution)/shard_map/ppermute | solution.py:51
  30.5 1.5 %collective-permute-start.15 = (bf16[64,896]{1,0:T(8,128)(2,1)S(1)}, bf16[64,896]{1,0:T(8,128)(2,1)S(1)}, u32[]{:S(2)}, u32[]{:S(2)}) collective-permute-start(bf16[64,896]{1,0:T(8,128)(2,1)S(1)} %get-tuple-element.89), channel_id=1, source_target_pairs={{0,16},{8,24},{16,0},{24,8},{1,17},{9,25},{17,1},{25,9},{2,18},{10... | collective-permute-start | bytes 344072 | tf_op jit(solution)/shard_map/ppermute | solution.py:51
  32.4 1.2 %collective-permute-done.12.refs_1_ = bf16[64,640]{1,0:T(8,128)(2,1)S(1)} collective-permute-done((bf16[64,640]{1,0:T(8,128)(2,1)S(1)}, bf16[64,640]{1,0:T(8,128)(2,1)S(1)}, u32[]{:S(2)}, u32[]{:S(2)}) %collective-permute-start.12) | collective-permute-done | bytes 81952 | tf_op jit(solution)/shard_map/ppermute | solution.py:51
  34.0 2.8 %collective-permute-done.15.refs_3_ = bf16[64,896]{1,0:T(8,128)(2,1)S(1)} collective-permute-done((bf16[64,896]{1,0:T(8,128)(2,1)S(1)}, bf16[64,896]{1,0:T(8,128)(2,1)S(1)}, u32[]{:S(2)}, u32[]{:S(2)}) %collective-permute-start.15) | collective-permute-done | bytes 114720 | tf_op jit(solution)/shard_map/ppermute | solution.py:51
  36.8 0.9 collective-permute-done.16.refs_4_
  37.7 0.7 combine.2
  38.5 1.0 collective-permute-start.21
  39.5 0.8 collective-permute-start.22
  40.3 1.7 %collective-permute-start.23 = (bf16[64,896]{1,0:T(8,128)(2,1)S(1)}, bf16[64,896]{1,0:T(8,128)(2,1)S(1)}, u32[]{:S(2)}, u32[]{:S(2)}) collective-permute-start(bf16[64,896]{1,0:T(8,128)(2,1)S(1)} %get-tuple-element.93.refs_0_), channel_id=1, source_target_pairs={{0,24},{8,16},{16,8},{24,0},{1,25},{9,17},{17,9},{25,1},{2,26},{10... | collective-permute-start | bytes 344072 | tf_op jit(solution)/shard_map/ppermute | solution.py:51
  42.0 0.9 collective-permute-start.18
  42.9 2.1 %collective-permute-start.19 = (bf16[64,896]{1,0:T(8,128)(2,1)S(1)}, bf16[64,896]{1,0:T(8,128)(2,1)S(1)}, u32[]{:S(2)}, u32[]{:S(2)}) collective-permute-start(bf16[64,896]{1,0:T(8,128)(2,1)S(1)} %get-tuple-element.93.refs_0_), channel_id=1, source_target_pairs={{0,4},{1,5},{2,6},{3,7},{4,0},{5,1},{6,2},{7,3},{8,12},{9,13},{10,... | collective-permute-start | bytes 344072 | tf_op jit(solution)/shard_map/ppermute | solution.py:51
  45.1 1.4 %collective-permute-start.20 = (bf16[64,896]{1,0:T(8,128)(2,1)S(1)}, bf16[64,896]{1,0:T(8,128)(2,1)S(1)}, u32[]{:S(2)}, u32[]{:S(2)}) collective-permute-start(bf16[64,896]{1,0:T(8,128)(2,1)S(1)} %get-tuple-element.93.refs_0_), channel_id=1, source_target_pairs={{0,6},{1,7},{2,4},{3,5},{4,2},{5,3},{6,0},{7,1},{8,14},{9,15},{10,... | collective-permute-start | bytes 344072 | tf_op jit(solution)/shard_map/ppermute | solution.py:51
  46.4 2.1 %rows_half.4 = (bf16[4,64,640]{2,1,0:T(8,128)(2,1)S(1)}, f32[4,64,640]{2,1,0:T(8,128)S(1)}) custom-call(s32[259]{0:T(512)S(1)} %concatenate.3.table, bf16[96,128,128]{2,1,0:T(8,128)(2,1)S(1)} %get-tuple-element.74.tile_ref, bf16[64,896]{1,0:T(8,128)(2,1)S(1)} %get-tuple-element.93.refs_0_, bf16[64,896]{1,0:T(8,128)(2,1)S(1)} %collective-permute-done.21.refs_1_, ...), custom_call_target="tpu_custom_call" | custom-call | tf_op jit(solution)/shard_map/rows_half/pallas_call | solution.py:360
  48.5 3.5 %collective-permute-done.19.refs_4_ = bf16[64,896]{1,0:T(8,128)(2,1)S(1)} collective-permute-done((bf16[64,896]{1,0:T(8,128)(2,1)S(1)}, bf16[64,896]{1,0:T(8,128)(2,1)S(1)}, u32[]{:S(2)}, u32[]{:S(2)}) %collective-permute-start.19) | collective-permute-done | bytes 114720 | tf_op jit(solution)/shard_map/ppermute | solution.py:51
  53.6 0.6 pair_sums.4
  54.3 1.9 %collective-permute-start.28 = (bf16[64,640]{1,0:T(8,128)(2,1)S(1)}, bf16[64,640]{1,0:T(8,128)(2,1)S(1)}, u32[]{:S(2)}, u32[]{:S(2)}) collective-permute-start(bf16[64,640]{1,0:T(8,128)(2,1)S(1)} %get-tuple-element.103), channel_id=1, source_target_pairs={{0,2},{1,3},{2,0},{3,1},{4,6},{5,7},{6,4},{7,5},{8,10},{9,11},{10,... | collective-permute-start | bytes 245768 | tf_op jit(solution)/shard_map/ppermute | solution.py:51
  56.1 1.2 %collective-permute-start.29 = (bf16[64,640]{1,0:T(8,128)(2,1)S(1)}, bf16[64,640]{1,0:T(8,128)(2,1)S(1)}, u32[]{:S(2)}, u32[]{:S(2)}) collective-permute-start(bf16[64,640]{1,0:T(8,128)(2,1)S(1)} %get-tuple-element.104), channel_id=1, source_target_pairs={{0,4},{1,5},{2,6},{3,7},{4,0},{5,1},{6,2},{7,3},{8,12},{9,13},{10,... | collective-permute-start | bytes 245768 | tf_op jit(solution)/shard_map/ppermute | solution.py:51
  57.4 1.3 %collective-permute-start.30 = (bf16[64,640]{1,0:T(8,128)(2,1)S(1)}, bf16[64,640]{1,0:T(8,128)(2,1)S(1)}, u32[]{:S(2)}, u32[]{:S(2)}) collective-permute-start(bf16[64,640]{1,0:T(8,128)(2,1)S(1)} %get-tuple-element.105), channel_id=1, source_target_pairs={{0,6},{1,7},{2,4},{3,5},{4,2},{5,3},{6,0},{7,1},{8,14},{9,15},{10,... | collective-permute-start | bytes 245768 | tf_op jit(solution)/shard_map/ppermute | solution.py:51
  58.7 2.1 %cols_half.4 = (f32[64,640]{1,0:T(8,128)S(1)}, f32[64,128]{1,0:T(8,128)S(1)}, bf16[64,896]{1,0:T(8,128)(2,1)S(1)}, bf16[64,896]{1,0:T(8,128)(2,1)S(1)}, bf16[64,896]{1,0:T(8,128)(2,1)S(1)}) custom-call(s32[259]{0:T(512)S(1)} %concatenate.3.table, bf16[96,128,128]{2,1,0:T(8,128)(2,1)S(1)} %get-tuple-element.73.tile_ref, ...), custom_call_target="tpu_custom_call" | custom-call | tf_op jit(solution)/shard_map/cols_half/pallas_call | solution.py:360
  60.8 1.1 collective-permute-start.31
  62.4 2.0 %collective-permute-start.33 = (bf16[64,896]{1,0:T(8,128)(2,1)S(1)}, bf16[64,896]{1,0:T(8,128)(2,1)S(1)}, u32[]{:S(2)}, u32[]{:S(2)}) collective-permute-start(bf16[64,896]{1,0:T(8,128)(2,1)S(1)} %get-tuple-element.109), channel_id=1, source_target_pairs={{0,24},{8,16},{16,8},{24,0},{1,25},{9,17},{17,9},{25,1},{2,26},{10... | collective-permute-start | bytes 344072 | tf_op jit(solution)/shard_map/ppermute | solution.py:51
  64.6 1.0 collective-permute-done.29.refs_1_
  65.6 0.9 collective-permute-done.31.refs_2_
  66.6 2.3 %collective-permute-done.32.refs_3_ = bf16[64,896]{1,0:T(8,128)(2,1)S(1)} collective-permute-done((bf16[64,896]{1,0:T(8,128)(2,1)S(1)}, bf16[64,896]{1,0:T(8,128)(2,1)S(1)}, u32[]{:S(2)}, u32[]{:S(2)}) %collective-permute-start.32) | collective-permute-done | bytes 114720 | tf_op jit(solution)/shard_map/ppermute | solution.py:51
  68.8 0.6 combine.3
  69.5 1.2 %collective-permute-start.38 = (bf16[64,896]{1,0:T(8,128)(2,1)S(1)}, bf16[64,896]{1,0:T(8,128)(2,1)S(1)}, u32[]{:S(2)}, u32[]{:S(2)}) collective-permute-start(bf16[64,896]{1,0:T(8,128)(2,1)S(1)} %get-tuple-element.110.refs_0_.refs_8_), channel_id=1, source_target_pairs={{0,8},{8,0},{16,24},{24,16},{1,9},{9,1},{17,25},{25,17},{2,10},{10... | collective-permute-start | bytes 344072 | tf_op jit(solution)/shard_map/ppermute | solution.py:51
  70.6 1.2 collective-permute-start.39
  71.8 1.2 %collective-permute-start.40 = (bf16[64,896]{1,0:T(8,128)(2,1)S(1)}, bf16[64,896]{1,0:T(8,128)(2,1)S(1)}, u32[]{:S(2)}, u32[]{:S(2)}) collective-permute-start(bf16[64,896]{1,0:T(8,128)(2,1)S(1)} %get-tuple-element.110.refs_0_.refs_8_), channel_id=1, source_target_pairs={{0,24},{8,16},{16,8},{24,0},{1,25},{9,17},{17,9},{25,1},{2,26},{10... | collective-permute-start | bytes 344072 | tf_op jit(solution)/shard_map/ppermute | solution.py:51
  73.0 0.8 collective-permute-start.35
  73.8 2.2 %collective-permute-start.36 = (bf16[64,896]{1,0:T(8,128)(2,1)S(1)}, bf16[64,896]{1,0:T(8,128)(2,1)S(1)}, u32[]{:S(2)}, u32[]{:S(2)}) collective-permute-start(bf16[64,896]{1,0:T(8,128)(2,1)S(1)} %get-tuple-element.110.refs_0_.refs_8_), channel_id=1, source_target_pairs={{0,4},{1,5},{2,6},{3,7},{4,0},{5,1},{6,2},{7,3},{8,12},{9,13},{10,... | collective-permute-start | bytes 344072 | tf_op jit(solution)/shard_map/ppermute | solution.py:51
  76.0 1.4 %collective-permute-start.37 = (bf16[64,896]{1,0:T(8,128)(2,1)S(1)}, bf16[64,896]{1,0:T(8,128)(2,1)S(1)}, u32[]{:S(2)}, u32[]{:S(2)}) collective-permute-start(bf16[64,896]{1,0:T(8,128)(2,1)S(1)} %get-tuple-element.110.refs_0_.refs_8_), channel_id=1, source_target_pairs={{0,6},{1,7},{2,4},{3,5},{4,2},{5,3},{6,0},{7,1},{8,14},{9,15},{10,... | collective-permute-start | bytes 344072 | tf_op jit(solution)/shard_map/ppermute | solution.py:51
  77.4 3.1 %coefficients.2.first_ref = f32[64,256]{1,0:T(8,128)S(1)} custom-call(f32[8,128]{1,0:T(8,128)S(1)} %shift.1.shift_ref, f32[64,128]{1,0:T(8,128)S(1)} %get-tuple-element.92.gram_ref.gram0_ref, f32[64,128]{1,0:T(8,128)S(1)} %get-tuple-element.111.gram1_ref), custom_call_target="tpu_custom_call" | custom-call | tf_op jit(solution)/shard_map/coefficients/pallas_call | solution.py:360
  80.5 2.1 %rows_half.5 = (bf16[4,64,640]{2,1,0:T(8,128)(2,1)S(1)}, f32[4,64,640]{2,1,0:T(8,128)S(1)}) custom-call(s32[259]{0:T(512)S(1)} %concatenate.3.table, bf16[96,128,128]{2,1,0:T(8,128)(2,1)S(1)} %get-tuple-element.74.tile_ref, bf16[64,896]{1,0:T(8,128)(2,1)S(1)} %get-tuple-element.110.refs_0_.refs_8_, ...), custom_call_target="tpu_custom_call" | custom-call | tf_op jit(solution)/shard_map/rows_half/pallas_call | solution.py:360
  84.5 0.6 pair_sums.5
  85.1 1.9 %collective-permute-start.48 = (bf16[64,640]{1,0:T(8,128)(2,1)S(1)}, bf16[64,640]{1,0:T(8,128)(2,1)S(1)}, u32[]{:S(2)}, u32[]{:S(2)}) collective-permute-start(bf16[64,640]{1,0:T(8,128)(2,1)S(1)} %get-tuple-element.125), channel_id=1, source_target_pairs={{0,2},{1,3},{2,0},{3,1},{4,6},{5,7},{6,4},{7,5},{8,10},{9,11},{10,... | collective-permute-start | bytes 245768 | tf_op jit(solution)/shard_map/ppermute | solution.py:51
  86.9 1.2 %collective-permute-start.49 = (bf16[64,640]{1,0:T(8,128)(2,1)S(1)}, bf16[64,640]{1,0:T(8,128)(2,1)S(1)}, u32[]{:S(2)}, u32[]{:S(2)}) collective-permute-start(bf16[64,640]{1,0:T(8,128)(2,1)S(1)} %get-tuple-element.126), channel_id=1, source_target_pairs={{0,4},{1,5},{2,6},{3,7},{4,0},{5,1},{6,2},{7,3},{8,12},{9,13},{10,... | collective-permute-start | bytes 245768 | tf_op jit(solution)/shard_map/ppermute | solution.py:51
  88.2 1.4 %collective-permute-start.50 = (bf16[64,640]{1,0:T(8,128)(2,1)S(1)}, bf16[64,640]{1,0:T(8,128)(2,1)S(1)}, u32[]{:S(2)}, u32[]{:S(2)}) collective-permute-start(bf16[64,640]{1,0:T(8,128)(2,1)S(1)} %get-tuple-element.127), channel_id=1, source_target_pairs={{0,6},{1,7},{2,4},{3,5},{4,2},{5,3},{6,0},{7,1},{8,14},{9,15},{10,... | collective-permute-start | bytes 245768 | tf_op jit(solution)/shard_map/ppermute | solution.py:51
  89.6 2.8 %cols_half.5 = (f32[64,640]{1,0:T(8,128)S(1)}, f32[64,192]{1,0:T(8,128)S(1)}, bf16[64,1024]{1,0:T(8,128)(2,1)S(1)}, bf16[64,1024]{1,0:T(8,128)(2,1)S(1)}, bf16[64,1024]{1,0:T(8,128)(2,1)S(1)}) custom-call(s32[259]{0:T(512)S(1)} %concatenate.3.table, bf16[96,128,128]{2,1,0:T(8,128)(2,1)S(1)} %get-tuple-element.73.tile_ref, ...), custom_call_target="tpu_custom_call" | custom-call | tf_op jit(solution)/shard_map/cols_half/pallas_call | solution.py:360
  92.3 1.1 collective-permute-start.44
  93.4 1.5 %collective-permute-start.45 = (bf16[64,1024]{1,0:T(8,128)(2,1)S(1)}, bf16[64,1024]{1,0:T(8,128)(2,1)S(1)}, u32[]{:S(2)}, u32[]{:S(2)}) collective-permute-start(bf16[64,1024]{1,0:T(8,128)(2,1)S(1)} %get-tuple-element.120), channel_id=1, source_target_pairs={{0,16},{8,24},{16,0},{24,8},{1,17},{9,25},{17,1},{25,9},{2,18},{10... | collective-permute-start | bytes 393224 | tf_op jit(solution)/shard_map/ppermute | solution.py:51
  94.9 1.0 collective-permute-start.46
  96.5 1.9 %collective-permute-done.44.refs_0_.refs_2_ = bf16[64,1024]{1,0:T(8,128)(2,1)S(1)} collective-permute-done((bf16[64,1024]{1,0:T(8,128)(2,1)S(1)}, bf16[64,1024]{1,0:T(8,128)(2,1)S(1)}, u32[]{:S(2)}, u32[]{:S(2)}) %collective-permute-start.44) | collective-permute-done | bytes 131104 | tf_op jit(solution)/shard_map/ppermute | solution.py:51
  98.4 2.8 %collective-permute-done.45.refs_1_.refs_3_ = bf16[64,1024]{1,0:T(8,128)(2,1)S(1)} collective-permute-done((bf16[64,1024]{1,0:T(8,128)(2,1)S(1)}, bf16[64,1024]{1,0:T(8,128)(2,1)S(1)}, u32[]{:S(2)}, u32[]{:S(2)}) %collective-permute-start.45) | collective-permute-done | bytes 131104 | tf_op jit(solution)/shard_map/ppermute | solution.py:51
  101.4 1.0 collective-permute-start.51
  102.3 2.1 %collective-permute-start.52 = (f32[64,64]{1,0:T(8,128)S(1)}, f32[64,64]{1,0:T(8,128)S(1)}, u32[]{:S(2)}, u32[]{:S(2)}) collective-permute-start(f32[64,64]{1,0:T(8,128)S(1)} %get-tuple-element.131), channel_id=1, source_target_pairs={{0,4},{1,5},{2,6},{3,7},{4,0},{5,1},{6,2},{7,3},{8,12},{9,13},{10,... | collective-permute-start | bytes 49160 | tf_op jit(solution)/shard_map/ppermute | solution.py:51
  104.4 1.4 %collective-permute-start.53 = (f32[64,64]{1,0:T(8,128)S(1)}, f32[64,64]{1,0:T(8,128)S(1)}, u32[]{:S(2)}, u32[]{:S(2)}) collective-permute-start(f32[64,64]{1,0:T(8,128)S(1)} %get-tuple-element.131), channel_id=1, source_target_pairs={{0,6},{1,7},{2,4},{3,5},{4,2},{5,3},{6,0},{7,1},{8,14},{9,15},{10,... | collective-permute-start | bytes 49160 | tf_op jit(solution)/shard_map/ppermute | solution.py:51
  105.8 6.2 %coefficients.3 = (f32[192,256]{1,0:T(8,128)S(1)}, f32[64,256]{1,0:T(8,128)S(1)}) custom-call(f32[8,128]{1,0:T(8,128)S(1)} %shift.1.shift_ref, f32[64,128]{1,0:T(8,128)S(1)} %get-tuple-element.92.gram_ref.gram0_ref, f32[64,128]{1,0:T(8,128)S(1)} %get-tuple-element.111.gram1_ref, f32[64,128]{1,0:T(8,128)S(1)} %get-tuple-element.132.gram2_ref, ...), custom_call_target="tpu_custom_call" | custom-call | tf_op jit(solution)/shard_map/coefficients/pallas_call | solution.py:360
  112.2 0.8 vectors.1.vectors_ref
  113.4 3.6 %finish.1 = (f32[64,640]{1,0:T(8,128)}, f32[64,640]{1,0:T(8,128)}) custom-call(f32[256,640]{1,0:T(8,128)S(1)} %vectors.1.vectors_ref, f32[64,256]{1,0:T(8,128)S(1)} %get-tuple-element.141.small_ref, f32[64,64]{1,0:T(8,128)S(1)} %add_add_fusion.both_ref, f32[64,64]{1,0:T(8,128)S(1)} %collective-permute-done.54.other_ref, ...), custom_call_target="tpu_custom_call" | custom-call | tf_op jit(solution)/shard_map/finish/pallas_call | solution.py:360
  (91 shorter events, 8.5 us)
Async XLA Ops:
  2.2 11.1 %copy-start.5 = (s32[1,1,32]{2,1,0:T(1,128)S(1)}, s32[1,1,32]{2,1,0:T(1,128)}, u32[]{:S(2)}) copy-start(s32[1,1,32]{2,1,0:T(1,128)} %param.14) | copy-start | bytes 388
  2.2 11.1 %copy-start.6 = (s32[1,1,64]{2,1,0:T(1,128)S(1)}, s32[1,1,64]{2,1,0:T(1,128)}, u32[]{:S(2)}) copy-start(s32[1,1,64]{2,1,0:T(1,128)} %param.19) | copy-start | bytes 772
  2.2 11.1 %copy-start.7 = (s32[1,1,32]{2,1,0:T(1,128)S(1)}, s32[1,1,32]{2,1,0:T(1,128)}, u32[]{:S(2)}) copy-start(s32[1,1,32]{2,1,0:T(1,128)} %param.15) | copy-start | bytes 388
  2.2 11.1 %copy-start.8 = (s32[1,1,64]{2,1,0:T(1,128)S(1)}, s32[1,1,64]{2,1,0:T(1,128)}, u32[]{:S(2)}) copy-start(s32[1,1,64]{2,1,0:T(1,128)} %param.20) | copy-start | bytes 772
  2.2 11.1 %copy-start.9 = (s32[1,1,64]{2,1,0:T(1,128)S(1)}, s32[1,1,64]{2,1,0:T(1,128)}, u32[]{:S(2)}) copy-start(s32[1,1,64]{2,1,0:T(1,128)} %param.21) | copy-start | bytes 772
  2.3 11.2 %copy-start = (bf16[1,1,32,128,128]{4,3,2,1,0:T(8,128)(2,1)S(1)}, bf16[1,1,32,128,128]{4,3,2,1,0:T(8,128)(2,1)}, u32[]{:S(2)}) copy-start(bf16[1,1,32,128,128]{4,3,2,1,0:T(8,128)(2,1)} %param.13) | copy-start | bytes 3145732
  2.3 11.2 %copy-start.3 = (bf16[1,1,64,32,128]{4,3,2,1,0:T(8,128)(2,1)S(1)}, bf16[1,1,64,32,128]{4,3,2,1,0:T(8,128)(2,1)}, u32[]{:S(2)}) copy-start(bf16[1,1,64,32,128]{4,3,2,1,0:T(8,128)(2,1)} %param.17) | copy-start | bytes 1572868
  2.3 11.2 %copy-start.4 = (bf16[1,1,64,32,128]{4,3,2,1,0:T(8,128)(2,1)S(1)}, bf16[1,1,64,32,128]{4,3,2,1,0:T(8,128)(2,1)}, u32[]{:S(2)}) copy-start(bf16[1,1,64,32,128]{4,3,2,1,0:T(8,128)(2,1)} %param.18) | copy-start | bytes 1572868
  2.6 9.2 %collective-permute-start.4 = (bf16[64,896]{1,0:T(8,128)(2,1)S(1)}, bf16[64,896]{1,0:T(8,128)(2,1)S(1)}, u32[]{:S(2)}, u32[]{:S(2)}) collective-permute-start(bf16[64,896]{1,0:T(8,128)(2,1)S(1)} %first_message.1.refs_0_), channel_id=1, source_target_pairs={{0,8},{8,0},{16,24},{24,16},{1,9},{9,1},{17,25},{25,17},{2,10},{10... | collective-permute-start | bytes 344072 | tf_op jit(solution)/shard_map/ppermute | solution.py:51
  5.6 11.1 %collective-permute-start.5 = (bf16[64,896]{1,0:T(8,128)(2,1)S(1)}, bf16[64,896]{1,0:T(8,128)(2,1)S(1)}, u32[]{:S(2)}, u32[]{:S(2)}) collective-permute-start(bf16[64,896]{1,0:T(8,128)(2,1)S(1)} %first_message.1.refs_0_), channel_id=1, source_target_pairs={{0,16},{8,24},{16,0},{24,8},{1,17},{9,25},{17,1},{25,9},{2,18},{10... | collective-permute-start | bytes 344072 | tf_op jit(solution)/shard_map/ppermute | solution.py:51
  7.1 9.6 %collective-permute-start.6 = (bf16[64,896]{1,0:T(8,128)(2,1)S(1)}, bf16[64,896]{1,0:T(8,128)(2,1)S(1)}, u32[]{:S(2)}, u32[]{:S(2)}) collective-permute-start(bf16[64,896]{1,0:T(8,128)(2,1)S(1)} %first_message.1.refs_0_), channel_id=1, source_target_pairs={{0,24},{8,16},{16,8},{24,0},{1,25},{9,17},{17,9},{25,1},{2,26},{10... | collective-permute-start | bytes 344072 | tf_op jit(solution)/shard_map/ppermute | solution.py:51
  7.2 11.7 %collective-permute-start.1 = (bf16[64,896]{1,0:T(8,128)(2,1)S(1)}, bf16[64,896]{1,0:T(8,128)(2,1)S(1)}, u32[]{:S(2)}, u32[]{:S(2)}) collective-permute-start(bf16[64,896]{1,0:T(8,128)(2,1)S(1)} %first_message.1.refs_0_), channel_id=1, source_target_pairs={{0,2},{1,3},{2,0},{3,1},{4,6},{5,7},{6,4},{7,5},{8,10},{9,11},{10,... | collective-permute-start | bytes 344072 | tf_op jit(solution)/shard_map/ppermute | solution.py:51
  9.2 10.9 %collective-permute-start.2 = (bf16[64,896]{1,0:T(8,128)(2,1)S(1)}, bf16[64,896]{1,0:T(8,128)(2,1)S(1)}, u32[]{:S(2)}, u32[]{:S(2)}) collective-permute-start(bf16[64,896]{1,0:T(8,128)(2,1)S(1)} %first_message.1.refs_0_), channel_id=1, source_target_pairs={{0,4},{1,5},{2,6},{3,7},{4,0},{5,1},{6,2},{7,3},{8,12},{9,13},{10,... | collective-permute-start | bytes 344072 | tf_op jit(solution)/shard_map/ppermute | solution.py:51
  11.8 8.3 %collective-permute-start.3 = (bf16[64,896]{1,0:T(8,128)(2,1)S(1)}, bf16[64,896]{1,0:T(8,128)(2,1)S(1)}, u32[]{:S(2)}, u32[]{:S(2)}) collective-permute-start(bf16[64,896]{1,0:T(8,128)(2,1)S(1)} %first_message.1.refs_0_), channel_id=1, source_target_pairs={{0,6},{1,7},{2,4},{3,5},{4,2},{5,3},{6,0},{7,1},{8,14},{9,15},{10,... | collective-permute-start | bytes 344072 | tf_op jit(solution)/shard_map/ppermute | solution.py:51
  20.1 1.6 %collective-permute-start.10 = (bf16[4,64,640]{2,1,0:T(8,128)(2,1)S(1)}, bf16[4,64,640]{2,1,0:T(8,128)(2,1)S(1)}, u32[]{:S(2)}, u32[]{:S(2)}) collective-permute-start(bf16[4,64,640]{2,1,0:T(8,128)(2,1)S(1)} %get-tuple-element.82), channel_id=1, source_target_pairs={{0,1},{1,0},{2,3},{3,2},{4,5},{5,4},{6,7},{7,6},{8,9},{9,8},{10,11... | collective-permute-start | bytes 983048 | tf_op jit(solution)/shard_map/ppermute | solution.py:51
  20.1 4.1 %collective-permute-start = (bf16[64,896]{1,0:T(8,128)(2,1)S(1)}, bf16[64,896]{1,0:T(8,128)(2,1)S(1)}, u32[]{:S(2)}, u32[]{:S(2)}) collective-permute-start(bf16[64,896]{1,0:T(8,128)(2,1)S(1)} %first_message.1.refs_0_), channel_id=1, source_target_pairs={{0,1},{1,0},{2,3},{3,2},{4,5},{5,4},{6,7},{7,6},{8,9},{9,8},{10,11... | collective-permute-start | bytes 344072 | tf_op jit(solution)/shard_map/ppermute | solution.py:51
  20.6 4.9 %collective-permute-start.7 = (bf16[64,896]{1,0:T(8,128)(2,1)S(1)}, bf16[64,896]{1,0:T(8,128)(2,1)S(1)}, u32[]{:S(2)}, u32[]{:S(2)}) collective-permute-start(bf16[64,896]{1,0:T(8,128)(2,1)S(1)} %collective-permute-done.1.refs_2_), channel_id=1, source_target_pairs={{0,1},{1,0},{2,3},{3,2},{4,5},{5,4},{6,7},{7,6},{8,9},{9,8},{10,11... | collective-permute-start | bytes 344072 | tf_op jit(solution)/shard_map/ppermute | solution.py:51
  20.6 6.2 %collective-permute-start.8 = (bf16[64,896]{1,0:T(8,128)(2,1)S(1)}, bf16[64,896]{1,0:T(8,128)(2,1)S(1)}, u32[]{:S(2)}, u32[]{:S(2)}) collective-permute-start(bf16[64,896]{1,0:T(8,128)(2,1)S(1)} %collective-permute-done.2.refs_4_), channel_id=1, source_target_pairs={{0,1},{1,0},{2,3},{3,2},{4,5},{5,4},{6,7},{7,6},{8,9},{9,8},{10,11... | collective-permute-start | bytes 344072 | tf_op jit(solution)/shard_map/ppermute | solution.py:51
  21.1 5.7 %collective-permute-start.9 = (bf16[64,896]{1,0:T(8,128)(2,1)S(1)}, bf16[64,896]{1,0:T(8,128)(2,1)S(1)}, u32[]{:S(2)}, u32[]{:S(2)}) collective-permute-start(bf16[64,896]{1,0:T(8,128)(2,1)S(1)} %collective-permute-done.3.refs_6_), channel_id=1, source_target_pairs={{0,1},{1,0},{2,3},{3,2},{4,5},{5,4},{6,7},{7,6},{8,9},{9,8},{10,11... | collective-permute-start | bytes 344072 | tf_op jit(solution)/shard_map/ppermute | solution.py:51
  22.3 9.7 %collective-permute-start.11 = (bf16[64,640]{1,0:T(8,128)(2,1)S(1)}, bf16[64,640]{1,0:T(8,128)(2,1)S(1)}, u32[]{:S(2)}, u32[]{:S(2)}) collective-permute-start(bf16[64,640]{1,0:T(8,128)(2,1)S(1)} %get-tuple-element.84), channel_id=1, source_target_pairs={{0,2},{1,3},{2,0},{3,1},{4,6},{5,7},{6,4},{7,5},{8,10},{9,11},{10,... | collective-permute-start | bytes 245768 | tf_op jit(solution)/shard_map/ppermute | solution.py:51
  24.2 9.5 %collective-permute-start.12 = (bf16[64,640]{1,0:T(8,128)(2,1)S(1)}, bf16[64,640]{1,0:T(8,128)(2,1)S(1)}, u32[]{:S(2)}, u32[]{:S(2)}) collective-permute-start(bf16[64,640]{1,0:T(8,128)(2,1)S(1)} %get-tuple-element.85), channel_id=1, source_target_pairs={{0,4},{1,5},{2,6},{3,7},{4,0},{5,1},{6,2},{7,3},{8,12},{9,13},{10,... | collective-permute-start | bytes 245768 | tf_op jit(solution)/shard_map/ppermute | solution.py:51
  25.4 8.2 %collective-permute-start.13 = (bf16[64,640]{1,0:T(8,128)(2,1)S(1)}, bf16[64,640]{1,0:T(8,128)(2,1)S(1)}, u32[]{:S(2)}, u32[]{:S(2)}) collective-permute-start(bf16[64,640]{1,0:T(8,128)(2,1)S(1)} %get-tuple-element.86), channel_id=1, source_target_pairs={{0,6},{1,7},{2,4},{3,5},{4,2},{5,3},{6,0},{7,1},{8,14},{9,15},{10,... | collective-permute-start | bytes 245768 | tf_op jit(solution)/shard_map/ppermute | solution.py:51
  26.8 10.9 %copy-start.2 = (f32[64,640]{1,0:T(8,128)S(1)}, f32[64,640]{1,0:T(8,128)}, u32[]{:S(2)}) copy-start(f32[64,640]{1,0:T(8,128)} %b_ref.1) | copy-start | bytes 491524
  28.9 5.1 %collective-permute-start.14 = (bf16[64,896]{1,0:T(8,128)(2,1)S(1)}, bf16[64,896]{1,0:T(8,128)(2,1)S(1)}, u32[]{:S(2)}, u32[]{:S(2)}) collective-permute-start(bf16[64,896]{1,0:T(8,128)(2,1)S(1)} %get-tuple-element.88), channel_id=1, source_target_pairs={{0,8},{8,0},{16,24},{24,16},{1,9},{9,1},{17,25},{25,17},{2,10},{10... | collective-permute-start | bytes 344072 | tf_op jit(solution)/shard_map/ppermute | solution.py:51
  30.5 6.4 %collective-permute-start.15 = (bf16[64,896]{1,0:T(8,128)(2,1)S(1)}, bf16[64,896]{1,0:T(8,128)(2,1)S(1)}, u32[]{:S(2)}, u32[]{:S(2)}) collective-permute-start(bf16[64,896]{1,0:T(8,128)(2,1)S(1)} %get-tuple-element.89), channel_id=1, source_target_pairs={{0,16},{8,24},{16,0},{24,8},{1,17},{9,25},{17,1},{25,9},{2,18},{10... | collective-permute-start | bytes 344072 | tf_op jit(solution)/shard_map/ppermute | solution.py:51
  32.0 5.7 %collective-permute-start.16 = (bf16[64,896]{1,0:T(8,128)(2,1)S(1)}, bf16[64,896]{1,0:T(8,128)(2,1)S(1)}, u32[]{:S(2)}, u32[]{:S(2)}) collective-permute-start(bf16[64,896]{1,0:T(8,128)(2,1)S(1)} %get-tuple-element.90), channel_id=1, source_target_pairs={{0,24},{8,16},{16,8},{24,0},{1,25},{9,17},{17,9},{25,1},{2,26},{10... | collective-permute-start | bytes 344072 | tf_op jit(solution)/shard_map/ppermute | solution.py:51
  38.5 6.6 %collective-permute-start.21 = (bf16[64,896]{1,0:T(8,128)(2,1)S(1)}, bf16[64,896]{1,0:T(8,128)(2,1)S(1)}, u32[]{:S(2)}, u32[]{:S(2)}) collective-permute-start(bf16[64,896]{1,0:T(8,128)(2,1)S(1)} %get-tuple-element.93.refs_0_), channel_id=1, source_target_pairs={{0,8},{8,0},{16,24},{24,16},{1,9},{9,1},{17,25},{25,17},{2,10},{10... | collective-permute-start | bytes 344072 | tf_op jit(solution)/shard_map/ppermute | solution.py:51
  39.5 6.9 %collective-permute-start.22 = (bf16[64,896]{1,0:T(8,128)(2,1)S(1)}, bf16[64,896]{1,0:T(8,128)(2,1)S(1)}, u32[]{:S(2)}, u32[]{:S(2)}) collective-permute-start(bf16[64,896]{1,0:T(8,128)(2,1)S(1)} %get-tuple-element.93.refs_0_), channel_id=1, source_target_pairs={{0,16},{8,24},{16,0},{24,8},{1,17},{9,25},{17,1},{25,9},{2,18},{10... | collective-permute-start | bytes 344072 | tf_op jit(solution)/shard_map/ppermute | solution.py:51
  40.3 6.1 %collective-permute-start.23 = (bf16[64,896]{1,0:T(8,128)(2,1)S(1)}, bf16[64,896]{1,0:T(8,128)(2,1)S(1)}, u32[]{:S(2)}, u32[]{:S(2)}) collective-permute-start(bf16[64,896]{1,0:T(8,128)(2,1)S(1)} %get-tuple-element.93.refs_0_), channel_id=1, source_target_pairs={{0,24},{8,16},{16,8},{24,0},{1,25},{9,17},{17,9},{25,1},{2,26},{10... | collective-permute-start | bytes 344072 | tf_op jit(solution)/shard_map/ppermute | solution.py:51
  42.0 6.5 %collective-permute-start.18 = (bf16[64,896]{1,0:T(8,128)(2,1)S(1)}, bf16[64,896]{1,0:T(8,128)(2,1)S(1)}, u32[]{:S(2)}, u32[]{:S(2)}) collective-permute-start(bf16[64,896]{1,0:T(8,128)(2,1)S(1)} %get-tuple-element.93.refs_0_), channel_id=1, source_target_pairs={{0,2},{1,3},{2,0},{3,1},{4,6},{5,7},{6,4},{7,5},{8,10},{9,11},{10,... | collective-permute-start | bytes 344072 | tf_op jit(solution)/shard_map/ppermute | solution.py:51
  42.9 9.1 %collective-permute-start.19 = (bf16[64,896]{1,0:T(8,128)(2,1)S(1)}, bf16[64,896]{1,0:T(8,128)(2,1)S(1)}, u32[]{:S(2)}, u32[]{:S(2)}) collective-permute-start(bf16[64,896]{1,0:T(8,128)(2,1)S(1)} %get-tuple-element.93.refs_0_), channel_id=1, source_target_pairs={{0,4},{1,5},{2,6},{3,7},{4,0},{5,1},{6,2},{7,3},{8,12},{9,13},{10,... | collective-permute-start | bytes 344072 | tf_op jit(solution)/shard_map/ppermute | solution.py:51
  45.1 6.9 %collective-permute-start.20 = (bf16[64,896]{1,0:T(8,128)(2,1)S(1)}, bf16[64,896]{1,0:T(8,128)(2,1)S(1)}, u32[]{:S(2)}, u32[]{:S(2)}) collective-permute-start(bf16[64,896]{1,0:T(8,128)(2,1)S(1)} %get-tuple-element.93.refs_0_), channel_id=1, source_target_pairs={{0,6},{1,7},{2,4},{3,5},{4,2},{5,3},{6,0},{7,1},{8,14},{9,15},{10,... | collective-permute-start | bytes 344072 | tf_op jit(solution)/shard_map/ppermute | solution.py:51
  52.0 1.6 %collective-permute-start.27 = (bf16[4,64,640]{2,1,0:T(8,128)(2,1)S(1)}, bf16[4,64,640]{2,1,0:T(8,128)(2,1)S(1)}, u32[]{:S(2)}, u32[]{:S(2)}) collective-permute-start(bf16[4,64,640]{2,1,0:T(8,128)(2,1)S(1)} %get-tuple-element.101), channel_id=1, source_target_pairs={{0,1},{1,0},{2,3},{3,2},{4,5},{5,4},{6,7},{7,6},{8,9},{9,8},{10,11... | collective-permute-start | bytes 983048 | tf_op jit(solution)/shard_map/ppermute | solution.py:51
  52.0 4.1 %collective-permute-start.17 = (bf16[64,896]{1,0:T(8,128)(2,1)S(1)}, bf16[64,896]{1,0:T(8,128)(2,1)S(1)}, u32[]{:S(2)}, u32[]{:S(2)}) collective-permute-start(bf16[64,896]{1,0:T(8,128)(2,1)S(1)} %get-tuple-element.93.refs_0_), channel_id=1, source_target_pairs={{0,1},{1,0},{2,3},{3,2},{4,5},{5,4},{6,7},{7,6},{8,9},{9,8},{10,11... | collective-permute-start | bytes 344072 | tf_op jit(solution)/shard_map/ppermute | solution.py:51
  52.5 4.9 %collective-permute-start.24 = (bf16[64,896]{1,0:T(8,128)(2,1)S(1)}, bf16[64,896]{1,0:T(8,128)(2,1)S(1)}, u32[]{:S(2)}, u32[]{:S(2)}) collective-permute-start(bf16[64,896]{1,0:T(8,128)(2,1)S(1)} %collective-permute-done.18.refs_2_), channel_id=1, source_target_pairs={{0,1},{1,0},{2,3},{3,2},{4,5},{5,4},{6,7},{7,6},{8,9},{9,8},{10,11... | collective-permute-start | bytes 344072 | tf_op jit(solution)/shard_map/ppermute | solution.py:51
  52.5 6.2 %collective-permute-start.25 = (bf16[64,896]{1,0:T(8,128)(2,1)S(1)}, bf16[64,896]{1,0:T(8,128)(2,1)S(1)}, u32[]{:S(2)}, u32[]{:S(2)}) collective-permute-start(bf16[64,896]{1,0:T(8,128)(2,1)S(1)} %collective-permute-done.19.refs_4_), channel_id=1, source_target_pairs={{0,1},{1,0},{2,3},{3,2},{4,5},{5,4},{6,7},{7,6},{8,9},{9,8},{10,11... | collective-permute-start | bytes 344072 | tf_op jit(solution)/shard_map/ppermute | solution.py:51
  53.0 5.7 %collective-permute-start.26 = (bf16[64,896]{1,0:T(8,128)(2,1)S(1)}, bf16[64,896]{1,0:T(8,128)(2,1)S(1)}, u32[]{:S(2)}, u32[]{:S(2)}) collective-permute-start(bf16[64,896]{1,0:T(8,128)(2,1)S(1)} %collective-permute-done.20.refs_6_), channel_id=1, source_target_pairs={{0,1},{1,0},{2,3},{3,2},{4,5},{5,4},{6,7},{7,6},{8,9},{9,8},{10,11... | collective-permute-start | bytes 344072 | tf_op jit(solution)/shard_map/ppermute | solution.py:51
  54.3 8.2 %collective-permute-start.28 = (bf16[64,640]{1,0:T(8,128)(2,1)S(1)}, bf16[64,640]{1,0:T(8,128)(2,1)S(1)}, u32[]{:S(2)}, u32[]{:S(2)}) collective-permute-start(bf16[64,640]{1,0:T(8,128)(2,1)S(1)} %get-tuple-element.103), channel_id=1, source_target_pairs={{0,2},{1,3},{2,0},{3,1},{4,6},{5,7},{6,4},{7,5},{8,10},{9,11},{10,... | collective-permute-start | bytes 245768 | tf_op jit(solution)/shard_map/ppermute | solution.py:51
  56.1 9.5 %collective-permute-start.29 = (bf16[64,640]{1,0:T(8,128)(2,1)S(1)}, bf16[64,640]{1,0:T(8,128)(2,1)S(1)}, u32[]{:S(2)}, u32[]{:S(2)}) collective-permute-start(bf16[64,640]{1,0:T(8,128)(2,1)S(1)} %get-tuple-element.104), channel_id=1, source_target_pairs={{0,4},{1,5},{2,6},{3,7},{4,0},{5,1},{6,2},{7,3},{8,12},{9,13},{10,... | collective-permute-start | bytes 245768 | tf_op jit(solution)/shard_map/ppermute | solution.py:51
  57.4 8.2 %collective-permute-start.30 = (bf16[64,640]{1,0:T(8,128)(2,1)S(1)}, bf16[64,640]{1,0:T(8,128)(2,1)S(1)}, u32[]{:S(2)}, u32[]{:S(2)}) collective-permute-start(bf16[64,640]{1,0:T(8,128)(2,1)S(1)} %get-tuple-element.105), channel_id=1, source_target_pairs={{0,6},{1,7},{2,4},{3,5},{4,2},{5,3},{6,0},{7,1},{8,14},{9,15},{10,... | collective-permute-start | bytes 245768 | tf_op jit(solution)/shard_map/ppermute | solution.py:51
  60.8 5.7 %collective-permute-start.31 = (bf16[64,896]{1,0:T(8,128)(2,1)S(1)}, bf16[64,896]{1,0:T(8,128)(2,1)S(1)}, u32[]{:S(2)}, u32[]{:S(2)}) collective-permute-start(bf16[64,896]{1,0:T(8,128)(2,1)S(1)} %get-tuple-element.107), channel_id=1, source_target_pairs={{0,8},{8,0},{16,24},{24,16},{1,9},{9,1},{17,25},{25,17},{2,10},{10... | collective-permute-start | bytes 344072 | tf_op jit(solution)/shard_map/ppermute | solution.py:51
  61.9 6.9 %collective-permute-start.32 = (bf16[64,896]{1,0:T(8,128)(2,1)S(1)}, bf16[64,896]{1,0:T(8,128)(2,1)S(1)}, u32[]{:S(2)}, u32[]{:S(2)}) collective-permute-start(bf16[64,896]{1,0:T(8,128)(2,1)S(1)} %get-tuple-element.108), channel_id=1, source_target_pairs={{0,16},{8,24},{16,0},{24,8},{1,17},{9,25},{17,1},{25,9},{2,18},{10... | collective-permute-start | bytes 344072 | tf_op jit(solution)/shard_map/ppermute | solution.py:51
  62.4 6.4 %collective-permute-start.33 = (bf16[64,896]{1,0:T(8,128)(2,1)S(1)}, bf16[64,896]{1,0:T(8,128)(2,1)S(1)}, u32[]{:S(2)}, u32[]{:S(2)}) collective-permute-start(bf16[64,896]{1,0:T(8,128)(2,1)S(1)} %get-tuple-element.109), channel_id=1, source_target_pairs={{0,24},{8,16},{16,8},{24,0},{1,25},{9,17},{17,9},{25,1},{2,26},{10... | collective-permute-start | bytes 344072 | tf_op jit(solution)/shard_map/ppermute | solution.py:51
  69.5 6.5 %collective-permute-start.38 = (bf16[64,896]{1,0:T(8,128)(2,1)S(1)}, bf16[64,896]{1,0:T(8,128)(2,1)S(1)}, u32[]{:S(2)}, u32[]{:S(2)}) collective-permute-start(bf16[64,896]{1,0:T(8,128)(2,1)S(1)} %get-tuple-element.110.refs_0_.refs_8_), channel_id=1, source_target_pairs={{0,8},{8,0},{16,24},{24,16},{1,9},{9,1},{17,25},{25,17},{2,10},{10... | collective-permute-start | bytes 344072 | tf_op jit(solution)/shard_map/ppermute | solution.py:51
  70.6 9.9 %collective-permute-start.39 = (bf16[64,896]{1,0:T(8,128)(2,1)S(1)}, bf16[64,896]{1,0:T(8,128)(2,1)S(1)}, u32[]{:S(2)}, u32[]{:S(2)}) collective-permute-start(bf16[64,896]{1,0:T(8,128)(2,1)S(1)} %get-tuple-element.110.refs_0_.refs_8_), channel_id=1, source_target_pairs={{0,16},{8,24},{16,0},{24,8},{1,17},{9,25},{17,1},{25,9},{2,18},{10... | collective-permute-start | bytes 344072 | tf_op jit(solution)/shard_map/ppermute | solution.py:51
  71.8 8.7 %collective-permute-start.40 = (bf16[64,896]{1,0:T(8,128)(2,1)S(1)}, bf16[64,896]{1,0:T(8,128)(2,1)S(1)}, u32[]{:S(2)}, u32[]{:S(2)}) collective-permute-start(bf16[64,896]{1,0:T(8,128)(2,1)S(1)} %get-tuple-element.110.refs_0_.refs_8_), channel_id=1, source_target_pairs={{0,24},{8,16},{16,8},{24,0},{1,25},{9,17},{17,9},{25,1},{2,26},{10... | collective-permute-start | bytes 344072 | tf_op jit(solution)/shard_map/ppermute | solution.py:51
  73.0 9.6 %collective-permute-start.35 = (bf16[64,896]{1,0:T(8,128)(2,1)S(1)}, bf16[64,896]{1,0:T(8,128)(2,1)S(1)}, u32[]{:S(2)}, u32[]{:S(2)}) collective-permute-start(bf16[64,896]{1,0:T(8,128)(2,1)S(1)} %get-tuple-element.110.refs_0_.refs_8_), channel_id=1, source_target_pairs={{0,2},{1,3},{2,0},{3,1},{4,6},{5,7},{6,4},{7,5},{8,10},{9,11},{10,... | collective-permute-start | bytes 344072 | tf_op jit(solution)/shard_map/ppermute | solution.py:51
  73.8 9.0 %collective-permute-start.36 = (bf16[64,896]{1,0:T(8,128)(2,1)S(1)}, bf16[64,896]{1,0:T(8,128)(2,1)S(1)}, u32[]{:S(2)}, u32[]{:S(2)}) collective-permute-start(bf16[64,896]{1,0:T(8,128)(2,1)S(1)} %get-tuple-element.110.refs_0_.refs_8_), channel_id=1, source_target_pairs={{0,4},{1,5},{2,6},{3,7},{4,0},{5,1},{6,2},{7,3},{8,12},{9,13},{10,... | collective-permute-start | bytes 344072 | tf_op jit(solution)/shard_map/ppermute | solution.py:51
  76.0 6.8 %collective-permute-start.37 = (bf16[64,896]{1,0:T(8,128)(2,1)S(1)}, bf16[64,896]{1,0:T(8,128)(2,1)S(1)}, u32[]{:S(2)}, u32[]{:S(2)}) collective-permute-start(bf16[64,896]{1,0:T(8,128)(2,1)S(1)} %get-tuple-element.110.refs_0_.refs_8_), channel_id=1, source_target_pairs={{0,6},{1,7},{2,4},{3,5},{4,2},{5,3},{6,0},{7,1},{8,14},{9,15},{10,... | collective-permute-start | bytes 344072 | tf_op jit(solution)/shard_map/ppermute | solution.py:51
  82.8 1.6 %collective-permute-start.47 = (bf16[4,64,640]{2,1,0:T(8,128)(2,1)S(1)}, bf16[4,64,640]{2,1,0:T(8,128)(2,1)S(1)}, u32[]{:S(2)}, u32[]{:S(2)}) collective-permute-start(bf16[4,64,640]{2,1,0:T(8,128)(2,1)S(1)} %get-tuple-element.123), channel_id=1, source_target_pairs={{0,1},{1,0},{2,3},{3,2},{4,5},{5,4},{6,7},{7,6},{8,9},{9,8},{10,11... | collective-permute-start | bytes 983048 | tf_op jit(solution)/shard_map/ppermute | solution.py:51
  82.8 4.1 %collective-permute-start.34 = (bf16[64,896]{1,0:T(8,128)(2,1)S(1)}, bf16[64,896]{1,0:T(8,128)(2,1)S(1)}, u32[]{:S(2)}, u32[]{:S(2)}) collective-permute-start(bf16[64,896]{1,0:T(8,128)(2,1)S(1)} %get-tuple-element.110.refs_0_.refs_8_), channel_id=1, source_target_pairs={{0,1},{1,0},{2,3},{3,2},{4,5},{5,4},{6,7},{7,6},{8,9},{9,8},{10,11... | collective-permute-start | bytes 344072 | tf_op jit(solution)/shard_map/ppermute | solution.py:51
  83.3 4.9 %collective-permute-start.41 = (bf16[64,896]{1,0:T(8,128)(2,1)S(1)}, bf16[64,896]{1,0:T(8,128)(2,1)S(1)}, u32[]{:S(2)}, u32[]{:S(2)}) collective-permute-start(bf16[64,896]{1,0:T(8,128)(2,1)S(1)} %collective-permute-done.35.refs_2_), channel_id=1, source_target_pairs={{0,1},{1,0},{2,3},{3,2},{4,5},{5,4},{6,7},{7,6},{8,9},{9,8},{10,11... | collective-permute-start | bytes 344072 | tf_op jit(solution)/shard_map/ppermute | solution.py:51
  83.3 6.2 %collective-permute-start.42 = (bf16[64,896]{1,0:T(8,128)(2,1)S(1)}, bf16[64,896]{1,0:T(8,128)(2,1)S(1)}, u32[]{:S(2)}, u32[]{:S(2)}) collective-permute-start(bf16[64,896]{1,0:T(8,128)(2,1)S(1)} %collective-permute-done.36.refs_4_), channel_id=1, source_target_pairs={{0,1},{1,0},{2,3},{3,2},{4,5},{5,4},{6,7},{7,6},{8,9},{9,8},{10,11... | collective-permute-start | bytes 344072 | tf_op jit(solution)/shard_map/ppermute | solution.py:51
  83.8 5.7 %collective-permute-start.43 = (bf16[64,896]{1,0:T(8,128)(2,1)S(1)}, bf16[64,896]{1,0:T(8,128)(2,1)S(1)}, u32[]{:S(2)}, u32[]{:S(2)}) collective-permute-start(bf16[64,896]{1,0:T(8,128)(2,1)S(1)} %collective-permute-done.37.refs_6_), channel_id=1, source_target_pairs={{0,1},{1,0},{2,3},{3,2},{4,5},{5,4},{6,7},{7,6},{8,9},{9,8},{10,11... | collective-permute-start | bytes 344072 | tf_op jit(solution)/shard_map/ppermute | solution.py:51
  85.1 9.8 %collective-permute-start.48 = (bf16[64,640]{1,0:T(8,128)(2,1)S(1)}, bf16[64,640]{1,0:T(8,128)(2,1)S(1)}, u32[]{:S(2)}, u32[]{:S(2)}) collective-permute-start(bf16[64,640]{1,0:T(8,128)(2,1)S(1)} %get-tuple-element.125), channel_id=1, source_target_pairs={{0,2},{1,3},{2,0},{3,1},{4,6},{5,7},{6,4},{7,5},{8,10},{9,11},{10,... | collective-permute-start | bytes 245768 | tf_op jit(solution)/shard_map/ppermute | solution.py:51
  86.9 9.5 %collective-permute-start.49 = (bf16[64,640]{1,0:T(8,128)(2,1)S(1)}, bf16[64,640]{1,0:T(8,128)(2,1)S(1)}, u32[]{:S(2)}, u32[]{:S(2)}) collective-permute-start(bf16[64,640]{1,0:T(8,128)(2,1)S(1)} %get-tuple-element.126), channel_id=1, source_target_pairs={{0,4},{1,5},{2,6},{3,7},{4,0},{5,1},{6,2},{7,3},{8,12},{9,13},{10,... | collective-permute-start | bytes 245768 | tf_op jit(solution)/shard_map/ppermute | solution.py:51
  88.2 8.2 %collective-permute-start.50 = (bf16[64,640]{1,0:T(8,128)(2,1)S(1)}, bf16[64,640]{1,0:T(8,128)(2,1)S(1)}, u32[]{:S(2)}, u32[]{:S(2)}) collective-permute-start(bf16[64,640]{1,0:T(8,128)(2,1)S(1)} %get-tuple-element.127), channel_id=1, source_target_pairs={{0,6},{1,7},{2,4},{3,5},{4,2},{5,3},{6,0},{7,1},{8,14},{9,15},{10,... | collective-permute-start | bytes 245768 | tf_op jit(solution)/shard_map/ppermute | solution.py:51
  92.3 6.1 %collective-permute-start.44 = (bf16[64,1024]{1,0:T(8,128)(2,1)S(1)}, bf16[64,1024]{1,0:T(8,128)(2,1)S(1)}, u32[]{:S(2)}, u32[]{:S(2)}) collective-permute-start(bf16[64,1024]{1,0:T(8,128)(2,1)S(1)} %get-tuple-element.119), channel_id=1, source_target_pairs={{0,8},{8,0},{16,24},{24,16},{1,9},{9,1},{17,25},{25,17},{2,10},{10... | collective-permute-start | bytes 393224 | tf_op jit(solution)/shard_map/ppermute | solution.py:51
  93.4 7.8 %collective-permute-start.45 = (bf16[64,1024]{1,0:T(8,128)(2,1)S(1)}, bf16[64,1024]{1,0:T(8,128)(2,1)S(1)}, u32[]{:S(2)}, u32[]{:S(2)}) collective-permute-start(bf16[64,1024]{1,0:T(8,128)(2,1)S(1)} %get-tuple-element.120), channel_id=1, source_target_pairs={{0,16},{8,24},{16,0},{24,8},{1,17},{9,25},{17,1},{25,9},{2,18},{10... | collective-permute-start | bytes 393224 | tf_op jit(solution)/shard_map/ppermute | solution.py:51
  94.9 6.3 %collective-permute-start.46 = (bf16[64,1024]{1,0:T(8,128)(2,1)S(1)}, bf16[64,1024]{1,0:T(8,128)(2,1)S(1)}, u32[]{:S(2)}, u32[]{:S(2)}) collective-permute-start(bf16[64,1024]{1,0:T(8,128)(2,1)S(1)} %get-tuple-element.121), channel_id=1, source_target_pairs={{0,24},{8,16},{16,8},{24,0},{1,25},{9,17},{17,9},{25,1},{2,26},{10... | collective-permute-start | bytes 393224 | tf_op jit(solution)/shard_map/ppermute | solution.py:51
  101.4 10.7 %collective-permute-start.51 = (f32[64,64]{1,0:T(8,128)S(1)}, f32[64,64]{1,0:T(8,128)S(1)}, u32[]{:S(2)}, u32[]{:S(2)}) collective-permute-start(f32[64,64]{1,0:T(8,128)S(1)} %get-tuple-element.131), channel_id=1, source_target_pairs={{0,2},{1,3},{2,0},{3,1},{4,6},{5,7},{6,4},{7,5},{8,10},{9,11},{10,... | collective-permute-start | bytes 49160 | tf_op jit(solution)/shard_map/ppermute | solution.py:51
  102.3 9.7 %collective-permute-start.52 = (f32[64,64]{1,0:T(8,128)S(1)}, f32[64,64]{1,0:T(8,128)S(1)}, u32[]{:S(2)}, u32[]{:S(2)}) collective-permute-start(f32[64,64]{1,0:T(8,128)S(1)} %get-tuple-element.131), channel_id=1, source_target_pairs={{0,4},{1,5},{2,6},{3,7},{4,0},{5,1},{6,2},{7,3},{8,12},{9,13},{10,... | collective-permute-start | bytes 49160 | tf_op jit(solution)/shard_map/ppermute | solution.py:51
  104.4 7.7 %collective-permute-start.53 = (f32[64,64]{1,0:T(8,128)S(1)}, f32[64,64]{1,0:T(8,128)S(1)}, u32[]{:S(2)}, u32[]{:S(2)}) collective-permute-start(f32[64,64]{1,0:T(8,128)S(1)} %get-tuple-element.131), channel_id=1, source_target_pairs={{0,6},{1,7},{2,4},{3,5},{4,2},{5,3},{6,0},{7,1},{8,14},{9,15},{10,... | collective-permute-start | bytes 49160 | tf_op jit(solution)/shard_map/ppermute | solution.py:51
  112.1 1.3 %collective-permute-start.54 = (f32[64,64]{1,0:T(8,128)S(1)}, f32[64,64]{1,0:T(8,128)S(1)}, u32[]{:S(2)}, u32[]{:S(2)}) collective-permute-start(f32[64,64]{1,0:T(8,128)S(1)} %add_add_fusion.both_ref), channel_id=1, source_target_pairs={{0,1},{1,0},{2,3},{3,2},{4,5},{5,4},{6,7},{7,6},{8,9},{9,8},{10,11... | collective-permute-start | bytes 49160 | tf_op jit(solution)/shard_map/ppermute | solution.py:51
  (1 other events, 0.9 us)

commit v4 on v3

--- a/solution.py
+++ b/solution.py
@@ -12,7 +12,6 @@
 HIGHEST = lax.Precision.HIGHEST
 GRAM = 128
 PIECES = 2
-PANEL = 8
 UNROLL = 32
 
 vmem = pl.BlockSpec(memory_space=pltpu.VMEM)
@@ -51,18 +50,17 @@
     return lax.ppermute(value, axis, [(i, i ^ flip) for i in range(size)])
 
 
-def put_gram(ref, width, gram):
+def put_gram(ref, first, gram):
     columns = gram.shape[1]
     for k in range(PIECES):
         piece = gram.astype(jnp.bfloat16)
-        ref[:, width + k * columns : width + (k + 1) * columns] = piece
+        ref[:, first + k * columns : first + (k + 1) * columns] = piece
         gram = gram - piece.astype(jnp.float32)
 
 
-def get_gram(ref, width):
-    columns = (ref.shape[1] - width) // PIECES
+def get_gram(ref, first, columns):
     parts = [
-        ref[:, width + k * columns : width + (k + 1) * columns].astype(jnp.float32)
+        ref[:, first + k * columns : first + (k + 1) * columns].astype(jnp.float32)
         for k in range(PIECES)
     ]
     return functools.reduce(jnp.add, reversed(parts))
@@ -128,8 +126,8 @@
 
 
 def rows_kernel(table, tile_ref, *refs):
-    blocks, (send_ref, keep_ref, cells, total) = refs[:-4], refs[-4:]
-    chips, _, width = send_ref.shape
+    blocks, (send_ref, keep_ref, gram_ref, cells, total) = refs[:-5], refs[-5:]
+    chips, _, width = keep_ref.shape
     leaf = cells.shape[-1]
     per = width // leaf
     me, core = table[0], table[1] % 2
@@ -142,14 +140,17 @@
             part = slice(j * leaf, (j + 1) * leaf)
             send_ref[z, :, part] = total[(2 * z + 1 - core) * per + j].astype(jnp.bfloat16)
             keep_ref[z, :, part] = total[(2 * z + core) * per + j]
+    gram = functools.reduce(jnp.add, [get_gram(ref, width, GRAM) for ref in blocks])
+    gram_ref[...] = gram
+    send_ref[chips] = jnp.zeros(send_ref.shape[1:], send_ref.dtype)
+    put_gram(send_ref.at[chips], 0, gram)
 
 
 def cols_kernel(rows, cols, table, tile_ref, *refs):
-    blocks, refs = refs[:cols], refs[cols:]
-    outs, (cells, total) = refs[-rows - 3 : -2], refs[-2:]
-    last = refs[: -rows - 3]
-    own_ref, gram_ref, messages = outs[0], outs[1], outs[2:]
-    width = own_ref.shape[1]
+    blocks, refs, (cells, total) = refs[:cols], refs[cols:-2], refs[-2:]
+    last = refs[: rows + 2] if len(refs) > rows else ()
+    outs = refs[len(last) : len(last) + rows]
+    width = outs[0].shape[1]
     leaf = cells.shape[-1]
     per = width // leaf
     me = table[0]
@@ -157,9 +158,10 @@
         place(table[1] ^ flip, ref, cells, per)
     slots = tile_ref.shape[0]
     tile_sums(table, 2, 2 + slots, tile_ref, cells, total)
-    gram = get_gram(blocks[0], width)
-    for ref in blocks[1:]:
-        gram = gram + get_gram(ref, width)
+    for flip, out in enumerate(outs):
+        for j in range(per):
+            part = total[(me ^ flip) * per + j]
+            out[:, j * leaf : (j + 1) * leaf] = part.astype(out.dtype)
     if last:
         vector_ref, diagonal_ref = last[rows:]
         vector = vector_ref[...]
@@ -171,39 +173,48 @@
                 image = total[(me ^ flip) * per + j].astype(jnp.bfloat16)
                 half = half + contract(cluster, image, ((1,), (1,)))
         both = both + 2.0 * half
-        gram = jnp.concatenate([gram, both], axis=1)
-    gram_ref[...] = gram
+        refs[-1][...] = both
+        for out in outs[1:]:
+            put_gram(out, width, both)
+
+
+def pair_kernel(table, keep_ref, gram_ref, got_ref, own_ref, own_gram_ref, *messages):
+    chips, _, width = keep_ref.shape
+    chip = table[1] // 2
+    gram = gram_ref[...] + get_gram(got_ref.at[chips], 0, GRAM)
+    own_gram_ref[...] = gram
     for flip, out in enumerate((own_ref, *messages)):
-        for j in range(per):
-            part = total[(me ^ flip) * per + j]
-            out[:, j * leaf : (j + 1) * leaf] = part.astype(out.dtype)
+        z = chip ^ flip
+        out[:, :width] = (keep_ref[z] + got_ref[z].astype(jnp.float32)).astype(out.dtype)
     for out in messages:
         put_gram(out, width, gram)
 
 
-def pair_kernel(table, keep_ref, got_ref, *outs):
-    chip = table[1] // 2
-    for flip, out in enumerate(outs):
-        z = chip ^ flip
-        out[...] = (keep_ref[z] + got_ref[z].astype(jnp.float32)).astype(out.dtype)
-
-
-def chip_sums_kernel(own_ref, *refs):
-    total = own_ref[...]
-    for ref in refs[:-1]:
-        total = total + ref[...].astype(jnp.float32)
-    refs[-1][...] = total
-
-
-def first_kernel(vector_ref, diagonal_ref, message_ref):
+def chip_sums_kernel(own_ref, gram_ref, *refs):
+    messages, (out_ref, total_ref) = refs[:-2], refs[-2:]
+    width = own_ref.shape[1]
+    total, gram = own_ref[...], gram_ref[...]
+    for ref in messages:
+        total = total + ref[:, :width].astype(jnp.float32)
+        gram = gram + get_gram(ref, width, GRAM)
+    out_ref[...] = total
+    total_ref[...] = gram
+
+
+def put_vector(vector, gram, plain_ref, wide_ref):
+    rounded = vector.astype(jnp.bfloat16)
+    width = vector.shape[1]
+    plain_ref[...] = rounded
+    wide_ref[:, :width] = rounded
+    put_gram(wide_ref, width, gram)
+
+
+def first_kernel(vector_ref, diagonal_ref, plain_ref, wide_ref):
     vector = vector_ref[...]
-    width = vector.shape[1]
-    message_ref[:, :width] = vector.astype(jnp.bfloat16)
     gram = contract(vector, vector, ((1,), (1,)), HIGHEST)
     weighted = jnp.sum(vector * vector * diagonal_ref[...], axis=1, keepdims=True)
-    put_gram(
-        message_ref, width, jnp.concatenate([gram, jnp.broadcast_to(weighted, gram.shape)], axis=1)
-    )
+    gram = jnp.concatenate([gram, jnp.broadcast_to(weighted, gram.shape)], axis=1)
+    put_vector(vector, gram, plain_ref, wide_ref)
 
 
 def off_diagonal(refs):
@@ -214,62 +225,45 @@
     return total
 
 
-def sum_grams(own_ref, refs, width):
-    gram = own_ref[...]
-    for ref in refs:
-        gram = gram + get_gram(ref, width)
-    return gram
-
-
-def combine_kernel(rows, first, vector_ref, diagonal_ref, shift_ref, gram_ref, *refs):
-    sums, (next_ref, message_ref, total_ref) = refs[:-3], refs[-3:]
-    width = vector_ref.shape[1]
+def rayleigh(gram):
+    cases = gram.shape[0]
+    norm = jnp.sum(identity(cases) * gram[:, :cases], keepdims=True)
+    return jnp.sum(gram[:, cases : cases + 1], keepdims=True) / norm
+
+
+def shift_kernel(gram_ref, shift_ref):
+    shift_ref[...] = jnp.broadcast_to(rayleigh(gram_ref[...]), shift_ref.shape)
+
+
+def combine_kernel(first, vector_ref, diagonal_ref, shift_ref, *refs):
+    sums, (next_ref, plain_ref, wide_ref) = refs[:-3], refs[-3:]
     vector = vector_ref[...]
-    gram = sum_grams(gram_ref, sums[1 - rows :], width)
-    if first:
-        cases = gram.shape[0]
-        row = lax.broadcasted_iota(jnp.int32, (cases, cases), 0)
-        column = lax.broadcasted_iota(jnp.int32, (cases, cases), 1)
-        norm = jnp.sum(jnp.where(row == column, gram[:, :cases], 0.0), keepdims=True)
-        shift = jnp.sum(gram[:, cases : cases + 1], keepdims=True) / norm
-    else:
-        shift = shift_ref[0:1, 0:1]
-    total_ref[...] = gram
+    shift = rayleigh(shift_ref[...]) if first else shift_ref[0:1, 0:1]
     following = (diagonal_ref[...] - shift) * vector + off_diagonal(sums)
     next_ref[...] = following
-    message_ref[:, :width] = following.astype(jnp.bfloat16)
     cross = contract(vector, following, ((1,), (1,)), HIGHEST)
     square = contract(following, following, ((1,), (1,)), HIGHEST)
-    put_gram(message_ref, width, jnp.concatenate([cross, square], axis=1))
-
-
-def shift_kernel(gram_ref, shift_ref):
-    gram = gram_ref[...]
-    cases = gram.shape[0]
-    row = lax.broadcasted_iota(jnp.int32, (cases, cases), 0)
-    column = lax.broadcasted_iota(jnp.int32, (cases, cases), 1)
-    norm = jnp.sum(jnp.where(row == column, gram[:, :cases], 0.0), keepdims=True)
-    shift = jnp.sum(gram[:, cases : cases + 1], keepdims=True) / norm
-    shift_ref[...] = jnp.broadcast_to(shift, shift_ref.shape)
-
-
-def last_gram_kernel(gram_ref, *refs):
-    messages, (total_ref, both_ref) = refs[:-2], refs[-2:]
-    width = messages[0].shape[1] - PIECES * gram_ref.shape[1]
-    gram = sum_grams(gram_ref, messages, width)
-    total_ref[...] = gram[:, :GRAM]
-    both_ref[...] = gram[:, GRAM:]
-
-
-def solve(*pairs):
+    put_vector(following, jnp.concatenate([cross, square], axis=1), plain_ref, wide_ref)
+
+
+def last_gram_kernel(both_ref, *refs):
+    messages, total_ref = refs[:-1], refs[-1]
+    cases = both_ref.shape[0]
+    total = both_ref[...]
+    for ref in messages:
+        total = total + get_gram(ref, ref.shape[1] - PIECES * cases, cases)
+    total_ref[...] = total
+
+
+def solve(*pairs, panel=8):
     size = pairs[0][0].shape[0]
     works = [jnp.concatenate(pair, axis=1) for pair in pairs]
     shape = works[0].shape
     row = lax.broadcasted_iota(jnp.int32, shape, 0)
-    for start in range(0, size, PANEL):
-        panel = range(start, start + PANEL)
-        spread = [[jnp.broadcast_to(w[:, k : k + 1], shape) for k in panel] for w in works]
-        for k in panel:
+    for start in range(0, size, panel):
+        pivots = range(start, start + panel)
+        spread = [[jnp.broadcast_to(w[:, k : k + 1], shape) for k in pivots] for w in works]
+        for k in pivots:
             for n, columns in enumerate(spread):
                 pivot = columns[0]
                 inverse = 1.0 / pivot[k : k + 1, :]
@@ -306,35 +300,62 @@
     out_ref[...] = jnp.concatenate([alpha0, rr1, r_b, d_b], axis=1)
 
 
-def second_coefficients_kernel(
-    shift_ref, gram0_ref, gram1_ref, gram2_ref, first_ref, big_ref, small_ref
-):
+def stack(*parts):
+    return jnp.concatenate(parts, axis=0)
+
+
+def side(*parts):
+    return jnp.concatenate(parts, axis=1)
+
+
+def basis_gram(gram0_ref, gram1_ref, gram2_ref):
     cases = gram0_ref.shape[0]
-    shift = shift_ref[0:1, 0:1]
     bb = gram0_ref[:, :cases]
     bu, uu = gram1_ref[:, :cases], gram1_ref[:, cases:]
     uv, vv = gram2_ref[:, :cases], gram2_ref[:, cases:]
-    bv = uu
-    alpha0, rr1, r_b, d_b = [first_ref[:, k * cases : (k + 1) * cases] for k in range(4)]
-    zero = jnp.zeros_like(bb)
-    stack = functools.partial(jnp.concatenate, axis=0)
-    side = functools.partial(jnp.concatenate, axis=1)
-    gram = stack([side([bb, bu, bv]), side([bu.T, uu, uv]), side([bv, uv.T, vv])])
-    r1 = stack([r_b, -alpha0, zero])
-    d1 = stack([d_b, -alpha0, zero])
-    s1 = stack([shift * d_b, d_b - shift * alpha0, -alpha0])
+    return stack(side(bb, bu, uu), side(bu.T, uu, uv), side(uu, uv.T, vv))
+
+
+def directions(shift_ref, first_ref):
+    cases = first_ref.shape[0]
+    shift = shift_ref[0:1, 0:1]
+    alpha0, _, r_b, d_b = [first_ref[:, k * cases : (k + 1) * cases] for k in range(4)]
+    zero = jnp.zeros_like(alpha0)
+    r1 = stack(r_b, -alpha0, zero)
+    d1 = stack(d_b, -alpha0, zero)
+    return r1, d1, stack(shift * d_b, d_b - shift * alpha0, -alpha0)
+
+
+def second_solve_kernel(shift_ref, gram0_ref, gram1_ref, gram2_ref, first_ref, out_ref):
+    cases = first_ref.shape[0]
+    gram = basis_gram(gram0_ref, gram1_ref, gram2_ref)
+    rr1 = first_ref[:, cases : 2 * cases]
+    _, d1, s1 = directions(shift_ref, first_ref)
     curvature1 = symmetric(mul_t(d1, mul(gram, s1)))
-    alpha1, inverse = solve((curvature1, rr1), (rr1, identity(cases)))
+    out_ref[...] = side(*solve((curvature1, rr1), (rr1, identity(cases))))
+
+
+def second_coefficients_kernel(
+    shift_ref, gram0_ref, gram1_ref, gram2_ref, first_ref, solve_ref, big_ref, small_ref
+):
+    cases = first_ref.shape[0]
+    shift = shift_ref[0:1, 0:1]
+    gram = basis_gram(gram0_ref, gram1_ref, gram2_ref)
+    r1, d1, s1 = directions(shift_ref, first_ref)
+    alpha1, inverse = solve_ref[:, :cases], solve_ref[:, cases:]
+    uu = gram1_ref[:, cases:]
+    uv, vv = gram2_ref[:, :cases], gram2_ref[:, cases:]
     r2 = r1 - mul(s1, alpha1)
     rr2 = symmetric(mul_t(r2, mul(gram, r2)))
     d2 = r2 + mul(d1, mul(inverse, rr2))
     d2_b, d2_u, d2_v = d2[:cases], d2[cases : 2 * cases], d2[2 * cases :]
-    s2 = stack([shift * d2_b, d2_b + shift * d2_u, d2_u])
-    with_y = mul_t(d2_b, uv + shift * bv) + mul_t(d2_u, vv + shift * uv)
+    s2 = stack(shift * d2_b, d2_b + shift * d2_u, d2_u)
+    with_y = mul_t(d2_b, uv + shift * uu) + mul_t(d2_u, vv + shift * uv)
     curvature2 = mul_t(d2, mul(gram, s2)) + mul(with_y, d2_v)
-    x2 = stack([alpha0, zero, zero]) + mul(d1, alpha1)
-    small_ref[...] = side([curvature2, rr2, d2_v, zero])
-    big_ref[...] = side([d2, r2, s2, x2])
+    zero = jnp.zeros_like(uu)
+    x2 = stack(first_ref[:, :cases], zero, zero) + mul(d1, alpha1)
+    small_ref[...] = side(curvature2, rr2, d2_v, zero)
+    big_ref[...] = side(d2, r2, s2, x2)
 
 
 def vectors_kernel(big_ref, b_ref, u_ref, v_ref, vectors_ref):
@@ -348,7 +369,8 @@
     d2, r2, s2, x2 = [vectors_ref[k * cases : (k + 1) * cases, :] for k in range(4)]
     curvature2, rr2, d2_v = [small_ref[:, k * cases : (k + 1) * cases] for k in range(3)]
     both = symmetric(both_ref[...] + other_ref[...])
-    (alpha2,) = solve((symmetric(curvature2 + mul_t(d2_v, mul(both, d2_v))), rr2))
+    curvature2 = symmetric(curvature2 + mul_t(d2_v, mul(both, d2_v)))
+    (alpha2,) = solve((curvature2, rr2), panel=16)
     y = diagonal_ref[...] * v_ref[...] + off_diagonal(sums)
     s2 = s2 + mul_t(d2_v, y)
     solution_ref[...] = x2 + mul_t(alpha2, d2)
@@ -419,91 +441,103 @@
         ],
     )
 
-    def apply(message, last=(), beside=()):
-        over_row = [partner_permute(message, "row", k) for k in range(1, rows)]
-        over_chip = [partner_permute(message, "col", 2 * k) for k in range(1, chips)]
-        send, keep = call(
+    def apply(plain, wide, last=(), beside=()):
+        over_row = [partner_permute(wide, "row", k) for k in range(1, rows)]
+        over_chip, flip = [], 1
+        while flip < chips:
+            over_chip += [partner_permute(m, "col", 2 * flip) for m in [plain, *over_chip]]
+            flip *= 2
+        send, keep, gram = call(
             rows_kernel,
             "rows_half",
-            [bf16(chips, cases, width), f32(chips, cases, width)],
+            [bf16(chips + 1, cases, width), f32(chips, cases, width), f32(cases, GRAM)],
             table,
             turned,
-            message,
+            wide,
             *over_row,
             scalars=(0,),
             scratch=[
                 pltpu.VMEM((rows * per, cases, leaf), jnp.bfloat16),
                 pltpu.VMEM((cols * per, cases, leaf), jnp.float32),
             ],
-            cost=0,
         )
         over_chip, beside, send, keep = lax.optimization_barrier((over_chip, beside, send, keep))
         got = partner_permute(send, "col", 1)
-        own_chip, *row_messages = call(
+        own_chip, gram, *row_messages = call(
             pair_kernel,
             "pair_sums",
-            [f32(cases, width)] + [bf16(cases, width)] * (chips - 1),
+            [f32(cases, width), f32(cases, GRAM)] + [bf16(cases, long)] * (chips - 1),
             table,
             keep,
+            gram,
             got,
             scalars=(0,),
         )
         from_chips = [partner_permute(m, "col", 2 * k) for k, m in enumerate(row_messages, 1)]
-        other_core = [partner_permute(v, "col", 1) for v in [message] + over_chip]
-        own_row = call(
-            chip_sums_kernel, "chip_sums", f32(cases, width), own_chip, *from_chips, cost=1
+        other_core = [partner_permute(v, "col", 1) for v in [plain] + over_chip]
+        own_row, gram = call(
+            chip_sums_kernel,
+            "chip_sums",
+            [f32(cases, width), f32(cases, GRAM)],
+            own_chip,
+            gram,
+            *from_chips,
+            cost=1,
         )
         row_group = [None] * cols
-        for k, (a, b) in enumerate(zip([message] + over_chip, other_core)):
+        for k, (a, b) in enumerate(zip([plain] + over_chip, other_core)):
             row_group[2 * k], row_group[2 * k + 1] = a, b
-        wide = GRAM + cases if last else GRAM
-        extra = [message, *over_row, *last] if last else []
-        own_col, gram, *col_messages = call(
+        behind = PIECES * cases if last else 0
+        own_col, *outs = call(
             functools.partial(cols_kernel, rows, cols),
             "cols_half",
-            [f32(cases, width), f32(cases, wide)]
-            + [bf16(cases, width + PIECES * wide)] * (rows - 1),
+            [f32(cases, width)]
+            + [bf16(cases, width + behind)] * (rows - 1)
+            + [f32(cases, cases)] * bool(last),
             table,
             tiles,
             *row_group,
-            *extra,
+            *([wide, *over_row, *last] if last else []),
             scalars=(0,),
             scratch=[
                 pltpu.VMEM((cols * per, cases, leaf), jnp.bfloat16),
                 pltpu.VMEM((rows * per, cases, leaf), jnp.float32),
             ],
-            cost=0,
-        )
-        from_rows = [partner_permute(m, "row", k) for k, m in enumerate(col_messages, 1)]
-        if last:
-            from_rows, _ = lax.optimization_barrier((from_rows, own_row))
-        return [own_row, own_col, *from_rows], from_rows, gram, beside
-
-    def advance(first, vector, shift, parts):
-        sums, from_rows, gram, _ = parts
+        )
+        from_rows = [partner_permute(m, "row", k) for k, m in enumerate(outs[: rows - 1], 1)]
+        if not last:
+            return [own_row, own_col, *from_rows], gram
+        solved = call(
+            second_solve_kernel, "solve", f32(cases, 2 * cases), shift, gram0, gram1, gram, beside
+        )
+        from_rows, solved = lax.optimization_barrier((from_rows, solved))
+        both = call(last_gram_kernel, "last_gram", f32(cases, cases), outs[-1], *from_rows)
+        return [own_row, own_col, *from_rows], gram, both, beside, solved
+
+    def advance(first, vector, shift, sums):
         return call(
-            functools.partial(combine_kernel, rows, first),
+            functools.partial(combine_kernel, first),
             "combine",
-            [f32(cases, width), bf16(cases, long), f32(cases, GRAM)],
+            [f32(cases, width), bf16(cases, width), bf16(cases, long)],
             vector,
             diagonal,
             shift,
-            gram,
             *sums,
         )
 
     b = right_side
-    message = call(first_kernel, "first_message", bf16(cases, long), b, diagonal, cost=10)
-    u, message, gram0 = advance(True, b, diagonal, apply(message))
+    plain, wide = call(
+        first_kernel, "first_message", [bf16(cases, width), bf16(cases, long)], b, diagonal, cost=10
+    )
+    sums, gram0 = apply(plain, wide)
+    u, plain, wide = advance(True, b, gram0, sums)
     shift = call(shift_kernel, "shift", f32(8, 128), gram0)
-    v, message, gram1 = advance(False, u, shift, apply(message))
+    sums, gram1 = apply(plain, wide)
+    v, plain, wide = advance(False, u, shift, sums)
     first = call(
         first_coefficients_kernel, "coefficients", f32(cases, 4 * cases), shift, gram0, gram1
     )
-    sums, from_rows, gram, first = apply(message, last=(v, diagonal), beside=first)
-    gram2, both = call(
-        last_gram_kernel, "last_gram", [f32(cases, GRAM), f32(cases, cases)], gram, *from_rows
-    )
+    sums, gram2, both, first, solved = apply(plain, wide, last=(v, diagonal), beside=first)
     over_chip = [partner_permute(both, "col", 2 * k) for k in range(1, chips)]
     big, small = call(
         second_coefficients_kernel,
@@ -514,6 +548,7 @@
         gram1,
         gram2,
         first,
+        solved,
     )
     over_chip, big = lax.optimization_barrier((over_chip, big))
     both = functools.reduce(jnp.add, over_chip, both)

time: 117 us -> 114 us (0.974)
  starting transfers between devices: 57.5 us -> 54.3 us
    ppermute x55, starting transfers between devices: 57.5 us -> 54.3 us  [partner_permute(): return lax.ppermute(value, axis, [(i, i ^ flip) for i in range(size)])]
    pallas_call x22 -> x23, Pallas kernels: 34.2 us -> 33.6 us  [call(): pl.pallas_call(kernel, out_shape=outs, in_specs=[spaces.get(k, vmem) for...]
  transfers between devices with their start and end apart: 55 -> 55, of which waited for: 17 -> 25; matrix products, arithmetic and copies ran while one was open for 0% -> 0% of each run, Pallas kernels for 25% -> 25%
where the time goes in v4:
time: 114 us
  starting transfers between devices  54.3 us (48%)
  Pallas kernels  33.6 us (29%)
  waiting for transfers between devices  22.5 us (20%)
  local copies, waits for them, and re-layouts  1.73 us (2%)
  between operations  1.68 us (1%)
    ppermute x55, starting transfers between devices, partner_permute(): return lax.ppermute(value, axis, [(i, i ^ flip) for i in range(size)])  54.3 us
    pallas_call x23, Pallas kernels, call(): pl.pallas_call(kernel, out_shape=outs, in_specs=[spaces.get(k, vmem) for...  33.6 us
    ppermute x55, waiting for transfers between devices, partner_permute(): return lax.ppermute(value, axis, [(i, i ^ flip) for i in range(size)])  22.5 us
  transfers between devices with their start and end apart: 55, of which 25 were waited for; matrix products, arithmetic and copies ran while one was open for 0% of the time, Pallas kernels for 25%

profile of v4, /device:TPU:0, one launch (start us, length us, event | category | flops | bytes accessed | tf_op | source)
XLA Modules:
  0.0 113.8 jit_solution(13856098303060099041)
XLA Ops:
  0.6 0.7 broadcast_in_dim.3.diagonal_ref.refs_13_
  1.3 0.9 copy-done.1
  2.6 3.1 %collective-permute-start = (bf16[64,640]{1,0:T(8,128)(2,1)S(1)}, bf16[64,640]{1,0:T(8,128)(2,1)S(1)}, u32[]{:S(2)}, u32[]{:S(2)}) collective-permute-start(bf16[64,640]{1,0:T(8,128)(2,1)S(1)} %get-tuple-element.85.refs_0_), channel_id=1, source_target_pairs={{0,2},{1,3},{2,0},{3,1},{4,6},{5,7},{6,4},{7,5},{8,10},{9,11},{10,... | collective-permute-start | bytes 245768 | tf_op jit(solution)/shard_map/ppermute | solution.py:50
  5.7 1.5 %collective-permute-start.3 = (bf16[64,896]{1,0:T(8,128)(2,1)S(1)}, bf16[64,896]{1,0:T(8,128)(2,1)S(1)}, u32[]{:S(2)}, u32[]{:S(2)}) collective-permute-start(bf16[64,896]{1,0:T(8,128)(2,1)S(1)} %get-tuple-element.87.refs_0_), channel_id=1, source_target_pairs={{0,8},{8,0},{16,24},{24,16},{1,9},{9,1},{17,25},{25,17},{2,10},{10... | collective-permute-start | bytes 344072 | tf_op jit(solution)/shard_map/ppermute | solution.py:50
  7.2 1.5 %collective-permute-start.4 = (bf16[64,896]{1,0:T(8,128)(2,1)S(1)}, bf16[64,896]{1,0:T(8,128)(2,1)S(1)}, u32[]{:S(2)}, u32[]{:S(2)}) collective-permute-start(bf16[64,896]{1,0:T(8,128)(2,1)S(1)} %get-tuple-element.87.refs_0_), channel_id=1, source_target_pairs={{0,16},{8,24},{16,0},{24,8},{1,17},{9,25},{17,1},{25,9},{2,18},{10... | collective-permute-start | bytes 344072 | tf_op jit(solution)/shard_map/ppermute | solution.py:50
  9.2 2.6 %collective-permute-start.1 = (bf16[64,640]{1,0:T(8,128)(2,1)S(1)}, bf16[64,640]{1,0:T(8,128)(2,1)S(1)}, u32[]{:S(2)}, u32[]{:S(2)}) collective-permute-start(bf16[64,640]{1,0:T(8,128)(2,1)S(1)} %get-tuple-element.85.refs_0_), channel_id=1, source_target_pairs={{0,4},{1,5},{2,6},{3,7},{4,0},{5,1},{6,2},{7,3},{8,12},{9,13},{10,... | collective-permute-start | bytes 245768 | tf_op jit(solution)/shard_map/ppermute | solution.py:50
  12.9 3.3 %dense_tiles.1 = (bf16[96,128,128]{2,1,0:T(8,128)(2,1)S(1)}, bf16[96,128,128]{2,1,0:T(8,128)(2,1)S(1)}) custom-call(s32[259]{0:T(512)S(1)} %concatenate.3.table, bf16[32,128,128]{2,1,0:T(8,128)(2,1)S(1)} %bitcast.12, bf16[64,32,128]{2,1,0:T(8,128)(2,1)S(1)} %bitcast.13, bf16[64,32,128]{2,1,0:T(8,128)(2,1)S(1)} %bitcast.14), custom_call_target="tpu_custom_call" | custom-call | tf_op jit(solution)/shard_map/dense_tiles/pallas_call | solution.py:382
  16.2 2.1 %rows_half.3 = (bf16[5,64,640]{2,1,0:T(8,128)(2,1)S(1)}, f32[4,64,640]{2,1,0:T(8,128)S(1)}, f32[64,128]{1,0:T(8,128)S(1)}) custom-call(s32[259]{0:T(512)S(1)} %concatenate.3.table, bf16[96,128,128]{2,1,0:T(8,128)(2,1)S(1)} %get-tuple-element.86.tile_ref, bf16[64,896]{1,0:T(8,128)(2,1)S(1)} %get-tuple-element.87.refs_0_, ...), custom_call_target="tpu_custom_call" | custom-call | tf_op jit(solution)/shard_map/rows_half/pallas_call | solution.py:382
  19.0 1.2 %collective-permute-done.6.got_ref = bf16[5,64,640]{2,1,0:T(8,128)(2,1)S(1)} collective-permute-done((bf16[5,64,640]{2,1,0:T(8,128)(2,1)S(1)}, bf16[5,64,640]{2,1,0:T(8,128)(2,1)S(1)}, u32[]{:S(2)}, u32[]{:S(2)}) %collective-permute-start.6) | collective-permute-done | bytes 409632 | tf_op jit(solution)/shard_map/ppermute | solution.py:50
  20.2 0.6 pair_sums.3
  20.9 0.6 collective-permute-start.7
  21.5 2.4 %collective-permute-start.8 = (bf16[64,896]{1,0:T(8,128)(2,1)S(1)}, bf16[64,896]{1,0:T(8,128)(2,1)S(1)}, u32[]{:S(2)}, u32[]{:S(2)}) collective-permute-start(bf16[64,896]{1,0:T(8,128)(2,1)S(1)} %get-tuple-element.96), channel_id=1, source_target_pairs={{0,4},{1,5},{2,6},{3,7},{4,0},{5,1},{6,2},{7,3},{8,12},{9,13},{10,... | collective-permute-start | bytes 344072 | tf_op jit(solution)/shard_map/ppermute | solution.py:50
  23.9 1.4 %collective-permute-start.9 = (bf16[64,896]{1,0:T(8,128)(2,1)S(1)}, bf16[64,896]{1,0:T(8,128)(2,1)S(1)}, u32[]{:S(2)}, u32[]{:S(2)}) collective-permute-start(bf16[64,896]{1,0:T(8,128)(2,1)S(1)} %get-tuple-element.97), channel_id=1, source_target_pairs={{0,6},{1,7},{2,4},{3,5},{4,2},{5,3},{6,0},{7,1},{8,14},{9,15},{10,... | collective-permute-start | bytes 344072 | tf_op jit(solution)/shard_map/ppermute | solution.py:50
  25.8 0.8 collective-permute-done.12.refs_5_
  26.8 2.0 %cols_half.3 = (f32[64,640]{1,0:T(8,128)S(1)}, bf16[64,640]{1,0:T(8,128)(2,1)S(1)}, bf16[64,640]{1,0:T(8,128)(2,1)S(1)}, bf16[64,640]{1,0:T(8,128)(2,1)S(1)}) custom-call(s32[259]{0:T(512)S(1)} %concatenate.3.table, bf16[96,128,128]{2,1,0:T(8,128)(2,1)S(1)} %get-tuple-element.84.tile_ref, bf16[64,640]{1,0:T(8,128)(2,1)S(1)} %get-tuple-element.85.refs_0_, ...), custom_call_target="tpu_custom_call" | custom-call | tf_op jit(solution)/shard_map/cols_half/pallas_call | solution.py:382
  28.8 1.9 %collective-permute-start.14 = (bf16[64,640]{1,0:T(8,128)(2,1)S(1)}, bf16[64,640]{1,0:T(8,128)(2,1)S(1)}, u32[]{:S(2)}, u32[]{:S(2)}) collective-permute-start(bf16[64,640]{1,0:T(8,128)(2,1)S(1)} %get-tuple-element.104), channel_id=1, source_target_pairs={{0,8},{8,0},{16,24},{24,16},{1,9},{9,1},{17,25},{25,17},{2,10},{10... | collective-permute-start | bytes 245768 | tf_op jit(solution)/shard_map/ppermute | solution.py:50
  30.7 1.5 %collective-permute-start.15 = (bf16[64,640]{1,0:T(8,128)(2,1)S(1)}, bf16[64,640]{1,0:T(8,128)(2,1)S(1)}, u32[]{:S(2)}, u32[]{:S(2)}) collective-permute-start(bf16[64,640]{1,0:T(8,128)(2,1)S(1)} %get-tuple-element.105), channel_id=1, source_target_pairs={{0,16},{8,24},{16,0},{24,8},{1,17},{9,25},{17,1},{25,9},{2,18},{10... | collective-permute-start | bytes 245768 | tf_op jit(solution)/shard_map/ppermute | solution.py:50
  32.4 0.7 collective-permute-done.9.refs_2_
  33.7 2.3 %collective-permute-done.15.refs_3_ = bf16[64,640]{1,0:T(8,128)(2,1)S(1)} collective-permute-done((bf16[64,640]{1,0:T(8,128)(2,1)S(1)}, bf16[64,640]{1,0:T(8,128)(2,1)S(1)}, u32[]{:S(2)}, u32[]{:S(2)}) %collective-permute-start.15) | collective-permute-done | bytes 81952 | tf_op jit(solution)/shard_map/ppermute | solution.py:50
  36.0 1.6 %collective-permute-done.16.refs_4_ = bf16[64,640]{1,0:T(8,128)(2,1)S(1)} collective-permute-done((bf16[64,640]{1,0:T(8,128)(2,1)S(1)}, bf16[64,640]{1,0:T(8,128)(2,1)S(1)}, u32[]{:S(2)}, u32[]{:S(2)}) %collective-permute-start.16) | collective-permute-done | bytes 81952 | tf_op jit(solution)/shard_map/ppermute | solution.py:50
  37.6 0.7 combine.2
  38.4 0.6 collective-permute-start.20
  39.0 0.8 collective-permute-start.21
  39.8 2.1 %collective-permute-start.22 = (bf16[64,896]{1,0:T(8,128)(2,1)S(1)}, bf16[64,896]{1,0:T(8,128)(2,1)S(1)}, u32[]{:S(2)}, u32[]{:S(2)}) collective-permute-start(bf16[64,896]{1,0:T(8,128)(2,1)S(1)} %get-tuple-element.109.refs_0_), channel_id=1, source_target_pairs={{0,24},{8,16},{16,8},{24,0},{1,25},{9,17},{17,9},{25,1},{2,26},{10... | collective-permute-start | bytes 344072 | tf_op jit(solution)/shard_map/ppermute | solution.py:50
  42.0 2.6 %collective-permute-start.18 = (bf16[64,640]{1,0:T(8,128)(2,1)S(1)}, bf16[64,640]{1,0:T(8,128)(2,1)S(1)}, u32[]{:S(2)}, u32[]{:S(2)}) collective-permute-start(bf16[64,640]{1,0:T(8,128)(2,1)S(1)} %get-tuple-element.108.refs_0_), channel_id=1, source_target_pairs={{0,4},{1,5},{2,6},{3,7},{4,0},{5,1},{6,2},{7,3},{8,12},{9,13},{10,... | collective-permute-start | bytes 245768 | tf_op jit(solution)/shard_map/ppermute | solution.py:50
  44.9 0.9 collective-permute-done.21.refs_2_
  45.8 2.1 %rows_half.4 = (bf16[5,64,640]{2,1,0:T(8,128)(2,1)S(1)}, f32[4,64,640]{2,1,0:T(8,128)S(1)}, f32[64,128]{1,0:T(8,128)S(1)}) custom-call(s32[259]{0:T(512)S(1)} %concatenate.3.table, bf16[96,128,128]{2,1,0:T(8,128)(2,1)S(1)} %get-tuple-element.86.tile_ref, bf16[64,896]{1,0:T(8,128)(2,1)S(1)} %get-tuple-element.109.refs_0_, ...), custom_call_target="tpu_custom_call" | custom-call | tf_op jit(solution)/shard_map/rows_half/pallas_call | solution.py:382
  47.9 2.8 %collective-permute-done.19.refs_6_ = bf16[64,640]{1,0:T(8,128)(2,1)S(1)} collective-permute-done((bf16[64,640]{1,0:T(8,128)(2,1)S(1)}, bf16[64,640]{1,0:T(8,128)(2,1)S(1)}, u32[]{:S(2)}, u32[]{:S(2)}) %collective-permute-start.19) | collective-permute-done | bytes 81952 | tf_op jit(solution)/shard_map/ppermute | solution.py:50
  51.3 1.2 %collective-permute-done.23.got_ref = bf16[5,64,640]{2,1,0:T(8,128)(2,1)S(1)} collective-permute-done((bf16[5,64,640]{2,1,0:T(8,128)(2,1)S(1)}, bf16[5,64,640]{2,1,0:T(8,128)(2,1)S(1)}, u32[]{:S(2)}, u32[]{:S(2)}) %collective-permute-start.23) | collective-permute-done | bytes 409632 | tf_op jit(solution)/shard_map/ppermute | solution.py:50
  52.5 0.6 pair_sums.4
  53.2 2.5 %collective-permute-start.25 = (bf16[64,896]{1,0:T(8,128)(2,1)S(1)}, bf16[64,896]{1,0:T(8,128)(2,1)S(1)}, u32[]{:S(2)}, u32[]{:S(2)}) collective-permute-start(bf16[64,896]{1,0:T(8,128)(2,1)S(1)} %get-tuple-element.118), channel_id=1, source_target_pairs={{0,4},{1,5},{2,6},{3,7},{4,0},{5,1},{6,2},{7,3},{8,12},{9,13},{10,... | collective-permute-start | bytes 344072 | tf_op jit(solution)/shard_map/ppermute | solution.py:50
  55.7 1.9 %collective-permute-start.26 = (bf16[64,896]{1,0:T(8,128)(2,1)S(1)}, bf16[64,896]{1,0:T(8,128)(2,1)S(1)}, u32[]{:S(2)}, u32[]{:S(2)}) collective-permute-start(bf16[64,896]{1,0:T(8,128)(2,1)S(1)} %get-tuple-element.119), channel_id=1, source_target_pairs={{0,6},{1,7},{2,4},{3,5},{4,2},{5,3},{6,0},{7,1},{8,14},{9,15},{10,... | collective-permute-start | bytes 344072 | tf_op jit(solution)/shard_map/ppermute | solution.py:50
  59.0 2.0 %cols_half.4 = (f32[64,640]{1,0:T(8,128)S(1)}, bf16[64,640]{1,0:T(8,128)(2,1)S(1)}, bf16[64,640]{1,0:T(8,128)(2,1)S(1)}, bf16[64,640]{1,0:T(8,128)(2,1)S(1)}) custom-call(s32[259]{0:T(512)S(1)} %concatenate.3.table, bf16[96,128,128]{2,1,0:T(8,128)(2,1)S(1)} %get-tuple-element.84.tile_ref, bf16[64,640]{1,0:T(8,128)(2,1)S(1)} %get-tuple-element.108.refs_0_, ...), custom_call_target="tpu_custom_call" | custom-call | tf_op jit(solution)/shard_map/cols_half/pallas_call | solution.py:382
  61.1 0.7 collective-permute-start.31
  61.8 1.1 collective-permute-start.32
  62.9 1.8 %collective-permute-start.33 = (bf16[64,640]{1,0:T(8,128)(2,1)S(1)}, bf16[64,640]{1,0:T(8,128)(2,1)S(1)}, u32[]{:S(2)}, u32[]{:S(2)}) collective-permute-start(bf16[64,640]{1,0:T(8,128)(2,1)S(1)} %get-tuple-element.127), channel_id=1, source_target_pairs={{0,24},{8,16},{16,8},{24,0},{1,25},{9,17},{17,9},{25,1},{2,26},{10... | collective-permute-start | bytes 245768 | tf_op jit(solution)/shard_map/ppermute | solution.py:50
  65.2 0.9 collective-permute-done.31.refs_2_
  66.2 2.0 %collective-permute-done.33.refs_4_ = bf16[64,640]{1,0:T(8,128)(2,1)S(1)} collective-permute-done((bf16[64,640]{1,0:T(8,128)(2,1)S(1)}, bf16[64,640]{1,0:T(8,128)(2,1)S(1)}, u32[]{:S(2)}, u32[]{:S(2)}) %collective-permute-start.33) | collective-permute-done | bytes 81952 | tf_op jit(solution)/shard_map/ppermute | solution.py:50
  68.2 0.6 combine.3
  68.9 1.2 %collective-permute-start.38 = (bf16[64,896]{1,0:T(8,128)(2,1)S(1)}, bf16[64,896]{1,0:T(8,128)(2,1)S(1)}, u32[]{:S(2)}, u32[]{:S(2)}) collective-permute-start(bf16[64,896]{1,0:T(8,128)(2,1)S(1)} %get-tuple-element.130.refs_0_.refs_8_), channel_id=1, source_target_pairs={{0,8},{8,0},{16,24},{24,16},{1,9},{9,1},{17,25},{25,17},{2,10},{10... | collective-permute-start | bytes 344072 | tf_op jit(solution)/shard_map/ppermute | solution.py:50
  70.1 1.2 %collective-permute-start.39 = (bf16[64,896]{1,0:T(8,128)(2,1)S(1)}, bf16[64,896]{1,0:T(8,128)(2,1)S(1)}, u32[]{:S(2)}, u32[]{:S(2)}) collective-permute-start(bf16[64,896]{1,0:T(8,128)(2,1)S(1)} %get-tuple-element.130.refs_0_.refs_8_), channel_id=1, source_target_pairs={{0,16},{8,24},{16,0},{24,8},{1,17},{9,25},{17,1},{25,9},{2,18},{10... | collective-permute-start | bytes 344072 | tf_op jit(solution)/shard_map/ppermute | solution.py:50
  71.3 1.2 %collective-permute-start.40 = (bf16[64,896]{1,0:T(8,128)(2,1)S(1)}, bf16[64,896]{1,0:T(8,128)(2,1)S(1)}, u32[]{:S(2)}, u32[]{:S(2)}) collective-permute-start(bf16[64,896]{1,0:T(8,128)(2,1)S(1)} %get-tuple-element.130.refs_0_.refs_8_), channel_id=1, source_target_pairs={{0,24},{8,16},{16,8},{24,0},{1,25},{9,17},{17,9},{25,1},{2,26},{10... | collective-permute-start | bytes 344072 | tf_op jit(solution)/shard_map/ppermute | solution.py:50
  72.5 3.0 %collective-permute-start.36 = (bf16[64,640]{1,0:T(8,128)(2,1)S(1)}, bf16[64,640]{1,0:T(8,128)(2,1)S(1)}, u32[]{:S(2)}, u32[]{:S(2)}) collective-permute-start(bf16[64,640]{1,0:T(8,128)(2,1)S(1)} %get-tuple-element.128.refs_0_), channel_id=1, source_target_pairs={{0,4},{1,5},{2,6},{3,7},{4,0},{5,1},{6,2},{7,3},{8,12},{9,13},{10,... | collective-permute-start | bytes 245768 | tf_op jit(solution)/shard_map/ppermute | solution.py:50
  75.4 3.1 %coefficients.2.first_ref = f32[64,256]{1,0:T(8,128)S(1)} custom-call(f32[8,128]{1,0:T(8,128)S(1)} %shift.1.shift_ref, f32[64,128]{1,0:T(8,128)S(1)} %get-tuple-element.98.shift_ref.gram_ref.gram0_ref, f32[64,128]{1,0:T(8,128)S(1)} %get-tuple-element.129.gram1_ref), custom_call_target="tpu_custom_call" | custom-call | tf_op jit(solution)/shard_map/coefficients/pallas_call | solution.py:382
  78.6 2.1 %rows_half.5 = (bf16[5,64,640]{2,1,0:T(8,128)(2,1)S(1)}, f32[4,64,640]{2,1,0:T(8,128)S(1)}, f32[64,128]{1,0:T(8,128)S(1)}) custom-call(s32[259]{0:T(512)S(1)} %concatenate.3.table, bf16[96,128,128]{2,1,0:T(8,128)(2,1)S(1)} %get-tuple-element.86.tile_ref, bf16[64,896]{1,0:T(8,128)(2,1)S(1)} %get-tuple-element.130.refs_0_.refs_8_, ...), custom_call_target="tpu_custom_call" | custom-call | tf_op jit(solution)/shard_map/rows_half/pallas_call | solution.py:382
  81.7 1.2 %collective-permute-done.47.got_ref = bf16[5,64,640]{2,1,0:T(8,128)(2,1)S(1)} collective-permute-done((bf16[5,64,640]{2,1,0:T(8,128)(2,1)S(1)}, bf16[5,64,640]{2,1,0:T(8,128)(2,1)S(1)}, u32[]{:S(2)}, u32[]{:S(2)}) %collective-permute-start.47) | collective-permute-done | bytes 409632 | tf_op jit(solution)/shard_map/ppermute | solution.py:50
  83.0 0.6 pair_sums.5
  83.6 1.5 %collective-permute-start.48 = (bf16[64,896]{1,0:T(8,128)(2,1)S(1)}, bf16[64,896]{1,0:T(8,128)(2,1)S(1)}, u32[]{:S(2)}, u32[]{:S(2)}) collective-permute-start(bf16[64,896]{1,0:T(8,128)(2,1)S(1)} %get-tuple-element.146), channel_id=1, source_target_pairs={{0,2},{1,3},{2,0},{3,1},{4,6},{5,7},{6,4},{7,5},{8,10},{9,11},{10,... | collective-permute-start | bytes 344072 | tf_op jit(solution)/shard_map/ppermute | solution.py:50
  85.1 1.4 %collective-permute-start.49 = (bf16[64,896]{1,0:T(8,128)(2,1)S(1)}, bf16[64,896]{1,0:T(8,128)(2,1)S(1)}, u32[]{:S(2)}, u32[]{:S(2)}) collective-permute-start(bf16[64,896]{1,0:T(8,128)(2,1)S(1)} %get-tuple-element.147), channel_id=1, source_target_pairs={{0,4},{1,5},{2,6},{3,7},{4,0},{5,1},{6,2},{7,3},{8,12},{9,13},{10,... | collective-permute-start | bytes 344072 | tf_op jit(solution)/shard_map/ppermute | solution.py:50
  86.5 1.6 %collective-permute-start.50 = (bf16[64,896]{1,0:T(8,128)(2,1)S(1)}, bf16[64,896]{1,0:T(8,128)(2,1)S(1)}, u32[]{:S(2)}, u32[]{:S(2)}) collective-permute-start(bf16[64,896]{1,0:T(8,128)(2,1)S(1)} %get-tuple-element.148), channel_id=1, source_target_pairs={{0,6},{1,7},{2,4},{3,5},{4,2},{5,3},{6,0},{7,1},{8,14},{9,15},{10,... | collective-permute-start | bytes 344072 | tf_op jit(solution)/shard_map/ppermute | solution.py:50
  88.6 0.8 collective-permute-done.42.refs_5_
  89.5 2.7 %cols_half.5 = (f32[64,640]{1,0:T(8,128)S(1)}, bf16[64,768]{1,0:T(8,128)(2,1)S(1)}, bf16[64,768]{1,0:T(8,128)(2,1)S(1)}, bf16[64,768]{1,0:T(8,128)(2,1)S(1)}, f32[64,64]{1,0:T(8,128)S(1)}) custom-call(s32[259]{0:T(512)S(1)} %concatenate.3.table, bf16[96,128,128]{2,1,0:T(8,128)(2,1)S(1)} %get-tuple-element.84.tile_ref, ...), custom_call_target="tpu_custom_call" | custom-call | tf_op jit(solution)/shard_map/cols_half/pallas_call | solution.py:382
  92.2 1.1 collective-permute-start.44
  93.3 1.1 collective-permute-start.45
  94.4 1.4 %collective-permute-start.46 = (bf16[64,768]{1,0:T(8,128)(2,1)S(1)}, bf16[64,768]{1,0:T(8,128)(2,1)S(1)}, u32[]{:S(2)}, u32[]{:S(2)}) collective-permute-start(bf16[64,768]{1,0:T(8,128)(2,1)S(1)} %get-tuple-element.140), channel_id=1, source_target_pairs={{0,24},{8,16},{16,8},{24,0},{1,25},{9,17},{17,9},{25,1},{2,26},{10... | collective-permute-start | bytes 294920 | tf_op jit(solution)/shard_map/ppermute | solution.py:50
  95.8 1.1 collective-permute-done.49.refs_1_
  97.0 3.3 %solve.1.solve_ref = f32[64,128]{1,0:T(8,128)S(1)} custom-call(f32[8,128]{1,0:T(8,128)S(1)} %shift.1.shift_ref, f32[64,128]{1,0:T(8,128)S(1)} %get-tuple-element.98.shift_ref.gram_ref.gram0_ref, f32[64,128]{1,0:T(8,128)S(1)} %get-tuple-element.129.gram1_ref, f32[64,128]{1,0:T(8,128)S(1)} %get-tuple-element.149.gram2_ref, f32[64,256]{1,0:T(8,128)S(1)} %coefficients.2.first_ref), custom_call_target="tpu_custom_call" | custom-call | tf_op jit(solution)/shard_map/solve/pallas_call | solution.py:382
  100.5 2.0 %collective-permute-start.51 = (f32[64,64]{1,0:T(8,128)S(1)}, f32[64,64]{1,0:T(8,128)S(1)}, u32[]{:S(2)}, u32[]{:S(2)}) collective-permute-start(f32[64,64]{1,0:T(8,128)S(1)} %last_gram.1), channel_id=1, source_target_pairs={{0,2},{1,3},{2,0},{3,1},{4,6},{5,7},{6,4},{7,5},{8,10},{9,11},{10,... | collective-permute-start | bytes 49160 | tf_op jit(solution)/shard_map/ppermute | solution.py:50
  102.5 1.0 collective-permute-start.52
  103.5 1.4 %collective-permute-start.53 = (f32[64,64]{1,0:T(8,128)S(1)}, f32[64,64]{1,0:T(8,128)S(1)}, u32[]{:S(2)}, u32[]{:S(2)}) collective-permute-start(f32[64,64]{1,0:T(8,128)S(1)} %last_gram.1), channel_id=1, source_target_pairs={{0,6},{1,7},{2,4},{3,5},{4,2},{5,3},{6,0},{7,1},{8,14},{9,15},{10,... | collective-permute-start | bytes 49160 | tf_op jit(solution)/shard_map/ppermute | solution.py:50
  104.9 2.7 %coefficients.3 = (f32[192,256]{1,0:T(8,128)S(1)}, f32[64,256]{1,0:T(8,128)S(1)}) custom-call(f32[8,128]{1,0:T(8,128)S(1)} %shift.1.shift_ref, f32[64,128]{1,0:T(8,128)S(1)} %get-tuple-element.98.shift_ref.gram_ref.gram0_ref, f32[64,128]{1,0:T(8,128)S(1)} %get-tuple-element.129.gram1_ref, f32[64,128]{1,0:T(8,128)S(1)} %get-tuple-element.149.gram2_ref, ...), custom_call_target="tpu_custom_call" | custom-call | tf_op jit(solution)/shard_map/coefficients/pallas_call | solution.py:382
  107.8 1.4 %collective-permute-done.53 = f32[64,64]{1,0:T(8,128)S(1)} collective-permute-done((f32[64,64]{1,0:T(8,128)S(1)}, f32[64,64]{1,0:T(8,128)S(1)}, u32[]{:S(2)}, u32[]{:S(2)}) %collective-permute-start.53) | collective-permute-done | bytes 16416 | tf_op jit(solution)/shard_map/ppermute | solution.py:50
  109.3 0.8 vectors.1.vectors_ref
  110.5 3.3 %finish.1 = (f32[64,640]{1,0:T(8,128)}, f32[64,640]{1,0:T(8,128)}) custom-call(f32[256,640]{1,0:T(8,128)S(1)} %vectors.1.vectors_ref, f32[64,256]{1,0:T(8,128)S(1)} %get-tuple-element.162.small_ref, f32[64,64]{1,0:T(8,128)S(1)} %add_add_fusion.both_ref, f32[64,64]{1,0:T(8,128)S(1)} %collective-permute-done.54.other_ref, ...), custom_call_target="tpu_custom_call" | custom-call | tf_op jit(solution)/shard_map/finish/pallas_call | solution.py:382
  (92 shorter events, 9.2 us)
Async XLA Ops:
  2.2 10.5 %copy-start.5 = (s32[1,1,32]{2,1,0:T(1,128)S(1)}, s32[1,1,32]{2,1,0:T(1,128)}, u32[]{:S(2)}) copy-start(s32[1,1,32]{2,1,0:T(1,128)} %param.14) | copy-start | bytes 388
  2.2 10.5 %copy-start.6 = (s32[1,1,64]{2,1,0:T(1,128)S(1)}, s32[1,1,64]{2,1,0:T(1,128)}, u32[]{:S(2)}) copy-start(s32[1,1,64]{2,1,0:T(1,128)} %param.19) | copy-start | bytes 772
  2.2 10.6 %copy-start.7 = (s32[1,1,32]{2,1,0:T(1,128)S(1)}, s32[1,1,32]{2,1,0:T(1,128)}, u32[]{:S(2)}) copy-start(s32[1,1,32]{2,1,0:T(1,128)} %param.15) | copy-start | bytes 388
  2.2 10.6 %copy-start.8 = (s32[1,1,64]{2,1,0:T(1,128)S(1)}, s32[1,1,64]{2,1,0:T(1,128)}, u32[]{:S(2)}) copy-start(s32[1,1,64]{2,1,0:T(1,128)} %param.20) | copy-start | bytes 772
  2.2 10.6 %copy-start.9 = (s32[1,1,64]{2,1,0:T(1,128)S(1)}, s32[1,1,64]{2,1,0:T(1,128)}, u32[]{:S(2)}) copy-start(s32[1,1,64]{2,1,0:T(1,128)} %param.21) | copy-start | bytes 772
  2.3 10.6 %copy-start = (bf16[1,1,32,128,128]{4,3,2,1,0:T(8,128)(2,1)S(1)}, bf16[1,1,32,128,128]{4,3,2,1,0:T(8,128)(2,1)}, u32[]{:S(2)}) copy-start(bf16[1,1,32,128,128]{4,3,2,1,0:T(8,128)(2,1)} %param.13) | copy-start | bytes 3145732
  2.3 10.6 %copy-start.3 = (bf16[1,1,64,32,128]{4,3,2,1,0:T(8,128)(2,1)S(1)}, bf16[1,1,64,32,128]{4,3,2,1,0:T(8,128)(2,1)}, u32[]{:S(2)}) copy-start(bf16[1,1,64,32,128]{4,3,2,1,0:T(8,128)(2,1)} %param.17) | copy-start | bytes 1572868
  2.3 10.6 %copy-start.4 = (bf16[1,1,64,32,128]{4,3,2,1,0:T(8,128)(2,1)S(1)}, bf16[1,1,64,32,128]{4,3,2,1,0:T(8,128)(2,1)}, u32[]{:S(2)}) copy-start(bf16[1,1,64,32,128]{4,3,2,1,0:T(8,128)(2,1)} %param.18) | copy-start | bytes 1572868
  2.6 9.2 %collective-permute-start = (bf16[64,640]{1,0:T(8,128)(2,1)S(1)}, bf16[64,640]{1,0:T(8,128)(2,1)S(1)}, u32[]{:S(2)}, u32[]{:S(2)}) collective-permute-start(bf16[64,640]{1,0:T(8,128)(2,1)S(1)} %get-tuple-element.85.refs_0_), channel_id=1, source_target_pairs={{0,2},{1,3},{2,0},{3,1},{4,6},{5,7},{6,4},{7,5},{8,10},{9,11},{10,... | collective-permute-start | bytes 245768 | tf_op jit(solution)/shard_map/ppermute | solution.py:50
  5.7 10.5 %collective-permute-start.3 = (bf16[64,896]{1,0:T(8,128)(2,1)S(1)}, bf16[64,896]{1,0:T(8,128)(2,1)S(1)}, u32[]{:S(2)}, u32[]{:S(2)}) collective-permute-start(bf16[64,896]{1,0:T(8,128)(2,1)S(1)} %get-tuple-element.87.refs_0_), channel_id=1, source_target_pairs={{0,8},{8,0},{16,24},{24,16},{1,9},{9,1},{17,25},{25,17},{2,10},{10... | collective-permute-start | bytes 344072 | tf_op jit(solution)/shard_map/ppermute | solution.py:50
  7.2 9.0 %collective-permute-start.4 = (bf16[64,896]{1,0:T(8,128)(2,1)S(1)}, bf16[64,896]{1,0:T(8,128)(2,1)S(1)}, u32[]{:S(2)}, u32[]{:S(2)}) collective-permute-start(bf16[64,896]{1,0:T(8,128)(2,1)S(1)} %get-tuple-element.87.refs_0_), channel_id=1, source_target_pairs={{0,16},{8,24},{16,0},{24,8},{1,17},{9,25},{17,1},{25,9},{2,18},{10... | collective-permute-start | bytes 344072 | tf_op jit(solution)/shard_map/ppermute | solution.py:50
  8.7 7.5 %collective-permute-start.5 = (bf16[64,896]{1,0:T(8,128)(2,1)S(1)}, bf16[64,896]{1,0:T(8,128)(2,1)S(1)}, u32[]{:S(2)}, u32[]{:S(2)}) collective-permute-start(bf16[64,896]{1,0:T(8,128)(2,1)S(1)} %get-tuple-element.87.refs_0_), channel_id=1, source_target_pairs={{0,24},{8,16},{16,8},{24,0},{1,25},{9,17},{17,9},{25,1},{2,26},{10... | collective-permute-start | bytes 344072 | tf_op jit(solution)/shard_map/ppermute | solution.py:50
  9.2 9.1 %collective-permute-start.1 = (bf16[64,640]{1,0:T(8,128)(2,1)S(1)}, bf16[64,640]{1,0:T(8,128)(2,1)S(1)}, u32[]{:S(2)}, u32[]{:S(2)}) collective-permute-start(bf16[64,640]{1,0:T(8,128)(2,1)S(1)} %get-tuple-element.85.refs_0_), channel_id=1, source_target_pairs={{0,4},{1,5},{2,6},{3,7},{4,0},{5,1},{6,2},{7,3},{8,12},{9,13},{10,... | collective-permute-start | bytes 245768 | tf_op jit(solution)/shard_map/ppermute | solution.py:50
  11.8 6.7 %collective-permute-start.2 = (bf16[64,640]{1,0:T(8,128)(2,1)S(1)}, bf16[64,640]{1,0:T(8,128)(2,1)S(1)}, u32[]{:S(2)}, u32[]{:S(2)}) collective-permute-start(bf16[64,640]{1,0:T(8,128)(2,1)S(1)} %collective-permute-done.refs_2_), channel_id=1, source_target_pairs={{0,4},{1,5},{2,6},{3,7},{4,0},{5,1},{6,2},{7,3},{8,12},{9,13},{10,... | collective-permute-start | bytes 245768 | tf_op jit(solution)/shard_map/ppermute | solution.py:50
  18.5 1.7 %collective-permute-start.6 = (bf16[5,64,640]{2,1,0:T(8,128)(2,1)S(1)}, bf16[5,64,640]{2,1,0:T(8,128)(2,1)S(1)}, u32[]{:S(2)}, u32[]{:S(2)}) collective-permute-start(bf16[5,64,640]{2,1,0:T(8,128)(2,1)S(1)} %get-tuple-element.92), channel_id=1, source_target_pairs={{0,1},{1,0},{2,3},{3,2},{4,5},{5,4},{6,7},{7,6},{8,9},{9,8},{10,11... | collective-permute-start | bytes 1228808 | tf_op jit(solution)/shard_map/ppermute | solution.py:50
  18.5 6.8 %collective-permute-start.10 = (bf16[64,640]{1,0:T(8,128)(2,1)S(1)}, bf16[64,640]{1,0:T(8,128)(2,1)S(1)}, u32[]{:S(2)}, u32[]{:S(2)}) collective-permute-start(bf16[64,640]{1,0:T(8,128)(2,1)S(1)} %get-tuple-element.85.refs_0_), channel_id=1, source_target_pairs={{0,1},{1,0},{2,3},{3,2},{4,5},{5,4},{6,7},{7,6},{8,9},{9,8},{10,11... | collective-permute-start | bytes 245768 | tf_op jit(solution)/shard_map/ppermute | solution.py:50
  19.0 6.3 %collective-permute-start.11 = (bf16[64,640]{1,0:T(8,128)(2,1)S(1)}, bf16[64,640]{1,0:T(8,128)(2,1)S(1)}, u32[]{:S(2)}, u32[]{:S(2)}) collective-permute-start(bf16[64,640]{1,0:T(8,128)(2,1)S(1)} %collective-permute-done.refs_2_), channel_id=1, source_target_pairs={{0,1},{1,0},{2,3},{3,2},{4,5},{5,4},{6,7},{7,6},{8,9},{9,8},{10,11... | collective-permute-start | bytes 245768 | tf_op jit(solution)/shard_map/ppermute | solution.py:50
  20.9 11.4 %collective-permute-start.7 = (bf16[64,896]{1,0:T(8,128)(2,1)S(1)}, bf16[64,896]{1,0:T(8,128)(2,1)S(1)}, u32[]{:S(2)}, u32[]{:S(2)}) collective-permute-start(bf16[64,896]{1,0:T(8,128)(2,1)S(1)} %get-tuple-element.95), channel_id=1, source_target_pairs={{0,2},{1,3},{2,0},{3,1},{4,6},{5,7},{6,4},{7,5},{8,10},{9,11},{10,... | collective-permute-start | bytes 344072 | tf_op jit(solution)/shard_map/ppermute | solution.py:50
  21.5 10.9 %collective-permute-start.8 = (bf16[64,896]{1,0:T(8,128)(2,1)S(1)}, bf16[64,896]{1,0:T(8,128)(2,1)S(1)}, u32[]{:S(2)}, u32[]{:S(2)}) collective-permute-start(bf16[64,896]{1,0:T(8,128)(2,1)S(1)} %get-tuple-element.96), channel_id=1, source_target_pairs={{0,4},{1,5},{2,6},{3,7},{4,0},{5,1},{6,2},{7,3},{8,12},{9,13},{10,... | collective-permute-start | bytes 344072 | tf_op jit(solution)/shard_map/ppermute | solution.py:50
  23.9 9.2 %collective-permute-start.9 = (bf16[64,896]{1,0:T(8,128)(2,1)S(1)}, bf16[64,896]{1,0:T(8,128)(2,1)S(1)}, u32[]{:S(2)}, u32[]{:S(2)}) collective-permute-start(bf16[64,896]{1,0:T(8,128)(2,1)S(1)} %get-tuple-element.97), channel_id=1, source_target_pairs={{0,6},{1,7},{2,4},{3,5},{4,2},{5,3},{6,0},{7,1},{8,14},{9,15},{10,... | collective-permute-start | bytes 344072 | tf_op jit(solution)/shard_map/ppermute | solution.py:50
  25.3 1.3 %collective-permute-start.12 = (bf16[64,640]{1,0:T(8,128)(2,1)S(1)}, bf16[64,640]{1,0:T(8,128)(2,1)S(1)}, u32[]{:S(2)}, u32[]{:S(2)}) collective-permute-start(bf16[64,640]{1,0:T(8,128)(2,1)S(1)} %collective-permute-done.1.refs_4_), channel_id=1, source_target_pairs={{0,1},{1,0},{2,3},{3,2},{4,5},{5,4},{6,7},{7,6},{8,9},{9,8},{10,11... | collective-permute-start | bytes 245768 | tf_op jit(solution)/shard_map/ppermute | solution.py:50
  25.3 1.4 %collective-permute-start.13 = (bf16[64,640]{1,0:T(8,128)(2,1)S(1)}, bf16[64,640]{1,0:T(8,128)(2,1)S(1)}, u32[]{:S(2)}, u32[]{:S(2)}) collective-permute-start(bf16[64,640]{1,0:T(8,128)(2,1)S(1)} %collective-permute-done.2.refs_6_), channel_id=1, source_target_pairs={{0,1},{1,0},{2,3},{3,2},{4,5},{5,4},{6,7},{7,6},{8,9},{9,8},{10,11... | collective-permute-start | bytes 245768 | tf_op jit(solution)/shard_map/ppermute | solution.py:50
  26.8 10.8 %copy-start.2 = (f32[64,640]{1,0:T(8,128)S(1)}, f32[64,640]{1,0:T(8,128)}, u32[]{:S(2)}) copy-start(f32[64,640]{1,0:T(8,128)} %b_ref.1) | copy-start | bytes 491524
  28.8 4.9 %collective-permute-start.14 = (bf16[64,640]{1,0:T(8,128)(2,1)S(1)}, bf16[64,640]{1,0:T(8,128)(2,1)S(1)}, u32[]{:S(2)}, u32[]{:S(2)}) collective-permute-start(bf16[64,640]{1,0:T(8,128)(2,1)S(1)} %get-tuple-element.104), channel_id=1, source_target_pairs={{0,8},{8,0},{16,24},{24,16},{1,9},{9,1},{17,25},{25,17},{2,10},{10... | collective-permute-start | bytes 245768 | tf_op jit(solution)/shard_map/ppermute | solution.py:50
  30.7 5.3 %collective-permute-start.15 = (bf16[64,640]{1,0:T(8,128)(2,1)S(1)}, bf16[64,640]{1,0:T(8,128)(2,1)S(1)}, u32[]{:S(2)}, u32[]{:S(2)}) collective-permute-start(bf16[64,640]{1,0:T(8,128)(2,1)S(1)} %get-tuple-element.105), channel_id=1, source_target_pairs={{0,16},{8,24},{16,0},{24,8},{1,17},{9,25},{17,1},{25,9},{2,18},{10... | collective-permute-start | bytes 245768 | tf_op jit(solution)/shard_map/ppermute | solution.py:50
  32.2 5.3 %collective-permute-start.16 = (bf16[64,640]{1,0:T(8,128)(2,1)S(1)}, bf16[64,640]{1,0:T(8,128)(2,1)S(1)}, u32[]{:S(2)}, u32[]{:S(2)}) collective-permute-start(bf16[64,640]{1,0:T(8,128)(2,1)S(1)} %get-tuple-element.106), channel_id=1, source_target_pairs={{0,24},{8,16},{16,8},{24,0},{1,25},{9,17},{17,9},{25,1},{2,26},{10... | collective-permute-start | bytes 245768 | tf_op jit(solution)/shard_map/ppermute | solution.py:50
  38.3 6.2 %collective-permute-start.17 = (bf16[64,640]{1,0:T(8,128)(2,1)S(1)}, bf16[64,640]{1,0:T(8,128)(2,1)S(1)}, u32[]{:S(2)}, u32[]{:S(2)}) collective-permute-start(bf16[64,640]{1,0:T(8,128)(2,1)S(1)} %get-tuple-element.108.refs_0_), channel_id=1, source_target_pairs={{0,2},{1,3},{2,0},{3,1},{4,6},{5,7},{6,4},{7,5},{8,10},{9,11},{10,... | collective-permute-start | bytes 245768 | tf_op jit(solution)/shard_map/ppermute | solution.py:50
  38.4 6.5 %collective-permute-start.20 = (bf16[64,896]{1,0:T(8,128)(2,1)S(1)}, bf16[64,896]{1,0:T(8,128)(2,1)S(1)}, u32[]{:S(2)}, u32[]{:S(2)}) collective-permute-start(bf16[64,896]{1,0:T(8,128)(2,1)S(1)} %get-tuple-element.109.refs_0_), channel_id=1, source_target_pairs={{0,8},{8,0},{16,24},{24,16},{1,9},{9,1},{17,25},{25,17},{2,10},{10... | collective-permute-start | bytes 344072 | tf_op jit(solution)/shard_map/ppermute | solution.py:50
  39.0 6.8 %collective-permute-start.21 = (bf16[64,896]{1,0:T(8,128)(2,1)S(1)}, bf16[64,896]{1,0:T(8,128)(2,1)S(1)}, u32[]{:S(2)}, u32[]{:S(2)}) collective-permute-start(bf16[64,896]{1,0:T(8,128)(2,1)S(1)} %get-tuple-element.109.refs_0_), channel_id=1, source_target_pairs={{0,16},{8,24},{16,0},{24,8},{1,17},{9,25},{17,1},{25,9},{2,18},{10... | collective-permute-start | bytes 344072 | tf_op jit(solution)/shard_map/ppermute | solution.py:50
  39.8 6.0 %collective-permute-start.22 = (bf16[64,896]{1,0:T(8,128)(2,1)S(1)}, bf16[64,896]{1,0:T(8,128)(2,1)S(1)}, u32[]{:S(2)}, u32[]{:S(2)}) collective-permute-start(bf16[64,896]{1,0:T(8,128)(2,1)S(1)} %get-tuple-element.109.refs_0_), channel_id=1, source_target_pairs={{0,24},{8,16},{16,8},{24,0},{1,25},{9,17},{17,9},{25,1},{2,26},{10... | collective-permute-start | bytes 344072 | tf_op jit(solution)/shard_map/ppermute | solution.py:50
  42.0 6.0 %collective-permute-start.18 = (bf16[64,640]{1,0:T(8,128)(2,1)S(1)}, bf16[64,640]{1,0:T(8,128)(2,1)S(1)}, u32[]{:S(2)}, u32[]{:S(2)}) collective-permute-start(bf16[64,640]{1,0:T(8,128)(2,1)S(1)} %get-tuple-element.108.refs_0_), channel_id=1, source_target_pairs={{0,4},{1,5},{2,6},{3,7},{4,0},{5,1},{6,2},{7,3},{8,12},{9,13},{10,... | collective-permute-start | bytes 245768 | tf_op jit(solution)/shard_map/ppermute | solution.py:50
  44.5 6.2 %collective-permute-start.19 = (bf16[64,640]{1,0:T(8,128)(2,1)S(1)}, bf16[64,640]{1,0:T(8,128)(2,1)S(1)}, u32[]{:S(2)}, u32[]{:S(2)}) collective-permute-start(bf16[64,640]{1,0:T(8,128)(2,1)S(1)} %collective-permute-done.17.refs_2_), channel_id=1, source_target_pairs={{0,4},{1,5},{2,6},{3,7},{4,0},{5,1},{6,2},{7,3},{8,12},{9,13},{10,... | collective-permute-start | bytes 245768 | tf_op jit(solution)/shard_map/ppermute | solution.py:50
  50.7 1.7 %collective-permute-start.23 = (bf16[5,64,640]{2,1,0:T(8,128)(2,1)S(1)}, bf16[5,64,640]{2,1,0:T(8,128)(2,1)S(1)}, u32[]{:S(2)}, u32[]{:S(2)}) collective-permute-start(bf16[5,64,640]{2,1,0:T(8,128)(2,1)S(1)} %get-tuple-element.114), channel_id=1, source_target_pairs={{0,1},{1,0},{2,3},{3,2},{4,5},{5,4},{6,7},{7,6},{8,9},{9,8},{10,11... | collective-permute-start | bytes 1228808 | tf_op jit(solution)/shard_map/ppermute | solution.py:50
  50.7 6.8 %collective-permute-start.27 = (bf16[64,640]{1,0:T(8,128)(2,1)S(1)}, bf16[64,640]{1,0:T(8,128)(2,1)S(1)}, u32[]{:S(2)}, u32[]{:S(2)}) collective-permute-start(bf16[64,640]{1,0:T(8,128)(2,1)S(1)} %get-tuple-element.108.refs_0_), channel_id=1, source_target_pairs={{0,1},{1,0},{2,3},{3,2},{4,5},{5,4},{6,7},{7,6},{8,9},{9,8},{10,11... | collective-permute-start | bytes 245768 | tf_op jit(solution)/shard_map/ppermute | solution.py:50
  51.2 6.3 %collective-permute-start.28 = (bf16[64,640]{1,0:T(8,128)(2,1)S(1)}, bf16[64,640]{1,0:T(8,128)(2,1)S(1)}, u32[]{:S(2)}, u32[]{:S(2)}) collective-permute-start(bf16[64,640]{1,0:T(8,128)(2,1)S(1)} %collective-permute-done.17.refs_2_), channel_id=1, source_target_pairs={{0,1},{1,0},{2,3},{3,2},{4,5},{5,4},{6,7},{7,6},{8,9},{9,8},{10,11... | collective-permute-start | bytes 245768 | tf_op jit(solution)/shard_map/ppermute | solution.py:50
  53.1 9.7 %collective-permute-start.24 = (bf16[64,896]{1,0:T(8,128)(2,1)S(1)}, bf16[64,896]{1,0:T(8,128)(2,1)S(1)}, u32[]{:S(2)}, u32[]{:S(2)}) collective-permute-start(bf16[64,896]{1,0:T(8,128)(2,1)S(1)} %get-tuple-element.117), channel_id=1, source_target_pairs={{0,2},{1,3},{2,0},{3,1},{4,6},{5,7},{6,4},{7,5},{8,10},{9,11},{10,... | collective-permute-start | bytes 344072 | tf_op jit(solution)/shard_map/ppermute | solution.py:50
  53.2 11.9 %collective-permute-start.25 = (bf16[64,896]{1,0:T(8,128)(2,1)S(1)}, bf16[64,896]{1,0:T(8,128)(2,1)S(1)}, u32[]{:S(2)}, u32[]{:S(2)}) collective-permute-start(bf16[64,896]{1,0:T(8,128)(2,1)S(1)} %get-tuple-element.118), channel_id=1, source_target_pairs={{0,4},{1,5},{2,6},{3,7},{4,0},{5,1},{6,2},{7,3},{8,12},{9,13},{10,... | collective-permute-start | bytes 344072 | tf_op jit(solution)/shard_map/ppermute | solution.py:50
  55.7 9.4 %collective-permute-start.26 = (bf16[64,896]{1,0:T(8,128)(2,1)S(1)}, bf16[64,896]{1,0:T(8,128)(2,1)S(1)}, u32[]{:S(2)}, u32[]{:S(2)}) collective-permute-start(bf16[64,896]{1,0:T(8,128)(2,1)S(1)} %get-tuple-element.119), channel_id=1, source_target_pairs={{0,6},{1,7},{2,4},{3,5},{4,2},{5,3},{6,0},{7,1},{8,14},{9,15},{10,... | collective-permute-start | bytes 344072 | tf_op jit(solution)/shard_map/ppermute | solution.py:50
  57.6 1.3 %collective-permute-start.29 = (bf16[64,640]{1,0:T(8,128)(2,1)S(1)}, bf16[64,640]{1,0:T(8,128)(2,1)S(1)}, u32[]{:S(2)}, u32[]{:S(2)}) collective-permute-start(bf16[64,640]{1,0:T(8,128)(2,1)S(1)} %collective-permute-done.18.refs_4_), channel_id=1, source_target_pairs={{0,1},{1,0},{2,3},{3,2},{4,5},{5,4},{6,7},{7,6},{8,9},{9,8},{10,11... | collective-permute-start | bytes 245768 | tf_op jit(solution)/shard_map/ppermute | solution.py:50
  57.6 1.4 %collective-permute-start.30 = (bf16[64,640]{1,0:T(8,128)(2,1)S(1)}, bf16[64,640]{1,0:T(8,128)(2,1)S(1)}, u32[]{:S(2)}, u32[]{:S(2)}) collective-permute-start(bf16[64,640]{1,0:T(8,128)(2,1)S(1)} %collective-permute-done.19.refs_6_), channel_id=1, source_target_pairs={{0,1},{1,0},{2,3},{3,2},{4,5},{5,4},{6,7},{7,6},{8,9},{9,8},{10,11... | collective-permute-start | bytes 245768 | tf_op jit(solution)/shard_map/ppermute | solution.py:50
  61.1 5.0 %collective-permute-start.31 = (bf16[64,640]{1,0:T(8,128)(2,1)S(1)}, bf16[64,640]{1,0:T(8,128)(2,1)S(1)}, u32[]{:S(2)}, u32[]{:S(2)}) collective-permute-start(bf16[64,640]{1,0:T(8,128)(2,1)S(1)} %get-tuple-element.125), channel_id=1, source_target_pairs={{0,8},{8,0},{16,24},{24,16},{1,9},{9,1},{17,25},{25,17},{2,10},{10... | collective-permute-start | bytes 245768 | tf_op jit(solution)/shard_map/ppermute | solution.py:50
  61.8 4.5 %collective-permute-start.32 = (bf16[64,640]{1,0:T(8,128)(2,1)S(1)}, bf16[64,640]{1,0:T(8,128)(2,1)S(1)}, u32[]{:S(2)}, u32[]{:S(2)}) collective-permute-start(bf16[64,640]{1,0:T(8,128)(2,1)S(1)} %get-tuple-element.126), channel_id=1, source_target_pairs={{0,16},{8,24},{16,0},{24,8},{1,17},{9,25},{17,1},{25,9},{2,18},{10... | collective-permute-start | bytes 245768 | tf_op jit(solution)/shard_map/ppermute | solution.py:50
  62.9 5.3 %collective-permute-start.33 = (bf16[64,640]{1,0:T(8,128)(2,1)S(1)}, bf16[64,640]{1,0:T(8,128)(2,1)S(1)}, u32[]{:S(2)}, u32[]{:S(2)}) collective-permute-start(bf16[64,640]{1,0:T(8,128)(2,1)S(1)} %get-tuple-element.127), channel_id=1, source_target_pairs={{0,24},{8,16},{16,8},{24,0},{1,25},{9,17},{17,9},{25,1},{2,26},{10... | collective-permute-start | bytes 245768 | tf_op jit(solution)/shard_map/ppermute | solution.py:50
  68.8 6.6 %collective-permute-start.35 = (bf16[64,640]{1,0:T(8,128)(2,1)S(1)}, bf16[64,640]{1,0:T(8,128)(2,1)S(1)}, u32[]{:S(2)}, u32[]{:S(2)}) collective-permute-start(bf16[64,640]{1,0:T(8,128)(2,1)S(1)} %get-tuple-element.128.refs_0_), channel_id=1, source_target_pairs={{0,2},{1,3},{2,0},{3,1},{4,6},{5,7},{6,4},{7,5},{8,10},{9,11},{10,... | collective-permute-start | bytes 245768 | tf_op jit(solution)/shard_map/ppermute | solution.py:50
  68.9 9.6 %collective-permute-start.38 = (bf16[64,896]{1,0:T(8,128)(2,1)S(1)}, bf16[64,896]{1,0:T(8,128)(2,1)S(1)}, u32[]{:S(2)}, u32[]{:S(2)}) collective-permute-start(bf16[64,896]{1,0:T(8,128)(2,1)S(1)} %get-tuple-element.130.refs_0_.refs_8_), channel_id=1, source_target_pairs={{0,8},{8,0},{16,24},{24,16},{1,9},{9,1},{17,25},{25,17},{2,10},{10... | collective-permute-start | bytes 344072 | tf_op jit(solution)/shard_map/ppermute | solution.py:50
  70.1 8.4 %collective-permute-start.39 = (bf16[64,896]{1,0:T(8,128)(2,1)S(1)}, bf16[64,896]{1,0:T(8,128)(2,1)S(1)}, u32[]{:S(2)}, u32[]{:S(2)}) collective-permute-start(bf16[64,896]{1,0:T(8,128)(2,1)S(1)} %get-tuple-element.130.refs_0_.refs_8_), channel_id=1, source_target_pairs={{0,16},{8,24},{16,0},{24,8},{1,17},{9,25},{17,1},{25,9},{2,18},{10... | collective-permute-start | bytes 344072 | tf_op jit(solution)/shard_map/ppermute | solution.py:50
  71.3 7.3 %collective-permute-start.40 = (bf16[64,896]{1,0:T(8,128)(2,1)S(1)}, bf16[64,896]{1,0:T(8,128)(2,1)S(1)}, u32[]{:S(2)}, u32[]{:S(2)}) collective-permute-start(bf16[64,896]{1,0:T(8,128)(2,1)S(1)} %get-tuple-element.130.refs_0_.refs_8_), channel_id=1, source_target_pairs={{0,24},{8,16},{16,8},{24,0},{1,25},{9,17},{17,9},{25,1},{2,26},{10... | collective-permute-start | bytes 344072 | tf_op jit(solution)/shard_map/ppermute | solution.py:50
  72.5 8.2 %collective-permute-start.36 = (bf16[64,640]{1,0:T(8,128)(2,1)S(1)}, bf16[64,640]{1,0:T(8,128)(2,1)S(1)}, u32[]{:S(2)}, u32[]{:S(2)}) collective-permute-start(bf16[64,640]{1,0:T(8,128)(2,1)S(1)} %get-tuple-element.128.refs_0_), channel_id=1, source_target_pairs={{0,4},{1,5},{2,6},{3,7},{4,0},{5,1},{6,2},{7,3},{8,12},{9,13},{10,... | collective-permute-start | bytes 245768 | tf_op jit(solution)/shard_map/ppermute | solution.py:50
  75.4 5.8 %collective-permute-start.37 = (bf16[64,640]{1,0:T(8,128)(2,1)S(1)}, bf16[64,640]{1,0:T(8,128)(2,1)S(1)}, u32[]{:S(2)}, u32[]{:S(2)}) collective-permute-start(bf16[64,640]{1,0:T(8,128)(2,1)S(1)} %collective-permute-done.35.refs_2_), channel_id=1, source_target_pairs={{0,4},{1,5},{2,6},{3,7},{4,0},{5,1},{6,2},{7,3},{8,12},{9,13},{10,... | collective-permute-start | bytes 245768 | tf_op jit(solution)/shard_map/ppermute | solution.py:50
  81.2 1.7 %collective-permute-start.47 = (bf16[5,64,640]{2,1,0:T(8,128)(2,1)S(1)}, bf16[5,64,640]{2,1,0:T(8,128)(2,1)S(1)}, u32[]{:S(2)}, u32[]{:S(2)}) collective-permute-start(bf16[5,64,640]{2,1,0:T(8,128)(2,1)S(1)} %get-tuple-element.143), channel_id=1, source_target_pairs={{0,1},{1,0},{2,3},{3,2},{4,5},{5,4},{6,7},{7,6},{8,9},{9,8},{10,11... | collective-permute-start | bytes 1228808 | tf_op jit(solution)/shard_map/ppermute | solution.py:50
  81.2 6.8 %collective-permute-start.34 = (bf16[64,640]{1,0:T(8,128)(2,1)S(1)}, bf16[64,640]{1,0:T(8,128)(2,1)S(1)}, u32[]{:S(2)}, u32[]{:S(2)}) collective-permute-start(bf16[64,640]{1,0:T(8,128)(2,1)S(1)} %get-tuple-element.128.refs_0_), channel_id=1, source_target_pairs={{0,1},{1,0},{2,3},{3,2},{4,5},{5,4},{6,7},{7,6},{8,9},{9,8},{10,11... | collective-permute-start | bytes 245768 | tf_op jit(solution)/shard_map/ppermute | solution.py:50
  81.7 6.3 %collective-permute-start.41 = (bf16[64,640]{1,0:T(8,128)(2,1)S(1)}, bf16[64,640]{1,0:T(8,128)(2,1)S(1)}, u32[]{:S(2)}, u32[]{:S(2)}) collective-permute-start(bf16[64,640]{1,0:T(8,128)(2,1)S(1)} %collective-permute-done.35.refs_2_), channel_id=1, source_target_pairs={{0,1},{1,0},{2,3},{3,2},{4,5},{5,4},{6,7},{7,6},{8,9},{9,8},{10,11... | collective-permute-start | bytes 245768 | tf_op jit(solution)/shard_map/ppermute | solution.py:50
  83.6 10.8 %collective-permute-start.48 = (bf16[64,896]{1,0:T(8,128)(2,1)S(1)}, bf16[64,896]{1,0:T(8,128)(2,1)S(1)}, u32[]{:S(2)}, u32[]{:S(2)}) collective-permute-start(bf16[64,896]{1,0:T(8,128)(2,1)S(1)} %get-tuple-element.146), channel_id=1, source_target_pairs={{0,2},{1,3},{2,0},{3,1},{4,6},{5,7},{6,4},{7,5},{8,10},{9,11},{10,... | collective-permute-start | bytes 344072 | tf_op jit(solution)/shard_map/ppermute | solution.py:50
  85.1 11.8 %collective-permute-start.49 = (bf16[64,896]{1,0:T(8,128)(2,1)S(1)}, bf16[64,896]{1,0:T(8,128)(2,1)S(1)}, u32[]{:S(2)}, u32[]{:S(2)}) collective-permute-start(bf16[64,896]{1,0:T(8,128)(2,1)S(1)} %get-tuple-element.147), channel_id=1, source_target_pairs={{0,4},{1,5},{2,6},{3,7},{4,0},{5,1},{6,2},{7,3},{8,12},{9,13},{10,... | collective-permute-start | bytes 344072 | tf_op jit(solution)/shard_map/ppermute | solution.py:50
  86.5 10.4 %collective-permute-start.50 = (bf16[64,896]{1,0:T(8,128)(2,1)S(1)}, bf16[64,896]{1,0:T(8,128)(2,1)S(1)}, u32[]{:S(2)}, u32[]{:S(2)}) collective-permute-start(bf16[64,896]{1,0:T(8,128)(2,1)S(1)} %get-tuple-element.148), channel_id=1, source_target_pairs={{0,6},{1,7},{2,4},{3,5},{4,2},{5,3},{6,0},{7,1},{8,14},{9,15},{10,... | collective-permute-start | bytes 344072 | tf_op jit(solution)/shard_map/ppermute | solution.py:50
  88.1 1.3 %collective-permute-start.42 = (bf16[64,640]{1,0:T(8,128)(2,1)S(1)}, bf16[64,640]{1,0:T(8,128)(2,1)S(1)}, u32[]{:S(2)}, u32[]{:S(2)}) collective-permute-start(bf16[64,640]{1,0:T(8,128)(2,1)S(1)} %collective-permute-done.36.refs_4_), channel_id=1, source_target_pairs={{0,1},{1,0},{2,3},{3,2},{4,5},{5,4},{6,7},{7,6},{8,9},{9,8},{10,11... | collective-permute-start | bytes 245768 | tf_op jit(solution)/shard_map/ppermute | solution.py:50
  88.1 1.4 %collective-permute-start.43 = (bf16[64,640]{1,0:T(8,128)(2,1)S(1)}, bf16[64,640]{1,0:T(8,128)(2,1)S(1)}, u32[]{:S(2)}, u32[]{:S(2)}) collective-permute-start(bf16[64,640]{1,0:T(8,128)(2,1)S(1)} %collective-permute-done.37.refs_6_), channel_id=1, source_target_pairs={{0,1},{1,0},{2,3},{3,2},{4,5},{5,4},{6,7},{7,6},{8,9},{9,8},{10,11... | collective-permute-start | bytes 245768 | tf_op jit(solution)/shard_map/ppermute | solution.py:50
  92.2 8.0 %collective-permute-start.44 = (bf16[64,768]{1,0:T(8,128)(2,1)S(1)}, bf16[64,768]{1,0:T(8,128)(2,1)S(1)}, u32[]{:S(2)}, u32[]{:S(2)}) collective-permute-start(bf16[64,768]{1,0:T(8,128)(2,1)S(1)} %get-tuple-element.138), channel_id=1, source_target_pairs={{0,8},{8,0},{16,24},{24,16},{1,9},{9,1},{17,25},{25,17},{2,10},{10... | collective-permute-start | bytes 294920 | tf_op jit(solution)/shard_map/ppermute | solution.py:50
  93.3 6.9 %collective-permute-start.45 = (bf16[64,768]{1,0:T(8,128)(2,1)S(1)}, bf16[64,768]{1,0:T(8,128)(2,1)S(1)}, u32[]{:S(2)}, u32[]{:S(2)}) collective-permute-start(bf16[64,768]{1,0:T(8,128)(2,1)S(1)} %get-tuple-element.139), channel_id=1, source_target_pairs={{0,16},{8,24},{16,0},{24,8},{1,17},{9,25},{17,1},{25,9},{2,18},{10... | collective-permute-start | bytes 294920 | tf_op jit(solution)/shard_map/ppermute | solution.py:50
  94.4 5.9 %collective-permute-start.46 = (bf16[64,768]{1,0:T(8,128)(2,1)S(1)}, bf16[64,768]{1,0:T(8,128)(2,1)S(1)}, u32[]{:S(2)}, u32[]{:S(2)}) collective-permute-start(bf16[64,768]{1,0:T(8,128)(2,1)S(1)} %get-tuple-element.140), channel_id=1, source_target_pairs={{0,24},{8,16},{16,8},{24,0},{1,25},{9,17},{17,9},{25,1},{2,26},{10... | collective-permute-start | bytes 294920 | tf_op jit(solution)/shard_map/ppermute | solution.py:50
  100.5 7.1 %collective-permute-start.51 = (f32[64,64]{1,0:T(8,128)S(1)}, f32[64,64]{1,0:T(8,128)S(1)}, u32[]{:S(2)}, u32[]{:S(2)}) collective-permute-start(f32[64,64]{1,0:T(8,128)S(1)} %last_gram.1), channel_id=1, source_target_pairs={{0,2},{1,3},{2,0},{3,1},{4,6},{5,7},{6,4},{7,5},{8,10},{9,11},{10,... | collective-permute-start | bytes 49160 | tf_op jit(solution)/shard_map/ppermute | solution.py:50
  102.5 5.4 %collective-permute-start.52 = (f32[64,64]{1,0:T(8,128)S(1)}, f32[64,64]{1,0:T(8,128)S(1)}, u32[]{:S(2)}, u32[]{:S(2)}) collective-permute-start(f32[64,64]{1,0:T(8,128)S(1)} %last_gram.1), channel_id=1, source_target_pairs={{0,4},{1,5},{2,6},{3,7},{4,0},{5,1},{6,2},{7,3},{8,12},{9,13},{10,... | collective-permute-start | bytes 49160 | tf_op jit(solution)/shard_map/ppermute | solution.py:50
  103.5 5.7 %collective-permute-start.53 = (f32[64,64]{1,0:T(8,128)S(1)}, f32[64,64]{1,0:T(8,128)S(1)}, u32[]{:S(2)}, u32[]{:S(2)}) collective-permute-start(f32[64,64]{1,0:T(8,128)S(1)} %last_gram.1), channel_id=1, source_target_pairs={{0,6},{1,7},{2,4},{3,5},{4,2},{5,3},{6,0},{7,1},{8,14},{9,15},{10,... | collective-permute-start | bytes 49160 | tf_op jit(solution)/shard_map/ppermute | solution.py:50
  109.2 1.3 %collective-permute-start.54 = (f32[64,64]{1,0:T(8,128)S(1)}, f32[64,64]{1,0:T(8,128)S(1)}, u32[]{:S(2)}, u32[]{:S(2)}) collective-permute-start(f32[64,64]{1,0:T(8,128)S(1)} %add_add_fusion.both_ref), channel_id=1, source_target_pairs={{0,1},{1,0},{2,3},{3,2},{4,5},{5,4},{6,7},{7,6},{8,9},{9,8},{10,11... | collective-permute-start | bytes 49160 | tf_op jit(solution)/shard_map/ppermute | solution.py:50
  (1 other events, 0.9 us)

commit v5 on v4

--- a/solution.py
+++ b/solution.py
@@ -225,20 +225,18 @@
     return total
 
 
-def rayleigh(gram):
+def shift_kernel(gram_ref, shift_ref):
+    gram = gram_ref[...]
     cases = gram.shape[0]
     norm = jnp.sum(identity(cases) * gram[:, :cases], keepdims=True)
-    return jnp.sum(gram[:, cases : cases + 1], keepdims=True) / norm
-
-
-def shift_kernel(gram_ref, shift_ref):
-    shift_ref[...] = jnp.broadcast_to(rayleigh(gram_ref[...]), shift_ref.shape)
-
-
-def combine_kernel(first, vector_ref, diagonal_ref, shift_ref, *refs):
+    quotient = jnp.sum(gram[:, cases : cases + 1], keepdims=True) / norm
+    shift_ref[...] = jnp.broadcast_to(quotient, shift_ref.shape)
+
+
+def combine_kernel(vector_ref, diagonal_ref, shift_ref, *refs):
     sums, (next_ref, plain_ref, wide_ref) = refs[:-3], refs[-3:]
     vector = vector_ref[...]
-    shift = rayleigh(shift_ref[...]) if first else shift_ref[0:1, 0:1]
+    shift = shift_ref[0:1, 0:1]
     following = (diagonal_ref[...] - shift) * vector + off_diagonal(sums)
     next_ref[...] = following
     cross = contract(vector, following, ((1,), (1,)), HIGHEST)
@@ -441,12 +439,13 @@
         ],
     )
 
-    def apply(plain, wide, last=(), beside=()):
+    def apply(plain, wide, during, last=()):
         over_row = [partner_permute(wide, "row", k) for k in range(1, rows)]
-        over_chip, flip = [], 1
-        while flip < chips:
-            over_chip += [partner_permute(m, "col", 2 * flip) for m in [plain, *over_chip]]
-            flip *= 2
+        held, flip = {0: plain}, chips // 2
+        while flip:
+            held |= {k ^ flip: partner_permute(m, "col", 2 * flip) for k, m in held.items()}
+            flip //= 2
+        over_chip = [held[k] for k in range(1, chips)]
         send, keep, gram = call(
             rows_kernel,
             "rows_half",
@@ -461,8 +460,10 @@
                 pltpu.VMEM((cols * per, cases, leaf), jnp.float32),
             ],
         )
-        over_chip, beside, send, keep = lax.optimization_barrier((over_chip, beside, send, keep))
+        over_chip, send, keep = lax.optimization_barrier((over_chip, send, keep))
         got = partner_permute(send, "col", 1)
+        other_core = [partner_permute(v, "col", 1) for v in [plain] + over_chip]
+        got, other_core = lax.optimization_barrier((got, other_core))
         own_chip, gram, *row_messages = call(
             pair_kernel,
             "pair_sums",
@@ -474,7 +475,6 @@
             scalars=(0,),
         )
         from_chips = [partner_permute(m, "col", 2 * k) for k, m in enumerate(row_messages, 1)]
-        other_core = [partner_permute(v, "col", 1) for v in [plain] + over_chip]
         own_row, gram = call(
             chip_sums_kernel,
             "chip_sums",
@@ -505,18 +505,17 @@
             ],
         )
         from_rows = [partner_permute(m, "row", k) for k, m in enumerate(outs[: rows - 1], 1)]
+        made = during(gram)
+        from_rows, made = lax.optimization_barrier((from_rows, made))
+        sums = [own_row, own_col, *from_rows]
         if not last:
-            return [own_row, own_col, *from_rows], gram
-        solved = call(
-            second_solve_kernel, "solve", f32(cases, 2 * cases), shift, gram0, gram1, gram, beside
-        )
-        from_rows, solved = lax.optimization_barrier((from_rows, solved))
+            return sums, gram, made
         both = call(last_gram_kernel, "last_gram", f32(cases, cases), outs[-1], *from_rows)
-        return [own_row, own_col, *from_rows], gram, both, beside, solved
-
-    def advance(first, vector, shift, sums):
+        return sums, gram, made, both
+
+    def advance(vector, shift, sums):
         return call(
-            functools.partial(combine_kernel, first),
+            combine_kernel,
             "combine",
             [f32(cases, width), bf16(cases, width), bf16(cases, long)],
             vector,
@@ -529,15 +528,26 @@
     plain, wide = call(
         first_kernel, "first_message", [bf16(cases, width), bf16(cases, long)], b, diagonal, cost=10
     )
-    sums, gram0 = apply(plain, wide)
-    u, plain, wide = advance(True, b, gram0, sums)
-    shift = call(shift_kernel, "shift", f32(8, 128), gram0)
-    sums, gram1 = apply(plain, wide)
-    v, plain, wide = advance(False, u, shift, sums)
-    first = call(
-        first_coefficients_kernel, "coefficients", f32(cases, 4 * cases), shift, gram0, gram1
-    )
-    sums, gram2, both, first, solved = apply(plain, wide, last=(v, diagonal), beside=first)
+    sums, gram0, shift = apply(
+        plain, wide, lambda gram: call(shift_kernel, "shift", f32(8, 128), gram)
+    )
+    u, plain, wide = advance(b, shift, sums)
+    sums, gram1, first = apply(
+        plain,
+        wide,
+        lambda gram: call(
+            first_coefficients_kernel, "coefficients", f32(cases, 4 * cases), shift, gram0, gram
+        ),
+    )
+    v, plain, wide = advance(u, shift, sums)
+    sums, gram2, solved, both = apply(
+        plain,
+        wide,
+        lambda gram: call(
+            second_solve_kernel, "solve", f32(cases, 2 * cases), shift, gram0, gram1, gram, first
+        ),
+        last=(v, diagonal),
+    )
     over_chip = [partner_permute(both, "col", 2 * k) for k in range(1, chips)]
     big, small = call(
         second_coefficients_kernel,

time: 114 us -> 111 us (0.974)
  waiting for transfers between devices: 22.5 us -> 17.2 us
  starting transfers between devices: 54.3 us -> 56.7 us
    ppermute x55, waiting for transfers between devices: 22.5 us -> 17.2 us  [partner_permute(): return lax.ppermute(value, axis, [(i, i ^ flip) for i in range(size)])]
    ppermute x55, starting transfers between devices: 54.3 us -> 56.7 us  [partner_permute(): return lax.ppermute(value, axis, [(i, i ^ flip) for i in range(size)])]
  transfers between devices with their start and end apart: 55 -> 55, of which waited for: 25 -> 25; matrix products, arithmetic and copies ran while one was open for 0% -> 0% of each run, Pallas kernels for 25% -> 24%
where the time goes in v5:
time: 111 us
  starting transfers between devices  56.7 us (51%)
  Pallas kernels  33.4 us (30%)
  waiting for transfers between devices  17.2 us (15%)
  local copies, waits for them, and re-layouts  1.73 us (2%)
  between operations  1.72 us (2%)
    ppermute x55, starting transfers between devices, partner_permute(): return lax.ppermute(value, axis, [(i, i ^ flip) for i in range(size)])  56.7 us
    pallas_call x23, Pallas kernels, call(): pl.pallas_call(kernel, out_shape=outs, in_specs=[spaces.get(k, vmem) for...  33.4 us
    ppermute x55, waiting for transfers between devices, partner_permute(): return lax.ppermute(value, axis, [(i, i ^ flip) for i in range(size)])  17.2 us
  transfers between devices with their start and end apart: 55, of which 25 were waited for; matrix products, arithmetic and copies ran while one was open for 0% of the time, Pallas kernels for 24%

profile of v5, /device:TPU:0, one launch (start us, length us, event | category | flops | bytes accessed | tf_op | source)
XLA Modules:
  0.0 110.8 jit_solution(15013849007928117517)
XLA Ops:
  0.6 0.7 broadcast_in_dim.3.diagonal_ref.refs_13_
  1.3 0.9 copy-done.1
  2.6 4.1 %collective-permute-start.1 = (bf16[64,640]{1,0:T(8,128)(2,1)S(1)}, bf16[64,640]{1,0:T(8,128)(2,1)S(1)}, u32[]{:S(2)}, u32[]{:S(2)}) collective-permute-start(bf16[64,640]{1,0:T(8,128)(2,1)S(1)} %get-tuple-element.107.refs_0_), channel_id=1, source_target_pairs={{0,4},{1,5},{2,6},{3,7},{4,0},{5,1},{6,2},{7,3},{8,12},{9,13},{10,... | collective-permute-start | bytes 245768 | tf_op jit(solution)/shard_map/ppermute | solution.py:50
  6.7 2.4 %collective-permute-start.5 = (bf16[64,896]{1,0:T(8,128)(2,1)S(1)}, bf16[64,896]{1,0:T(8,128)(2,1)S(1)}, u32[]{:S(2)}, u32[]{:S(2)}) collective-permute-start(bf16[64,896]{1,0:T(8,128)(2,1)S(1)} %get-tuple-element.109.refs_0_), channel_id=1, source_target_pairs={{0,24},{8,16},{16,8},{24,0},{1,25},{9,17},{17,9},{25,1},{2,26},{10... | collective-permute-start | bytes 344072 | tf_op jit(solution)/shard_map/ppermute | solution.py:50
  9.2 0.5 collective-permute-start.4
  9.7 0.5 collective-permute-start.3
  10.2 1.6 %collective-permute-start = (bf16[64,640]{1,0:T(8,128)(2,1)S(1)}, bf16[64,640]{1,0:T(8,128)(2,1)S(1)}, u32[]{:S(2)}, u32[]{:S(2)}) collective-permute-start(bf16[64,640]{1,0:T(8,128)(2,1)S(1)} %get-tuple-element.107.refs_0_), channel_id=1, source_target_pairs={{0,2},{1,3},{2,0},{3,1},{4,6},{5,7},{6,4},{7,5},{8,10},{9,11},{10,... | collective-permute-start | bytes 245768 | tf_op jit(solution)/shard_map/ppermute | solution.py:50
  13.0 3.3 %dense_tiles.1 = (bf16[96,128,128]{2,1,0:T(8,128)(2,1)S(1)}, bf16[96,128,128]{2,1,0:T(8,128)(2,1)S(1)}) custom-call(s32[259]{0:T(512)S(1)} %concatenate.3.table, bf16[32,128,128]{2,1,0:T(8,128)(2,1)S(1)} %bitcast.12, bf16[64,32,128]{2,1,0:T(8,128)(2,1)S(1)} %bitcast.13, bf16[64,32,128]{2,1,0:T(8,128)(2,1)S(1)} %bitcast.14), custom_call_target="tpu_custom_call" | custom-call | tf_op jit(solution)/shard_map/dense_tiles/pallas_call | solution.py:380
  16.3 2.1 %rows_half.3 = (bf16[5,64,640]{2,1,0:T(8,128)(2,1)S(1)}, f32[4,64,640]{2,1,0:T(8,128)S(1)}, f32[64,128]{1,0:T(8,128)S(1)}) custom-call(s32[259]{0:T(512)S(1)} %concatenate.3.table, bf16[96,128,128]{2,1,0:T(8,128)(2,1)S(1)} %get-tuple-element.108.tile_ref, bf16[64,896]{1,0:T(8,128)(2,1)S(1)} %get-tuple-element.109.refs_0_, ...), custom_call_target="tpu_custom_call" | custom-call | tf_op jit(solution)/shard_map/rows_half/pallas_call | solution.py:380
  19.6 0.8 collective-permute-done.7.refs_1_
  20.8 0.6 pair_sums.3
  21.5 1.6 %collective-permute-start.14 = (bf16[64,896]{1,0:T(8,128)(2,1)S(1)}, bf16[64,896]{1,0:T(8,128)(2,1)S(1)}, u32[]{:S(2)}, u32[]{:S(2)}) collective-permute-start(bf16[64,896]{1,0:T(8,128)(2,1)S(1)} %get-tuple-element.128), channel_id=1, source_target_pairs={{0,2},{1,3},{2,0},{3,1},{4,6},{5,7},{6,4},{7,5},{8,10},{9,11},{10,... | collective-permute-start | bytes 344072 | tf_op jit(solution)/shard_map/ppermute | solution.py:50
  23.1 1.4 %collective-permute-start.15 = (bf16[64,896]{1,0:T(8,128)(2,1)S(1)}, bf16[64,896]{1,0:T(8,128)(2,1)S(1)}, u32[]{:S(2)}, u32[]{:S(2)}) collective-permute-start(bf16[64,896]{1,0:T(8,128)(2,1)S(1)} %get-tuple-element.129), channel_id=1, source_target_pairs={{0,4},{1,5},{2,6},{3,7},{4,0},{5,1},{6,2},{7,3},{8,12},{9,13},{10,... | collective-permute-start | bytes 344072 | tf_op jit(solution)/shard_map/ppermute | solution.py:50
  24.5 1.4 %collective-permute-start.16 = (bf16[64,896]{1,0:T(8,128)(2,1)S(1)}, bf16[64,896]{1,0:T(8,128)(2,1)S(1)}, u32[]{:S(2)}, u32[]{:S(2)}) collective-permute-start(bf16[64,896]{1,0:T(8,128)(2,1)S(1)} %get-tuple-element.130), channel_id=1, source_target_pairs={{0,6},{1,7},{2,4},{3,5},{4,2},{5,3},{6,0},{7,1},{8,14},{9,15},{10,... | collective-permute-start | bytes 344072 | tf_op jit(solution)/shard_map/ppermute | solution.py:50
  25.9 2.0 %cols_half.3 = (f32[64,640]{1,0:T(8,128)S(1)}, bf16[64,640]{1,0:T(8,128)(2,1)S(1)}, bf16[64,640]{1,0:T(8,128)(2,1)S(1)}, bf16[64,640]{1,0:T(8,128)(2,1)S(1)}) custom-call(s32[259]{0:T(512)S(1)} %concatenate.3.table, bf16[96,128,128]{2,1,0:T(8,128)(2,1)S(1)} %get-tuple-element.106.tile_ref, bf16[64,640]{1,0:T(8,128)(2,1)S(1)} %get-tuple-element.107.refs_0_, ...), custom_call_target="tpu_custom_call" | custom-call | tf_op jit(solution)/shard_map/cols_half/pallas_call | solution.py:380
  28.0 1.6 %collective-permute-start.11 = (bf16[64,640]{1,0:T(8,128)(2,1)S(1)}, bf16[64,640]{1,0:T(8,128)(2,1)S(1)}, u32[]{:S(2)}, u32[]{:S(2)}) collective-permute-start(bf16[64,640]{1,0:T(8,128)(2,1)S(1)} %get-tuple-element.120), channel_id=1, source_target_pairs={{0,8},{8,0},{16,24},{24,16},{1,9},{9,1},{17,25},{25,17},{2,10},{10... | collective-permute-start | bytes 245768 | tf_op jit(solution)/shard_map/ppermute | solution.py:50
  29.5 1.5 %collective-permute-start.12 = (bf16[64,640]{1,0:T(8,128)(2,1)S(1)}, bf16[64,640]{1,0:T(8,128)(2,1)S(1)}, u32[]{:S(2)}, u32[]{:S(2)}) collective-permute-start(bf16[64,640]{1,0:T(8,128)(2,1)S(1)} %get-tuple-element.121), channel_id=1, source_target_pairs={{0,16},{8,24},{16,0},{24,8},{1,17},{9,25},{17,1},{25,9},{2,18},{10... | collective-permute-start | bytes 245768 | tf_op jit(solution)/shard_map/ppermute | solution.py:50
  31.5 3.3 %collective-permute-done.15.refs_1_ = bf16[64,896]{1,0:T(8,128)(2,1)S(1)} collective-permute-done((bf16[64,896]{1,0:T(8,128)(2,1)S(1)}, bf16[64,896]{1,0:T(8,128)(2,1)S(1)}, u32[]{:S(2)}, u32[]{:S(2)}) %collective-permute-start.15) | collective-permute-done | bytes 114720 | tf_op jit(solution)/shard_map/ppermute | solution.py:50
  35.1 1.3 %collective-permute-done.13.refs_4_ = bf16[64,640]{1,0:T(8,128)(2,1)S(1)} collective-permute-done((bf16[64,640]{1,0:T(8,128)(2,1)S(1)}, bf16[64,640]{1,0:T(8,128)(2,1)S(1)}, u32[]{:S(2)}, u32[]{:S(2)}) %collective-permute-start.13) | collective-permute-done | bytes 81952 | tf_op jit(solution)/shard_map/ppermute | solution.py:50
  36.4 0.6 combine.2
  37.0 2.2 %collective-permute-start.18 = (bf16[64,640]{1,0:T(8,128)(2,1)S(1)}, bf16[64,640]{1,0:T(8,128)(2,1)S(1)}, u32[]{:S(2)}, u32[]{:S(2)}) collective-permute-start(bf16[64,640]{1,0:T(8,128)(2,1)S(1)} %get-tuple-element.139.refs_0_), channel_id=1, source_target_pairs={{0,4},{1,5},{2,6},{3,7},{4,0},{5,1},{6,2},{7,3},{8,12},{9,13},{10,... | collective-permute-start | bytes 245768 | tf_op jit(solution)/shard_map/ppermute | solution.py:50
  39.2 2.4 %collective-permute-start.22 = (bf16[64,896]{1,0:T(8,128)(2,1)S(1)}, bf16[64,896]{1,0:T(8,128)(2,1)S(1)}, u32[]{:S(2)}, u32[]{:S(2)}) collective-permute-start(bf16[64,896]{1,0:T(8,128)(2,1)S(1)} %get-tuple-element.140.refs_0_), channel_id=1, source_target_pairs={{0,24},{8,16},{16,8},{24,0},{1,25},{9,17},{17,9},{25,1},{2,26},{10... | collective-permute-start | bytes 344072 | tf_op jit(solution)/shard_map/ppermute | solution.py:50
  41.6 0.5 collective-permute-start.21
  42.1 0.5 collective-permute-start.20
  42.7 0.9 collective-permute-start.17
  43.5 1.1 %collective-permute-start.19 = (bf16[64,640]{1,0:T(8,128)(2,1)S(1)}, bf16[64,640]{1,0:T(8,128)(2,1)S(1)}, u32[]{:S(2)}, u32[]{:S(2)}) collective-permute-start(bf16[64,640]{1,0:T(8,128)(2,1)S(1)} %collective-permute-done.18.refs_4_), channel_id=1, source_target_pairs={{0,2},{1,3},{2,0},{3,1},{4,6},{5,7},{6,4},{7,5},{8,10},{9,11},{10,... | collective-permute-start | bytes 245768 | tf_op jit(solution)/shard_map/ppermute | solution.py:50
  44.7 0.7 collective-permute-done.22.refs_3_
  45.4 1.4 %collective-permute-done.21.refs_2_ = bf16[64,896]{1,0:T(8,128)(2,1)S(1)} collective-permute-done((bf16[64,896]{1,0:T(8,128)(2,1)S(1)}, bf16[64,896]{1,0:T(8,128)(2,1)S(1)}, u32[]{:S(2)}, u32[]{:S(2)}) %collective-permute-start.21) | collective-permute-done | bytes 114720 | tf_op jit(solution)/shard_map/ppermute | solution.py:50
  47.1 2.1 %rows_half.4 = (bf16[5,64,640]{2,1,0:T(8,128)(2,1)S(1)}, f32[4,64,640]{2,1,0:T(8,128)S(1)}, f32[64,128]{1,0:T(8,128)S(1)}) custom-call(s32[259]{0:T(512)S(1)} %concatenate.3.table, bf16[96,128,128]{2,1,0:T(8,128)(2,1)S(1)} %get-tuple-element.108.tile_ref, bf16[64,896]{1,0:T(8,128)(2,1)S(1)} %get-tuple-element.140.refs_0_, ...), custom_call_target="tpu_custom_call" | custom-call | tf_op jit(solution)/shard_map/rows_half/pallas_call | solution.py:380
  50.4 0.8 collective-permute-done.24.refs_1_
  51.6 0.6 pair_sums.4
  52.3 1.5 %collective-permute-start.29 = (bf16[64,896]{1,0:T(8,128)(2,1)S(1)}, bf16[64,896]{1,0:T(8,128)(2,1)S(1)}, u32[]{:S(2)}, u32[]{:S(2)}) collective-permute-start(bf16[64,896]{1,0:T(8,128)(2,1)S(1)} %get-tuple-element.153), channel_id=1, source_target_pairs={{0,4},{1,5},{2,6},{3,7},{4,0},{5,1},{6,2},{7,3},{8,12},{9,13},{10,... | collective-permute-start | bytes 344072 | tf_op jit(solution)/shard_map/ppermute | solution.py:50
  53.8 2.8 %collective-permute-start.30 = (bf16[64,896]{1,0:T(8,128)(2,1)S(1)}, bf16[64,896]{1,0:T(8,128)(2,1)S(1)}, u32[]{:S(2)}, u32[]{:S(2)}) collective-permute-start(bf16[64,896]{1,0:T(8,128)(2,1)S(1)} %get-tuple-element.154), channel_id=1, source_target_pairs={{0,6},{1,7},{2,4},{3,5},{4,2},{5,3},{6,0},{7,1},{8,14},{9,15},{10,... | collective-permute-start | bytes 344072 | tf_op jit(solution)/shard_map/ppermute | solution.py:50
  56.7 2.0 %cols_half.4 = (f32[64,640]{1,0:T(8,128)S(1)}, bf16[64,640]{1,0:T(8,128)(2,1)S(1)}, bf16[64,640]{1,0:T(8,128)(2,1)S(1)}, bf16[64,640]{1,0:T(8,128)(2,1)S(1)}) custom-call(s32[259]{0:T(512)S(1)} %concatenate.3.table, bf16[96,128,128]{2,1,0:T(8,128)(2,1)S(1)} %get-tuple-element.106.tile_ref, bf16[64,640]{1,0:T(8,128)(2,1)S(1)} %get-tuple-element.139.refs_0_, ...), custom_call_target="tpu_custom_call" | custom-call | tf_op jit(solution)/shard_map/cols_half/pallas_call | solution.py:380
  58.7 1.4 %collective-permute-start.31 = (bf16[64,640]{1,0:T(8,128)(2,1)S(1)}, bf16[64,640]{1,0:T(8,128)(2,1)S(1)}, u32[]{:S(2)}, u32[]{:S(2)}) collective-permute-start(bf16[64,640]{1,0:T(8,128)(2,1)S(1)} %get-tuple-element.161), channel_id=1, source_target_pairs={{0,8},{8,0},{16,24},{24,16},{1,9},{9,1},{17,25},{25,17},{2,10},{10... | collective-permute-start | bytes 245768 | tf_op jit(solution)/shard_map/ppermute | solution.py:50
  60.1 0.7 collective-permute-start.32
  60.8 1.4 %collective-permute-start.33 = (bf16[64,640]{1,0:T(8,128)(2,1)S(1)}, bf16[64,640]{1,0:T(8,128)(2,1)S(1)}, u32[]{:S(2)}, u32[]{:S(2)}) collective-permute-start(bf16[64,640]{1,0:T(8,128)(2,1)S(1)} %get-tuple-element.163), channel_id=1, source_target_pairs={{0,24},{8,16},{16,8},{24,0},{1,25},{9,17},{17,9},{25,1},{2,26},{10... | collective-permute-start | bytes 245768 | tf_op jit(solution)/shard_map/ppermute | solution.py:50
  62.3 1.9 %collective-permute-done.29.refs_1_ = bf16[64,896]{1,0:T(8,128)(2,1)S(1)} collective-permute-done((bf16[64,896]{1,0:T(8,128)(2,1)S(1)}, bf16[64,896]{1,0:T(8,128)(2,1)S(1)}, u32[]{:S(2)}, u32[]{:S(2)}) %collective-permute-start.29) | collective-permute-done | bytes 114720 | tf_op jit(solution)/shard_map/ppermute | solution.py:50
  64.3 3.1 %coefficients.2.first_ref = f32[64,256]{1,0:T(8,128)S(1)} custom-call(f32[8,128]{1,0:T(8,128)S(1)} %shift.1.shift_ref, f32[64,128]{1,0:T(8,128)S(1)} %get-tuple-element.131.gram_ref.gram0_ref, f32[64,128]{1,0:T(8,128)S(1)} %get-tuple-element.164.gram1_ref), custom_call_target="tpu_custom_call" | custom-call | tf_op jit(solution)/shard_map/coefficients/pallas_call | solution.py:380
  67.4 0.6 combine.3
  68.0 2.3 %collective-permute-start.35 = (bf16[64,640]{1,0:T(8,128)(2,1)S(1)}, bf16[64,640]{1,0:T(8,128)(2,1)S(1)}, u32[]{:S(2)}, u32[]{:S(2)}) collective-permute-start(bf16[64,640]{1,0:T(8,128)(2,1)S(1)} %get-tuple-element.168.refs_0_), channel_id=1, source_target_pairs={{0,4},{1,5},{2,6},{3,7},{4,0},{5,1},{6,2},{7,3},{8,12},{9,13},{10,... | collective-permute-start | bytes 245768 | tf_op jit(solution)/shard_map/ppermute | solution.py:50
  70.3 1.8 %collective-permute-start.39 = (bf16[64,896]{1,0:T(8,128)(2,1)S(1)}, bf16[64,896]{1,0:T(8,128)(2,1)S(1)}, u32[]{:S(2)}, u32[]{:S(2)}) collective-permute-start(bf16[64,896]{1,0:T(8,128)(2,1)S(1)} %get-tuple-element.169.refs_0_.refs_8_), channel_id=1, source_target_pairs={{0,24},{8,16},{16,8},{24,0},{1,25},{9,17},{17,9},{25,1},{2,26},{10... | collective-permute-start | bytes 344072 | tf_op jit(solution)/shard_map/ppermute | solution.py:50
  72.1 1.0 collective-permute-start.38
  73.1 0.7 collective-permute-start.37
  74.3 1.5 %collective-permute-start.36 = (bf16[64,640]{1,0:T(8,128)(2,1)S(1)}, bf16[64,640]{1,0:T(8,128)(2,1)S(1)}, u32[]{:S(2)}, u32[]{:S(2)}) collective-permute-start(bf16[64,640]{1,0:T(8,128)(2,1)S(1)} %collective-permute-done.35.refs_4_), channel_id=1, source_target_pairs={{0,2},{1,3},{2,0},{3,1},{4,6},{5,7},{6,4},{7,5},{8,10},{9,11},{10,... | collective-permute-start | bytes 245768 | tf_op jit(solution)/shard_map/ppermute | solution.py:50
  75.8 1.0 collective-permute-done.39.refs_3_.refs_11_
  76.8 0.8 collective-permute-done.38.refs_2_.refs_10_
  77.9 2.1 %rows_half.5 = (bf16[5,64,640]{2,1,0:T(8,128)(2,1)S(1)}, f32[4,64,640]{2,1,0:T(8,128)S(1)}, f32[64,128]{1,0:T(8,128)S(1)}) custom-call(s32[259]{0:T(512)S(1)} %concatenate.3.table, bf16[96,128,128]{2,1,0:T(8,128)(2,1)S(1)} %get-tuple-element.108.tile_ref, bf16[64,896]{1,0:T(8,128)(2,1)S(1)} %get-tuple-element.169.refs_0_.refs_8_, ...), custom_call_target="tpu_custom_call" | custom-call | tf_op jit(solution)/shard_map/rows_half/pallas_call | solution.py:380
  81.2 0.8 collective-permute-done.41.refs_1_
  82.4 0.6 pair_sums.5
  83.4 2.6 %collective-permute-start.49 = (bf16[64,896]{1,0:T(8,128)(2,1)S(1)}, bf16[64,896]{1,0:T(8,128)(2,1)S(1)}, u32[]{:S(2)}, u32[]{:S(2)}) collective-permute-start(bf16[64,896]{1,0:T(8,128)(2,1)S(1)} %get-tuple-element.191), channel_id=1, source_target_pairs={{0,4},{1,5},{2,6},{3,7},{4,0},{5,1},{6,2},{7,3},{8,12},{9,13},{10,... | collective-permute-start | bytes 344072 | tf_op jit(solution)/shard_map/ppermute | solution.py:50
  86.0 1.5 %collective-permute-start.50 = (bf16[64,896]{1,0:T(8,128)(2,1)S(1)}, bf16[64,896]{1,0:T(8,128)(2,1)S(1)}, u32[]{:S(2)}, u32[]{:S(2)}) collective-permute-start(bf16[64,896]{1,0:T(8,128)(2,1)S(1)} %get-tuple-element.192), channel_id=1, source_target_pairs={{0,6},{1,7},{2,4},{3,5},{4,2},{5,3},{6,0},{7,1},{8,14},{9,15},{10,... | collective-permute-start | bytes 344072 | tf_op jit(solution)/shard_map/ppermute | solution.py:50
  87.5 2.7 %cols_half.5 = (f32[64,640]{1,0:T(8,128)S(1)}, bf16[64,768]{1,0:T(8,128)(2,1)S(1)}, bf16[64,768]{1,0:T(8,128)(2,1)S(1)}, bf16[64,768]{1,0:T(8,128)(2,1)S(1)}, f32[64,64]{1,0:T(8,128)S(1)}) custom-call(s32[259]{0:T(512)S(1)} %concatenate.3.table, bf16[96,128,128]{2,1,0:T(8,128)(2,1)S(1)} %get-tuple-element.106.tile_ref, ...), custom_call_target="tpu_custom_call" | custom-call | tf_op jit(solution)/shard_map/cols_half/pallas_call | solution.py:380
  90.2 1.0 collective-permute-start.45
  91.2 1.0 collective-permute-start.46
  92.2 1.5 %collective-permute-start.47 = (bf16[64,768]{1,0:T(8,128)(2,1)S(1)}, bf16[64,768]{1,0:T(8,128)(2,1)S(1)}, u32[]{:S(2)}, u32[]{:S(2)}) collective-permute-start(bf16[64,768]{1,0:T(8,128)(2,1)S(1)} %get-tuple-element.184), channel_id=1, source_target_pairs={{0,24},{8,16},{16,8},{24,0},{1,25},{9,17},{17,9},{25,1},{2,26},{10... | collective-permute-start | bytes 294920 | tf_op jit(solution)/shard_map/ppermute | solution.py:50
  93.7 1.5 %collective-permute-done.49.refs_1_ = bf16[64,896]{1,0:T(8,128)(2,1)S(1)} collective-permute-done((bf16[64,896]{1,0:T(8,128)(2,1)S(1)}, bf16[64,896]{1,0:T(8,128)(2,1)S(1)}, u32[]{:S(2)}, u32[]{:S(2)}) %collective-permute-start.49) | collective-permute-done | bytes 114720 | tf_op jit(solution)/shard_map/ppermute | solution.py:50
  95.3 3.3 %solve.1.solve_ref = f32[64,128]{1,0:T(8,128)S(1)} custom-call(f32[8,128]{1,0:T(8,128)S(1)} %shift.1.shift_ref, f32[64,128]{1,0:T(8,128)S(1)} %get-tuple-element.131.gram_ref.gram0_ref, f32[64,128]{1,0:T(8,128)S(1)} %get-tuple-element.164.gram1_ref, f32[64,128]{1,0:T(8,128)S(1)} %get-tuple-element.193.gram2_ref, f32[64,256]{1,0:T(8,128)S(1)} %coefficients.2.first_ref), custom_call_target="tpu_custom_call" | custom-call | tf_op jit(solution)/shard_map/solve/pallas_call | solution.py:380
  98.8 2.3 %collective-permute-start.53 = (f32[64,64]{1,0:T(8,128)S(1)}, f32[64,64]{1,0:T(8,128)S(1)}, u32[]{:S(2)}, u32[]{:S(2)}) collective-permute-start(f32[64,64]{1,0:T(8,128)S(1)} %last_gram.1), channel_id=1, source_target_pairs={{0,6},{1,7},{2,4},{3,5},{4,2},{5,3},{6,0},{7,1},{8,14},{9,15},{10,... | collective-permute-start | bytes 49160 | tf_op jit(solution)/shard_map/ppermute | solution.py:50
  101.1 1.2 %collective-permute-start.52 = (f32[64,64]{1,0:T(8,128)S(1)}, f32[64,64]{1,0:T(8,128)S(1)}, u32[]{:S(2)}, u32[]{:S(2)}) collective-permute-start(f32[64,64]{1,0:T(8,128)S(1)} %last_gram.1), channel_id=1, source_target_pairs={{0,4},{1,5},{2,6},{3,7},{4,0},{5,1},{6,2},{7,3},{8,12},{9,13},{10,... | collective-permute-start | bytes 49160 | tf_op jit(solution)/shard_map/ppermute | solution.py:50
  102.3 0.9 collective-permute-start.51
  103.2 2.7 %coefficients.3 = (f32[192,256]{1,0:T(8,128)S(1)}, f32[64,256]{1,0:T(8,128)S(1)}) custom-call(f32[8,128]{1,0:T(8,128)S(1)} %shift.1.shift_ref, f32[64,128]{1,0:T(8,128)S(1)} %get-tuple-element.131.gram_ref.gram0_ref, f32[64,128]{1,0:T(8,128)S(1)} %get-tuple-element.164.gram1_ref, f32[64,128]{1,0:T(8,128)S(1)} %get-tuple-element.193.gram2_ref, ...), custom_call_target="tpu_custom_call" | custom-call | tf_op jit(solution)/shard_map/coefficients/pallas_call | solution.py:380
  106.4 0.8 vectors.1.vectors_ref
  107.5 3.3 %finish.1 = (f32[64,640]{1,0:T(8,128)}, f32[64,640]{1,0:T(8,128)}) custom-call(f32[256,640]{1,0:T(8,128)S(1)} %vectors.1.vectors_ref, f32[64,256]{1,0:T(8,128)S(1)} %get-tuple-element.206.small_ref, f32[64,64]{1,0:T(8,128)S(1)} %add_add_fusion.both_ref, f32[64,64]{1,0:T(8,128)S(1)} %collective-permute-done.54.other_ref, ...), custom_call_target="tpu_custom_call" | custom-call | tf_op jit(solution)/shard_map/finish/pallas_call | solution.py:380
  (92 shorter events, 9.0 us)
Async XLA Ops:
  2.2 10.7 %copy-start.5 = (s32[1,1,32]{2,1,0:T(1,128)S(1)}, s32[1,1,32]{2,1,0:T(1,128)}, u32[]{:S(2)}) copy-start(s32[1,1,32]{2,1,0:T(1,128)} %param.14) | copy-start | bytes 388
  2.2 10.7 %copy-start.6 = (s32[1,1,64]{2,1,0:T(1,128)S(1)}, s32[1,1,64]{2,1,0:T(1,128)}, u32[]{:S(2)}) copy-start(s32[1,1,64]{2,1,0:T(1,128)} %param.19) | copy-start | bytes 772
  2.2 10.7 %copy-start.7 = (s32[1,1,32]{2,1,0:T(1,128)S(1)}, s32[1,1,32]{2,1,0:T(1,128)}, u32[]{:S(2)}) copy-start(s32[1,1,32]{2,1,0:T(1,128)} %param.15) | copy-start | bytes 388
  2.2 10.7 %copy-start.8 = (s32[1,1,64]{2,1,0:T(1,128)S(1)}, s32[1,1,64]{2,1,0:T(1,128)}, u32[]{:S(2)}) copy-start(s32[1,1,64]{2,1,0:T(1,128)} %param.20) | copy-start | bytes 772
  2.2 10.7 %copy-start.9 = (s32[1,1,64]{2,1,0:T(1,128)S(1)}, s32[1,1,64]{2,1,0:T(1,128)}, u32[]{:S(2)}) copy-start(s32[1,1,64]{2,1,0:T(1,128)} %param.21) | copy-start | bytes 772
  2.3 10.8 %copy-start = (bf16[1,1,32,128,128]{4,3,2,1,0:T(8,128)(2,1)S(1)}, bf16[1,1,32,128,128]{4,3,2,1,0:T(8,128)(2,1)}, u32[]{:S(2)}) copy-start(bf16[1,1,32,128,128]{4,3,2,1,0:T(8,128)(2,1)} %param.13) | copy-start | bytes 3145732
  2.3 10.8 %copy-start.3 = (bf16[1,1,64,32,128]{4,3,2,1,0:T(8,128)(2,1)S(1)}, bf16[1,1,64,32,128]{4,3,2,1,0:T(8,128)(2,1)}, u32[]{:S(2)}) copy-start(bf16[1,1,64,32,128]{4,3,2,1,0:T(8,128)(2,1)} %param.17) | copy-start | bytes 1572868
  2.3 10.8 %copy-start.4 = (bf16[1,1,64,32,128]{4,3,2,1,0:T(8,128)(2,1)S(1)}, bf16[1,1,64,32,128]{4,3,2,1,0:T(8,128)(2,1)}, u32[]{:S(2)}) copy-start(bf16[1,1,64,32,128]{4,3,2,1,0:T(8,128)(2,1)} %param.18) | copy-start | bytes 1572868
  2.6 9.2 %collective-permute-start.1 = (bf16[64,640]{1,0:T(8,128)(2,1)S(1)}, bf16[64,640]{1,0:T(8,128)(2,1)S(1)}, u32[]{:S(2)}, u32[]{:S(2)}) collective-permute-start(bf16[64,640]{1,0:T(8,128)(2,1)S(1)} %get-tuple-element.107.refs_0_), channel_id=1, source_target_pairs={{0,4},{1,5},{2,6},{3,7},{4,0},{5,1},{6,2},{7,3},{8,12},{9,13},{10,... | collective-permute-start | bytes 245768 | tf_op jit(solution)/shard_map/ppermute | solution.py:50
  6.7 9.6 %collective-permute-start.5 = (bf16[64,896]{1,0:T(8,128)(2,1)S(1)}, bf16[64,896]{1,0:T(8,128)(2,1)S(1)}, u32[]{:S(2)}, u32[]{:S(2)}) collective-permute-start(bf16[64,896]{1,0:T(8,128)(2,1)S(1)} %get-tuple-element.109.refs_0_), channel_id=1, source_target_pairs={{0,24},{8,16},{16,8},{24,0},{1,25},{9,17},{17,9},{25,1},{2,26},{10... | collective-permute-start | bytes 344072 | tf_op jit(solution)/shard_map/ppermute | solution.py:50
  9.2 7.2 %collective-permute-start.4 = (bf16[64,896]{1,0:T(8,128)(2,1)S(1)}, bf16[64,896]{1,0:T(8,128)(2,1)S(1)}, u32[]{:S(2)}, u32[]{:S(2)}) collective-permute-start(bf16[64,896]{1,0:T(8,128)(2,1)S(1)} %get-tuple-element.109.refs_0_), channel_id=1, source_target_pairs={{0,16},{8,24},{16,0},{24,8},{1,17},{9,25},{17,1},{25,9},{2,18},{10... | collective-permute-start | bytes 344072 | tf_op jit(solution)/shard_map/ppermute | solution.py:50
  9.7 6.7 %collective-permute-start.3 = (bf16[64,896]{1,0:T(8,128)(2,1)S(1)}, bf16[64,896]{1,0:T(8,128)(2,1)S(1)}, u32[]{:S(2)}, u32[]{:S(2)}) collective-permute-start(bf16[64,896]{1,0:T(8,128)(2,1)S(1)} %get-tuple-element.109.refs_0_), channel_id=1, source_target_pairs={{0,8},{8,0},{16,24},{24,16},{1,9},{9,1},{17,25},{25,17},{2,10},{10... | collective-permute-start | bytes 344072 | tf_op jit(solution)/shard_map/ppermute | solution.py:50
  10.2 8.2 %collective-permute-start = (bf16[64,640]{1,0:T(8,128)(2,1)S(1)}, bf16[64,640]{1,0:T(8,128)(2,1)S(1)}, u32[]{:S(2)}, u32[]{:S(2)}) collective-permute-start(bf16[64,640]{1,0:T(8,128)(2,1)S(1)} %get-tuple-element.107.refs_0_), channel_id=1, source_target_pairs={{0,2},{1,3},{2,0},{3,1},{4,6},{5,7},{6,4},{7,5},{8,10},{9,11},{10,... | collective-permute-start | bytes 245768 | tf_op jit(solution)/shard_map/ppermute | solution.py:50
  11.8 6.7 %collective-permute-start.2 = (bf16[64,640]{1,0:T(8,128)(2,1)S(1)}, bf16[64,640]{1,0:T(8,128)(2,1)S(1)}, u32[]{:S(2)}, u32[]{:S(2)}) collective-permute-start(bf16[64,640]{1,0:T(8,128)(2,1)S(1)} %collective-permute-done.1.refs_4_), channel_id=1, source_target_pairs={{0,2},{1,3},{2,0},{3,1},{4,6},{5,7},{6,4},{7,5},{8,10},{9,11},{10,... | collective-permute-start | bytes 245768 | tf_op jit(solution)/shard_map/ppermute | solution.py:50
  18.5 2.4 %collective-permute-start.6 = (bf16[5,64,640]{2,1,0:T(8,128)(2,1)S(1)}, bf16[5,64,640]{2,1,0:T(8,128)(2,1)S(1)}, u32[]{:S(2)}, u32[]{:S(2)}) collective-permute-start(bf16[5,64,640]{2,1,0:T(8,128)(2,1)S(1)} %get-tuple-element.112), channel_id=1, source_target_pairs={{0,1},{1,0},{2,3},{3,2},{4,5},{5,4},{6,7},{7,6},{8,9},{9,8},{10,11... | collective-permute-start | bytes 1228808 | tf_op jit(solution)/shard_map/ppermute | solution.py:50
  18.5 1.9 %collective-permute-start.7 = (bf16[64,640]{1,0:T(8,128)(2,1)S(1)}, bf16[64,640]{1,0:T(8,128)(2,1)S(1)}, u32[]{:S(2)}, u32[]{:S(2)}) collective-permute-start(bf16[64,640]{1,0:T(8,128)(2,1)S(1)} %get-tuple-element.107.refs_0_), channel_id=1, source_target_pairs={{0,1},{1,0},{2,3},{3,2},{4,5},{5,4},{6,7},{7,6},{8,9},{9,8},{10,11... | collective-permute-start | bytes 245768 | tf_op jit(solution)/shard_map/ppermute | solution.py:50
  19.0 1.5 %collective-permute-start.8 = (bf16[64,640]{1,0:T(8,128)(2,1)S(1)}, bf16[64,640]{1,0:T(8,128)(2,1)S(1)}, u32[]{:S(2)}, u32[]{:S(2)}) collective-permute-start(bf16[64,640]{1,0:T(8,128)(2,1)S(1)} %collective-permute-done.refs_2_), channel_id=1, source_target_pairs={{0,1},{1,0},{2,3},{3,2},{4,5},{5,4},{6,7},{7,6},{8,9},{9,8},{10,11... | collective-permute-start | bytes 245768 | tf_op jit(solution)/shard_map/ppermute | solution.py:50
  19.1 1.5 %collective-permute-start.9 = (bf16[64,640]{1,0:T(8,128)(2,1)S(1)}, bf16[64,640]{1,0:T(8,128)(2,1)S(1)}, u32[]{:S(2)}, u32[]{:S(2)}) collective-permute-start(bf16[64,640]{1,0:T(8,128)(2,1)S(1)} %collective-permute-done.1.refs_4_), channel_id=1, source_target_pairs={{0,1},{1,0},{2,3},{3,2},{4,5},{5,4},{6,7},{7,6},{8,9},{9,8},{10,11... | collective-permute-start | bytes 245768 | tf_op jit(solution)/shard_map/ppermute | solution.py:50
  19.6 1.3 %collective-permute-start.10 = (bf16[64,640]{1,0:T(8,128)(2,1)S(1)}, bf16[64,640]{1,0:T(8,128)(2,1)S(1)}, u32[]{:S(2)}, u32[]{:S(2)}) collective-permute-start(bf16[64,640]{1,0:T(8,128)(2,1)S(1)} %collective-permute-done.2.refs_6_), channel_id=1, source_target_pairs={{0,1},{1,0},{2,3},{3,2},{4,5},{5,4},{6,7},{7,6},{8,9},{9,8},{10,11... | collective-permute-start | bytes 245768 | tf_op jit(solution)/shard_map/ppermute | solution.py:50
  21.5 9.6 %collective-permute-start.14 = (bf16[64,896]{1,0:T(8,128)(2,1)S(1)}, bf16[64,896]{1,0:T(8,128)(2,1)S(1)}, u32[]{:S(2)}, u32[]{:S(2)}) collective-permute-start(bf16[64,896]{1,0:T(8,128)(2,1)S(1)} %get-tuple-element.128), channel_id=1, source_target_pairs={{0,2},{1,3},{2,0},{3,1},{4,6},{5,7},{6,4},{7,5},{8,10},{9,11},{10,... | collective-permute-start | bytes 344072 | tf_op jit(solution)/shard_map/ppermute | solution.py:50
  23.1 11.7 %collective-permute-start.15 = (bf16[64,896]{1,0:T(8,128)(2,1)S(1)}, bf16[64,896]{1,0:T(8,128)(2,1)S(1)}, u32[]{:S(2)}, u32[]{:S(2)}) collective-permute-start(bf16[64,896]{1,0:T(8,128)(2,1)S(1)} %get-tuple-element.129), channel_id=1, source_target_pairs={{0,4},{1,5},{2,6},{3,7},{4,0},{5,1},{6,2},{7,3},{8,12},{9,13},{10,... | collective-permute-start | bytes 344072 | tf_op jit(solution)/shard_map/ppermute | solution.py:50
  24.5 10.3 %collective-permute-start.16 = (bf16[64,896]{1,0:T(8,128)(2,1)S(1)}, bf16[64,896]{1,0:T(8,128)(2,1)S(1)}, u32[]{:S(2)}, u32[]{:S(2)}) collective-permute-start(bf16[64,896]{1,0:T(8,128)(2,1)S(1)} %get-tuple-element.130), channel_id=1, source_target_pairs={{0,6},{1,7},{2,4},{3,5},{4,2},{5,3},{6,0},{7,1},{8,14},{9,15},{10,... | collective-permute-start | bytes 344072 | tf_op jit(solution)/shard_map/ppermute | solution.py:50
  25.9 10.5 %copy-start.2 = (f32[64,640]{1,0:T(8,128)S(1)}, f32[64,640]{1,0:T(8,128)}, u32[]{:S(2)}) copy-start(f32[64,640]{1,0:T(8,128)} %b_ref.1) | copy-start | bytes 491524
  28.0 7.1 %collective-permute-start.11 = (bf16[64,640]{1,0:T(8,128)(2,1)S(1)}, bf16[64,640]{1,0:T(8,128)(2,1)S(1)}, u32[]{:S(2)}, u32[]{:S(2)}) collective-permute-start(bf16[64,640]{1,0:T(8,128)(2,1)S(1)} %get-tuple-element.120), channel_id=1, source_target_pairs={{0,8},{8,0},{16,24},{24,16},{1,9},{9,1},{17,25},{25,17},{2,10},{10... | collective-permute-start | bytes 245768 | tf_op jit(solution)/shard_map/ppermute | solution.py:50
  29.5 5.6 %collective-permute-start.12 = (bf16[64,640]{1,0:T(8,128)(2,1)S(1)}, bf16[64,640]{1,0:T(8,128)(2,1)S(1)}, u32[]{:S(2)}, u32[]{:S(2)}) collective-permute-start(bf16[64,640]{1,0:T(8,128)(2,1)S(1)} %get-tuple-element.121), channel_id=1, source_target_pairs={{0,16},{8,24},{16,0},{24,8},{1,17},{9,25},{17,1},{25,9},{2,18},{10... | collective-permute-start | bytes 245768 | tf_op jit(solution)/shard_map/ppermute | solution.py:50
  31.1 5.3 %collective-permute-start.13 = (bf16[64,640]{1,0:T(8,128)(2,1)S(1)}, bf16[64,640]{1,0:T(8,128)(2,1)S(1)}, u32[]{:S(2)}, u32[]{:S(2)}) collective-permute-start(bf16[64,640]{1,0:T(8,128)(2,1)S(1)} %get-tuple-element.122), channel_id=1, source_target_pairs={{0,24},{8,16},{16,8},{24,0},{1,25},{9,17},{17,9},{25,1},{2,26},{10... | collective-permute-start | bytes 245768 | tf_op jit(solution)/shard_map/ppermute | solution.py:50
  37.0 6.5 %collective-permute-start.18 = (bf16[64,640]{1,0:T(8,128)(2,1)S(1)}, bf16[64,640]{1,0:T(8,128)(2,1)S(1)}, u32[]{:S(2)}, u32[]{:S(2)}) collective-permute-start(bf16[64,640]{1,0:T(8,128)(2,1)S(1)} %get-tuple-element.139.refs_0_), channel_id=1, source_target_pairs={{0,4},{1,5},{2,6},{3,7},{4,0},{5,1},{6,2},{7,3},{8,12},{9,13},{10,... | collective-permute-start | bytes 245768 | tf_op jit(solution)/shard_map/ppermute | solution.py:50
  39.2 6.2 %collective-permute-start.22 = (bf16[64,896]{1,0:T(8,128)(2,1)S(1)}, bf16[64,896]{1,0:T(8,128)(2,1)S(1)}, u32[]{:S(2)}, u32[]{:S(2)}) collective-permute-start(bf16[64,896]{1,0:T(8,128)(2,1)S(1)} %get-tuple-element.140.refs_0_), channel_id=1, source_target_pairs={{0,24},{8,16},{16,8},{24,0},{1,25},{9,17},{17,9},{25,1},{2,26},{10... | collective-permute-start | bytes 344072 | tf_op jit(solution)/shard_map/ppermute | solution.py:50
  41.6 5.2 %collective-permute-start.21 = (bf16[64,896]{1,0:T(8,128)(2,1)S(1)}, bf16[64,896]{1,0:T(8,128)(2,1)S(1)}, u32[]{:S(2)}, u32[]{:S(2)}) collective-permute-start(bf16[64,896]{1,0:T(8,128)(2,1)S(1)} %get-tuple-element.140.refs_0_), channel_id=1, source_target_pairs={{0,16},{8,24},{16,0},{24,8},{1,17},{9,25},{17,1},{25,9},{2,18},{10... | collective-permute-start | bytes 344072 | tf_op jit(solution)/shard_map/ppermute | solution.py:50
  42.1 5.0 %collective-permute-start.20 = (bf16[64,896]{1,0:T(8,128)(2,1)S(1)}, bf16[64,896]{1,0:T(8,128)(2,1)S(1)}, u32[]{:S(2)}, u32[]{:S(2)}) collective-permute-start(bf16[64,896]{1,0:T(8,128)(2,1)S(1)} %get-tuple-element.140.refs_0_), channel_id=1, source_target_pairs={{0,8},{8,0},{16,24},{24,16},{1,9},{9,1},{17,25},{25,17},{2,10},{10... | collective-permute-start | bytes 344072 | tf_op jit(solution)/shard_map/ppermute | solution.py:50
  42.7 6.5 %collective-permute-start.17 = (bf16[64,640]{1,0:T(8,128)(2,1)S(1)}, bf16[64,640]{1,0:T(8,128)(2,1)S(1)}, u32[]{:S(2)}, u32[]{:S(2)}) collective-permute-start(bf16[64,640]{1,0:T(8,128)(2,1)S(1)} %get-tuple-element.139.refs_0_), channel_id=1, source_target_pairs={{0,2},{1,3},{2,0},{3,1},{4,6},{5,7},{6,4},{7,5},{8,10},{9,11},{10,... | collective-permute-start | bytes 245768 | tf_op jit(solution)/shard_map/ppermute | solution.py:50
  43.5 5.7 %collective-permute-start.19 = (bf16[64,640]{1,0:T(8,128)(2,1)S(1)}, bf16[64,640]{1,0:T(8,128)(2,1)S(1)}, u32[]{:S(2)}, u32[]{:S(2)}) collective-permute-start(bf16[64,640]{1,0:T(8,128)(2,1)S(1)} %collective-permute-done.18.refs_4_), channel_id=1, source_target_pairs={{0,2},{1,3},{2,0},{3,1},{4,6},{5,7},{6,4},{7,5},{8,10},{9,11},{10,... | collective-permute-start | bytes 245768 | tf_op jit(solution)/shard_map/ppermute | solution.py:50
  49.2 2.4 %collective-permute-start.23 = (bf16[5,64,640]{2,1,0:T(8,128)(2,1)S(1)}, bf16[5,64,640]{2,1,0:T(8,128)(2,1)S(1)}, u32[]{:S(2)}, u32[]{:S(2)}) collective-permute-start(bf16[5,64,640]{2,1,0:T(8,128)(2,1)S(1)} %get-tuple-element.145), channel_id=1, source_target_pairs={{0,1},{1,0},{2,3},{3,2},{4,5},{5,4},{6,7},{7,6},{8,9},{9,8},{10,11... | collective-permute-start | bytes 1228808 | tf_op jit(solution)/shard_map/ppermute | solution.py:50
  49.3 1.9 %collective-permute-start.24 = (bf16[64,640]{1,0:T(8,128)(2,1)S(1)}, bf16[64,640]{1,0:T(8,128)(2,1)S(1)}, u32[]{:S(2)}, u32[]{:S(2)}) collective-permute-start(bf16[64,640]{1,0:T(8,128)(2,1)S(1)} %get-tuple-element.139.refs_0_), channel_id=1, source_target_pairs={{0,1},{1,0},{2,3},{3,2},{4,5},{5,4},{6,7},{7,6},{8,9},{9,8},{10,11... | collective-permute-start | bytes 245768 | tf_op jit(solution)/shard_map/ppermute | solution.py:50
  49.8 1.5 %collective-permute-start.25 = (bf16[64,640]{1,0:T(8,128)(2,1)S(1)}, bf16[64,640]{1,0:T(8,128)(2,1)S(1)}, u32[]{:S(2)}, u32[]{:S(2)}) collective-permute-start(bf16[64,640]{1,0:T(8,128)(2,1)S(1)} %collective-permute-done.17.refs_2_), channel_id=1, source_target_pairs={{0,1},{1,0},{2,3},{3,2},{4,5},{5,4},{6,7},{7,6},{8,9},{9,8},{10,11... | collective-permute-start | bytes 245768 | tf_op jit(solution)/shard_map/ppermute | solution.py:50
  49.9 1.5 %collective-permute-start.26 = (bf16[64,640]{1,0:T(8,128)(2,1)S(1)}, bf16[64,640]{1,0:T(8,128)(2,1)S(1)}, u32[]{:S(2)}, u32[]{:S(2)}) collective-permute-start(bf16[64,640]{1,0:T(8,128)(2,1)S(1)} %collective-permute-done.18.refs_4_), channel_id=1, source_target_pairs={{0,1},{1,0},{2,3},{3,2},{4,5},{5,4},{6,7},{7,6},{8,9},{9,8},{10,11... | collective-permute-start | bytes 245768 | tf_op jit(solution)/shard_map/ppermute | solution.py:50
  50.3 1.3 %collective-permute-start.27 = (bf16[64,640]{1,0:T(8,128)(2,1)S(1)}, bf16[64,640]{1,0:T(8,128)(2,1)S(1)}, u32[]{:S(2)}, u32[]{:S(2)}) collective-permute-start(bf16[64,640]{1,0:T(8,128)(2,1)S(1)} %collective-permute-done.19.refs_6_), channel_id=1, source_target_pairs={{0,1},{1,0},{2,3},{3,2},{4,5},{5,4},{6,7},{7,6},{8,9},{9,8},{10,11... | collective-permute-start | bytes 245768 | tf_op jit(solution)/shard_map/ppermute | solution.py:50
  52.2 8.6 %collective-permute-start.28 = (bf16[64,896]{1,0:T(8,128)(2,1)S(1)}, bf16[64,896]{1,0:T(8,128)(2,1)S(1)}, u32[]{:S(2)}, u32[]{:S(2)}) collective-permute-start(bf16[64,896]{1,0:T(8,128)(2,1)S(1)} %get-tuple-element.152), channel_id=1, source_target_pairs={{0,2},{1,3},{2,0},{3,1},{4,6},{5,7},{6,4},{7,5},{8,10},{9,11},{10,... | collective-permute-start | bytes 344072 | tf_op jit(solution)/shard_map/ppermute | solution.py:50
  52.3 11.9 %collective-permute-start.29 = (bf16[64,896]{1,0:T(8,128)(2,1)S(1)}, bf16[64,896]{1,0:T(8,128)(2,1)S(1)}, u32[]{:S(2)}, u32[]{:S(2)}) collective-permute-start(bf16[64,896]{1,0:T(8,128)(2,1)S(1)} %get-tuple-element.153), channel_id=1, source_target_pairs={{0,4},{1,5},{2,6},{3,7},{4,0},{5,1},{6,2},{7,3},{8,12},{9,13},{10,... | collective-permute-start | bytes 344072 | tf_op jit(solution)/shard_map/ppermute | solution.py:50
  53.8 10.4 %collective-permute-start.30 = (bf16[64,896]{1,0:T(8,128)(2,1)S(1)}, bf16[64,896]{1,0:T(8,128)(2,1)S(1)}, u32[]{:S(2)}, u32[]{:S(2)}) collective-permute-start(bf16[64,896]{1,0:T(8,128)(2,1)S(1)} %get-tuple-element.154), channel_id=1, source_target_pairs={{0,6},{1,7},{2,4},{3,5},{4,2},{5,3},{6,0},{7,1},{8,14},{9,15},{10,... | collective-permute-start | bytes 344072 | tf_op jit(solution)/shard_map/ppermute | solution.py:50
  58.7 8.6 %collective-permute-start.31 = (bf16[64,640]{1,0:T(8,128)(2,1)S(1)}, bf16[64,640]{1,0:T(8,128)(2,1)S(1)}, u32[]{:S(2)}, u32[]{:S(2)}) collective-permute-start(bf16[64,640]{1,0:T(8,128)(2,1)S(1)} %get-tuple-element.161), channel_id=1, source_target_pairs={{0,8},{8,0},{16,24},{24,16},{1,9},{9,1},{17,25},{25,17},{2,10},{10... | collective-permute-start | bytes 245768 | tf_op jit(solution)/shard_map/ppermute | solution.py:50
  60.1 7.3 %collective-permute-start.32 = (bf16[64,640]{1,0:T(8,128)(2,1)S(1)}, bf16[64,640]{1,0:T(8,128)(2,1)S(1)}, u32[]{:S(2)}, u32[]{:S(2)}) collective-permute-start(bf16[64,640]{1,0:T(8,128)(2,1)S(1)} %get-tuple-element.162), channel_id=1, source_target_pairs={{0,16},{8,24},{16,0},{24,8},{1,17},{9,25},{17,1},{25,9},{2,18},{10... | collective-permute-start | bytes 245768 | tf_op jit(solution)/shard_map/ppermute | solution.py:50
  60.8 6.5 %collective-permute-start.33 = (bf16[64,640]{1,0:T(8,128)(2,1)S(1)}, bf16[64,640]{1,0:T(8,128)(2,1)S(1)}, u32[]{:S(2)}, u32[]{:S(2)}) collective-permute-start(bf16[64,640]{1,0:T(8,128)(2,1)S(1)} %get-tuple-element.163), channel_id=1, source_target_pairs={{0,24},{8,16},{16,8},{24,0},{1,25},{9,17},{17,9},{25,1},{2,26},{10... | collective-permute-start | bytes 245768 | tf_op jit(solution)/shard_map/ppermute | solution.py:50
  68.0 6.3 %collective-permute-start.35 = (bf16[64,640]{1,0:T(8,128)(2,1)S(1)}, bf16[64,640]{1,0:T(8,128)(2,1)S(1)}, u32[]{:S(2)}, u32[]{:S(2)}) collective-permute-start(bf16[64,640]{1,0:T(8,128)(2,1)S(1)} %get-tuple-element.168.refs_0_), channel_id=1, source_target_pairs={{0,4},{1,5},{2,6},{3,7},{4,0},{5,1},{6,2},{7,3},{8,12},{9,13},{10,... | collective-permute-start | bytes 245768 | tf_op jit(solution)/shard_map/ppermute | solution.py:50
  70.3 6.5 %collective-permute-start.39 = (bf16[64,896]{1,0:T(8,128)(2,1)S(1)}, bf16[64,896]{1,0:T(8,128)(2,1)S(1)}, u32[]{:S(2)}, u32[]{:S(2)}) collective-permute-start(bf16[64,896]{1,0:T(8,128)(2,1)S(1)} %get-tuple-element.169.refs_0_.refs_8_), channel_id=1, source_target_pairs={{0,24},{8,16},{16,8},{24,0},{1,25},{9,17},{17,9},{25,1},{2,26},{10... | collective-permute-start | bytes 344072 | tf_op jit(solution)/shard_map/ppermute | solution.py:50
  72.1 5.5 %collective-permute-start.38 = (bf16[64,896]{1,0:T(8,128)(2,1)S(1)}, bf16[64,896]{1,0:T(8,128)(2,1)S(1)}, u32[]{:S(2)}, u32[]{:S(2)}) collective-permute-start(bf16[64,896]{1,0:T(8,128)(2,1)S(1)} %get-tuple-element.169.refs_0_.refs_8_), channel_id=1, source_target_pairs={{0,16},{8,24},{16,0},{24,8},{1,17},{9,25},{17,1},{25,9},{2,18},{10... | collective-permute-start | bytes 344072 | tf_op jit(solution)/shard_map/ppermute | solution.py:50
  73.1 4.8 %collective-permute-start.37 = (bf16[64,896]{1,0:T(8,128)(2,1)S(1)}, bf16[64,896]{1,0:T(8,128)(2,1)S(1)}, u32[]{:S(2)}, u32[]{:S(2)}) collective-permute-start(bf16[64,896]{1,0:T(8,128)(2,1)S(1)} %get-tuple-element.169.refs_0_.refs_8_), channel_id=1, source_target_pairs={{0,8},{8,0},{16,24},{24,16},{1,9},{9,1},{17,25},{25,17},{2,10},{10... | collective-permute-start | bytes 344072 | tf_op jit(solution)/shard_map/ppermute | solution.py:50
  73.8 6.2 %collective-permute-start.34 = (bf16[64,640]{1,0:T(8,128)(2,1)S(1)}, bf16[64,640]{1,0:T(8,128)(2,1)S(1)}, u32[]{:S(2)}, u32[]{:S(2)}) collective-permute-start(bf16[64,640]{1,0:T(8,128)(2,1)S(1)} %get-tuple-element.168.refs_0_), channel_id=1, source_target_pairs={{0,2},{1,3},{2,0},{3,1},{4,6},{5,7},{6,4},{7,5},{8,10},{9,11},{10,... | collective-permute-start | bytes 245768 | tf_op jit(solution)/shard_map/ppermute | solution.py:50
  74.3 5.7 %collective-permute-start.36 = (bf16[64,640]{1,0:T(8,128)(2,1)S(1)}, bf16[64,640]{1,0:T(8,128)(2,1)S(1)}, u32[]{:S(2)}, u32[]{:S(2)}) collective-permute-start(bf16[64,640]{1,0:T(8,128)(2,1)S(1)} %collective-permute-done.35.refs_4_), channel_id=1, source_target_pairs={{0,2},{1,3},{2,0},{3,1},{4,6},{5,7},{6,4},{7,5},{8,10},{9,11},{10,... | collective-permute-start | bytes 245768 | tf_op jit(solution)/shard_map/ppermute | solution.py:50
  80.0 2.4 %collective-permute-start.40 = (bf16[5,64,640]{2,1,0:T(8,128)(2,1)S(1)}, bf16[5,64,640]{2,1,0:T(8,128)(2,1)S(1)}, u32[]{:S(2)}, u32[]{:S(2)}) collective-permute-start(bf16[5,64,640]{2,1,0:T(8,128)(2,1)S(1)} %get-tuple-element.172), channel_id=1, source_target_pairs={{0,1},{1,0},{2,3},{3,2},{4,5},{5,4},{6,7},{7,6},{8,9},{9,8},{10,11... | collective-permute-start | bytes 1228808 | tf_op jit(solution)/shard_map/ppermute | solution.py:50
  80.1 1.9 %collective-permute-start.41 = (bf16[64,640]{1,0:T(8,128)(2,1)S(1)}, bf16[64,640]{1,0:T(8,128)(2,1)S(1)}, u32[]{:S(2)}, u32[]{:S(2)}) collective-permute-start(bf16[64,640]{1,0:T(8,128)(2,1)S(1)} %get-tuple-element.168.refs_0_), channel_id=1, source_target_pairs={{0,1},{1,0},{2,3},{3,2},{4,5},{5,4},{6,7},{7,6},{8,9},{9,8},{10,11... | collective-permute-start | bytes 245768 | tf_op jit(solution)/shard_map/ppermute | solution.py:50
  80.6 1.5 %collective-permute-start.42 = (bf16[64,640]{1,0:T(8,128)(2,1)S(1)}, bf16[64,640]{1,0:T(8,128)(2,1)S(1)}, u32[]{:S(2)}, u32[]{:S(2)}) collective-permute-start(bf16[64,640]{1,0:T(8,128)(2,1)S(1)} %collective-permute-done.34.refs_2_), channel_id=1, source_target_pairs={{0,1},{1,0},{2,3},{3,2},{4,5},{5,4},{6,7},{7,6},{8,9},{9,8},{10,11... | collective-permute-start | bytes 245768 | tf_op jit(solution)/shard_map/ppermute | solution.py:50
  80.7 1.5 %collective-permute-start.43 = (bf16[64,640]{1,0:T(8,128)(2,1)S(1)}, bf16[64,640]{1,0:T(8,128)(2,1)S(1)}, u32[]{:S(2)}, u32[]{:S(2)}) collective-permute-start(bf16[64,640]{1,0:T(8,128)(2,1)S(1)} %collective-permute-done.35.refs_4_), channel_id=1, source_target_pairs={{0,1},{1,0},{2,3},{3,2},{4,5},{5,4},{6,7},{7,6},{8,9},{9,8},{10,11... | collective-permute-start | bytes 245768 | tf_op jit(solution)/shard_map/ppermute | solution.py:50
  81.1 1.3 %collective-permute-start.44 = (bf16[64,640]{1,0:T(8,128)(2,1)S(1)}, bf16[64,640]{1,0:T(8,128)(2,1)S(1)}, u32[]{:S(2)}, u32[]{:S(2)}) collective-permute-start(bf16[64,640]{1,0:T(8,128)(2,1)S(1)} %collective-permute-done.36.refs_6_), channel_id=1, source_target_pairs={{0,1},{1,0},{2,3},{3,2},{4,5},{5,4},{6,7},{7,6},{8,9},{9,8},{10,11... | collective-permute-start | bytes 245768 | tf_op jit(solution)/shard_map/ppermute | solution.py:50
  83.0 9.2 %collective-permute-start.48 = (bf16[64,896]{1,0:T(8,128)(2,1)S(1)}, bf16[64,896]{1,0:T(8,128)(2,1)S(1)}, u32[]{:S(2)}, u32[]{:S(2)}) collective-permute-start(bf16[64,896]{1,0:T(8,128)(2,1)S(1)} %get-tuple-element.190), channel_id=1, source_target_pairs={{0,2},{1,3},{2,0},{3,1},{4,6},{5,7},{6,4},{7,5},{8,10},{9,11},{10,... | collective-permute-start | bytes 344072 | tf_op jit(solution)/shard_map/ppermute | solution.py:50
  83.4 11.8 %collective-permute-start.49 = (bf16[64,896]{1,0:T(8,128)(2,1)S(1)}, bf16[64,896]{1,0:T(8,128)(2,1)S(1)}, u32[]{:S(2)}, u32[]{:S(2)}) collective-permute-start(bf16[64,896]{1,0:T(8,128)(2,1)S(1)} %get-tuple-element.191), channel_id=1, source_target_pairs={{0,4},{1,5},{2,6},{3,7},{4,0},{5,1},{6,2},{7,3},{8,12},{9,13},{10,... | collective-permute-start | bytes 344072 | tf_op jit(solution)/shard_map/ppermute | solution.py:50
  86.0 9.2 %collective-permute-start.50 = (bf16[64,896]{1,0:T(8,128)(2,1)S(1)}, bf16[64,896]{1,0:T(8,128)(2,1)S(1)}, u32[]{:S(2)}, u32[]{:S(2)}) collective-permute-start(bf16[64,896]{1,0:T(8,128)(2,1)S(1)} %get-tuple-element.192), channel_id=1, source_target_pairs={{0,6},{1,7},{2,4},{3,5},{4,2},{5,3},{6,0},{7,1},{8,14},{9,15},{10,... | collective-permute-start | bytes 344072 | tf_op jit(solution)/shard_map/ppermute | solution.py:50
  90.2 8.4 %collective-permute-start.45 = (bf16[64,768]{1,0:T(8,128)(2,1)S(1)}, bf16[64,768]{1,0:T(8,128)(2,1)S(1)}, u32[]{:S(2)}, u32[]{:S(2)}) collective-permute-start(bf16[64,768]{1,0:T(8,128)(2,1)S(1)} %get-tuple-element.182), channel_id=1, source_target_pairs={{0,8},{8,0},{16,24},{24,16},{1,9},{9,1},{17,25},{25,17},{2,10},{10... | collective-permute-start | bytes 294920 | tf_op jit(solution)/shard_map/ppermute | solution.py:50
  91.2 7.4 %collective-permute-start.46 = (bf16[64,768]{1,0:T(8,128)(2,1)S(1)}, bf16[64,768]{1,0:T(8,128)(2,1)S(1)}, u32[]{:S(2)}, u32[]{:S(2)}) collective-permute-start(bf16[64,768]{1,0:T(8,128)(2,1)S(1)} %get-tuple-element.183), channel_id=1, source_target_pairs={{0,16},{8,24},{16,0},{24,8},{1,17},{9,25},{17,1},{25,9},{2,18},{10... | collective-permute-start | bytes 294920 | tf_op jit(solution)/shard_map/ppermute | solution.py:50
  92.2 6.4 %collective-permute-start.47 = (bf16[64,768]{1,0:T(8,128)(2,1)S(1)}, bf16[64,768]{1,0:T(8,128)(2,1)S(1)}, u32[]{:S(2)}, u32[]{:S(2)}) collective-permute-start(bf16[64,768]{1,0:T(8,128)(2,1)S(1)} %get-tuple-element.184), channel_id=1, source_target_pairs={{0,24},{8,16},{16,8},{24,0},{1,25},{9,17},{17,9},{25,1},{2,26},{10... | collective-permute-start | bytes 294920 | tf_op jit(solution)/shard_map/ppermute | solution.py:50
  98.8 7.2 %collective-permute-start.53 = (f32[64,64]{1,0:T(8,128)S(1)}, f32[64,64]{1,0:T(8,128)S(1)}, u32[]{:S(2)}, u32[]{:S(2)}) collective-permute-start(f32[64,64]{1,0:T(8,128)S(1)} %last_gram.1), channel_id=1, source_target_pairs={{0,6},{1,7},{2,4},{3,5},{4,2},{5,3},{6,0},{7,1},{8,14},{9,15},{10,... | collective-permute-start | bytes 49160 | tf_op jit(solution)/shard_map/ppermute | solution.py:50
  101.1 4.8 %collective-permute-start.52 = (f32[64,64]{1,0:T(8,128)S(1)}, f32[64,64]{1,0:T(8,128)S(1)}, u32[]{:S(2)}, u32[]{:S(2)}) collective-permute-start(f32[64,64]{1,0:T(8,128)S(1)} %last_gram.1), channel_id=1, source_target_pairs={{0,4},{1,5},{2,6},{3,7},{4,0},{5,1},{6,2},{7,3},{8,12},{9,13},{10,... | collective-permute-start | bytes 49160 | tf_op jit(solution)/shard_map/ppermute | solution.py:50
  102.3 4.0 %collective-permute-start.51 = (f32[64,64]{1,0:T(8,128)S(1)}, f32[64,64]{1,0:T(8,128)S(1)}, u32[]{:S(2)}, u32[]{:S(2)}) collective-permute-start(f32[64,64]{1,0:T(8,128)S(1)} %last_gram.1), channel_id=1, source_target_pairs={{0,2},{1,3},{2,0},{3,1},{4,6},{5,7},{6,4},{7,5},{8,10},{9,11},{10,... | collective-permute-start | bytes 49160 | tf_op jit(solution)/shard_map/ppermute | solution.py:50
  106.3 1.3 %collective-permute-start.54 = (f32[64,64]{1,0:T(8,128)S(1)}, f32[64,64]{1,0:T(8,128)S(1)}, u32[]{:S(2)}, u32[]{:S(2)}) collective-permute-start(f32[64,64]{1,0:T(8,128)S(1)} %add_add_fusion.both_ref), channel_id=1, source_target_pairs={{0,1},{1,0},{2,3},{3,2},{4,5},{5,4},{6,7},{7,6},{8,9},{9,8},{10,11... | collective-permute-start | bytes 49160 | tf_op jit(solution)/shard_map/ppermute | solution.py:50
  (1 other events, 0.9 us)

commit v6 on v5

--- a/solution.py
+++ b/solution.py
@@ -8,15 +8,13 @@
 from jax.sharding import PartitionSpec as P
 
 VMEM_BYTES = 24 * 1024 * 1024
-DENSE_BYTES = 24 * 1024 * 1024
 HIGHEST = lax.Precision.HIGHEST
 GRAM = 128
 PIECES = 2
-UNROLL = 32
+UNROLL = 96
 
 vmem = pl.BlockSpec(memory_space=pltpu.VMEM)
 smem = pl.BlockSpec(memory_space=pltpu.SMEM)
-hbm = pl.BlockSpec(memory_space=pltpu.HBM)
 
 
 def f32(*shape):
@@ -66,44 +64,27 @@
     return functools.reduce(jnp.add, reversed(parts))
 
 
-def dense_kernel(
-    table, near_ref, left_ref, right_ref, tile_ref, turned_ref, lefts, rights, sems
-):
+def dense_kernel(table, near_ref, left_ref, right_ref, tile_ref, turned_ref):
     near_slots, far_slots = near_ref.shape[0], left_ref.shape[0]
     ranks = 2 + 2 * (near_slots + far_slots)
     count = table[ranks + far_slots]
-    copies = [
-        pltpu.make_async_copy(source, target, sems.at[k])
-        for k, (source, target) in enumerate(
-            [
-                (left_ref, lefts),
-                (right_ref, rights),
-                (near_ref, tile_ref.at[pl.ds(0, near_slots)]),
-            ]
-        )
-    ]
-    for copy in copies:
-        copy.start()
-    copies[0].wait()
-    copies[1].wait()
 
     def far(s, _):
-        row = lax.broadcasted_iota(jnp.int32, lefts.shape[1:], 0)
-        left = jnp.where(row < table[ranks + s], lefts[s].astype(jnp.float32), 0.0)
-        left, right = left.astype(jnp.bfloat16), rights[s]
+        row = lax.broadcasted_iota(jnp.int32, left_ref.shape[1:], 0)
+        left = jnp.where(row < table[ranks + s], left_ref[s].astype(jnp.float32), 0.0)
+        left, right = left.astype(jnp.bfloat16), right_ref[s]
         tile_ref[near_slots + s] = contract(left, right, ((0,), (0,))).astype(jnp.bfloat16)
         turned_ref[near_slots + s] = contract(right, left, ((0,), (0,))).astype(jnp.bfloat16)
         return 0
 
     def near(s, _):
-        tile = tile_ref[s]
+        tile = near_ref[s]
         tile = jnp.where(s < count, tile, jnp.zeros_like(tile))
         tile_ref[s] = tile
         turned_ref[s] = tile.T
         return 0
 
     lax.fori_loop(0, far_slots, far, 0, unroll=16)
-    copies[2].wait()
     lax.fori_loop(0, near_slots, near, 0, unroll=8)
 
 
@@ -375,15 +356,14 @@
     residual_ref[...] = r2 - mul_t(alpha2, s2)
 
 
-def call(kernel, name, outs, *args, scratch=(), scalars=(), far=(), cost=0, room=VMEM_BYTES):
-    spaces = {**dict.fromkeys(scalars, smem), **dict.fromkeys(far, hbm)}
+def call(kernel, name, outs, *args, scratch=(), scalars=(), cost=0):
     return pl.pallas_call(
         kernel,
         out_shape=outs,
-        in_specs=[spaces.get(k, vmem) for k in range(len(args))],
+        in_specs=[smem if k in scalars else vmem for k in range(len(args))],
         out_specs=jax.tree.map(lambda _: vmem, outs),
         scratch_shapes=list(scratch),
-        compiler_params=pltpu.CompilerParams(vmem_limit_bytes=room),
+        compiler_params=pltpu.CompilerParams(vmem_limit_bytes=VMEM_BYTES),
         cost_estimate=pl.CostEstimate(flops=int(cost * 1e9), bytes_accessed=0, transcendentals=0),
         name=name,
     )(*args)
@@ -430,13 +410,6 @@
         far_left[0, 0],
         far_right[0, 0],
         scalars=(0,),
-        far=(1, 2, 3),
-        room=DENSE_BYTES,
-        scratch=[
-            pltpu.VMEM(far_left.shape[2:], jnp.bfloat16),
-            pltpu.VMEM(far_right.shape[2:], jnp.bfloat16),
-            pltpu.SemaphoreType.DMA((3,)),
-        ],
     )
 
     def apply(plain, wide, during, last=()):

time: 111 us -> 110 us (level)
  Pallas kernels: 33.4 us -> 31.2 us
    pallas_call x23, Pallas kernels: 33.4 us -> 31.2 us  [call(): pl.pallas_call(kernel, out_shape=outs, in_specs=[smem if k in scalars els...]
  transfers between devices with their start and end apart: 55 -> 55, of which waited for: 25 -> 25; matrix products, arithmetic and copies ran while one was open for 0% -> 0% of each run, Pallas kernels for 24% -> 22%
where the time goes in v6:
time: 110 us
  starting transfers between devices  57 us (52%)
  Pallas kernels  31.2 us (28%)
  waiting for transfers between devices  18.3 us (17%)
  local copies, waits for them, and re-layouts  1.73 us (2%)
  between operations  1.71 us (2%)
    ppermute x55, starting transfers between devices, partner_permute(): return lax.ppermute(value, axis, [(i, i ^ flip) for i in range(size)])  57 us
    pallas_call x23, Pallas kernels, call(): pl.pallas_call(kernel, out_shape=outs, in_specs=[smem if k in scalars els...  31.2 us
    ppermute x55, waiting for transfers between devices, partner_permute(): return lax.ppermute(value, axis, [(i, i ^ flip) for i in range(size)])  18.3 us
  transfers between devices with their start and end apart: 55, of which 25 were waited for; matrix products, arithmetic and copies ran while one was open for 0% of the time, Pallas kernels for 22%

profile of v6, /device:TPU:0, one launch (start us, length us, event | category | flops | bytes accessed | tf_op | source)
XLA Modules:
  0.0 109.9 jit_solution(15155291304347944965)
XLA Ops:
  0.6 0.7 broadcast_in_dim.3.diagonal_ref.refs_13_
  1.3 0.9 copy-done.1
  2.6 4.1 %collective-permute-start.1 = (bf16[64,640]{1,0:T(8,128)(2,1)S(1)}, bf16[64,640]{1,0:T(8,128)(2,1)S(1)}, u32[]{:S(2)}, u32[]{:S(2)}) collective-permute-start(bf16[64,640]{1,0:T(8,128)(2,1)S(1)} %get-tuple-element.107.refs_0_), channel_id=1, source_target_pairs={{0,4},{1,5},{2,6},{3,7},{4,0},{5,1},{6,2},{7,3},{8,12},{9,13},{10,... | collective-permute-start | bytes 245768 | tf_op jit(solution)/shard_map/ppermute | solution.py:48
  6.7 2.4 %collective-permute-start.5 = (bf16[64,896]{1,0:T(8,128)(2,1)S(1)}, bf16[64,896]{1,0:T(8,128)(2,1)S(1)}, u32[]{:S(2)}, u32[]{:S(2)}) collective-permute-start(bf16[64,896]{1,0:T(8,128)(2,1)S(1)} %get-tuple-element.109.refs_0_), channel_id=1, source_target_pairs={{0,24},{8,16},{16,8},{24,0},{1,25},{9,17},{17,9},{25,1},{2,26},{10... | collective-permute-start | bytes 344072 | tf_op jit(solution)/shard_map/ppermute | solution.py:48
  9.2 0.5 collective-permute-start.4
  9.7 0.5 collective-permute-start.3
  10.2 1.6 %collective-permute-start = (bf16[64,640]{1,0:T(8,128)(2,1)S(1)}, bf16[64,640]{1,0:T(8,128)(2,1)S(1)}, u32[]{:S(2)}, u32[]{:S(2)}) collective-permute-start(bf16[64,640]{1,0:T(8,128)(2,1)S(1)} %get-tuple-element.107.refs_0_), channel_id=1, source_target_pairs={{0,2},{1,3},{2,0},{3,1},{4,6},{5,7},{6,4},{7,5},{8,10},{9,11},{10,... | collective-permute-start | bytes 245768 | tf_op jit(solution)/shard_map/ppermute | solution.py:48
  13.0 3.1 %dense_tiles.1 = (bf16[96,128,128]{2,1,0:T(8,128)(2,1)S(1)}, bf16[96,128,128]{2,1,0:T(8,128)(2,1)S(1)}) custom-call(s32[259]{0:T(512)S(1)} %concatenate.3.table, bf16[32,128,128]{2,1,0:T(8,128)(2,1)S(1)} %bitcast.12, bf16[64,32,128]{2,1,0:T(8,128)(2,1)S(1)} %bitcast.13, bf16[64,32,128]{2,1,0:T(8,128)(2,1)S(1)} %bitcast.14), custom_call_target="tpu_custom_call" | custom-call | tf_op jit(solution)/shard_map/dense_tiles/pallas_call | solution.py:360
  16.2 1.7 %rows_half.3 = (bf16[5,64,640]{2,1,0:T(8,128)(2,1)S(1)}, f32[4,64,640]{2,1,0:T(8,128)S(1)}, f32[64,128]{1,0:T(8,128)S(1)}) custom-call(s32[259]{0:T(512)S(1)} %concatenate.3.table, bf16[96,128,128]{2,1,0:T(8,128)(2,1)S(1)} %get-tuple-element.108.tile_ref, bf16[64,896]{1,0:T(8,128)(2,1)S(1)} %get-tuple-element.109.refs_0_, ...), custom_call_target="tpu_custom_call" | custom-call | tf_op jit(solution)/shard_map/rows_half/pallas_call | solution.py:360
  19.1 0.8 collective-permute-done.7.refs_1_
  20.3 0.6 pair_sums.3
  20.9 1.6 %collective-permute-start.14 = (bf16[64,896]{1,0:T(8,128)(2,1)S(1)}, bf16[64,896]{1,0:T(8,128)(2,1)S(1)}, u32[]{:S(2)}, u32[]{:S(2)}) collective-permute-start(bf16[64,896]{1,0:T(8,128)(2,1)S(1)} %get-tuple-element.128), channel_id=1, source_target_pairs={{0,2},{1,3},{2,0},{3,1},{4,6},{5,7},{6,4},{7,5},{8,10},{9,11},{10,... | collective-permute-start | bytes 344072 | tf_op jit(solution)/shard_map/ppermute | solution.py:48
  22.6 1.4 %collective-permute-start.15 = (bf16[64,896]{1,0:T(8,128)(2,1)S(1)}, bf16[64,896]{1,0:T(8,128)(2,1)S(1)}, u32[]{:S(2)}, u32[]{:S(2)}) collective-permute-start(bf16[64,896]{1,0:T(8,128)(2,1)S(1)} %get-tuple-element.129), channel_id=1, source_target_pairs={{0,4},{1,5},{2,6},{3,7},{4,0},{5,1},{6,2},{7,3},{8,12},{9,13},{10,... | collective-permute-start | bytes 344072 | tf_op jit(solution)/shard_map/ppermute | solution.py:48
  24.0 1.4 %collective-permute-start.16 = (bf16[64,896]{1,0:T(8,128)(2,1)S(1)}, bf16[64,896]{1,0:T(8,128)(2,1)S(1)}, u32[]{:S(2)}, u32[]{:S(2)}) collective-permute-start(bf16[64,896]{1,0:T(8,128)(2,1)S(1)} %get-tuple-element.130), channel_id=1, source_target_pairs={{0,6},{1,7},{2,4},{3,5},{4,2},{5,3},{6,0},{7,1},{8,14},{9,15},{10,... | collective-permute-start | bytes 344072 | tf_op jit(solution)/shard_map/ppermute | solution.py:48
  25.4 1.7 %cols_half.3 = (f32[64,640]{1,0:T(8,128)S(1)}, bf16[64,640]{1,0:T(8,128)(2,1)S(1)}, bf16[64,640]{1,0:T(8,128)(2,1)S(1)}, bf16[64,640]{1,0:T(8,128)(2,1)S(1)}) custom-call(s32[259]{0:T(512)S(1)} %concatenate.3.table, bf16[96,128,128]{2,1,0:T(8,128)(2,1)S(1)} %get-tuple-element.106.tile_ref, bf16[64,640]{1,0:T(8,128)(2,1)S(1)} %get-tuple-element.107.refs_0_, ...), custom_call_target="tpu_custom_call" | custom-call | tf_op jit(solution)/shard_map/cols_half/pallas_call | solution.py:360
  27.1 1.6 %collective-permute-start.11 = (bf16[64,640]{1,0:T(8,128)(2,1)S(1)}, bf16[64,640]{1,0:T(8,128)(2,1)S(1)}, u32[]{:S(2)}, u32[]{:S(2)}) collective-permute-start(bf16[64,640]{1,0:T(8,128)(2,1)S(1)} %get-tuple-element.120), channel_id=1, source_target_pairs={{0,8},{8,0},{16,24},{24,16},{1,9},{9,1},{17,25},{25,17},{2,10},{10... | collective-permute-start | bytes 245768 | tf_op jit(solution)/shard_map/ppermute | solution.py:48
  28.7 1.5 %collective-permute-start.12 = (bf16[64,640]{1,0:T(8,128)(2,1)S(1)}, bf16[64,640]{1,0:T(8,128)(2,1)S(1)}, u32[]{:S(2)}, u32[]{:S(2)}) collective-permute-start(bf16[64,640]{1,0:T(8,128)(2,1)S(1)} %get-tuple-element.121), channel_id=1, source_target_pairs={{0,16},{8,24},{16,0},{24,8},{1,17},{9,25},{17,1},{25,9},{2,18},{10... | collective-permute-start | bytes 245768 | tf_op jit(solution)/shard_map/ppermute | solution.py:48
  30.7 3.6 %collective-permute-done.15.refs_1_ = bf16[64,896]{1,0:T(8,128)(2,1)S(1)} collective-permute-done((bf16[64,896]{1,0:T(8,128)(2,1)S(1)}, bf16[64,896]{1,0:T(8,128)(2,1)S(1)}, u32[]{:S(2)}, u32[]{:S(2)}) %collective-permute-start.15) | collective-permute-done | bytes 114720 | tf_op jit(solution)/shard_map/ppermute | solution.py:48
  34.6 1.0 collective-permute-done.13.refs_4_
  35.5 0.6 combine.2
  36.1 2.5 %collective-permute-start.18 = (bf16[64,640]{1,0:T(8,128)(2,1)S(1)}, bf16[64,640]{1,0:T(8,128)(2,1)S(1)}, u32[]{:S(2)}, u32[]{:S(2)}) collective-permute-start(bf16[64,640]{1,0:T(8,128)(2,1)S(1)} %get-tuple-element.139.refs_0_), channel_id=1, source_target_pairs={{0,4},{1,5},{2,6},{3,7},{4,0},{5,1},{6,2},{7,3},{8,12},{9,13},{10,... | collective-permute-start | bytes 245768 | tf_op jit(solution)/shard_map/ppermute | solution.py:48
  38.6 2.4 %collective-permute-start.22 = (bf16[64,896]{1,0:T(8,128)(2,1)S(1)}, bf16[64,896]{1,0:T(8,128)(2,1)S(1)}, u32[]{:S(2)}, u32[]{:S(2)}) collective-permute-start(bf16[64,896]{1,0:T(8,128)(2,1)S(1)} %get-tuple-element.140.refs_0_), channel_id=1, source_target_pairs={{0,24},{8,16},{16,8},{24,0},{1,25},{9,17},{17,9},{25,1},{2,26},{10... | collective-permute-start | bytes 344072 | tf_op jit(solution)/shard_map/ppermute | solution.py:48
  41.1 0.5 collective-permute-start.21
  41.6 0.5 collective-permute-start.20
  42.1 0.6 collective-permute-start.17
  42.7 1.5 %collective-permute-start.19 = (bf16[64,640]{1,0:T(8,128)(2,1)S(1)}, bf16[64,640]{1,0:T(8,128)(2,1)S(1)}, u32[]{:S(2)}, u32[]{:S(2)}) collective-permute-start(bf16[64,640]{1,0:T(8,128)(2,1)S(1)} %collective-permute-done.18.refs_4_), channel_id=1, source_target_pairs={{0,2},{1,3},{2,0},{3,1},{4,6},{5,7},{6,4},{7,5},{8,10},{9,11},{10,... | collective-permute-start | bytes 245768 | tf_op jit(solution)/shard_map/ppermute | solution.py:48
  44.1 0.7 collective-permute-done.22.refs_3_
  44.9 1.4 %collective-permute-done.21.refs_2_ = bf16[64,896]{1,0:T(8,128)(2,1)S(1)} collective-permute-done((bf16[64,896]{1,0:T(8,128)(2,1)S(1)}, bf16[64,896]{1,0:T(8,128)(2,1)S(1)}, u32[]{:S(2)}, u32[]{:S(2)}) %collective-permute-start.21) | collective-permute-done | bytes 114720 | tf_op jit(solution)/shard_map/ppermute | solution.py:48
  46.5 1.7 %rows_half.4 = (bf16[5,64,640]{2,1,0:T(8,128)(2,1)S(1)}, f32[4,64,640]{2,1,0:T(8,128)S(1)}, f32[64,128]{1,0:T(8,128)S(1)}) custom-call(s32[259]{0:T(512)S(1)} %concatenate.3.table, bf16[96,128,128]{2,1,0:T(8,128)(2,1)S(1)} %get-tuple-element.108.tile_ref, bf16[64,896]{1,0:T(8,128)(2,1)S(1)} %get-tuple-element.140.refs_0_, ...), custom_call_target="tpu_custom_call" | custom-call | tf_op jit(solution)/shard_map/rows_half/pallas_call | solution.py:360
  49.4 0.8 collective-permute-done.24.refs_1_
  50.7 0.6 pair_sums.4
  51.6 1.7 %collective-permute-start.29 = (bf16[64,896]{1,0:T(8,128)(2,1)S(1)}, bf16[64,896]{1,0:T(8,128)(2,1)S(1)}, u32[]{:S(2)}, u32[]{:S(2)}) collective-permute-start(bf16[64,896]{1,0:T(8,128)(2,1)S(1)} %get-tuple-element.153), channel_id=1, source_target_pairs={{0,4},{1,5},{2,6},{3,7},{4,0},{5,1},{6,2},{7,3},{8,12},{9,13},{10,... | collective-permute-start | bytes 344072 | tf_op jit(solution)/shard_map/ppermute | solution.py:48
  53.3 2.5 %collective-permute-start.30 = (bf16[64,896]{1,0:T(8,128)(2,1)S(1)}, bf16[64,896]{1,0:T(8,128)(2,1)S(1)}, u32[]{:S(2)}, u32[]{:S(2)}) collective-permute-start(bf16[64,896]{1,0:T(8,128)(2,1)S(1)} %get-tuple-element.154), channel_id=1, source_target_pairs={{0,6},{1,7},{2,4},{3,5},{4,2},{5,3},{6,0},{7,1},{8,14},{9,15},{10,... | collective-permute-start | bytes 344072 | tf_op jit(solution)/shard_map/ppermute | solution.py:48
  55.7 1.7 %cols_half.4 = (f32[64,640]{1,0:T(8,128)S(1)}, bf16[64,640]{1,0:T(8,128)(2,1)S(1)}, bf16[64,640]{1,0:T(8,128)(2,1)S(1)}, bf16[64,640]{1,0:T(8,128)(2,1)S(1)}) custom-call(s32[259]{0:T(512)S(1)} %concatenate.3.table, bf16[96,128,128]{2,1,0:T(8,128)(2,1)S(1)} %get-tuple-element.106.tile_ref, bf16[64,640]{1,0:T(8,128)(2,1)S(1)} %get-tuple-element.139.refs_0_, ...), custom_call_target="tpu_custom_call" | custom-call | tf_op jit(solution)/shard_map/cols_half/pallas_call | solution.py:360
  57.5 1.4 %collective-permute-start.31 = (bf16[64,640]{1,0:T(8,128)(2,1)S(1)}, bf16[64,640]{1,0:T(8,128)(2,1)S(1)}, u32[]{:S(2)}, u32[]{:S(2)}) collective-permute-start(bf16[64,640]{1,0:T(8,128)(2,1)S(1)} %get-tuple-element.161), channel_id=1, source_target_pairs={{0,8},{8,0},{16,24},{24,16},{1,9},{9,1},{17,25},{25,17},{2,10},{10... | collective-permute-start | bytes 245768 | tf_op jit(solution)/shard_map/ppermute | solution.py:48
  58.9 0.8 collective-permute-start.32
  59.6 1.4 %collective-permute-start.33 = (bf16[64,640]{1,0:T(8,128)(2,1)S(1)}, bf16[64,640]{1,0:T(8,128)(2,1)S(1)}, u32[]{:S(2)}, u32[]{:S(2)}) collective-permute-start(bf16[64,640]{1,0:T(8,128)(2,1)S(1)} %get-tuple-element.163), channel_id=1, source_target_pairs={{0,24},{8,16},{16,8},{24,0},{1,25},{9,17},{17,9},{25,1},{2,26},{10... | collective-permute-start | bytes 245768 | tf_op jit(solution)/shard_map/ppermute | solution.py:48
  61.0 2.4 %collective-permute-done.29.refs_1_ = bf16[64,896]{1,0:T(8,128)(2,1)S(1)} collective-permute-done((bf16[64,896]{1,0:T(8,128)(2,1)S(1)}, bf16[64,896]{1,0:T(8,128)(2,1)S(1)}, u32[]{:S(2)}, u32[]{:S(2)}) %collective-permute-start.29) | collective-permute-done | bytes 114720 | tf_op jit(solution)/shard_map/ppermute | solution.py:48
  63.5 3.1 %coefficients.2.first_ref = f32[64,256]{1,0:T(8,128)S(1)} custom-call(f32[8,128]{1,0:T(8,128)S(1)} %shift.1.shift_ref, f32[64,128]{1,0:T(8,128)S(1)} %get-tuple-element.131.gram_ref.gram0_ref, f32[64,128]{1,0:T(8,128)S(1)} %get-tuple-element.164.gram1_ref), custom_call_target="tpu_custom_call" | custom-call | tf_op jit(solution)/shard_map/coefficients/pallas_call | solution.py:360
  66.6 0.6 combine.3
  67.3 2.1 %collective-permute-start.35 = (bf16[64,640]{1,0:T(8,128)(2,1)S(1)}, bf16[64,640]{1,0:T(8,128)(2,1)S(1)}, u32[]{:S(2)}, u32[]{:S(2)}) collective-permute-start(bf16[64,640]{1,0:T(8,128)(2,1)S(1)} %get-tuple-element.168.refs_0_), channel_id=1, source_target_pairs={{0,4},{1,5},{2,6},{3,7},{4,0},{5,1},{6,2},{7,3},{8,12},{9,13},{10,... | collective-permute-start | bytes 245768 | tf_op jit(solution)/shard_map/ppermute | solution.py:48
  69.4 2.1 %collective-permute-start.39 = (bf16[64,896]{1,0:T(8,128)(2,1)S(1)}, bf16[64,896]{1,0:T(8,128)(2,1)S(1)}, u32[]{:S(2)}, u32[]{:S(2)}) collective-permute-start(bf16[64,896]{1,0:T(8,128)(2,1)S(1)} %get-tuple-element.169.refs_0_.refs_8_), channel_id=1, source_target_pairs={{0,24},{8,16},{16,8},{24,0},{1,25},{9,17},{17,9},{25,1},{2,26},{10... | collective-permute-start | bytes 344072 | tf_op jit(solution)/shard_map/ppermute | solution.py:48
  71.5 0.6 collective-permute-start.38
  72.2 0.7 collective-permute-start.37
  73.2 1.7 %collective-permute-start.36 = (bf16[64,640]{1,0:T(8,128)(2,1)S(1)}, bf16[64,640]{1,0:T(8,128)(2,1)S(1)}, u32[]{:S(2)}, u32[]{:S(2)}) collective-permute-start(bf16[64,640]{1,0:T(8,128)(2,1)S(1)} %collective-permute-done.35.refs_4_), channel_id=1, source_target_pairs={{0,2},{1,3},{2,0},{3,1},{4,6},{5,7},{6,4},{7,5},{8,10},{9,11},{10,... | collective-permute-start | bytes 245768 | tf_op jit(solution)/shard_map/ppermute | solution.py:48
  74.9 1.5 %collective-permute-done.39.refs_3_.refs_11_ = bf16[64,896]{1,0:T(8,128)(2,1)S(1)} collective-permute-done((bf16[64,896]{1,0:T(8,128)(2,1)S(1)}, bf16[64,896]{1,0:T(8,128)(2,1)S(1)}, u32[]{:S(2)}, u32[]{:S(2)}) %collective-permute-start.39) | collective-permute-done | bytes 114720 | tf_op jit(solution)/shard_map/ppermute | solution.py:48
  76.4 0.6 collective-permute-done.38.refs_2_.refs_10_
  77.0 1.9 %rows_half.5 = (bf16[5,64,640]{2,1,0:T(8,128)(2,1)S(1)}, f32[4,64,640]{2,1,0:T(8,128)S(1)}, f32[64,128]{1,0:T(8,128)S(1)}) custom-call(s32[259]{0:T(512)S(1)} %concatenate.3.table, bf16[96,128,128]{2,1,0:T(8,128)(2,1)S(1)} %get-tuple-element.108.tile_ref, bf16[64,896]{1,0:T(8,128)(2,1)S(1)} %get-tuple-element.169.refs_0_.refs_8_, ...), custom_call_target="tpu_custom_call" | custom-call | tf_op jit(solution)/shard_map/rows_half/pallas_call | solution.py:360
  80.0 0.8 collective-permute-done.41.refs_1_
  81.2 0.6 pair_sums.5
  82.3 2.5 %collective-permute-start.49 = (bf16[64,896]{1,0:T(8,128)(2,1)S(1)}, bf16[64,896]{1,0:T(8,128)(2,1)S(1)}, u32[]{:S(2)}, u32[]{:S(2)}) collective-permute-start(bf16[64,896]{1,0:T(8,128)(2,1)S(1)} %get-tuple-element.191), channel_id=1, source_target_pairs={{0,4},{1,5},{2,6},{3,7},{4,0},{5,1},{6,2},{7,3},{8,12},{9,13},{10,... | collective-permute-start | bytes 344072 | tf_op jit(solution)/shard_map/ppermute | solution.py:48
  84.9 1.4 %collective-permute-start.50 = (bf16[64,896]{1,0:T(8,128)(2,1)S(1)}, bf16[64,896]{1,0:T(8,128)(2,1)S(1)}, u32[]{:S(2)}, u32[]{:S(2)}) collective-permute-start(bf16[64,896]{1,0:T(8,128)(2,1)S(1)} %get-tuple-element.192), channel_id=1, source_target_pairs={{0,6},{1,7},{2,4},{3,5},{4,2},{5,3},{6,0},{7,1},{8,14},{9,15},{10,... | collective-permute-start | bytes 344072 | tf_op jit(solution)/shard_map/ppermute | solution.py:48
  86.3 2.2 %cols_half.5 = (f32[64,640]{1,0:T(8,128)S(1)}, bf16[64,768]{1,0:T(8,128)(2,1)S(1)}, bf16[64,768]{1,0:T(8,128)(2,1)S(1)}, bf16[64,768]{1,0:T(8,128)(2,1)S(1)}, f32[64,64]{1,0:T(8,128)S(1)}) custom-call(s32[259]{0:T(512)S(1)} %concatenate.3.table, bf16[96,128,128]{2,1,0:T(8,128)(2,1)S(1)} %get-tuple-element.106.tile_ref, ...), custom_call_target="tpu_custom_call" | custom-call | tf_op jit(solution)/shard_map/cols_half/pallas_call | solution.py:360
  88.6 1.0 collective-permute-start.45
  89.5 1.1 collective-permute-start.46
  90.6 1.5 %collective-permute-start.47 = (bf16[64,768]{1,0:T(8,128)(2,1)S(1)}, bf16[64,768]{1,0:T(8,128)(2,1)S(1)}, u32[]{:S(2)}, u32[]{:S(2)}) collective-permute-start(bf16[64,768]{1,0:T(8,128)(2,1)S(1)} %get-tuple-element.184), channel_id=1, source_target_pairs={{0,24},{8,16},{16,8},{24,0},{1,25},{9,17},{17,9},{25,1},{2,26},{10... | collective-permute-start | bytes 294920 | tf_op jit(solution)/shard_map/ppermute | solution.py:48
  92.1 2.1 %collective-permute-done.49.refs_1_ = bf16[64,896]{1,0:T(8,128)(2,1)S(1)} collective-permute-done((bf16[64,896]{1,0:T(8,128)(2,1)S(1)}, bf16[64,896]{1,0:T(8,128)(2,1)S(1)}, u32[]{:S(2)}, u32[]{:S(2)}) %collective-permute-start.49) | collective-permute-done | bytes 114720 | tf_op jit(solution)/shard_map/ppermute | solution.py:48
  94.3 3.3 %solve.1.solve_ref = f32[64,128]{1,0:T(8,128)S(1)} custom-call(f32[8,128]{1,0:T(8,128)S(1)} %shift.1.shift_ref, f32[64,128]{1,0:T(8,128)S(1)} %get-tuple-element.131.gram_ref.gram0_ref, f32[64,128]{1,0:T(8,128)S(1)} %get-tuple-element.164.gram1_ref, f32[64,128]{1,0:T(8,128)S(1)} %get-tuple-element.193.gram2_ref, f32[64,256]{1,0:T(8,128)S(1)} %coefficients.2.first_ref), custom_call_target="tpu_custom_call" | custom-call | tf_op jit(solution)/shard_map/solve/pallas_call | solution.py:360
  97.7 2.4 %collective-permute-start.53 = (f32[64,64]{1,0:T(8,128)S(1)}, f32[64,64]{1,0:T(8,128)S(1)}, u32[]{:S(2)}, u32[]{:S(2)}) collective-permute-start(f32[64,64]{1,0:T(8,128)S(1)} %last_gram.1), channel_id=1, source_target_pairs={{0,6},{1,7},{2,4},{3,5},{4,2},{5,3},{6,0},{7,1},{8,14},{9,15},{10,... | collective-permute-start | bytes 49160 | tf_op jit(solution)/shard_map/ppermute | solution.py:48
  100.2 1.1 collective-permute-start.52
  101.2 1.0 collective-permute-start.51
  102.2 2.7 %coefficients.3 = (f32[192,256]{1,0:T(8,128)S(1)}, f32[64,256]{1,0:T(8,128)S(1)}) custom-call(f32[8,128]{1,0:T(8,128)S(1)} %shift.1.shift_ref, f32[64,128]{1,0:T(8,128)S(1)} %get-tuple-element.131.gram_ref.gram0_ref, f32[64,128]{1,0:T(8,128)S(1)} %get-tuple-element.164.gram1_ref, f32[64,128]{1,0:T(8,128)S(1)} %get-tuple-element.193.gram2_ref, ...), custom_call_target="tpu_custom_call" | custom-call | tf_op jit(solution)/shard_map/coefficients/pallas_call | solution.py:360
  105.4 0.8 vectors.1.vectors_ref
  106.6 3.3 %finish.1 = (f32[64,640]{1,0:T(8,128)}, f32[64,640]{1,0:T(8,128)}) custom-call(f32[256,640]{1,0:T(8,128)S(1)} %vectors.1.vectors_ref, f32[64,256]{1,0:T(8,128)S(1)} %get-tuple-element.206.small_ref, f32[64,64]{1,0:T(8,128)S(1)} %add_add_fusion.both_ref, f32[64,64]{1,0:T(8,128)S(1)} %collective-permute-done.54.other_ref, ...), custom_call_target="tpu_custom_call" | custom-call | tf_op jit(solution)/shard_map/finish/pallas_call | solution.py:360
  (92 shorter events, 9.0 us)
Async XLA Ops:
  2.2 10.7 %copy-start.5 = (s32[1,1,32]{2,1,0:T(1,128)S(1)}, s32[1,1,32]{2,1,0:T(1,128)}, u32[]{:S(2)}) copy-start(s32[1,1,32]{2,1,0:T(1,128)} %param.14) | copy-start | bytes 388
  2.2 10.7 %copy-start.6 = (s32[1,1,64]{2,1,0:T(1,128)S(1)}, s32[1,1,64]{2,1,0:T(1,128)}, u32[]{:S(2)}) copy-start(s32[1,1,64]{2,1,0:T(1,128)} %param.19) | copy-start | bytes 772
  2.2 10.7 %copy-start.7 = (s32[1,1,32]{2,1,0:T(1,128)S(1)}, s32[1,1,32]{2,1,0:T(1,128)}, u32[]{:S(2)}) copy-start(s32[1,1,32]{2,1,0:T(1,128)} %param.15) | copy-start | bytes 388
  2.2 10.7 %copy-start.8 = (s32[1,1,64]{2,1,0:T(1,128)S(1)}, s32[1,1,64]{2,1,0:T(1,128)}, u32[]{:S(2)}) copy-start(s32[1,1,64]{2,1,0:T(1,128)} %param.20) | copy-start | bytes 772
  2.2 10.7 %copy-start.9 = (s32[1,1,64]{2,1,0:T(1,128)S(1)}, s32[1,1,64]{2,1,0:T(1,128)}, u32[]{:S(2)}) copy-start(s32[1,1,64]{2,1,0:T(1,128)} %param.21) | copy-start | bytes 772
  2.3 10.8 %copy-start = (bf16[1,1,32,128,128]{4,3,2,1,0:T(8,128)(2,1)S(1)}, bf16[1,1,32,128,128]{4,3,2,1,0:T(8,128)(2,1)}, u32[]{:S(2)}) copy-start(bf16[1,1,32,128,128]{4,3,2,1,0:T(8,128)(2,1)} %param.13) | copy-start | bytes 3145732
  2.3 10.8 %copy-start.3 = (bf16[1,1,64,32,128]{4,3,2,1,0:T(8,128)(2,1)S(1)}, bf16[1,1,64,32,128]{4,3,2,1,0:T(8,128)(2,1)}, u32[]{:S(2)}) copy-start(bf16[1,1,64,32,128]{4,3,2,1,0:T(8,128)(2,1)} %param.17) | copy-start | bytes 1572868
  2.3 10.8 %copy-start.4 = (bf16[1,1,64,32,128]{4,3,2,1,0:T(8,128)(2,1)S(1)}, bf16[1,1,64,32,128]{4,3,2,1,0:T(8,128)(2,1)}, u32[]{:S(2)}) copy-start(bf16[1,1,64,32,128]{4,3,2,1,0:T(8,128)(2,1)} %param.18) | copy-start | bytes 1572868
  2.6 9.2 %collective-permute-start.1 = (bf16[64,640]{1,0:T(8,128)(2,1)S(1)}, bf16[64,640]{1,0:T(8,128)(2,1)S(1)}, u32[]{:S(2)}, u32[]{:S(2)}) collective-permute-start(bf16[64,640]{1,0:T(8,128)(2,1)S(1)} %get-tuple-element.107.refs_0_), channel_id=1, source_target_pairs={{0,4},{1,5},{2,6},{3,7},{4,0},{5,1},{6,2},{7,3},{8,12},{9,13},{10,... | collective-permute-start | bytes 245768 | tf_op jit(solution)/shard_map/ppermute | solution.py:48
  6.7 9.4 %collective-permute-start.5 = (bf16[64,896]{1,0:T(8,128)(2,1)S(1)}, bf16[64,896]{1,0:T(8,128)(2,1)S(1)}, u32[]{:S(2)}, u32[]{:S(2)}) collective-permute-start(bf16[64,896]{1,0:T(8,128)(2,1)S(1)} %get-tuple-element.109.refs_0_), channel_id=1, source_target_pairs={{0,24},{8,16},{16,8},{24,0},{1,25},{9,17},{17,9},{25,1},{2,26},{10... | collective-permute-start | bytes 344072 | tf_op jit(solution)/shard_map/ppermute | solution.py:48
  9.2 7.0 %collective-permute-start.4 = (bf16[64,896]{1,0:T(8,128)(2,1)S(1)}, bf16[64,896]{1,0:T(8,128)(2,1)S(1)}, u32[]{:S(2)}, u32[]{:S(2)}) collective-permute-start(bf16[64,896]{1,0:T(8,128)(2,1)S(1)} %get-tuple-element.109.refs_0_), channel_id=1, source_target_pairs={{0,16},{8,24},{16,0},{24,8},{1,17},{9,25},{17,1},{25,9},{2,18},{10... | collective-permute-start | bytes 344072 | tf_op jit(solution)/shard_map/ppermute | solution.py:48
  9.7 6.5 %collective-permute-start.3 = (bf16[64,896]{1,0:T(8,128)(2,1)S(1)}, bf16[64,896]{1,0:T(8,128)(2,1)S(1)}, u32[]{:S(2)}, u32[]{:S(2)}) collective-permute-start(bf16[64,896]{1,0:T(8,128)(2,1)S(1)} %get-tuple-element.109.refs_0_), channel_id=1, source_target_pairs={{0,8},{8,0},{16,24},{24,16},{1,9},{9,1},{17,25},{25,17},{2,10},{10... | collective-permute-start | bytes 344072 | tf_op jit(solution)/shard_map/ppermute | solution.py:48
  10.2 7.7 %collective-permute-start = (bf16[64,640]{1,0:T(8,128)(2,1)S(1)}, bf16[64,640]{1,0:T(8,128)(2,1)S(1)}, u32[]{:S(2)}, u32[]{:S(2)}) collective-permute-start(bf16[64,640]{1,0:T(8,128)(2,1)S(1)} %get-tuple-element.107.refs_0_), channel_id=1, source_target_pairs={{0,2},{1,3},{2,0},{3,1},{4,6},{5,7},{6,4},{7,5},{8,10},{9,11},{10,... | collective-permute-start | bytes 245768 | tf_op jit(solution)/shard_map/ppermute | solution.py:48
  11.8 6.1 %collective-permute-start.2 = (bf16[64,640]{1,0:T(8,128)(2,1)S(1)}, bf16[64,640]{1,0:T(8,128)(2,1)S(1)}, u32[]{:S(2)}, u32[]{:S(2)}) collective-permute-start(bf16[64,640]{1,0:T(8,128)(2,1)S(1)} %collective-permute-done.1.refs_4_), channel_id=1, source_target_pairs={{0,2},{1,3},{2,0},{3,1},{4,6},{5,7},{6,4},{7,5},{8,10},{9,11},{10,... | collective-permute-start | bytes 245768 | tf_op jit(solution)/shard_map/ppermute | solution.py:48
  17.9 2.4 %collective-permute-start.6 = (bf16[5,64,640]{2,1,0:T(8,128)(2,1)S(1)}, bf16[5,64,640]{2,1,0:T(8,128)(2,1)S(1)}, u32[]{:S(2)}, u32[]{:S(2)}) collective-permute-start(bf16[5,64,640]{2,1,0:T(8,128)(2,1)S(1)} %get-tuple-element.112), channel_id=1, source_target_pairs={{0,1},{1,0},{2,3},{3,2},{4,5},{5,4},{6,7},{7,6},{8,9},{9,8},{10,11... | collective-permute-start | bytes 1228808 | tf_op jit(solution)/shard_map/ppermute | solution.py:48
  18.0 1.9 %collective-permute-start.7 = (bf16[64,640]{1,0:T(8,128)(2,1)S(1)}, bf16[64,640]{1,0:T(8,128)(2,1)S(1)}, u32[]{:S(2)}, u32[]{:S(2)}) collective-permute-start(bf16[64,640]{1,0:T(8,128)(2,1)S(1)} %get-tuple-element.107.refs_0_), channel_id=1, source_target_pairs={{0,1},{1,0},{2,3},{3,2},{4,5},{5,4},{6,7},{7,6},{8,9},{9,8},{10,11... | collective-permute-start | bytes 245768 | tf_op jit(solution)/shard_map/ppermute | solution.py:48
  18.5 1.5 %collective-permute-start.8 = (bf16[64,640]{1,0:T(8,128)(2,1)S(1)}, bf16[64,640]{1,0:T(8,128)(2,1)S(1)}, u32[]{:S(2)}, u32[]{:S(2)}) collective-permute-start(bf16[64,640]{1,0:T(8,128)(2,1)S(1)} %collective-permute-done.refs_2_), channel_id=1, source_target_pairs={{0,1},{1,0},{2,3},{3,2},{4,5},{5,4},{6,7},{7,6},{8,9},{9,8},{10,11... | collective-permute-start | bytes 245768 | tf_op jit(solution)/shard_map/ppermute | solution.py:48
  18.6 1.5 %collective-permute-start.9 = (bf16[64,640]{1,0:T(8,128)(2,1)S(1)}, bf16[64,640]{1,0:T(8,128)(2,1)S(1)}, u32[]{:S(2)}, u32[]{:S(2)}) collective-permute-start(bf16[64,640]{1,0:T(8,128)(2,1)S(1)} %collective-permute-done.1.refs_4_), channel_id=1, source_target_pairs={{0,1},{1,0},{2,3},{3,2},{4,5},{5,4},{6,7},{7,6},{8,9},{9,8},{10,11... | collective-permute-start | bytes 245768 | tf_op jit(solution)/shard_map/ppermute | solution.py:48
  19.0 1.3 %collective-permute-start.10 = (bf16[64,640]{1,0:T(8,128)(2,1)S(1)}, bf16[64,640]{1,0:T(8,128)(2,1)S(1)}, u32[]{:S(2)}, u32[]{:S(2)}) collective-permute-start(bf16[64,640]{1,0:T(8,128)(2,1)S(1)} %collective-permute-done.2.refs_6_), channel_id=1, source_target_pairs={{0,1},{1,0},{2,3},{3,2},{4,5},{5,4},{6,7},{7,6},{8,9},{9,8},{10,11... | collective-permute-start | bytes 245768 | tf_op jit(solution)/shard_map/ppermute | solution.py:48
  20.9 9.3 %collective-permute-start.14 = (bf16[64,896]{1,0:T(8,128)(2,1)S(1)}, bf16[64,896]{1,0:T(8,128)(2,1)S(1)}, u32[]{:S(2)}, u32[]{:S(2)}) collective-permute-start(bf16[64,896]{1,0:T(8,128)(2,1)S(1)} %get-tuple-element.128), channel_id=1, source_target_pairs={{0,2},{1,3},{2,0},{3,1},{4,6},{5,7},{6,4},{7,5},{8,10},{9,11},{10,... | collective-permute-start | bytes 344072 | tf_op jit(solution)/shard_map/ppermute | solution.py:48
  22.6 11.7 %collective-permute-start.15 = (bf16[64,896]{1,0:T(8,128)(2,1)S(1)}, bf16[64,896]{1,0:T(8,128)(2,1)S(1)}, u32[]{:S(2)}, u32[]{:S(2)}) collective-permute-start(bf16[64,896]{1,0:T(8,128)(2,1)S(1)} %get-tuple-element.129), channel_id=1, source_target_pairs={{0,4},{1,5},{2,6},{3,7},{4,0},{5,1},{6,2},{7,3},{8,12},{9,13},{10,... | collective-permute-start | bytes 344072 | tf_op jit(solution)/shard_map/ppermute | solution.py:48
  24.0 10.3 %collective-permute-start.16 = (bf16[64,896]{1,0:T(8,128)(2,1)S(1)}, bf16[64,896]{1,0:T(8,128)(2,1)S(1)}, u32[]{:S(2)}, u32[]{:S(2)}) collective-permute-start(bf16[64,896]{1,0:T(8,128)(2,1)S(1)} %get-tuple-element.130), channel_id=1, source_target_pairs={{0,6},{1,7},{2,4},{3,5},{4,2},{5,3},{6,0},{7,1},{8,14},{9,15},{10,... | collective-permute-start | bytes 344072 | tf_op jit(solution)/shard_map/ppermute | solution.py:48
  25.4 10.2 %copy-start.2 = (f32[64,640]{1,0:T(8,128)S(1)}, f32[64,640]{1,0:T(8,128)}, u32[]{:S(2)}) copy-start(f32[64,640]{1,0:T(8,128)} %b_ref.1) | copy-start | bytes 491524
  27.1 7.4 %collective-permute-start.11 = (bf16[64,640]{1,0:T(8,128)(2,1)S(1)}, bf16[64,640]{1,0:T(8,128)(2,1)S(1)}, u32[]{:S(2)}, u32[]{:S(2)}) collective-permute-start(bf16[64,640]{1,0:T(8,128)(2,1)S(1)} %get-tuple-element.120), channel_id=1, source_target_pairs={{0,8},{8,0},{16,24},{24,16},{1,9},{9,1},{17,25},{25,17},{2,10},{10... | collective-permute-start | bytes 245768 | tf_op jit(solution)/shard_map/ppermute | solution.py:48
  28.7 5.9 %collective-permute-start.12 = (bf16[64,640]{1,0:T(8,128)(2,1)S(1)}, bf16[64,640]{1,0:T(8,128)(2,1)S(1)}, u32[]{:S(2)}, u32[]{:S(2)}) collective-permute-start(bf16[64,640]{1,0:T(8,128)(2,1)S(1)} %get-tuple-element.121), channel_id=1, source_target_pairs={{0,16},{8,24},{16,0},{24,8},{1,17},{9,25},{17,1},{25,9},{2,18},{10... | collective-permute-start | bytes 245768 | tf_op jit(solution)/shard_map/ppermute | solution.py:48
  30.2 5.3 %collective-permute-start.13 = (bf16[64,640]{1,0:T(8,128)(2,1)S(1)}, bf16[64,640]{1,0:T(8,128)(2,1)S(1)}, u32[]{:S(2)}, u32[]{:S(2)}) collective-permute-start(bf16[64,640]{1,0:T(8,128)(2,1)S(1)} %get-tuple-element.122), channel_id=1, source_target_pairs={{0,24},{8,16},{16,8},{24,0},{1,25},{9,17},{17,9},{25,1},{2,26},{10... | collective-permute-start | bytes 245768 | tf_op jit(solution)/shard_map/ppermute | solution.py:48
  36.1 6.5 %collective-permute-start.18 = (bf16[64,640]{1,0:T(8,128)(2,1)S(1)}, bf16[64,640]{1,0:T(8,128)(2,1)S(1)}, u32[]{:S(2)}, u32[]{:S(2)}) collective-permute-start(bf16[64,640]{1,0:T(8,128)(2,1)S(1)} %get-tuple-element.139.refs_0_), channel_id=1, source_target_pairs={{0,4},{1,5},{2,6},{3,7},{4,0},{5,1},{6,2},{7,3},{8,12},{9,13},{10,... | collective-permute-start | bytes 245768 | tf_op jit(solution)/shard_map/ppermute | solution.py:48
  38.6 6.2 %collective-permute-start.22 = (bf16[64,896]{1,0:T(8,128)(2,1)S(1)}, bf16[64,896]{1,0:T(8,128)(2,1)S(1)}, u32[]{:S(2)}, u32[]{:S(2)}) collective-permute-start(bf16[64,896]{1,0:T(8,128)(2,1)S(1)} %get-tuple-element.140.refs_0_), channel_id=1, source_target_pairs={{0,24},{8,16},{16,8},{24,0},{1,25},{9,17},{17,9},{25,1},{2,26},{10... | collective-permute-start | bytes 344072 | tf_op jit(solution)/shard_map/ppermute | solution.py:48
  41.1 5.2 %collective-permute-start.21 = (bf16[64,896]{1,0:T(8,128)(2,1)S(1)}, bf16[64,896]{1,0:T(8,128)(2,1)S(1)}, u32[]{:S(2)}, u32[]{:S(2)}) collective-permute-start(bf16[64,896]{1,0:T(8,128)(2,1)S(1)} %get-tuple-element.140.refs_0_), channel_id=1, source_target_pairs={{0,16},{8,24},{16,0},{24,8},{1,17},{9,25},{17,1},{25,9},{2,18},{10... | collective-permute-start | bytes 344072 | tf_op jit(solution)/shard_map/ppermute | solution.py:48
  41.6 5.0 %collective-permute-start.20 = (bf16[64,896]{1,0:T(8,128)(2,1)S(1)}, bf16[64,896]{1,0:T(8,128)(2,1)S(1)}, u32[]{:S(2)}, u32[]{:S(2)}) collective-permute-start(bf16[64,896]{1,0:T(8,128)(2,1)S(1)} %get-tuple-element.140.refs_0_), channel_id=1, source_target_pairs={{0,8},{8,0},{16,24},{24,16},{1,9},{9,1},{17,25},{25,17},{2,10},{10... | collective-permute-start | bytes 344072 | tf_op jit(solution)/shard_map/ppermute | solution.py:48
  42.1 6.1 %collective-permute-start.17 = (bf16[64,640]{1,0:T(8,128)(2,1)S(1)}, bf16[64,640]{1,0:T(8,128)(2,1)S(1)}, u32[]{:S(2)}, u32[]{:S(2)}) collective-permute-start(bf16[64,640]{1,0:T(8,128)(2,1)S(1)} %get-tuple-element.139.refs_0_), channel_id=1, source_target_pairs={{0,2},{1,3},{2,0},{3,1},{4,6},{5,7},{6,4},{7,5},{8,10},{9,11},{10,... | collective-permute-start | bytes 245768 | tf_op jit(solution)/shard_map/ppermute | solution.py:48
  42.7 5.6 %collective-permute-start.19 = (bf16[64,640]{1,0:T(8,128)(2,1)S(1)}, bf16[64,640]{1,0:T(8,128)(2,1)S(1)}, u32[]{:S(2)}, u32[]{:S(2)}) collective-permute-start(bf16[64,640]{1,0:T(8,128)(2,1)S(1)} %collective-permute-done.18.refs_4_), channel_id=1, source_target_pairs={{0,2},{1,3},{2,0},{3,1},{4,6},{5,7},{6,4},{7,5},{8,10},{9,11},{10,... | collective-permute-start | bytes 245768 | tf_op jit(solution)/shard_map/ppermute | solution.py:48
  48.3 2.4 %collective-permute-start.23 = (bf16[5,64,640]{2,1,0:T(8,128)(2,1)S(1)}, bf16[5,64,640]{2,1,0:T(8,128)(2,1)S(1)}, u32[]{:S(2)}, u32[]{:S(2)}) collective-permute-start(bf16[5,64,640]{2,1,0:T(8,128)(2,1)S(1)} %get-tuple-element.145), channel_id=1, source_target_pairs={{0,1},{1,0},{2,3},{3,2},{4,5},{5,4},{6,7},{7,6},{8,9},{9,8},{10,11... | collective-permute-start | bytes 1228808 | tf_op jit(solution)/shard_map/ppermute | solution.py:48
  48.4 1.9 %collective-permute-start.24 = (bf16[64,640]{1,0:T(8,128)(2,1)S(1)}, bf16[64,640]{1,0:T(8,128)(2,1)S(1)}, u32[]{:S(2)}, u32[]{:S(2)}) collective-permute-start(bf16[64,640]{1,0:T(8,128)(2,1)S(1)} %get-tuple-element.139.refs_0_), channel_id=1, source_target_pairs={{0,1},{1,0},{2,3},{3,2},{4,5},{5,4},{6,7},{7,6},{8,9},{9,8},{10,11... | collective-permute-start | bytes 245768 | tf_op jit(solution)/shard_map/ppermute | solution.py:48
  48.9 1.5 %collective-permute-start.25 = (bf16[64,640]{1,0:T(8,128)(2,1)S(1)}, bf16[64,640]{1,0:T(8,128)(2,1)S(1)}, u32[]{:S(2)}, u32[]{:S(2)}) collective-permute-start(bf16[64,640]{1,0:T(8,128)(2,1)S(1)} %collective-permute-done.17.refs_2_), channel_id=1, source_target_pairs={{0,1},{1,0},{2,3},{3,2},{4,5},{5,4},{6,7},{7,6},{8,9},{9,8},{10,11... | collective-permute-start | bytes 245768 | tf_op jit(solution)/shard_map/ppermute | solution.py:48
  48.9 1.5 %collective-permute-start.26 = (bf16[64,640]{1,0:T(8,128)(2,1)S(1)}, bf16[64,640]{1,0:T(8,128)(2,1)S(1)}, u32[]{:S(2)}, u32[]{:S(2)}) collective-permute-start(bf16[64,640]{1,0:T(8,128)(2,1)S(1)} %collective-permute-done.18.refs_4_), channel_id=1, source_target_pairs={{0,1},{1,0},{2,3},{3,2},{4,5},{5,4},{6,7},{7,6},{8,9},{9,8},{10,11... | collective-permute-start | bytes 245768 | tf_op jit(solution)/shard_map/ppermute | solution.py:48
  49.4 1.3 %collective-permute-start.27 = (bf16[64,640]{1,0:T(8,128)(2,1)S(1)}, bf16[64,640]{1,0:T(8,128)(2,1)S(1)}, u32[]{:S(2)}, u32[]{:S(2)}) collective-permute-start(bf16[64,640]{1,0:T(8,128)(2,1)S(1)} %collective-permute-done.19.refs_6_), channel_id=1, source_target_pairs={{0,1},{1,0},{2,3},{3,2},{4,5},{5,4},{6,7},{7,6},{8,9},{9,8},{10,11... | collective-permute-start | bytes 245768 | tf_op jit(solution)/shard_map/ppermute | solution.py:48
  51.3 8.4 %collective-permute-start.28 = (bf16[64,896]{1,0:T(8,128)(2,1)S(1)}, bf16[64,896]{1,0:T(8,128)(2,1)S(1)}, u32[]{:S(2)}, u32[]{:S(2)}) collective-permute-start(bf16[64,896]{1,0:T(8,128)(2,1)S(1)} %get-tuple-element.152), channel_id=1, source_target_pairs={{0,2},{1,3},{2,0},{3,1},{4,6},{5,7},{6,4},{7,5},{8,10},{9,11},{10,... | collective-permute-start | bytes 344072 | tf_op jit(solution)/shard_map/ppermute | solution.py:48
  51.6 11.9 %collective-permute-start.29 = (bf16[64,896]{1,0:T(8,128)(2,1)S(1)}, bf16[64,896]{1,0:T(8,128)(2,1)S(1)}, u32[]{:S(2)}, u32[]{:S(2)}) collective-permute-start(bf16[64,896]{1,0:T(8,128)(2,1)S(1)} %get-tuple-element.153), channel_id=1, source_target_pairs={{0,4},{1,5},{2,6},{3,7},{4,0},{5,1},{6,2},{7,3},{8,12},{9,13},{10,... | collective-permute-start | bytes 344072 | tf_op jit(solution)/shard_map/ppermute | solution.py:48
  53.3 10.2 %collective-permute-start.30 = (bf16[64,896]{1,0:T(8,128)(2,1)S(1)}, bf16[64,896]{1,0:T(8,128)(2,1)S(1)}, u32[]{:S(2)}, u32[]{:S(2)}) collective-permute-start(bf16[64,896]{1,0:T(8,128)(2,1)S(1)} %get-tuple-element.154), channel_id=1, source_target_pairs={{0,6},{1,7},{2,4},{3,5},{4,2},{5,3},{6,0},{7,1},{8,14},{9,15},{10,... | collective-permute-start | bytes 344072 | tf_op jit(solution)/shard_map/ppermute | solution.py:48
  57.5 9.1 %collective-permute-start.31 = (bf16[64,640]{1,0:T(8,128)(2,1)S(1)}, bf16[64,640]{1,0:T(8,128)(2,1)S(1)}, u32[]{:S(2)}, u32[]{:S(2)}) collective-permute-start(bf16[64,640]{1,0:T(8,128)(2,1)S(1)} %get-tuple-element.161), channel_id=1, source_target_pairs={{0,8},{8,0},{16,24},{24,16},{1,9},{9,1},{17,25},{25,17},{2,10},{10... | collective-permute-start | bytes 245768 | tf_op jit(solution)/shard_map/ppermute | solution.py:48
  58.9 7.7 %collective-permute-start.32 = (bf16[64,640]{1,0:T(8,128)(2,1)S(1)}, bf16[64,640]{1,0:T(8,128)(2,1)S(1)}, u32[]{:S(2)}, u32[]{:S(2)}) collective-permute-start(bf16[64,640]{1,0:T(8,128)(2,1)S(1)} %get-tuple-element.162), channel_id=1, source_target_pairs={{0,16},{8,24},{16,0},{24,8},{1,17},{9,25},{17,1},{25,9},{2,18},{10... | collective-permute-start | bytes 245768 | tf_op jit(solution)/shard_map/ppermute | solution.py:48
  59.6 7.0 %collective-permute-start.33 = (bf16[64,640]{1,0:T(8,128)(2,1)S(1)}, bf16[64,640]{1,0:T(8,128)(2,1)S(1)}, u32[]{:S(2)}, u32[]{:S(2)}) collective-permute-start(bf16[64,640]{1,0:T(8,128)(2,1)S(1)} %get-tuple-element.163), channel_id=1, source_target_pairs={{0,24},{8,16},{16,8},{24,0},{1,25},{9,17},{17,9},{25,1},{2,26},{10... | collective-permute-start | bytes 245768 | tf_op jit(solution)/shard_map/ppermute | solution.py:48
  67.3 6.0 %collective-permute-start.35 = (bf16[64,640]{1,0:T(8,128)(2,1)S(1)}, bf16[64,640]{1,0:T(8,128)(2,1)S(1)}, u32[]{:S(2)}, u32[]{:S(2)}) collective-permute-start(bf16[64,640]{1,0:T(8,128)(2,1)S(1)} %get-tuple-element.168.refs_0_), channel_id=1, source_target_pairs={{0,4},{1,5},{2,6},{3,7},{4,0},{5,1},{6,2},{7,3},{8,12},{9,13},{10,... | collective-permute-start | bytes 245768 | tf_op jit(solution)/shard_map/ppermute | solution.py:48
  69.4 7.0 %collective-permute-start.39 = (bf16[64,896]{1,0:T(8,128)(2,1)S(1)}, bf16[64,896]{1,0:T(8,128)(2,1)S(1)}, u32[]{:S(2)}, u32[]{:S(2)}) collective-permute-start(bf16[64,896]{1,0:T(8,128)(2,1)S(1)} %get-tuple-element.169.refs_0_.refs_8_), channel_id=1, source_target_pairs={{0,24},{8,16},{16,8},{24,0},{1,25},{9,17},{17,9},{25,1},{2,26},{10... | collective-permute-start | bytes 344072 | tf_op jit(solution)/shard_map/ppermute | solution.py:48
  71.5 5.4 %collective-permute-start.38 = (bf16[64,896]{1,0:T(8,128)(2,1)S(1)}, bf16[64,896]{1,0:T(8,128)(2,1)S(1)}, u32[]{:S(2)}, u32[]{:S(2)}) collective-permute-start(bf16[64,896]{1,0:T(8,128)(2,1)S(1)} %get-tuple-element.169.refs_0_.refs_8_), channel_id=1, source_target_pairs={{0,16},{8,24},{16,0},{24,8},{1,17},{9,25},{17,1},{25,9},{2,18},{10... | collective-permute-start | bytes 344072 | tf_op jit(solution)/shard_map/ppermute | solution.py:48
  72.2 4.8 %collective-permute-start.37 = (bf16[64,896]{1,0:T(8,128)(2,1)S(1)}, bf16[64,896]{1,0:T(8,128)(2,1)S(1)}, u32[]{:S(2)}, u32[]{:S(2)}) collective-permute-start(bf16[64,896]{1,0:T(8,128)(2,1)S(1)} %get-tuple-element.169.refs_0_.refs_8_), channel_id=1, source_target_pairs={{0,8},{8,0},{16,24},{24,16},{1,9},{9,1},{17,25},{25,17},{2,10},{10... | collective-permute-start | bytes 344072 | tf_op jit(solution)/shard_map/ppermute | solution.py:48
  72.9 6.0 %collective-permute-start.34 = (bf16[64,640]{1,0:T(8,128)(2,1)S(1)}, bf16[64,640]{1,0:T(8,128)(2,1)S(1)}, u32[]{:S(2)}, u32[]{:S(2)}) collective-permute-start(bf16[64,640]{1,0:T(8,128)(2,1)S(1)} %get-tuple-element.168.refs_0_), channel_id=1, source_target_pairs={{0,2},{1,3},{2,0},{3,1},{4,6},{5,7},{6,4},{7,5},{8,10},{9,11},{10,... | collective-permute-start | bytes 245768 | tf_op jit(solution)/shard_map/ppermute | solution.py:48
  73.2 5.6 %collective-permute-start.36 = (bf16[64,640]{1,0:T(8,128)(2,1)S(1)}, bf16[64,640]{1,0:T(8,128)(2,1)S(1)}, u32[]{:S(2)}, u32[]{:S(2)}) collective-permute-start(bf16[64,640]{1,0:T(8,128)(2,1)S(1)} %collective-permute-done.35.refs_4_), channel_id=1, source_target_pairs={{0,2},{1,3},{2,0},{3,1},{4,6},{5,7},{6,4},{7,5},{8,10},{9,11},{10,... | collective-permute-start | bytes 245768 | tf_op jit(solution)/shard_map/ppermute | solution.py:48
  78.9 2.4 %collective-permute-start.40 = (bf16[5,64,640]{2,1,0:T(8,128)(2,1)S(1)}, bf16[5,64,640]{2,1,0:T(8,128)(2,1)S(1)}, u32[]{:S(2)}, u32[]{:S(2)}) collective-permute-start(bf16[5,64,640]{2,1,0:T(8,128)(2,1)S(1)} %get-tuple-element.172), channel_id=1, source_target_pairs={{0,1},{1,0},{2,3},{3,2},{4,5},{5,4},{6,7},{7,6},{8,9},{9,8},{10,11... | collective-permute-start | bytes 1228808 | tf_op jit(solution)/shard_map/ppermute | solution.py:48
  78.9 1.9 %collective-permute-start.41 = (bf16[64,640]{1,0:T(8,128)(2,1)S(1)}, bf16[64,640]{1,0:T(8,128)(2,1)S(1)}, u32[]{:S(2)}, u32[]{:S(2)}) collective-permute-start(bf16[64,640]{1,0:T(8,128)(2,1)S(1)} %get-tuple-element.168.refs_0_), channel_id=1, source_target_pairs={{0,1},{1,0},{2,3},{3,2},{4,5},{5,4},{6,7},{7,6},{8,9},{9,8},{10,11... | collective-permute-start | bytes 245768 | tf_op jit(solution)/shard_map/ppermute | solution.py:48
  79.4 1.5 %collective-permute-start.42 = (bf16[64,640]{1,0:T(8,128)(2,1)S(1)}, bf16[64,640]{1,0:T(8,128)(2,1)S(1)}, u32[]{:S(2)}, u32[]{:S(2)}) collective-permute-start(bf16[64,640]{1,0:T(8,128)(2,1)S(1)} %collective-permute-done.34.refs_2_), channel_id=1, source_target_pairs={{0,1},{1,0},{2,3},{3,2},{4,5},{5,4},{6,7},{7,6},{8,9},{9,8},{10,11... | collective-permute-start | bytes 245768 | tf_op jit(solution)/shard_map/ppermute | solution.py:48
  79.5 1.5 %collective-permute-start.43 = (bf16[64,640]{1,0:T(8,128)(2,1)S(1)}, bf16[64,640]{1,0:T(8,128)(2,1)S(1)}, u32[]{:S(2)}, u32[]{:S(2)}) collective-permute-start(bf16[64,640]{1,0:T(8,128)(2,1)S(1)} %collective-permute-done.35.refs_4_), channel_id=1, source_target_pairs={{0,1},{1,0},{2,3},{3,2},{4,5},{5,4},{6,7},{7,6},{8,9},{9,8},{10,11... | collective-permute-start | bytes 245768 | tf_op jit(solution)/shard_map/ppermute | solution.py:48
  80.0 1.3 %collective-permute-start.44 = (bf16[64,640]{1,0:T(8,128)(2,1)S(1)}, bf16[64,640]{1,0:T(8,128)(2,1)S(1)}, u32[]{:S(2)}, u32[]{:S(2)}) collective-permute-start(bf16[64,640]{1,0:T(8,128)(2,1)S(1)} %collective-permute-done.36.refs_6_), channel_id=1, source_target_pairs={{0,1},{1,0},{2,3},{3,2},{4,5},{5,4},{6,7},{7,6},{8,9},{9,8},{10,11... | collective-permute-start | bytes 245768 | tf_op jit(solution)/shard_map/ppermute | solution.py:48
  81.9 8.7 %collective-permute-start.48 = (bf16[64,896]{1,0:T(8,128)(2,1)S(1)}, bf16[64,896]{1,0:T(8,128)(2,1)S(1)}, u32[]{:S(2)}, u32[]{:S(2)}) collective-permute-start(bf16[64,896]{1,0:T(8,128)(2,1)S(1)} %get-tuple-element.190), channel_id=1, source_target_pairs={{0,2},{1,3},{2,0},{3,1},{4,6},{5,7},{6,4},{7,5},{8,10},{9,11},{10,... | collective-permute-start | bytes 344072 | tf_op jit(solution)/shard_map/ppermute | solution.py:48
  82.3 11.8 %collective-permute-start.49 = (bf16[64,896]{1,0:T(8,128)(2,1)S(1)}, bf16[64,896]{1,0:T(8,128)(2,1)S(1)}, u32[]{:S(2)}, u32[]{:S(2)}) collective-permute-start(bf16[64,896]{1,0:T(8,128)(2,1)S(1)} %get-tuple-element.191), channel_id=1, source_target_pairs={{0,4},{1,5},{2,6},{3,7},{4,0},{5,1},{6,2},{7,3},{8,12},{9,13},{10,... | collective-permute-start | bytes 344072 | tf_op jit(solution)/shard_map/ppermute | solution.py:48
  84.9 9.3 %collective-permute-start.50 = (bf16[64,896]{1,0:T(8,128)(2,1)S(1)}, bf16[64,896]{1,0:T(8,128)(2,1)S(1)}, u32[]{:S(2)}, u32[]{:S(2)}) collective-permute-start(bf16[64,896]{1,0:T(8,128)(2,1)S(1)} %get-tuple-element.192), channel_id=1, source_target_pairs={{0,6},{1,7},{2,4},{3,5},{4,2},{5,3},{6,0},{7,1},{8,14},{9,15},{10,... | collective-permute-start | bytes 344072 | tf_op jit(solution)/shard_map/ppermute | solution.py:48
  88.6 9.0 %collective-permute-start.45 = (bf16[64,768]{1,0:T(8,128)(2,1)S(1)}, bf16[64,768]{1,0:T(8,128)(2,1)S(1)}, u32[]{:S(2)}, u32[]{:S(2)}) collective-permute-start(bf16[64,768]{1,0:T(8,128)(2,1)S(1)} %get-tuple-element.182), channel_id=1, source_target_pairs={{0,8},{8,0},{16,24},{24,16},{1,9},{9,1},{17,25},{25,17},{2,10},{10... | collective-permute-start | bytes 294920 | tf_op jit(solution)/shard_map/ppermute | solution.py:48
  89.5 8.0 %collective-permute-start.46 = (bf16[64,768]{1,0:T(8,128)(2,1)S(1)}, bf16[64,768]{1,0:T(8,128)(2,1)S(1)}, u32[]{:S(2)}, u32[]{:S(2)}) collective-permute-start(bf16[64,768]{1,0:T(8,128)(2,1)S(1)} %get-tuple-element.183), channel_id=1, source_target_pairs={{0,16},{8,24},{16,0},{24,8},{1,17},{9,25},{17,1},{25,9},{2,18},{10... | collective-permute-start | bytes 294920 | tf_op jit(solution)/shard_map/ppermute | solution.py:48
  90.6 7.0 %collective-permute-start.47 = (bf16[64,768]{1,0:T(8,128)(2,1)S(1)}, bf16[64,768]{1,0:T(8,128)(2,1)S(1)}, u32[]{:S(2)}, u32[]{:S(2)}) collective-permute-start(bf16[64,768]{1,0:T(8,128)(2,1)S(1)} %get-tuple-element.184), channel_id=1, source_target_pairs={{0,24},{8,16},{16,8},{24,0},{1,25},{9,17},{17,9},{25,1},{2,26},{10... | collective-permute-start | bytes 294920 | tf_op jit(solution)/shard_map/ppermute | solution.py:48
  97.7 7.1 %collective-permute-start.53 = (f32[64,64]{1,0:T(8,128)S(1)}, f32[64,64]{1,0:T(8,128)S(1)}, u32[]{:S(2)}, u32[]{:S(2)}) collective-permute-start(f32[64,64]{1,0:T(8,128)S(1)} %last_gram.1), channel_id=1, source_target_pairs={{0,6},{1,7},{2,4},{3,5},{4,2},{5,3},{6,0},{7,1},{8,14},{9,15},{10,... | collective-permute-start | bytes 49160 | tf_op jit(solution)/shard_map/ppermute | solution.py:48
  100.2 4.8 %collective-permute-start.52 = (f32[64,64]{1,0:T(8,128)S(1)}, f32[64,64]{1,0:T(8,128)S(1)}, u32[]{:S(2)}, u32[]{:S(2)}) collective-permute-start(f32[64,64]{1,0:T(8,128)S(1)} %last_gram.1), channel_id=1, source_target_pairs={{0,4},{1,5},{2,6},{3,7},{4,0},{5,1},{6,2},{7,3},{8,12},{9,13},{10,... | collective-permute-start | bytes 49160 | tf_op jit(solution)/shard_map/ppermute | solution.py:48
  101.2 4.1 %collective-permute-start.51 = (f32[64,64]{1,0:T(8,128)S(1)}, f32[64,64]{1,0:T(8,128)S(1)}, u32[]{:S(2)}, u32[]{:S(2)}) collective-permute-start(f32[64,64]{1,0:T(8,128)S(1)} %last_gram.1), channel_id=1, source_target_pairs={{0,2},{1,3},{2,0},{3,1},{4,6},{5,7},{6,4},{7,5},{8,10},{9,11},{10,... | collective-permute-start | bytes 49160 | tf_op jit(solution)/shard_map/ppermute | solution.py:48
  105.3 1.3 %collective-permute-start.54 = (f32[64,64]{1,0:T(8,128)S(1)}, f32[64,64]{1,0:T(8,128)S(1)}, u32[]{:S(2)}, u32[]{:S(2)}) collective-permute-start(f32[64,64]{1,0:T(8,128)S(1)} %add_add_fusion.both_ref), channel_id=1, source_target_pairs={{0,1},{1,0},{2,3},{3,2},{4,5},{5,4},{6,7},{7,6},{8,9},{9,8},{10,11... | collective-permute-start | bytes 49160 | tf_op jit(solution)/shard_map/ppermute | solution.py:48
  (1 other events, 0.9 us)

commit v7 on v6

--- a/solution.py
+++ b/solution.py
@@ -129,7 +129,7 @@
 
 def cols_kernel(rows, cols, table, tile_ref, *refs):
     blocks, refs, (cells, total) = refs[:cols], refs[cols:-2], refs[-2:]
-    last = refs[: rows + 2] if len(refs) > rows else ()
+    last = refs[: rows + 1] if len(refs) > rows else ()
     outs = refs[len(last) : len(last) + rows]
     width = outs[0].shape[1]
     leaf = cells.shape[-1]
@@ -144,9 +144,7 @@
             part = total[(me ^ flip) * per + j]
             out[:, j * leaf : (j + 1) * leaf] = part.astype(out.dtype)
     if last:
-        vector_ref, diagonal_ref = last[rows:]
-        vector = vector_ref[...]
-        both = contract(vector, vector * diagonal_ref[...], ((1,), (1,)), HIGHEST)
+        both = last[rows][...]
         half = jnp.zeros_like(both)
         for flip, ref in enumerate(last[:rows]):
             for j in range(per):
@@ -223,6 +221,11 @@
     cross = contract(vector, following, ((1,), (1,)), HIGHEST)
     square = contract(following, following, ((1,), (1,)), HIGHEST)
     put_vector(following, jnp.concatenate([cross, square], axis=1), plain_ref, wide_ref)
+
+
+def weighted_kernel(vector_ref, diagonal_ref, out_ref):
+    vector = vector_ref[...]
+    out_ref[...] = contract(vector, vector * diagonal_ref[...], ((1,), (1,)), HIGHEST)
 
 
 def last_gram_kernel(both_ref, *refs):
@@ -419,13 +422,17 @@
             held |= {k ^ flip: partner_permute(m, "col", 2 * flip) for k, m in held.items()}
             flip //= 2
         over_chip = [held[k] for k in range(1, chips)]
+        held_wide = wide
+        if last:
+            weighted = call(weighted_kernel, "weighted", f32(cases, cases), *last)
+            held_wide, weighted = lax.optimization_barrier((wide, weighted))
         send, keep, gram = call(
             rows_kernel,
             "rows_half",
             [bf16(chips + 1, cases, width), f32(chips, cases, width), f32(cases, GRAM)],
             table,
             turned,
-            wide,
+            held_wide,
             *over_row,
             scalars=(0,),
             scratch=[
@@ -470,7 +477,7 @@
             table,
             tiles,
             *row_group,
-            *([wide, *over_row, *last] if last else []),
+            *([held_wide, *over_row, weighted] if last else []),
             scalars=(0,),
             scratch=[
                 pltpu.VMEM((cols * per, cases, leaf), jnp.bfloat16),

time: 110 us -> 110 us (level)
    pallas_call x23 -> x24, Pallas kernels: 31.2 us -> 31.7 us  [call(): pl.pallas_call(kernel, out_shape=outs, in_specs=[smem if k in scalars els...]
  transfers between devices with their start and end apart: 55 -> 55, of which waited for: 25 -> 25; matrix products, arithmetic and copies ran while one was open for 0% -> 0% of each run, Pallas kernels for 22% -> 23%
where the time goes in v7:
time: 110 us
  starting transfers between devices  57 us (52%)
  Pallas kernels  31.7 us (29%)
  waiting for transfers between devices  17.7 us (16%)
  local copies, waits for them, and re-layouts  1.73 us (2%)
  between operations  1.72 us (2%)
    ppermute x55, starting transfers between devices, partner_permute(): return lax.ppermute(value, axis, [(i, i ^ flip) for i in range(size)])  57 us
    pallas_call x24, Pallas kernels, call(): pl.pallas_call(kernel, out_shape=outs, in_specs=[smem if k in scalars els...  31.7 us
    ppermute x55, waiting for transfers between devices, partner_permute(): return lax.ppermute(value, axis, [(i, i ^ flip) for i in range(size)])  17.7 us
  transfers between devices with their start and end apart: 55, of which 25 were waited for; matrix products, arithmetic and copies ran while one was open for 0% of the time, Pallas kernels for 23%

profile of v7, /device:TPU:0, one launch (start us, length us, event | category | flops | bytes accessed | tf_op | source)
XLA Modules:
  0.0 109.9 jit_solution(12825326739137735506)
XLA Ops:
  0.6 0.7 broadcast_in_dim.3.diagonal_ref
  1.3 0.9 copy-done.1
  2.6 4.1 %collective-permute-start.1 = (bf16[64,640]{1,0:T(8,128)(2,1)S(1)}, bf16[64,640]{1,0:T(8,128)(2,1)S(1)}, u32[]{:S(2)}, u32[]{:S(2)}) collective-permute-start(bf16[64,640]{1,0:T(8,128)(2,1)S(1)} %get-tuple-element.109.refs_0_), channel_id=1, source_target_pairs={{0,4},{1,5},{2,6},{3,7},{4,0},{5,1},{6,2},{7,3},{8,12},{9,13},{10,... | collective-permute-start | bytes 245768 | tf_op jit(solution)/shard_map/ppermute | solution.py:48
  6.7 2.4 %collective-permute-start.5 = (bf16[64,896]{1,0:T(8,128)(2,1)S(1)}, bf16[64,896]{1,0:T(8,128)(2,1)S(1)}, u32[]{:S(2)}, u32[]{:S(2)}) collective-permute-start(bf16[64,896]{1,0:T(8,128)(2,1)S(1)} %get-tuple-element.111.refs_0_), channel_id=1, source_target_pairs={{0,24},{8,16},{16,8},{24,0},{1,25},{9,17},{17,9},{25,1},{2,26},{10... | collective-permute-start | bytes 344072 | tf_op jit(solution)/shard_map/ppermute | solution.py:48
  9.2 0.5 collective-permute-start.4
  9.7 0.5 collective-permute-start.3
  10.2 1.6 %collective-permute-start = (bf16[64,640]{1,0:T(8,128)(2,1)S(1)}, bf16[64,640]{1,0:T(8,128)(2,1)S(1)}, u32[]{:S(2)}, u32[]{:S(2)}) collective-permute-start(bf16[64,640]{1,0:T(8,128)(2,1)S(1)} %get-tuple-element.109.refs_0_), channel_id=1, source_target_pairs={{0,2},{1,3},{2,0},{3,1},{4,6},{5,7},{6,4},{7,5},{8,10},{9,11},{10,... | collective-permute-start | bytes 245768 | tf_op jit(solution)/shard_map/ppermute | solution.py:48
  13.0 3.1 %dense_tiles.1 = (bf16[96,128,128]{2,1,0:T(8,128)(2,1)S(1)}, bf16[96,128,128]{2,1,0:T(8,128)(2,1)S(1)}) custom-call(s32[259]{0:T(512)S(1)} %concatenate.3.table, bf16[32,128,128]{2,1,0:T(8,128)(2,1)S(1)} %bitcast.12, bf16[64,32,128]{2,1,0:T(8,128)(2,1)S(1)} %bitcast.13, bf16[64,32,128]{2,1,0:T(8,128)(2,1)S(1)} %bitcast.14), custom_call_target="tpu_custom_call" | custom-call | tf_op jit(solution)/shard_map/dense_tiles/pallas_call | solution.py:363
  16.2 1.7 %rows_half.3 = (bf16[5,64,640]{2,1,0:T(8,128)(2,1)S(1)}, f32[4,64,640]{2,1,0:T(8,128)S(1)}, f32[64,128]{1,0:T(8,128)S(1)}) custom-call(s32[259]{0:T(512)S(1)} %concatenate.3.table, bf16[96,128,128]{2,1,0:T(8,128)(2,1)S(1)} %get-tuple-element.110.tile_ref, bf16[64,896]{1,0:T(8,128)(2,1)S(1)} %get-tuple-element.111.refs_0_, ...), custom_call_target="tpu_custom_call" | custom-call | tf_op jit(solution)/shard_map/rows_half/pallas_call | solution.py:363
  19.1 0.8 collective-permute-done.7.refs_1_
  20.3 0.6 pair_sums.3
  20.9 1.6 %collective-permute-start.14 = (bf16[64,896]{1,0:T(8,128)(2,1)S(1)}, bf16[64,896]{1,0:T(8,128)(2,1)S(1)}, u32[]{:S(2)}, u32[]{:S(2)}) collective-permute-start(bf16[64,896]{1,0:T(8,128)(2,1)S(1)} %get-tuple-element.130), channel_id=1, source_target_pairs={{0,2},{1,3},{2,0},{3,1},{4,6},{5,7},{6,4},{7,5},{8,10},{9,11},{10,... | collective-permute-start | bytes 344072 | tf_op jit(solution)/shard_map/ppermute | solution.py:48
  22.6 1.4 %collective-permute-start.15 = (bf16[64,896]{1,0:T(8,128)(2,1)S(1)}, bf16[64,896]{1,0:T(8,128)(2,1)S(1)}, u32[]{:S(2)}, u32[]{:S(2)}) collective-permute-start(bf16[64,896]{1,0:T(8,128)(2,1)S(1)} %get-tuple-element.131), channel_id=1, source_target_pairs={{0,4},{1,5},{2,6},{3,7},{4,0},{5,1},{6,2},{7,3},{8,12},{9,13},{10,... | collective-permute-start | bytes 344072 | tf_op jit(solution)/shard_map/ppermute | solution.py:48
  24.0 1.4 %collective-permute-start.16 = (bf16[64,896]{1,0:T(8,128)(2,1)S(1)}, bf16[64,896]{1,0:T(8,128)(2,1)S(1)}, u32[]{:S(2)}, u32[]{:S(2)}) collective-permute-start(bf16[64,896]{1,0:T(8,128)(2,1)S(1)} %get-tuple-element.132), channel_id=1, source_target_pairs={{0,6},{1,7},{2,4},{3,5},{4,2},{5,3},{6,0},{7,1},{8,14},{9,15},{10,... | collective-permute-start | bytes 344072 | tf_op jit(solution)/shard_map/ppermute | solution.py:48
  25.4 1.7 %cols_half.3 = (f32[64,640]{1,0:T(8,128)S(1)}, bf16[64,640]{1,0:T(8,128)(2,1)S(1)}, bf16[64,640]{1,0:T(8,128)(2,1)S(1)}, bf16[64,640]{1,0:T(8,128)(2,1)S(1)}) custom-call(s32[259]{0:T(512)S(1)} %concatenate.3.table, bf16[96,128,128]{2,1,0:T(8,128)(2,1)S(1)} %get-tuple-element.108.tile_ref, bf16[64,640]{1,0:T(8,128)(2,1)S(1)} %get-tuple-element.109.refs_0_, ...), custom_call_target="tpu_custom_call" | custom-call | tf_op jit(solution)/shard_map/cols_half/pallas_call | solution.py:363
  27.1 1.6 %collective-permute-start.11 = (bf16[64,640]{1,0:T(8,128)(2,1)S(1)}, bf16[64,640]{1,0:T(8,128)(2,1)S(1)}, u32[]{:S(2)}, u32[]{:S(2)}) collective-permute-start(bf16[64,640]{1,0:T(8,128)(2,1)S(1)} %get-tuple-element.122), channel_id=1, source_target_pairs={{0,8},{8,0},{16,24},{24,16},{1,9},{9,1},{17,25},{25,17},{2,10},{10... | collective-permute-start | bytes 245768 | tf_op jit(solution)/shard_map/ppermute | solution.py:48
  28.7 1.5 %collective-permute-start.12 = (bf16[64,640]{1,0:T(8,128)(2,1)S(1)}, bf16[64,640]{1,0:T(8,128)(2,1)S(1)}, u32[]{:S(2)}, u32[]{:S(2)}) collective-permute-start(bf16[64,640]{1,0:T(8,128)(2,1)S(1)} %get-tuple-element.123), channel_id=1, source_target_pairs={{0,16},{8,24},{16,0},{24,8},{1,17},{9,25},{17,1},{25,9},{2,18},{10... | collective-permute-start | bytes 245768 | tf_op jit(solution)/shard_map/ppermute | solution.py:48
  30.7 3.6 %collective-permute-done.15.refs_1_ = bf16[64,896]{1,0:T(8,128)(2,1)S(1)} collective-permute-done((bf16[64,896]{1,0:T(8,128)(2,1)S(1)}, bf16[64,896]{1,0:T(8,128)(2,1)S(1)}, u32[]{:S(2)}, u32[]{:S(2)}) %collective-permute-start.15) | collective-permute-done | bytes 114720 | tf_op jit(solution)/shard_map/ppermute | solution.py:48
  34.5 1.0 collective-permute-done.13.refs_4_
  35.5 0.6 combine.2
  36.1 2.5 %collective-permute-start.18 = (bf16[64,640]{1,0:T(8,128)(2,1)S(1)}, bf16[64,640]{1,0:T(8,128)(2,1)S(1)}, u32[]{:S(2)}, u32[]{:S(2)}) collective-permute-start(bf16[64,640]{1,0:T(8,128)(2,1)S(1)} %get-tuple-element.141.refs_0_), channel_id=1, source_target_pairs={{0,4},{1,5},{2,6},{3,7},{4,0},{5,1},{6,2},{7,3},{8,12},{9,13},{10,... | collective-permute-start | bytes 245768 | tf_op jit(solution)/shard_map/ppermute | solution.py:48
  38.6 2.4 %collective-permute-start.22 = (bf16[64,896]{1,0:T(8,128)(2,1)S(1)}, bf16[64,896]{1,0:T(8,128)(2,1)S(1)}, u32[]{:S(2)}, u32[]{:S(2)}) collective-permute-start(bf16[64,896]{1,0:T(8,128)(2,1)S(1)} %get-tuple-element.142.refs_0_), channel_id=1, source_target_pairs={{0,24},{8,16},{16,8},{24,0},{1,25},{9,17},{17,9},{25,1},{2,26},{10... | collective-permute-start | bytes 344072 | tf_op jit(solution)/shard_map/ppermute | solution.py:48
  41.1 0.5 collective-permute-start.21
  41.6 0.5 collective-permute-start.20
  42.1 0.6 collective-permute-start.17
  42.7 1.5 %collective-permute-start.19 = (bf16[64,640]{1,0:T(8,128)(2,1)S(1)}, bf16[64,640]{1,0:T(8,128)(2,1)S(1)}, u32[]{:S(2)}, u32[]{:S(2)}) collective-permute-start(bf16[64,640]{1,0:T(8,128)(2,1)S(1)} %collective-permute-done.18.refs_4_), channel_id=1, source_target_pairs={{0,2},{1,3},{2,0},{3,1},{4,6},{5,7},{6,4},{7,5},{8,10},{9,11},{10,... | collective-permute-start | bytes 245768 | tf_op jit(solution)/shard_map/ppermute | solution.py:48
  44.1 0.7 collective-permute-done.22.refs_3_
  44.9 1.4 %collective-permute-done.21.refs_2_ = bf16[64,896]{1,0:T(8,128)(2,1)S(1)} collective-permute-done((bf16[64,896]{1,0:T(8,128)(2,1)S(1)}, bf16[64,896]{1,0:T(8,128)(2,1)S(1)}, u32[]{:S(2)}, u32[]{:S(2)}) %collective-permute-start.21) | collective-permute-done | bytes 114720 | tf_op jit(solution)/shard_map/ppermute | solution.py:48
  46.5 1.7 %rows_half.4 = (bf16[5,64,640]{2,1,0:T(8,128)(2,1)S(1)}, f32[4,64,640]{2,1,0:T(8,128)S(1)}, f32[64,128]{1,0:T(8,128)S(1)}) custom-call(s32[259]{0:T(512)S(1)} %concatenate.3.table, bf16[96,128,128]{2,1,0:T(8,128)(2,1)S(1)} %get-tuple-element.110.tile_ref, bf16[64,896]{1,0:T(8,128)(2,1)S(1)} %get-tuple-element.142.refs_0_, ...), custom_call_target="tpu_custom_call" | custom-call | tf_op jit(solution)/shard_map/rows_half/pallas_call | solution.py:363
  49.5 0.8 collective-permute-done.24.refs_1_
  50.7 0.6 pair_sums.4
  51.6 1.7 %collective-permute-start.29 = (bf16[64,896]{1,0:T(8,128)(2,1)S(1)}, bf16[64,896]{1,0:T(8,128)(2,1)S(1)}, u32[]{:S(2)}, u32[]{:S(2)}) collective-permute-start(bf16[64,896]{1,0:T(8,128)(2,1)S(1)} %get-tuple-element.155), channel_id=1, source_target_pairs={{0,4},{1,5},{2,6},{3,7},{4,0},{5,1},{6,2},{7,3},{8,12},{9,13},{10,... | collective-permute-start | bytes 344072 | tf_op jit(solution)/shard_map/ppermute | solution.py:48
  53.3 2.5 %collective-permute-start.30 = (bf16[64,896]{1,0:T(8,128)(2,1)S(1)}, bf16[64,896]{1,0:T(8,128)(2,1)S(1)}, u32[]{:S(2)}, u32[]{:S(2)}) collective-permute-start(bf16[64,896]{1,0:T(8,128)(2,1)S(1)} %get-tuple-element.156), channel_id=1, source_target_pairs={{0,6},{1,7},{2,4},{3,5},{4,2},{5,3},{6,0},{7,1},{8,14},{9,15},{10,... | collective-permute-start | bytes 344072 | tf_op jit(solution)/shard_map/ppermute | solution.py:48
  55.7 1.7 %cols_half.4 = (f32[64,640]{1,0:T(8,128)S(1)}, bf16[64,640]{1,0:T(8,128)(2,1)S(1)}, bf16[64,640]{1,0:T(8,128)(2,1)S(1)}, bf16[64,640]{1,0:T(8,128)(2,1)S(1)}) custom-call(s32[259]{0:T(512)S(1)} %concatenate.3.table, bf16[96,128,128]{2,1,0:T(8,128)(2,1)S(1)} %get-tuple-element.108.tile_ref, bf16[64,640]{1,0:T(8,128)(2,1)S(1)} %get-tuple-element.141.refs_0_, ...), custom_call_target="tpu_custom_call" | custom-call | tf_op jit(solution)/shard_map/cols_half/pallas_call | solution.py:363
  57.5 1.4 %collective-permute-start.31 = (bf16[64,640]{1,0:T(8,128)(2,1)S(1)}, bf16[64,640]{1,0:T(8,128)(2,1)S(1)}, u32[]{:S(2)}, u32[]{:S(2)}) collective-permute-start(bf16[64,640]{1,0:T(8,128)(2,1)S(1)} %get-tuple-element.163), channel_id=1, source_target_pairs={{0,8},{8,0},{16,24},{24,16},{1,9},{9,1},{17,25},{25,17},{2,10},{10... | collective-permute-start | bytes 245768 | tf_op jit(solution)/shard_map/ppermute | solution.py:48
  58.9 0.8 collective-permute-start.32
  59.6 1.4 %collective-permute-start.33 = (bf16[64,640]{1,0:T(8,128)(2,1)S(1)}, bf16[64,640]{1,0:T(8,128)(2,1)S(1)}, u32[]{:S(2)}, u32[]{:S(2)}) collective-permute-start(bf16[64,640]{1,0:T(8,128)(2,1)S(1)} %get-tuple-element.165), channel_id=1, source_target_pairs={{0,24},{8,16},{16,8},{24,0},{1,25},{9,17},{17,9},{25,1},{2,26},{10... | collective-permute-start | bytes 245768 | tf_op jit(solution)/shard_map/ppermute | solution.py:48
  61.0 2.4 %collective-permute-done.29.refs_1_ = bf16[64,896]{1,0:T(8,128)(2,1)S(1)} collective-permute-done((bf16[64,896]{1,0:T(8,128)(2,1)S(1)}, bf16[64,896]{1,0:T(8,128)(2,1)S(1)}, u32[]{:S(2)}, u32[]{:S(2)}) %collective-permute-start.29) | collective-permute-done | bytes 114720 | tf_op jit(solution)/shard_map/ppermute | solution.py:48
  63.5 3.1 %coefficients.2.first_ref = f32[64,256]{1,0:T(8,128)S(1)} custom-call(f32[8,128]{1,0:T(8,128)S(1)} %shift.1.shift_ref, f32[64,128]{1,0:T(8,128)S(1)} %get-tuple-element.133.gram_ref.gram0_ref, f32[64,128]{1,0:T(8,128)S(1)} %get-tuple-element.166.gram1_ref), custom_call_target="tpu_custom_call" | custom-call | tf_op jit(solution)/shard_map/coefficients/pallas_call | solution.py:363
  66.6 0.6 combine.3
  67.3 2.1 %collective-permute-start.35 = (bf16[64,640]{1,0:T(8,128)(2,1)S(1)}, bf16[64,640]{1,0:T(8,128)(2,1)S(1)}, u32[]{:S(2)}, u32[]{:S(2)}) collective-permute-start(bf16[64,640]{1,0:T(8,128)(2,1)S(1)} %get-tuple-element.170.refs_0_), channel_id=1, source_target_pairs={{0,4},{1,5},{2,6},{3,7},{4,0},{5,1},{6,2},{7,3},{8,12},{9,13},{10,... | collective-permute-start | bytes 245768 | tf_op jit(solution)/shard_map/ppermute | solution.py:48
  69.4 2.2 %collective-permute-start.39 = (bf16[64,896]{1,0:T(8,128)(2,1)S(1)}, bf16[64,896]{1,0:T(8,128)(2,1)S(1)}, u32[]{:S(2)}, u32[]{:S(2)}) collective-permute-start(bf16[64,896]{1,0:T(8,128)(2,1)S(1)} %get-tuple-element.173.refs_0_.refs_8_), channel_id=1, source_target_pairs={{0,24},{8,16},{16,8},{24,0},{1,25},{9,17},{17,9},{25,1},{2,26},{10... | collective-permute-start | bytes 344072 | tf_op jit(solution)/shard_map/ppermute | solution.py:48
  71.5 0.6 collective-permute-start.38
  72.2 0.7 collective-permute-start.37
  73.2 1.7 %collective-permute-start.36 = (bf16[64,640]{1,0:T(8,128)(2,1)S(1)}, bf16[64,640]{1,0:T(8,128)(2,1)S(1)}, u32[]{:S(2)}, u32[]{:S(2)}) collective-permute-start(bf16[64,640]{1,0:T(8,128)(2,1)S(1)} %collective-permute-done.35.refs_4_), channel_id=1, source_target_pairs={{0,2},{1,3},{2,0},{3,1},{4,6},{5,7},{6,4},{7,5},{8,10},{9,11},{10,... | collective-permute-start | bytes 245768 | tf_op jit(solution)/shard_map/ppermute | solution.py:48
  75.2 1.1 %collective-permute-done.39.refs_3_.refs_11_ = bf16[64,896]{1,0:T(8,128)(2,1)S(1)} collective-permute-done((bf16[64,896]{1,0:T(8,128)(2,1)S(1)}, bf16[64,896]{1,0:T(8,128)(2,1)S(1)}, u32[]{:S(2)}, u32[]{:S(2)}) %collective-permute-start.39) | collective-permute-done | bytes 114720 | tf_op jit(solution)/shard_map/ppermute | solution.py:48
  76.4 0.6 collective-permute-done.38.refs_2_.refs_10_
  77.0 1.9 %rows_half.5 = (bf16[5,64,640]{2,1,0:T(8,128)(2,1)S(1)}, f32[4,64,640]{2,1,0:T(8,128)S(1)}, f32[64,128]{1,0:T(8,128)S(1)}) custom-call(s32[259]{0:T(512)S(1)} %concatenate.3.table, bf16[96,128,128]{2,1,0:T(8,128)(2,1)S(1)} %get-tuple-element.110.tile_ref, bf16[64,896]{1,0:T(8,128)(2,1)S(1)} %get-tuple-element.173.refs_0_.refs_8_, ...), custom_call_target="tpu_custom_call" | custom-call | tf_op jit(solution)/shard_map/rows_half/pallas_call | solution.py:363
  80.1 0.8 collective-permute-done.41.refs_1_
  81.3 0.6 pair_sums.5
  82.3 2.6 %collective-permute-start.49 = (bf16[64,896]{1,0:T(8,128)(2,1)S(1)}, bf16[64,896]{1,0:T(8,128)(2,1)S(1)}, u32[]{:S(2)}, u32[]{:S(2)}) collective-permute-start(bf16[64,896]{1,0:T(8,128)(2,1)S(1)} %get-tuple-element.195), channel_id=1, source_target_pairs={{0,4},{1,5},{2,6},{3,7},{4,0},{5,1},{6,2},{7,3},{8,12},{9,13},{10,... | collective-permute-start | bytes 344072 | tf_op jit(solution)/shard_map/ppermute | solution.py:48
  85.0 1.4 %collective-permute-start.50 = (bf16[64,896]{1,0:T(8,128)(2,1)S(1)}, bf16[64,896]{1,0:T(8,128)(2,1)S(1)}, u32[]{:S(2)}, u32[]{:S(2)}) collective-permute-start(bf16[64,896]{1,0:T(8,128)(2,1)S(1)} %get-tuple-element.196), channel_id=1, source_target_pairs={{0,6},{1,7},{2,4},{3,5},{4,2},{5,3},{6,0},{7,1},{8,14},{9,15},{10,... | collective-permute-start | bytes 344072 | tf_op jit(solution)/shard_map/ppermute | solution.py:48
  86.4 2.4 %cols_half.5 = (f32[64,640]{1,0:T(8,128)S(1)}, bf16[64,768]{1,0:T(8,128)(2,1)S(1)}, bf16[64,768]{1,0:T(8,128)(2,1)S(1)}, bf16[64,768]{1,0:T(8,128)(2,1)S(1)}, f32[64,64]{1,0:T(8,128)S(1)}) custom-call(s32[259]{0:T(512)S(1)} %concatenate.3.table, bf16[96,128,128]{2,1,0:T(8,128)(2,1)S(1)} %get-tuple-element.108.tile_ref, ...), custom_call_target="tpu_custom_call" | custom-call | tf_op jit(solution)/shard_map/cols_half/pallas_call | solution.py:363
  88.8 1.0 collective-permute-start.45
  89.8 1.0 collective-permute-start.46
  90.8 1.5 %collective-permute-start.47 = (bf16[64,768]{1,0:T(8,128)(2,1)S(1)}, bf16[64,768]{1,0:T(8,128)(2,1)S(1)}, u32[]{:S(2)}, u32[]{:S(2)}) collective-permute-start(bf16[64,768]{1,0:T(8,128)(2,1)S(1)} %get-tuple-element.188), channel_id=1, source_target_pairs={{0,24},{8,16},{16,8},{24,0},{1,25},{9,17},{17,9},{25,1},{2,26},{10... | collective-permute-start | bytes 294920 | tf_op jit(solution)/shard_map/ppermute | solution.py:48
  92.3 1.9 %collective-permute-done.49.refs_1_ = bf16[64,896]{1,0:T(8,128)(2,1)S(1)} collective-permute-done((bf16[64,896]{1,0:T(8,128)(2,1)S(1)}, bf16[64,896]{1,0:T(8,128)(2,1)S(1)}, u32[]{:S(2)}, u32[]{:S(2)}) %collective-permute-start.49) | collective-permute-done | bytes 114720 | tf_op jit(solution)/shard_map/ppermute | solution.py:48
  94.3 3.3 %solve.1.solve_ref = f32[64,128]{1,0:T(8,128)S(1)} custom-call(f32[8,128]{1,0:T(8,128)S(1)} %shift.1.shift_ref, f32[64,128]{1,0:T(8,128)S(1)} %get-tuple-element.133.gram_ref.gram0_ref, f32[64,128]{1,0:T(8,128)S(1)} %get-tuple-element.166.gram1_ref, f32[64,128]{1,0:T(8,128)S(1)} %get-tuple-element.197.gram2_ref, f32[64,256]{1,0:T(8,128)S(1)} %coefficients.2.first_ref), custom_call_target="tpu_custom_call" | custom-call | tf_op jit(solution)/shard_map/solve/pallas_call | solution.py:363
  97.7 2.4 %collective-permute-start.53 = (f32[64,64]{1,0:T(8,128)S(1)}, f32[64,64]{1,0:T(8,128)S(1)}, u32[]{:S(2)}, u32[]{:S(2)}) collective-permute-start(f32[64,64]{1,0:T(8,128)S(1)} %last_gram.1), channel_id=1, source_target_pairs={{0,6},{1,7},{2,4},{3,5},{4,2},{5,3},{6,0},{7,1},{8,14},{9,15},{10,... | collective-permute-start | bytes 49160 | tf_op jit(solution)/shard_map/ppermute | solution.py:48
  100.2 1.1 collective-permute-start.52
  101.2 1.0 collective-permute-start.51
  102.2 2.7 %coefficients.3 = (f32[192,256]{1,0:T(8,128)S(1)}, f32[64,256]{1,0:T(8,128)S(1)}) custom-call(f32[8,128]{1,0:T(8,128)S(1)} %shift.1.shift_ref, f32[64,128]{1,0:T(8,128)S(1)} %get-tuple-element.133.gram_ref.gram0_ref, f32[64,128]{1,0:T(8,128)S(1)} %get-tuple-element.166.gram1_ref, f32[64,128]{1,0:T(8,128)S(1)} %get-tuple-element.197.gram2_ref, ...), custom_call_target="tpu_custom_call" | custom-call | tf_op jit(solution)/shard_map/coefficients/pallas_call | solution.py:363
  105.4 0.8 vectors.1.vectors_ref
  106.6 3.3 %finish.1 = (f32[64,640]{1,0:T(8,128)}, f32[64,640]{1,0:T(8,128)}) custom-call(f32[256,640]{1,0:T(8,128)S(1)} %vectors.1.vectors_ref, f32[64,256]{1,0:T(8,128)S(1)} %get-tuple-element.210.small_ref, f32[64,64]{1,0:T(8,128)S(1)} %add_add_fusion.both_ref, f32[64,64]{1,0:T(8,128)S(1)} %collective-permute-done.54.other_ref, ...), custom_call_target="tpu_custom_call" | custom-call | tf_op jit(solution)/shard_map/finish/pallas_call | solution.py:363
  (93 shorter events, 9.3 us)
Async XLA Ops:
  2.2 10.7 %copy-start.5 = (s32[1,1,32]{2,1,0:T(1,128)S(1)}, s32[1,1,32]{2,1,0:T(1,128)}, u32[]{:S(2)}) copy-start(s32[1,1,32]{2,1,0:T(1,128)} %param.14) | copy-start | bytes 388
  2.2 10.7 %copy-start.6 = (s32[1,1,64]{2,1,0:T(1,128)S(1)}, s32[1,1,64]{2,1,0:T(1,128)}, u32[]{:S(2)}) copy-start(s32[1,1,64]{2,1,0:T(1,128)} %param.19) | copy-start | bytes 772
  2.2 10.7 %copy-start.7 = (s32[1,1,32]{2,1,0:T(1,128)S(1)}, s32[1,1,32]{2,1,0:T(1,128)}, u32[]{:S(2)}) copy-start(s32[1,1,32]{2,1,0:T(1,128)} %param.15) | copy-start | bytes 388
  2.2 10.7 %copy-start.8 = (s32[1,1,64]{2,1,0:T(1,128)S(1)}, s32[1,1,64]{2,1,0:T(1,128)}, u32[]{:S(2)}) copy-start(s32[1,1,64]{2,1,0:T(1,128)} %param.20) | copy-start | bytes 772
  2.2 10.7 %copy-start.9 = (s32[1,1,64]{2,1,0:T(1,128)S(1)}, s32[1,1,64]{2,1,0:T(1,128)}, u32[]{:S(2)}) copy-start(s32[1,1,64]{2,1,0:T(1,128)} %param.21) | copy-start | bytes 772
  2.3 10.8 %copy-start = (bf16[1,1,32,128,128]{4,3,2,1,0:T(8,128)(2,1)S(1)}, bf16[1,1,32,128,128]{4,3,2,1,0:T(8,128)(2,1)}, u32[]{:S(2)}) copy-start(bf16[1,1,32,128,128]{4,3,2,1,0:T(8,128)(2,1)} %param.13) | copy-start | bytes 3145732
  2.3 10.8 %copy-start.3 = (bf16[1,1,64,32,128]{4,3,2,1,0:T(8,128)(2,1)S(1)}, bf16[1,1,64,32,128]{4,3,2,1,0:T(8,128)(2,1)}, u32[]{:S(2)}) copy-start(bf16[1,1,64,32,128]{4,3,2,1,0:T(8,128)(2,1)} %param.17) | copy-start | bytes 1572868
  2.3 10.8 %copy-start.4 = (bf16[1,1,64,32,128]{4,3,2,1,0:T(8,128)(2,1)S(1)}, bf16[1,1,64,32,128]{4,3,2,1,0:T(8,128)(2,1)}, u32[]{:S(2)}) copy-start(bf16[1,1,64,32,128]{4,3,2,1,0:T(8,128)(2,1)} %param.18) | copy-start | bytes 1572868
  2.6 9.2 %collective-permute-start.1 = (bf16[64,640]{1,0:T(8,128)(2,1)S(1)}, bf16[64,640]{1,0:T(8,128)(2,1)S(1)}, u32[]{:S(2)}, u32[]{:S(2)}) collective-permute-start(bf16[64,640]{1,0:T(8,128)(2,1)S(1)} %get-tuple-element.109.refs_0_), channel_id=1, source_target_pairs={{0,4},{1,5},{2,6},{3,7},{4,0},{5,1},{6,2},{7,3},{8,12},{9,13},{10,... | collective-permute-start | bytes 245768 | tf_op jit(solution)/shard_map/ppermute | solution.py:48
  6.7 9.4 %collective-permute-start.5 = (bf16[64,896]{1,0:T(8,128)(2,1)S(1)}, bf16[64,896]{1,0:T(8,128)(2,1)S(1)}, u32[]{:S(2)}, u32[]{:S(2)}) collective-permute-start(bf16[64,896]{1,0:T(8,128)(2,1)S(1)} %get-tuple-element.111.refs_0_), channel_id=1, source_target_pairs={{0,24},{8,16},{16,8},{24,0},{1,25},{9,17},{17,9},{25,1},{2,26},{10... | collective-permute-start | bytes 344072 | tf_op jit(solution)/shard_map/ppermute | solution.py:48
  9.2 7.0 %collective-permute-start.4 = (bf16[64,896]{1,0:T(8,128)(2,1)S(1)}, bf16[64,896]{1,0:T(8,128)(2,1)S(1)}, u32[]{:S(2)}, u32[]{:S(2)}) collective-permute-start(bf16[64,896]{1,0:T(8,128)(2,1)S(1)} %get-tuple-element.111.refs_0_), channel_id=1, source_target_pairs={{0,16},{8,24},{16,0},{24,8},{1,17},{9,25},{17,1},{25,9},{2,18},{10... | collective-permute-start | bytes 344072 | tf_op jit(solution)/shard_map/ppermute | solution.py:48
  9.7 6.5 %collective-permute-start.3 = (bf16[64,896]{1,0:T(8,128)(2,1)S(1)}, bf16[64,896]{1,0:T(8,128)(2,1)S(1)}, u32[]{:S(2)}, u32[]{:S(2)}) collective-permute-start(bf16[64,896]{1,0:T(8,128)(2,1)S(1)} %get-tuple-element.111.refs_0_), channel_id=1, source_target_pairs={{0,8},{8,0},{16,24},{24,16},{1,9},{9,1},{17,25},{25,17},{2,10},{10... | collective-permute-start | bytes 344072 | tf_op jit(solution)/shard_map/ppermute | solution.py:48
  10.2 7.7 %collective-permute-start = (bf16[64,640]{1,0:T(8,128)(2,1)S(1)}, bf16[64,640]{1,0:T(8,128)(2,1)S(1)}, u32[]{:S(2)}, u32[]{:S(2)}) collective-permute-start(bf16[64,640]{1,0:T(8,128)(2,1)S(1)} %get-tuple-element.109.refs_0_), channel_id=1, source_target_pairs={{0,2},{1,3},{2,0},{3,1},{4,6},{5,7},{6,4},{7,5},{8,10},{9,11},{10,... | collective-permute-start | bytes 245768 | tf_op jit(solution)/shard_map/ppermute | solution.py:48
  11.8 6.1 %collective-permute-start.2 = (bf16[64,640]{1,0:T(8,128)(2,1)S(1)}, bf16[64,640]{1,0:T(8,128)(2,1)S(1)}, u32[]{:S(2)}, u32[]{:S(2)}) collective-permute-start(bf16[64,640]{1,0:T(8,128)(2,1)S(1)} %collective-permute-done.1.refs_4_), channel_id=1, source_target_pairs={{0,2},{1,3},{2,0},{3,1},{4,6},{5,7},{6,4},{7,5},{8,10},{9,11},{10,... | collective-permute-start | bytes 245768 | tf_op jit(solution)/shard_map/ppermute | solution.py:48
  17.9 2.4 %collective-permute-start.6 = (bf16[5,64,640]{2,1,0:T(8,128)(2,1)S(1)}, bf16[5,64,640]{2,1,0:T(8,128)(2,1)S(1)}, u32[]{:S(2)}, u32[]{:S(2)}) collective-permute-start(bf16[5,64,640]{2,1,0:T(8,128)(2,1)S(1)} %get-tuple-element.114), channel_id=1, source_target_pairs={{0,1},{1,0},{2,3},{3,2},{4,5},{5,4},{6,7},{7,6},{8,9},{9,8},{10,11... | collective-permute-start | bytes 1228808 | tf_op jit(solution)/shard_map/ppermute | solution.py:48
  18.0 1.9 %collective-permute-start.7 = (bf16[64,640]{1,0:T(8,128)(2,1)S(1)}, bf16[64,640]{1,0:T(8,128)(2,1)S(1)}, u32[]{:S(2)}, u32[]{:S(2)}) collective-permute-start(bf16[64,640]{1,0:T(8,128)(2,1)S(1)} %get-tuple-element.109.refs_0_), channel_id=1, source_target_pairs={{0,1},{1,0},{2,3},{3,2},{4,5},{5,4},{6,7},{7,6},{8,9},{9,8},{10,11... | collective-permute-start | bytes 245768 | tf_op jit(solution)/shard_map/ppermute | solution.py:48
  18.5 1.5 %collective-permute-start.8 = (bf16[64,640]{1,0:T(8,128)(2,1)S(1)}, bf16[64,640]{1,0:T(8,128)(2,1)S(1)}, u32[]{:S(2)}, u32[]{:S(2)}) collective-permute-start(bf16[64,640]{1,0:T(8,128)(2,1)S(1)} %collective-permute-done.refs_2_), channel_id=1, source_target_pairs={{0,1},{1,0},{2,3},{3,2},{4,5},{5,4},{6,7},{7,6},{8,9},{9,8},{10,11... | collective-permute-start | bytes 245768 | tf_op jit(solution)/shard_map/ppermute | solution.py:48
  18.6 1.5 %collective-permute-start.9 = (bf16[64,640]{1,0:T(8,128)(2,1)S(1)}, bf16[64,640]{1,0:T(8,128)(2,1)S(1)}, u32[]{:S(2)}, u32[]{:S(2)}) collective-permute-start(bf16[64,640]{1,0:T(8,128)(2,1)S(1)} %collective-permute-done.1.refs_4_), channel_id=1, source_target_pairs={{0,1},{1,0},{2,3},{3,2},{4,5},{5,4},{6,7},{7,6},{8,9},{9,8},{10,11... | collective-permute-start | bytes 245768 | tf_op jit(solution)/shard_map/ppermute | solution.py:48
  19.0 1.3 %collective-permute-start.10 = (bf16[64,640]{1,0:T(8,128)(2,1)S(1)}, bf16[64,640]{1,0:T(8,128)(2,1)S(1)}, u32[]{:S(2)}, u32[]{:S(2)}) collective-permute-start(bf16[64,640]{1,0:T(8,128)(2,1)S(1)} %collective-permute-done.2.refs_6_), channel_id=1, source_target_pairs={{0,1},{1,0},{2,3},{3,2},{4,5},{5,4},{6,7},{7,6},{8,9},{9,8},{10,11... | collective-permute-start | bytes 245768 | tf_op jit(solution)/shard_map/ppermute | solution.py:48
  20.9 9.3 %collective-permute-start.14 = (bf16[64,896]{1,0:T(8,128)(2,1)S(1)}, bf16[64,896]{1,0:T(8,128)(2,1)S(1)}, u32[]{:S(2)}, u32[]{:S(2)}) collective-permute-start(bf16[64,896]{1,0:T(8,128)(2,1)S(1)} %get-tuple-element.130), channel_id=1, source_target_pairs={{0,2},{1,3},{2,0},{3,1},{4,6},{5,7},{6,4},{7,5},{8,10},{9,11},{10,... | collective-permute-start | bytes 344072 | tf_op jit(solution)/shard_map/ppermute | solution.py:48
  22.6 11.7 %collective-permute-start.15 = (bf16[64,896]{1,0:T(8,128)(2,1)S(1)}, bf16[64,896]{1,0:T(8,128)(2,1)S(1)}, u32[]{:S(2)}, u32[]{:S(2)}) collective-permute-start(bf16[64,896]{1,0:T(8,128)(2,1)S(1)} %get-tuple-element.131), channel_id=1, source_target_pairs={{0,4},{1,5},{2,6},{3,7},{4,0},{5,1},{6,2},{7,3},{8,12},{9,13},{10,... | collective-permute-start | bytes 344072 | tf_op jit(solution)/shard_map/ppermute | solution.py:48
  24.0 10.3 %collective-permute-start.16 = (bf16[64,896]{1,0:T(8,128)(2,1)S(1)}, bf16[64,896]{1,0:T(8,128)(2,1)S(1)}, u32[]{:S(2)}, u32[]{:S(2)}) collective-permute-start(bf16[64,896]{1,0:T(8,128)(2,1)S(1)} %get-tuple-element.132), channel_id=1, source_target_pairs={{0,6},{1,7},{2,4},{3,5},{4,2},{5,3},{6,0},{7,1},{8,14},{9,15},{10,... | collective-permute-start | bytes 344072 | tf_op jit(solution)/shard_map/ppermute | solution.py:48
  25.4 10.2 %copy-start.2 = (f32[64,640]{1,0:T(8,128)S(1)}, f32[64,640]{1,0:T(8,128)}, u32[]{:S(2)}) copy-start(f32[64,640]{1,0:T(8,128)} %b_ref.1) | copy-start | bytes 491524
  27.1 7.4 %collective-permute-start.11 = (bf16[64,640]{1,0:T(8,128)(2,1)S(1)}, bf16[64,640]{1,0:T(8,128)(2,1)S(1)}, u32[]{:S(2)}, u32[]{:S(2)}) collective-permute-start(bf16[64,640]{1,0:T(8,128)(2,1)S(1)} %get-tuple-element.122), channel_id=1, source_target_pairs={{0,8},{8,0},{16,24},{24,16},{1,9},{9,1},{17,25},{25,17},{2,10},{10... | collective-permute-start | bytes 245768 | tf_op jit(solution)/shard_map/ppermute | solution.py:48
  28.7 5.9 %collective-permute-start.12 = (bf16[64,640]{1,0:T(8,128)(2,1)S(1)}, bf16[64,640]{1,0:T(8,128)(2,1)S(1)}, u32[]{:S(2)}, u32[]{:S(2)}) collective-permute-start(bf16[64,640]{1,0:T(8,128)(2,1)S(1)} %get-tuple-element.123), channel_id=1, source_target_pairs={{0,16},{8,24},{16,0},{24,8},{1,17},{9,25},{17,1},{25,9},{2,18},{10... | collective-permute-start | bytes 245768 | tf_op jit(solution)/shard_map/ppermute | solution.py:48
  30.2 5.3 %collective-permute-start.13 = (bf16[64,640]{1,0:T(8,128)(2,1)S(1)}, bf16[64,640]{1,0:T(8,128)(2,1)S(1)}, u32[]{:S(2)}, u32[]{:S(2)}) collective-permute-start(bf16[64,640]{1,0:T(8,128)(2,1)S(1)} %get-tuple-element.124), channel_id=1, source_target_pairs={{0,24},{8,16},{16,8},{24,0},{1,25},{9,17},{17,9},{25,1},{2,26},{10... | collective-permute-start | bytes 245768 | tf_op jit(solution)/shard_map/ppermute | solution.py:48
  36.1 6.5 %collective-permute-start.18 = (bf16[64,640]{1,0:T(8,128)(2,1)S(1)}, bf16[64,640]{1,0:T(8,128)(2,1)S(1)}, u32[]{:S(2)}, u32[]{:S(2)}) collective-permute-start(bf16[64,640]{1,0:T(8,128)(2,1)S(1)} %get-tuple-element.141.refs_0_), channel_id=1, source_target_pairs={{0,4},{1,5},{2,6},{3,7},{4,0},{5,1},{6,2},{7,3},{8,12},{9,13},{10,... | collective-permute-start | bytes 245768 | tf_op jit(solution)/shard_map/ppermute | solution.py:48
  38.6 6.2 %collective-permute-start.22 = (bf16[64,896]{1,0:T(8,128)(2,1)S(1)}, bf16[64,896]{1,0:T(8,128)(2,1)S(1)}, u32[]{:S(2)}, u32[]{:S(2)}) collective-permute-start(bf16[64,896]{1,0:T(8,128)(2,1)S(1)} %get-tuple-element.142.refs_0_), channel_id=1, source_target_pairs={{0,24},{8,16},{16,8},{24,0},{1,25},{9,17},{17,9},{25,1},{2,26},{10... | collective-permute-start | bytes 344072 | tf_op jit(solution)/shard_map/ppermute | solution.py:48
  41.1 5.2 %collective-permute-start.21 = (bf16[64,896]{1,0:T(8,128)(2,1)S(1)}, bf16[64,896]{1,0:T(8,128)(2,1)S(1)}, u32[]{:S(2)}, u32[]{:S(2)}) collective-permute-start(bf16[64,896]{1,0:T(8,128)(2,1)S(1)} %get-tuple-element.142.refs_0_), channel_id=1, source_target_pairs={{0,16},{8,24},{16,0},{24,8},{1,17},{9,25},{17,1},{25,9},{2,18},{10... | collective-permute-start | bytes 344072 | tf_op jit(solution)/shard_map/ppermute | solution.py:48
  41.6 5.0 %collective-permute-start.20 = (bf16[64,896]{1,0:T(8,128)(2,1)S(1)}, bf16[64,896]{1,0:T(8,128)(2,1)S(1)}, u32[]{:S(2)}, u32[]{:S(2)}) collective-permute-start(bf16[64,896]{1,0:T(8,128)(2,1)S(1)} %get-tuple-element.142.refs_0_), channel_id=1, source_target_pairs={{0,8},{8,0},{16,24},{24,16},{1,9},{9,1},{17,25},{25,17},{2,10},{10... | collective-permute-start | bytes 344072 | tf_op jit(solution)/shard_map/ppermute | solution.py:48
  42.1 6.2 %collective-permute-start.17 = (bf16[64,640]{1,0:T(8,128)(2,1)S(1)}, bf16[64,640]{1,0:T(8,128)(2,1)S(1)}, u32[]{:S(2)}, u32[]{:S(2)}) collective-permute-start(bf16[64,640]{1,0:T(8,128)(2,1)S(1)} %get-tuple-element.141.refs_0_), channel_id=1, source_target_pairs={{0,2},{1,3},{2,0},{3,1},{4,6},{5,7},{6,4},{7,5},{8,10},{9,11},{10,... | collective-permute-start | bytes 245768 | tf_op jit(solution)/shard_map/ppermute | solution.py:48
  42.7 5.6 %collective-permute-start.19 = (bf16[64,640]{1,0:T(8,128)(2,1)S(1)}, bf16[64,640]{1,0:T(8,128)(2,1)S(1)}, u32[]{:S(2)}, u32[]{:S(2)}) collective-permute-start(bf16[64,640]{1,0:T(8,128)(2,1)S(1)} %collective-permute-done.18.refs_4_), channel_id=1, source_target_pairs={{0,2},{1,3},{2,0},{3,1},{4,6},{5,7},{6,4},{7,5},{8,10},{9,11},{10,... | collective-permute-start | bytes 245768 | tf_op jit(solution)/shard_map/ppermute | solution.py:48
  48.3 2.4 %collective-permute-start.23 = (bf16[5,64,640]{2,1,0:T(8,128)(2,1)S(1)}, bf16[5,64,640]{2,1,0:T(8,128)(2,1)S(1)}, u32[]{:S(2)}, u32[]{:S(2)}) collective-permute-start(bf16[5,64,640]{2,1,0:T(8,128)(2,1)S(1)} %get-tuple-element.147), channel_id=1, source_target_pairs={{0,1},{1,0},{2,3},{3,2},{4,5},{5,4},{6,7},{7,6},{8,9},{9,8},{10,11... | collective-permute-start | bytes 1228808 | tf_op jit(solution)/shard_map/ppermute | solution.py:48
  48.4 1.9 %collective-permute-start.24 = (bf16[64,640]{1,0:T(8,128)(2,1)S(1)}, bf16[64,640]{1,0:T(8,128)(2,1)S(1)}, u32[]{:S(2)}, u32[]{:S(2)}) collective-permute-start(bf16[64,640]{1,0:T(8,128)(2,1)S(1)} %get-tuple-element.141.refs_0_), channel_id=1, source_target_pairs={{0,1},{1,0},{2,3},{3,2},{4,5},{5,4},{6,7},{7,6},{8,9},{9,8},{10,11... | collective-permute-start | bytes 245768 | tf_op jit(solution)/shard_map/ppermute | solution.py:48
  48.9 1.5 %collective-permute-start.25 = (bf16[64,640]{1,0:T(8,128)(2,1)S(1)}, bf16[64,640]{1,0:T(8,128)(2,1)S(1)}, u32[]{:S(2)}, u32[]{:S(2)}) collective-permute-start(bf16[64,640]{1,0:T(8,128)(2,1)S(1)} %collective-permute-done.17.refs_2_), channel_id=1, source_target_pairs={{0,1},{1,0},{2,3},{3,2},{4,5},{5,4},{6,7},{7,6},{8,9},{9,8},{10,11... | collective-permute-start | bytes 245768 | tf_op jit(solution)/shard_map/ppermute | solution.py:48
  48.9 1.5 %collective-permute-start.26 = (bf16[64,640]{1,0:T(8,128)(2,1)S(1)}, bf16[64,640]{1,0:T(8,128)(2,1)S(1)}, u32[]{:S(2)}, u32[]{:S(2)}) collective-permute-start(bf16[64,640]{1,0:T(8,128)(2,1)S(1)} %collective-permute-done.18.refs_4_), channel_id=1, source_target_pairs={{0,1},{1,0},{2,3},{3,2},{4,5},{5,4},{6,7},{7,6},{8,9},{9,8},{10,11... | collective-permute-start | bytes 245768 | tf_op jit(solution)/shard_map/ppermute | solution.py:48
  49.4 1.3 %collective-permute-start.27 = (bf16[64,640]{1,0:T(8,128)(2,1)S(1)}, bf16[64,640]{1,0:T(8,128)(2,1)S(1)}, u32[]{:S(2)}, u32[]{:S(2)}) collective-permute-start(bf16[64,640]{1,0:T(8,128)(2,1)S(1)} %collective-permute-done.19.refs_6_), channel_id=1, source_target_pairs={{0,1},{1,0},{2,3},{3,2},{4,5},{5,4},{6,7},{7,6},{8,9},{9,8},{10,11... | collective-permute-start | bytes 245768 | tf_op jit(solution)/shard_map/ppermute | solution.py:48
  51.3 8.3 %collective-permute-start.28 = (bf16[64,896]{1,0:T(8,128)(2,1)S(1)}, bf16[64,896]{1,0:T(8,128)(2,1)S(1)}, u32[]{:S(2)}, u32[]{:S(2)}) collective-permute-start(bf16[64,896]{1,0:T(8,128)(2,1)S(1)} %get-tuple-element.154), channel_id=1, source_target_pairs={{0,2},{1,3},{2,0},{3,1},{4,6},{5,7},{6,4},{7,5},{8,10},{9,11},{10,... | collective-permute-start | bytes 344072 | tf_op jit(solution)/shard_map/ppermute | solution.py:48
  51.6 11.9 %collective-permute-start.29 = (bf16[64,896]{1,0:T(8,128)(2,1)S(1)}, bf16[64,896]{1,0:T(8,128)(2,1)S(1)}, u32[]{:S(2)}, u32[]{:S(2)}) collective-permute-start(bf16[64,896]{1,0:T(8,128)(2,1)S(1)} %get-tuple-element.155), channel_id=1, source_target_pairs={{0,4},{1,5},{2,6},{3,7},{4,0},{5,1},{6,2},{7,3},{8,12},{9,13},{10,... | collective-permute-start | bytes 344072 | tf_op jit(solution)/shard_map/ppermute | solution.py:48
  53.3 10.2 %collective-permute-start.30 = (bf16[64,896]{1,0:T(8,128)(2,1)S(1)}, bf16[64,896]{1,0:T(8,128)(2,1)S(1)}, u32[]{:S(2)}, u32[]{:S(2)}) collective-permute-start(bf16[64,896]{1,0:T(8,128)(2,1)S(1)} %get-tuple-element.156), channel_id=1, source_target_pairs={{0,6},{1,7},{2,4},{3,5},{4,2},{5,3},{6,0},{7,1},{8,14},{9,15},{10,... | collective-permute-start | bytes 344072 | tf_op jit(solution)/shard_map/ppermute | solution.py:48
  57.5 9.1 %collective-permute-start.31 = (bf16[64,640]{1,0:T(8,128)(2,1)S(1)}, bf16[64,640]{1,0:T(8,128)(2,1)S(1)}, u32[]{:S(2)}, u32[]{:S(2)}) collective-permute-start(bf16[64,640]{1,0:T(8,128)(2,1)S(1)} %get-tuple-element.163), channel_id=1, source_target_pairs={{0,8},{8,0},{16,24},{24,16},{1,9},{9,1},{17,25},{25,17},{2,10},{10... | collective-permute-start | bytes 245768 | tf_op jit(solution)/shard_map/ppermute | solution.py:48
  58.9 7.7 %collective-permute-start.32 = (bf16[64,640]{1,0:T(8,128)(2,1)S(1)}, bf16[64,640]{1,0:T(8,128)(2,1)S(1)}, u32[]{:S(2)}, u32[]{:S(2)}) collective-permute-start(bf16[64,640]{1,0:T(8,128)(2,1)S(1)} %get-tuple-element.164), channel_id=1, source_target_pairs={{0,16},{8,24},{16,0},{24,8},{1,17},{9,25},{17,1},{25,9},{2,18},{10... | collective-permute-start | bytes 245768 | tf_op jit(solution)/shard_map/ppermute | solution.py:48
  59.6 7.0 %collective-permute-start.33 = (bf16[64,640]{1,0:T(8,128)(2,1)S(1)}, bf16[64,640]{1,0:T(8,128)(2,1)S(1)}, u32[]{:S(2)}, u32[]{:S(2)}) collective-permute-start(bf16[64,640]{1,0:T(8,128)(2,1)S(1)} %get-tuple-element.165), channel_id=1, source_target_pairs={{0,24},{8,16},{16,8},{24,0},{1,25},{9,17},{17,9},{25,1},{2,26},{10... | collective-permute-start | bytes 245768 | tf_op jit(solution)/shard_map/ppermute | solution.py:48
  67.3 6.0 %collective-permute-start.35 = (bf16[64,640]{1,0:T(8,128)(2,1)S(1)}, bf16[64,640]{1,0:T(8,128)(2,1)S(1)}, u32[]{:S(2)}, u32[]{:S(2)}) collective-permute-start(bf16[64,640]{1,0:T(8,128)(2,1)S(1)} %get-tuple-element.170.refs_0_), channel_id=1, source_target_pairs={{0,4},{1,5},{2,6},{3,7},{4,0},{5,1},{6,2},{7,3},{8,12},{9,13},{10,... | collective-permute-start | bytes 245768 | tf_op jit(solution)/shard_map/ppermute | solution.py:48
  69.4 7.0 %collective-permute-start.39 = (bf16[64,896]{1,0:T(8,128)(2,1)S(1)}, bf16[64,896]{1,0:T(8,128)(2,1)S(1)}, u32[]{:S(2)}, u32[]{:S(2)}) collective-permute-start(bf16[64,896]{1,0:T(8,128)(2,1)S(1)} %get-tuple-element.173.refs_0_.refs_8_), channel_id=1, source_target_pairs={{0,24},{8,16},{16,8},{24,0},{1,25},{9,17},{17,9},{25,1},{2,26},{10... | collective-permute-start | bytes 344072 | tf_op jit(solution)/shard_map/ppermute | solution.py:48
  71.5 5.4 %collective-permute-start.38 = (bf16[64,896]{1,0:T(8,128)(2,1)S(1)}, bf16[64,896]{1,0:T(8,128)(2,1)S(1)}, u32[]{:S(2)}, u32[]{:S(2)}) collective-permute-start(bf16[64,896]{1,0:T(8,128)(2,1)S(1)} %get-tuple-element.173.refs_0_.refs_8_), channel_id=1, source_target_pairs={{0,16},{8,24},{16,0},{24,8},{1,17},{9,25},{17,1},{25,9},{2,18},{10... | collective-permute-start | bytes 344072 | tf_op jit(solution)/shard_map/ppermute | solution.py:48
  72.2 4.8 %collective-permute-start.37 = (bf16[64,896]{1,0:T(8,128)(2,1)S(1)}, bf16[64,896]{1,0:T(8,128)(2,1)S(1)}, u32[]{:S(2)}, u32[]{:S(2)}) collective-permute-start(bf16[64,896]{1,0:T(8,128)(2,1)S(1)} %get-tuple-element.173.refs_0_.refs_8_), channel_id=1, source_target_pairs={{0,8},{8,0},{16,24},{24,16},{1,9},{9,1},{17,25},{25,17},{2,10},{10... | collective-permute-start | bytes 344072 | tf_op jit(solution)/shard_map/ppermute | solution.py:48
  72.9 6.0 %collective-permute-start.34 = (bf16[64,640]{1,0:T(8,128)(2,1)S(1)}, bf16[64,640]{1,0:T(8,128)(2,1)S(1)}, u32[]{:S(2)}, u32[]{:S(2)}) collective-permute-start(bf16[64,640]{1,0:T(8,128)(2,1)S(1)} %get-tuple-element.170.refs_0_), channel_id=1, source_target_pairs={{0,2},{1,3},{2,0},{3,1},{4,6},{5,7},{6,4},{7,5},{8,10},{9,11},{10,... | collective-permute-start | bytes 245768 | tf_op jit(solution)/shard_map/ppermute | solution.py:48
  73.2 5.7 %collective-permute-start.36 = (bf16[64,640]{1,0:T(8,128)(2,1)S(1)}, bf16[64,640]{1,0:T(8,128)(2,1)S(1)}, u32[]{:S(2)}, u32[]{:S(2)}) collective-permute-start(bf16[64,640]{1,0:T(8,128)(2,1)S(1)} %collective-permute-done.35.refs_4_), channel_id=1, source_target_pairs={{0,2},{1,3},{2,0},{3,1},{4,6},{5,7},{6,4},{7,5},{8,10},{9,11},{10,... | collective-permute-start | bytes 245768 | tf_op jit(solution)/shard_map/ppermute | solution.py:48
  78.9 2.4 %collective-permute-start.40 = (bf16[5,64,640]{2,1,0:T(8,128)(2,1)S(1)}, bf16[5,64,640]{2,1,0:T(8,128)(2,1)S(1)}, u32[]{:S(2)}, u32[]{:S(2)}) collective-permute-start(bf16[5,64,640]{2,1,0:T(8,128)(2,1)S(1)} %get-tuple-element.176), channel_id=1, source_target_pairs={{0,1},{1,0},{2,3},{3,2},{4,5},{5,4},{6,7},{7,6},{8,9},{9,8},{10,11... | collective-permute-start | bytes 1228808 | tf_op jit(solution)/shard_map/ppermute | solution.py:48
  79.0 1.9 %collective-permute-start.41 = (bf16[64,640]{1,0:T(8,128)(2,1)S(1)}, bf16[64,640]{1,0:T(8,128)(2,1)S(1)}, u32[]{:S(2)}, u32[]{:S(2)}) collective-permute-start(bf16[64,640]{1,0:T(8,128)(2,1)S(1)} %get-tuple-element.170.refs_0_), channel_id=1, source_target_pairs={{0,1},{1,0},{2,3},{3,2},{4,5},{5,4},{6,7},{7,6},{8,9},{9,8},{10,11... | collective-permute-start | bytes 245768 | tf_op jit(solution)/shard_map/ppermute | solution.py:48
  79.5 1.5 %collective-permute-start.42 = (bf16[64,640]{1,0:T(8,128)(2,1)S(1)}, bf16[64,640]{1,0:T(8,128)(2,1)S(1)}, u32[]{:S(2)}, u32[]{:S(2)}) collective-permute-start(bf16[64,640]{1,0:T(8,128)(2,1)S(1)} %collective-permute-done.34.refs_2_), channel_id=1, source_target_pairs={{0,1},{1,0},{2,3},{3,2},{4,5},{5,4},{6,7},{7,6},{8,9},{9,8},{10,11... | collective-permute-start | bytes 245768 | tf_op jit(solution)/shard_map/ppermute | solution.py:48
  79.6 1.5 %collective-permute-start.43 = (bf16[64,640]{1,0:T(8,128)(2,1)S(1)}, bf16[64,640]{1,0:T(8,128)(2,1)S(1)}, u32[]{:S(2)}, u32[]{:S(2)}) collective-permute-start(bf16[64,640]{1,0:T(8,128)(2,1)S(1)} %collective-permute-done.35.refs_4_), channel_id=1, source_target_pairs={{0,1},{1,0},{2,3},{3,2},{4,5},{5,4},{6,7},{7,6},{8,9},{9,8},{10,11... | collective-permute-start | bytes 245768 | tf_op jit(solution)/shard_map/ppermute | solution.py:48
  80.0 1.3 %collective-permute-start.44 = (bf16[64,640]{1,0:T(8,128)(2,1)S(1)}, bf16[64,640]{1,0:T(8,128)(2,1)S(1)}, u32[]{:S(2)}, u32[]{:S(2)}) collective-permute-start(bf16[64,640]{1,0:T(8,128)(2,1)S(1)} %collective-permute-done.36.refs_6_), channel_id=1, source_target_pairs={{0,1},{1,0},{2,3},{3,2},{4,5},{5,4},{6,7},{7,6},{8,9},{9,8},{10,11... | collective-permute-start | bytes 245768 | tf_op jit(solution)/shard_map/ppermute | solution.py:48
  81.9 8.9 %collective-permute-start.48 = (bf16[64,896]{1,0:T(8,128)(2,1)S(1)}, bf16[64,896]{1,0:T(8,128)(2,1)S(1)}, u32[]{:S(2)}, u32[]{:S(2)}) collective-permute-start(bf16[64,896]{1,0:T(8,128)(2,1)S(1)} %get-tuple-element.194), channel_id=1, source_target_pairs={{0,2},{1,3},{2,0},{3,1},{4,6},{5,7},{6,4},{7,5},{8,10},{9,11},{10,... | collective-permute-start | bytes 344072 | tf_op jit(solution)/shard_map/ppermute | solution.py:48
  82.3 11.8 %collective-permute-start.49 = (bf16[64,896]{1,0:T(8,128)(2,1)S(1)}, bf16[64,896]{1,0:T(8,128)(2,1)S(1)}, u32[]{:S(2)}, u32[]{:S(2)}) collective-permute-start(bf16[64,896]{1,0:T(8,128)(2,1)S(1)} %get-tuple-element.195), channel_id=1, source_target_pairs={{0,4},{1,5},{2,6},{3,7},{4,0},{5,1},{6,2},{7,3},{8,12},{9,13},{10,... | collective-permute-start | bytes 344072 | tf_op jit(solution)/shard_map/ppermute | solution.py:48
  85.0 9.2 %collective-permute-start.50 = (bf16[64,896]{1,0:T(8,128)(2,1)S(1)}, bf16[64,896]{1,0:T(8,128)(2,1)S(1)}, u32[]{:S(2)}, u32[]{:S(2)}) collective-permute-start(bf16[64,896]{1,0:T(8,128)(2,1)S(1)} %get-tuple-element.196), channel_id=1, source_target_pairs={{0,6},{1,7},{2,4},{3,5},{4,2},{5,3},{6,0},{7,1},{8,14},{9,15},{10,... | collective-permute-start | bytes 344072 | tf_op jit(solution)/shard_map/ppermute | solution.py:48
  88.8 8.8 %collective-permute-start.45 = (bf16[64,768]{1,0:T(8,128)(2,1)S(1)}, bf16[64,768]{1,0:T(8,128)(2,1)S(1)}, u32[]{:S(2)}, u32[]{:S(2)}) collective-permute-start(bf16[64,768]{1,0:T(8,128)(2,1)S(1)} %get-tuple-element.186), channel_id=1, source_target_pairs={{0,8},{8,0},{16,24},{24,16},{1,9},{9,1},{17,25},{25,17},{2,10},{10... | collective-permute-start | bytes 294920 | tf_op jit(solution)/shard_map/ppermute | solution.py:48
  89.8 7.8 %collective-permute-start.46 = (bf16[64,768]{1,0:T(8,128)(2,1)S(1)}, bf16[64,768]{1,0:T(8,128)(2,1)S(1)}, u32[]{:S(2)}, u32[]{:S(2)}) collective-permute-start(bf16[64,768]{1,0:T(8,128)(2,1)S(1)} %get-tuple-element.187), channel_id=1, source_target_pairs={{0,16},{8,24},{16,0},{24,8},{1,17},{9,25},{17,1},{25,9},{2,18},{10... | collective-permute-start | bytes 294920 | tf_op jit(solution)/shard_map/ppermute | solution.py:48
  90.8 6.8 %collective-permute-start.47 = (bf16[64,768]{1,0:T(8,128)(2,1)S(1)}, bf16[64,768]{1,0:T(8,128)(2,1)S(1)}, u32[]{:S(2)}, u32[]{:S(2)}) collective-permute-start(bf16[64,768]{1,0:T(8,128)(2,1)S(1)} %get-tuple-element.188), channel_id=1, source_target_pairs={{0,24},{8,16},{16,8},{24,0},{1,25},{9,17},{17,9},{25,1},{2,26},{10... | collective-permute-start | bytes 294920 | tf_op jit(solution)/shard_map/ppermute | solution.py:48
  97.7 7.2 %collective-permute-start.53 = (f32[64,64]{1,0:T(8,128)S(1)}, f32[64,64]{1,0:T(8,128)S(1)}, u32[]{:S(2)}, u32[]{:S(2)}) collective-permute-start(f32[64,64]{1,0:T(8,128)S(1)} %last_gram.1), channel_id=1, source_target_pairs={{0,6},{1,7},{2,4},{3,5},{4,2},{5,3},{6,0},{7,1},{8,14},{9,15},{10,... | collective-permute-start | bytes 49160 | tf_op jit(solution)/shard_map/ppermute | solution.py:48
  100.2 4.8 %collective-permute-start.52 = (f32[64,64]{1,0:T(8,128)S(1)}, f32[64,64]{1,0:T(8,128)S(1)}, u32[]{:S(2)}, u32[]{:S(2)}) collective-permute-start(f32[64,64]{1,0:T(8,128)S(1)} %last_gram.1), channel_id=1, source_target_pairs={{0,4},{1,5},{2,6},{3,7},{4,0},{5,1},{6,2},{7,3},{8,12},{9,13},{10,... | collective-permute-start | bytes 49160 | tf_op jit(solution)/shard_map/ppermute | solution.py:48
  101.2 4.1 %collective-permute-start.51 = (f32[64,64]{1,0:T(8,128)S(1)}, f32[64,64]{1,0:T(8,128)S(1)}, u32[]{:S(2)}, u32[]{:S(2)}) collective-permute-start(f32[64,64]{1,0:T(8,128)S(1)} %last_gram.1), channel_id=1, source_target_pairs={{0,2},{1,3},{2,0},{3,1},{4,6},{5,7},{6,4},{7,5},{8,10},{9,11},{10,... | collective-permute-start | bytes 49160 | tf_op jit(solution)/shard_map/ppermute | solution.py:48
  105.3 1.3 %collective-permute-start.54 = (f32[64,64]{1,0:T(8,128)S(1)}, f32[64,64]{1,0:T(8,128)S(1)}, u32[]{:S(2)}, u32[]{:S(2)}) collective-permute-start(f32[64,64]{1,0:T(8,128)S(1)} %add_add_fusion.both_ref), channel_id=1, source_target_pairs={{0,1},{1,0},{2,3},{3,2},{4,5},{5,4},{6,7},{7,6},{8,9},{9,8},{10,11... | collective-permute-start | bytes 49160 | tf_op jit(solution)/shard_map/ppermute | solution.py:48
  (1 other events, 0.9 us)
